TPU v7x, 32 devices: a whole 2x2x4 slice. The times are simulated.
32 devices in a mesh: groups: 2 (over y), dp: 16 (over z, x, core).
Axes of the slice: x: 2, y: 2, z: 4, core: 2. Of those that a mesh axis runs over, the one named last changes fastest.
Arguments:
- tile_values: float32 [4096, 128, 128], P(('groups', 'dp')), parts along dimension 0, may hold values from 0.0001 to 1
- tile_row: int32 [4096], P(('groups', 'dp')), parts along dimension 0, may hold values from 0 to 31, as said below
- tile_owner: int32 [4096, 1], P(('groups', 'dp')), parts along dimension 0, may hold values from 0 to 15; in each aligned block of 128 rows (0 to 127, 128 to 255, ...) at most 16 rows name the same one
- tile_sub: int32 [4096], P(('groups', 'dp')), parts along dimension 0, may hold values from 0 to 15
- labels: int32 [8192], P(('groups', 'dp')), parts along dimension 0, may hold values from 0 to 511
Outputs:
- centroids: bfloat16 [1024, 32768], P('groups', 'dp'), parts along dimension 0
- similarity: float32 [8192], P(('groups', 'dp')), parts along dimension 0
There are 2 independent parts, one for each index of `groups`. A program takes and returns all parts, laid end to end along the dimension named above; each array names one. Nothing has to cross between parts.
Inputs may be any that keep to these rules, and one draw needn't show every extreme that they name: `tile_owner`: among the 128 tiles of one index of dp (aligned blocks), at most 16 name the same column group, a bound that some block reaches. `tile_row`: most tiles belong to a row block of their own index of dp; others to any row block.
All inputs are finite; a program needn't handle non-finite values.
Results may differ from a plain program's by a relative error of at most 0.0038.
Values may be sent and summed in bfloat16 or wider, within the bound.
No kernel may reach another device: no remote copies, remote signals or barrier semaphores. Data moves between devices by JAX's collectives and lax.ppermute only.
A program may use at most 128 MiB of HBM per device.

v0:
```python
import functools
import math

import jax
import jax.numpy as jnp
import numpy as np
from jax import lax
from jax.experimental import pallas as pl
from jax.experimental.pallas import tpu as pltpu
from jax.sharding import PartitionSpec as P

K = 512
TB_OWN = 16
LANES = 128
EPSILON = 1e-06
CODE_TOP = 65535.0
CODE_SHIFT = 32768
VMEM_BYTES = 56 * 1024 * 1024
STEP_TILES = 16
PARTS = (0.0, 5 / 16, 10 / 16, 14 / 16, 1.0)
CACHED_BLOCKS = 64
QUAD = 4
NT = (((1,), (1,)), ((), ()))


def lane_sums(values):
    ones = jnp.ones((8, LANES), jnp.bfloat16)
    high = values.astype(jnp.bfloat16)
    low = (values - high.astype(jnp.float32)).astype(jnp.bfloat16)
    return lax.dot_general(ones, high, NT, preferred_element_type=jnp.float32) + lax.dot_general(
        ones, low, NT, preferred_element_type=jnp.float32
    )


def params():
    return pltpu.CompilerParams(vmem_limit_bytes=VMEM_BYTES)


SMEM = pl.BlockSpec(memory_space=pltpu.SMEM)
VMEM = pl.BlockSpec(memory_space=pltpu.VMEM)
ANY = pl.BlockSpec(memory_space=pl.ANY)


def pack_kernel(cuts, owner_ref, x_ref, *refs):
    parts = len(cuts) - 1
    outs = refs[:parts]
    coded, used, place, sems = refs[parts:]
    step = pl.program_id(0)
    tiles = x_ref.shape[0]
    devices = used.shape[0]

    @pl.when(step == 0)
    def _():
        def clear(d, carry):
            used[d] = 0
            return carry

        lax.fori_loop(0, devices, clear, 0)

    def act(t, what):
        spot = place[t]
        owner, rank = spot // cuts[-1], spot % cuts[-1]
        for q in range(parts):

            @pl.when((rank >= cuts[q]) & (rank < cuts[q + 1]))
            def _(q=q):
                copy = pltpu.make_async_copy(
                    coded.at[t], outs[q].at[owner, rank - cuts[q]], sems.at[t]
                )
                what(copy)

    def one_tile(i, carry):
        t = step * tiles + i
        x = x_ref[i]
        root = x * lax.rsqrt(x)
        code = (root * CODE_TOP + 0.5).astype(jnp.int32) - CODE_SHIFT
        coded[t] = code.astype(jnp.int16)
        owner = owner_ref[t]
        rank = used[owner]
        used[owner] = rank + 1
        place[t] = owner * cuts[-1] + rank
        act(t, lambda copy: copy.start())
        return carry

    lax.fori_loop(0, tiles, one_tile, 0)

    @pl.when(step == pl.num_programs(0) - 1)
    def _():
        def finish(t, carry):
            act(t, lambda copy: copy.wait())
            return carry

        lax.fori_loop(0, coded.shape[0], finish, 0)


def pack(tile_values, owner, devices, cuts):
    tiles = tile_values.shape[0]
    step = math.gcd(STEP_TILES, tiles)
    return pl.pallas_call(
        functools.partial(pack_kernel, cuts),
        grid=(tiles // step,),
        in_specs=[SMEM, pl.BlockSpec((step, LANES, LANES), lambda i: (i, 0, 0))],
        out_specs=[ANY] * (len(cuts) - 1),
        out_shape=[
            jax.ShapeDtypeStruct((devices, high - low, LANES, LANES), jnp.int16)
            for low, high in zip(cuts, cuts[1:])
        ],
        scratch_shapes=[
            pltpu.VMEM((tiles, LANES, LANES), jnp.int16),
            pltpu.SMEM((devices,), jnp.int32),
            pltpu.SMEM((tiles,), jnp.int32),
            pltpu.SemaphoreType.DMA((tiles,)),
        ],
        compiler_params=params(),
        cost_estimate=pl.CostEstimate(
            flops=8 * tile_values.size,
            bytes_accessed=6 * tile_values.size,
            transcendentals=tile_values.size,
        ),
        name="pack",
    )(owner, tile_values)


def norms_kernel(row_ref, x_ref, sq_ref, square):
    step = pl.program_id(0)
    tiles = x_ref.shape[0]

    @pl.when(step == 0)
    def _():
        square[...] = jnp.zeros_like(square)

    def one_tile(i, carry):
        x = x_ref[i]
        square[row_ref[step * tiles + i]] += x * x
        return carry

    lax.fori_loop(0, tiles, one_tile, 0)

    @pl.when(step == pl.num_programs(0) - 1)
    def _():
        def reduce_block(r, carry):
            sq_ref[pl.ds(r, 1), :] = lane_sums(square[r])[:1]
            return carry

        lax.fori_loop(0, square.shape[0], reduce_block, 0)


def norms(tile_values, tile_row, blocks):
    tiles = tile_values.shape[0]
    step = math.gcd(STEP_TILES, tiles)
    return pl.pallas_call(
        norms_kernel,
        grid=(tiles // step,),
        in_specs=[SMEM, pl.BlockSpec((step, LANES, LANES), lambda i: (i, 0, 0))],
        out_specs=pl.BlockSpec((blocks, LANES), lambda i: (0, 0)),
        out_shape=jax.ShapeDtypeStruct((blocks, LANES), jnp.float32),
        scratch_shapes=[pltpu.VMEM((blocks, LANES, LANES), jnp.float32)],
        compiler_params=params(),
        cost_estimate=pl.CostEstimate(
            flops=8 * tile_values.size, bytes_accessed=4 * tile_values.size, transcendentals=0
        ),
        name="norms",
    )(tile_row, tile_values)


def fold_kernel(cap, low, part, first, last, order_ref, bound_ref, meta_ref, labels_ref, inv_ref,
                x_ref, *refs):
    normed, sums = refs[0 if first else 1], refs[1 if first else 2]
    if first:
        sums[...] = jnp.zeros_like(sums)
    else:
        pltpu.sync_copy(refs[0], sums)
    cluster = lax.broadcasted_iota(jnp.int32, (K, LANES), 0)

    def decoded(slot, row):
        at = (slot // cap, slot % cap - low)
        root = x_ref[at].astype(jnp.int32).astype(jnp.float32) + float(CODE_SHIFT)
        tile = (root * root * inv_ref[row]).astype(jnp.bfloat16)
        normed[at] = tile
        return tile

    def picked(row):
        hot = cluster == labels_ref[pl.ds(row, 1), :]
        return jnp.where(hot, 1.0, 0.0).astype(jnp.bfloat16)

    def one_sub(sub, carry):
        start = bound_ref[part * (TB_OWN + 1) + sub]
        end = bound_ref[part * (TB_OWN + 1) + sub + 1]
        at = (slice(None), pl.ds(pl.multiple_of(sub * LANES, LANES), LANES))

        def one_pair(p, carry):
            place = start + 2 * p
            more = place + 1 < end
            slot_a = order_ref[place]
            slot_b = order_ref[jnp.where(more, place + 1, place)]
            row_a, row_b = meta_ref[slot_a] // TB_OWN, meta_ref[slot_b] // TB_OWN
            tiles = jnp.concatenate([decoded(slot_a, row_a), decoded(slot_b, row_b)], axis=0)
            none = labels_ref.shape[0] - 1
            pick = jnp.concatenate([picked(row_a), picked(jnp.where(more, row_b, none))], axis=1)
            sums[at] += jnp.dot(pick, tiles, preferred_element_type=jnp.float32)
            return carry

        lax.fori_loop(0, (end - start + 1) // 2, one_pair, 0)
        return carry

    lax.fori_loop(0, TB_OWN, one_sub, 0)
    if last:
        total = jnp.zeros((K, LANES), jnp.float32)
        for sub in range(TB_OWN):
            part = sums[:, sub * LANES : (sub + 1) * LANES]
            total = total + part * part
        refs[-1][...] = lane_sums(total)


def fold(cap, low, part, order, bounds, meta, labels, inverse, x, sums, last):
    first = sums is None
    out_shape = [
        jax.ShapeDtypeStruct(x.shape, jnp.bfloat16),
        jax.ShapeDtypeStruct((K, TB_OWN * LANES), jnp.float32),
    ]
    if last:
        out_shape += [jax.ShapeDtypeStruct((8, K), jnp.float32)]
    return pl.pallas_call(
        functools.partial(fold_kernel, cap, low, part, first, last),
        in_specs=[SMEM] * 3 + [VMEM] * 3 + ([] if first else [ANY]),
        out_specs=[VMEM] * len(out_shape),
        out_shape=out_shape,
        compiler_params=params(),
        cost_estimate=pl.CostEstimate(
            flops=x.size * K * 8,
            bytes_accessed=4 * x.size + 4 * inverse.size + 8 * K * TB_OWN * LANES,
            transcendentals=0,
        ),
        name="fold",
    )(order, bounds, meta, labels, inverse, x, *([] if first else [sums]))


def score_kernel(parts, cached, order_ref, bound_ref, meta_ref, place_ref, hot_ref, sums_ref, *refs):
    normed, out_ref = refs[:parts], refs[parts]
    narrow, tiles, products, hot_some, sems = refs[parts + 1 :]
    copies, base = [], 0
    for q, n_ref in enumerate(normed):
        count = n_ref.shape[0]
        copies.append(pltpu.make_async_copy(n_ref, tiles.at[pl.ds(base, count)], sems.at[q]))
        base += count
    for copy in copies:
        copy.start()
    products[...] = jnp.zeros_like(products)
    narrow[...] = sums_ref[...].astype(jnp.bfloat16)
    for copy in copies:
        copy.wait()
    none = products.shape[0] - 1

    def one_sub(sub, carry):
        start, end = bound_ref[sub], bound_ref[sub + 1]
        at = (slice(None), pl.ds(pl.multiple_of(sub * LANES, LANES), LANES))

        def one_quad(p, carry):
            rows, spots = [], []
            for j in range(QUAD):
                place = start + QUAD * p + j
                held = place < end
                slot = order_ref[jnp.where(held, place, start)]
                rows.append(jnp.where(held, meta_ref[slot] // TB_OWN, none))
                spots.append(place_ref[slot])
            if cached:
                hots = [hot_ref[row] for row in rows]
            else:
                for j, row in enumerate(rows):
                    pltpu.sync_copy(hot_ref.at[row], hot_some.at[j])
                hots = [hot_some[j] for j in range(QUAD)]
            pick = jnp.concatenate(hots, axis=0)
            chosen = jnp.dot(pick, narrow[at], preferred_element_type=jnp.float32)
            for j in range(QUAD):
                part = chosen[j * LANES : (j + 1) * LANES]
                products[rows[j]] += part * tiles[spots[j]].astype(jnp.float32)
            return carry

        lax.fori_loop(0, (end - start + QUAD - 1) // QUAD, one_quad, 0)
        return carry

    lax.fori_loop(0, TB_OWN, one_sub, 0)

    def reduce_block(r, carry):
        out_ref[pl.ds(r, 1), :] = lane_sums(products[r])[:1]
        return carry

    lax.fori_loop(0, none, reduce_block, 0)


def score(order, bounds, meta, place, hot, sums, normed):
    blocks = hot.shape[0] - 1
    cached = blocks <= CACHED_BLOCKS
    flat = [x.reshape((-1, LANES, LANES)) for x in normed]
    slots = sum(x.shape[0] for x in flat)
    return pl.pallas_call(
        functools.partial(score_kernel, len(flat), cached),
        in_specs=[SMEM] * 4 + [VMEM if cached else ANY, VMEM] + [ANY] * len(flat),
        out_specs=VMEM,
        out_shape=jax.ShapeDtypeStruct((blocks, LANES), jnp.float32),
        scratch_shapes=[
            pltpu.VMEM(sums.shape, jnp.bfloat16),
            pltpu.VMEM((slots, LANES, LANES), jnp.bfloat16),
            pltpu.VMEM((blocks + 1, LANES, LANES), jnp.float32),
            pltpu.VMEM((QUAD, LANES, K), jnp.bfloat16),
            pltpu.SemaphoreType.DMA((len(flat),)),
        ],
        compiler_params=params(),
        cost_estimate=pl.CostEstimate(
            flops=slots * LANES * LANES * K * 2,
            bytes_accessed=slots * 2 * LANES * LANES + 4 * sums.size,
            transcendentals=0,
        ),
        name="score",
    )(order, bounds, meta, place, hot, sums, *flat)


def to_all(values):
    devices = lax.axis_size("dp")
    rows = jnp.broadcast_to(values[None], (devices, *values.shape))
    return lax.all_to_all(rows, "dp", split_axis=0, concat_axis=0, tiled=True)


def sorted_slots(key, top):
    slots = jnp.arange(key.shape[0], dtype=jnp.int32)
    ahead = (key[None, :] < key[:, None]) | (
        (key[None, :] == key[:, None]) & (slots[None, :] < slots[:, None])
    )
    position = jnp.sum(ahead.astype(jnp.int32), axis=1)
    here = position[None, :] == slots[:, None]
    order = jnp.sum(jnp.where(here, slots[None, :], 0), axis=1)
    levels = jnp.arange(top + 1, dtype=jnp.int32)
    bounds = jnp.sum((key[None, :] < levels[:, None]).astype(jnp.int32), axis=1)
    return order, bounds


def shards(tile_values, tile_row, tile_owner, tile_sub, labels):
    devices = lax.axis_size("dp")
    tiles = tile_values.shape[0]
    home = labels.shape[0]
    blocks = home // LANES * devices
    cap = max(2, 2 * tiles // devices)
    cuts = tuple(sorted({int(cap * share) for share in PARTS}))
    parts = len(cuts) - 1
    here = lax.axis_index("dp").astype(jnp.int32)
    owner = tile_owner[:, 0]

    described = jnp.concatenate([labels, owner, tile_row * TB_OWN + tile_sub])
    all_described = to_all(described)
    outgoing = pack(tile_values, owner, devices, cuts)
    incoming = [
        lax.all_to_all(x, "dp", split_axis=0, concat_axis=0, tiled=True) for x in outgoing
    ]
    after, unused = lax.optimization_barrier((tile_values, outgoing[0]))
    partial_sq = norms(after, tile_row, blocks)
    row_sq = jnp.sum(to_all(partial_sq), axis=0)

    all_labels = all_described[:, :home].reshape(blocks, LANES)
    padded_labels = jnp.concatenate([all_labels, jnp.full((1, LANES), -1, jnp.int32)])
    hot = (padded_labels[:, :, None] == jnp.arange(K, dtype=jnp.int32)).astype(jnp.bfloat16)
    mine = all_described[:, home : home + tiles] == here
    code = all_described[:, home + tiles :]
    earlier = jnp.arange(tiles)[:, None] < jnp.arange(tiles)[None, :]
    rank = jnp.dot(
        mine.astype(jnp.bfloat16), earlier.astype(jnp.bfloat16), preferred_element_type=jnp.float32
    ).astype(jnp.int32)
    chosen = mine[:, None, :] & (rank[:, None, :] == jnp.arange(cap)[None, :, None])
    meta = jnp.sum(jnp.where(chosen, code[:, None, :] + 1, 0), axis=2).reshape(-1) - 1
    sub = jnp.where(meta < 0, TB_OWN, meta % TB_OWN)
    slot_rank = np.arange(devices * cap) % cap
    slot_part = np.searchsorted(np.array(cuts), slot_rank, side="right") - 1
    low, high = np.array(cuts)[slot_part], np.array(cuts)[slot_part + 1]
    place = (devices * low + np.arange(devices * cap) // cap * (high - low) + slot_rank - low)
    place = jnp.asarray(place, jnp.int32)
    fold_key = jnp.asarray(slot_part * (TB_OWN + 1), jnp.int32) + sub
    fold_order, fold_bounds = sorted_slots(fold_key, parts * (TB_OWN + 1))
    score_order, score_bounds = sorted_slots(sub, TB_OWN)

    inverse = lax.rsqrt(row_sq + EPSILON)
    scale = jnp.broadcast_to((inverse * (1.0 / CODE_TOP**2))[:, :, None], (blocks, LANES, LANES))
    sums, normed = None, []
    for q in range(parts):
        got = fold(
            cap, cuts[q], q, fold_order, fold_bounds, meta, padded_labels, scale,
            incoming[q], sums, q == parts - 1,
        )
        normed.append(got[0])
        sums = got[1]
    cluster_sq = jnp.sum(to_all(got[2][0]), axis=0)
    own_scale = lax.rsqrt(cluster_sq + EPSILON)
    partial = score(score_order, score_bounds, meta, place, hot, sums, normed)
    returned = lax.all_to_all(
        partial.reshape(devices, home), "dp", split_axis=0, concat_axis=0, tiled=True
    )
    vocab_size = TB_OWN * LANES * devices
    centroid = sums * own_scale[:, None]
    centroids = (centroid * math.sqrt(vocab_size)).astype(jnp.bfloat16)
    is_label = labels[:, None] == jnp.arange(K, dtype=jnp.int32)[None, :]
    doc_scale = jnp.sum(jnp.where(is_label, own_scale[None, :], 0.0), axis=1)
    return (centroids, jnp.sum(returned, axis=0) * doc_scale)


def solution(mesh):
    return jax.shard_map(
        shards,
        mesh=mesh,
        in_specs=(
            P(("groups", "dp"), None, None),
            P(("groups", "dp")),
            P(("groups", "dp"), None),
            P(("groups", "dp")),
            P(("groups", "dp")),
        ),
        out_specs=(P("groups", "dp"), P(("groups", "dp"))),
        check_vma=False,
    )
```

profile of v0, /device:TPU:0, one launch (start us, length us, event | category | flops | bytes accessed | tf_op | source)
XLA Modules:
  0.0 361.0 jit_solution(10285818174665955035)
XLA Ops:
  1.3 0.7 pad_add_fusion
  2.6 7.4 %all-to-all-start = ((s32[16,1,512]{2,1,0:T(1,128)}), s32[16,1,512]{2,1,0:T(1,128)S(1)}, u32[]{:S(2)}, u32[]{:S(2)}) async-start(s32[16,1,512]{2,1,0:T(1,128)} %broadcast_in_dim.46), calls=%async_computation | async-start | bytes 65536 | tf_op jit(solution)/shard_map/all_to_all | solution.py:321
  10.0 11.8 %pack.1 = (s16[16,5,128,128]{3,2,1,0:T(8,128)(2,1)}, s16[16,5,128,128]{3,2,1,0:T(8,128)(2,1)}, s16[16,4,128,128]{3,2,1,0:T(8,128)(2,1)}, s16[16,2,128,128]{3,2,1,0:T(8,128)(2,1)}) custom-call(s32[128]{0:T(128)} %bitcast.21, f32[128,128,128]{2,1,0:T(8,128)} %x_ref.2), custom_call_target="tpu_custom_call" | custom-call | flops 16777216 | bytes 12582912 | tf_op jit(solution)/shard_map/pack/pallas_call | solution.py:99
  21.8 11.9 %norms.1 = f32[32,128]{1,0:T(8,128)} custom-call(s32[128]{0:T(128)} %row_ref.1, f32[128,128,128]{2,1,0:T(8,128)} %x_ref.2), custom_call_target="tpu_custom_call" | custom-call | flops 16777216 | bytes 8388608 | tf_op jit(solution)/shard_map/norms/pallas_call | solution.py:151
  33.8 0.9 broadcast_in_dim.51
  34.7 15.8 %all_to_all.49 = f32[16,32,128]{2,1,0:T(8,128)S(1)} all-to-all(f32[16,32,128]{2,1,0:T(8,128)S(1)} %broadcast_in_dim.51), channel_id=1, replica_groups=mesh['groups'=2,'dp'=16] {'dp'}, dimensions={0} | all-to-all | bytes 524288 | tf_op jit(solution)/shard_map/all_to_all | solution.py:321
  50.5 51.7 %all_to_all.50.x_ref = s16[16,4,128,128]{3,2,1,0:T(8,128)(2,1)} all-to-all(s16[16,4,128,128]{3,2,1,0:T(8,128)(2,1)} %get-tuple-element.19), channel_id=1, replica_groups=mesh['groups'=2,'dp'=16] {'dp'}, dimensions={0} | all-to-all | bytes 4194304 | tf_op jit(solution)/shard_map/all_to_all | solution.py:352
  102.2 63.5 %all_to_all.51.x_ref = s16[16,5,128,128]{3,2,1,0:T(8,128)(2,1)} all-to-all(s16[16,5,128,128]{3,2,1,0:T(8,128)(2,1)S(1)} %copy-done.1), channel_id=1, replica_groups=mesh['groups'=2,'dp'=16] {'dp'}, dimensions={0} | all-to-all | bytes 5242880 | tf_op jit(solution)/shard_map/all_to_all | solution.py:352
  165.7 5.1 %all-to-all-start.5 = ((s16[16,5,128,128]{3,2,1,0:T(8,128)(2,1)}), s16[16,5,128,128]{3,2,1,0:T(8,128)(2,1)S(1)}, u32[]{:S(2)}, u32[]{:S(2)}) async-start(s16[16,5,128,128]{3,2,1,0:T(8,128)(2,1)} %get-tuple-element.16), calls=%async_computation.5 | async-start | bytes 5242880 | tf_op jit(solution)/shard_map/all_to_all | solution.py:352
  174.7 46.4 %all-to-all-done.5.x_ref = s16[16,5,128,128]{3,2,1,0:T(8,128)(2,1)S(1)} async-done(((s16[16,5,128,128]{3,2,1,0:T(8,128)(2,1)}), s16[16,5,128,128]{3,2,1,0:T(8,128)(2,1)S(1)}, u32[]{:S(2)}, u32[]{:S(2)}) %all-to-all-start.5) | async-done | bytes 2621472 | tf_op jit(solution)/shard_map/all_to_all | solution.py:352
  221.1 13.4 %all-to-all-start.2 = ((s16[16,2,128,128]{3,2,1,0:T(8,128)(2,1)}), s16[16,2,128,128]{3,2,1,0:T(8,128)(2,1)}, u32[]{:S(2)}, u32[]{:S(2)}) async-start(s16[16,2,128,128]{3,2,1,0:T(8,128)(2,1)} %get-tuple-element.18), calls=%async_computation.2 | async-start | bytes 2097152 | tf_op jit(solution)/shard_map/all_to_all | solution.py:352
  234.5 2.5 fusion.hot_ref
  237.0 1.9 broadcast_in_dim.52.inv_ref
  239.0 16.4 %fold.4 = (bf16[16,5,128,128]{3,2,1,0:T(8,128)(2,1)}, f32[512,2048]{1,0:T(8,128)}) custom-call(s32[256]{0:T(256)} %select_reduce_fusion.2.order_ref, s32[69]{0:T(128)} %convert_reduce_fusion.2.bound_ref, s32[256]{0:T(256)} %copy-done.3, s32[33,128]{1,0:T(8,128)} %copy-done.2, f32[32,128,128]{2,1,0:T(8,128)} %broadcast_in_dim.52.inv_ref, ...), custom_call_target="tpu_custom_call" | custom-call | flops 5368709120 | bytes 15728640 | tf_op jit(solution)/shard_map/fold/pallas_call | solution.py:223
  255.4 14.2 %fold.5 = (bf16[16,5,128,128]{3,2,1,0:T(8,128)(2,1)}, f32[512,2048]{1,0:T(8,128)}) custom-call(s32[256]{0:T(256)} %select_reduce_fusion.2.order_ref, s32[69]{0:T(128)} %convert_reduce_fusion.2.bound_ref, s32[256]{0:T(256)} %copy-done.3, s32[33,128]{1,0:T(8,128)} %copy-done.2, f32[32,128,128]{2,1,0:T(8,128)} %broadcast_in_dim.52.inv_ref, ...), custom_call_target="tpu_custom_call" | custom-call | flops 5368709120 | bytes 15728640 | tf_op jit(solution)/shard_map/fold/pallas_call | solution.py:223
  269.6 7.7 %fold.6 = (bf16[16,4,128,128]{3,2,1,0:T(8,128)(2,1)}, f32[512,2048]{1,0:T(8,128)}) custom-call(s32[256]{0:T(256)} %select_reduce_fusion.2.order_ref, s32[69]{0:T(128)} %convert_reduce_fusion.2.bound_ref, s32[256]{0:T(256)} %copy-done.3, s32[33,128]{1,0:T(8,128)} %copy-done.2, f32[32,128,128]{2,1,0:T(8,128)} %broadcast_in_dim.52.inv_ref, ...), custom_call_target="tpu_custom_call" | custom-call | flops 4294967296 | bytes 14680064 | tf_op jit(solution)/shard_map/fold/pallas_call | solution.py:223
  277.3 6.4 %fold.7 = (bf16[16,2,128,128]{3,2,1,0:T(8,128)(2,1)}, f32[512,2048]{1,0:T(8,128)}, f32[8,512]{1,0:T(8,128)}) custom-call(s32[256]{0:T(256)} %select_reduce_fusion.2.order_ref, s32[69]{0:T(128)} %convert_reduce_fusion.2.bound_ref, s32[256]{0:T(256)} %copy-done.3, s32[33,128]{1,0:T(8,128)} %copy-done.2, f32[32,128,128]{2,1,0:T(8,128)} %broadcast_in_dim.52.inv_ref, ...), custom_call_target="tpu_custom_call" | custom-call | flops 2147483648 | bytes 12582912 | tf_op jit(solution)/shard_map/fold/pallas_call | solution.py:223
  283.6 24.4 %score.1 = f32[32,128]{1,0:T(8,128)} custom-call(s32[256]{0:T(256)} %select_reduce_fusion.1.order_ref, s32[17]{0:T(128)} %convert_reduce_fusion.3.bound_ref, s32[256]{0:T(256)} %copy-done.3, s32[256]{0:T(256)} %constant.45.clone.place_ref, bf16[33,128,512]{2,1,0:T(8,128)(2,1)} %fusion.hot_ref, f32[512,2048]{1,0:T(8,128)} %get-tuple-element.24.sums_ref, ...), custom_call_target="tpu_custom_call" | custom-call | flops 4294967296 | bytes 12582912 | tf_op jit(solution)/shard_map/score/pallas_call | solution.py:296
  308.1 30.9 %all-to-all-start.7 = ((f32[16,1,256]{2,1,0:T(1,128)}), f32[16,1,256]{2,1,0:T(1,128)S(1)}, u32[]{:S(2)}, u32[]{:S(2)}) async-start(f32[16,1,256]{2,1,0:T(1,128)} %bitcast.18), calls=%async_computation.7 | async-start | bytes 32768 | tf_op jit(solution)/shard_map/all_to_all | solution.py:392
  339.0 0.7 slice.17
  339.7 5.8 %all-to-all-done.7 = f32[16,1,256]{2,1,0:T(1,128)S(1)} async-done(((f32[16,1,256]{2,1,0:T(1,128)}), f32[16,1,256]{2,1,0:T(1,128)S(1)}, u32[]{:S(2)}, u32[]{:S(2)}) %all-to-all-start.7) | async-done | bytes 16416 | tf_op jit(solution)/shard_map/all_to_all | solution.py:392
  346.1 3.5 all-to-all-start.6
  349.7 6.6 %all-to-all-done.6 = f32[16,1,512]{2,1,0:T(1,128)S(1)} async-done(((f32[16,1,512]{2,1,0:T(1,128)}), f32[16,1,512]{2,1,0:T(1,128)S(1)}, u32[]{:S(2)}, u32[]{:S(2)}) %all-to-all-start.6) | async-done | bytes 32800 | tf_op jit(solution)/shard_map/all_to_all | solution.py:321
  356.3 3.9 %multiply_convert_fusion = bf16[512,2048]{1,0:T(8,128)(2,1)} fusion(f32[512,2048]{1,0:T(8,128)} %get-tuple-element.24.sums_ref, f32[512]{0:T(512)S(1)} %add_rsqrt_fusion), kind=kLoop, calls=%fused_computation.2 | loop fusion | flops 3145728 | bytes 6293504 | tf_op jit(solution)/shard_map/convert_element_type | solution.py:397
  (41 shorter events, 6.6 us)
Async XLA Ops:
  2.6 31.1 %all-to-all-start = ((s32[16,1,512]{2,1,0:T(1,128)}), s32[16,1,512]{2,1,0:T(1,128)S(1)}, u32[]{:S(2)}, u32[]{:S(2)}) async-start(s32[16,1,512]{2,1,0:T(1,128)} %broadcast_in_dim.46), calls=%async_computation | async-start | bytes 65536 | tf_op jit(solution)/shard_map/all_to_all | solution.py:321
  33.8 68.5 %copy-start.1 = (s16[16,5,128,128]{3,2,1,0:T(8,128)(2,1)S(1)}, s16[16,5,128,128]{3,2,1,0:T(8,128)(2,1)}, u32[]{:S(2)}) copy-start(s16[16,5,128,128]{3,2,1,0:T(8,128)(2,1)} %get-tuple-element.20) | copy-start | bytes 7864324
  102.2 69.3 %copy-start.5 = (s32[256]{0:T(256)S(1)}, s32[256]{0:T(256)}, u32[]{:S(2)}) copy-start(s32[256]{0:T(256)} %constant.46.clone) | copy-start | bytes 3076
  165.7 55.4 %all-to-all-start.5 = ((s16[16,5,128,128]{3,2,1,0:T(8,128)(2,1)}), s16[16,5,128,128]{3,2,1,0:T(8,128)(2,1)S(1)}, u32[]{:S(2)}, u32[]{:S(2)}) async-start(s16[16,5,128,128]{3,2,1,0:T(8,128)(2,1)} %get-tuple-element.16), calls=%async_computation.5 | async-start | bytes 5242880 | tf_op jit(solution)/shard_map/all_to_all | solution.py:352
  171.5 67.4 %copy-start.3 = (s32[256]{0:T(256)}, s32[256]{0:T(256)S(1)}, u32[]{:S(2)}) copy-start(s32[256]{0:T(256)S(1)} %sub.7.meta_ref) | copy-start | bytes 3076
  171.6 67.4 %copy-start.2 = (s32[33,128]{1,0:T(8,128)}, s32[33,128]{1,0:T(8,128)S(1)}, u32[]{:S(2)}) copy-start(s32[33,128]{1,0:T(8,128)S(1)} %concatenate.7.labels_ref) | copy-start | bytes 50692
  221.1 17.8 %copy-start = (s16[16,5,128,128]{3,2,1,0:T(8,128)(2,1)}, s16[16,5,128,128]{3,2,1,0:T(8,128)(2,1)S(1)}, u32[]{:S(2)}) copy-start(s16[16,5,128,128]{3,2,1,0:T(8,128)(2,1)S(1)} %all-to-all-done.5.x_ref) | copy-start | bytes 7864324
  221.1 56.2 %all-to-all-start.2 = ((s16[16,2,128,128]{3,2,1,0:T(8,128)(2,1)}), s16[16,2,128,128]{3,2,1,0:T(8,128)(2,1)}, u32[]{:S(2)}, u32[]{:S(2)}) async-start(s16[16,2,128,128]{3,2,1,0:T(8,128)(2,1)} %get-tuple-element.18), calls=%async_computation.2 | async-start | bytes 2097152 | tf_op jit(solution)/shard_map/all_to_all | solution.py:352
  308.1 52.1 %copy-start.4 = (s32[256]{0:T(256)S(1)}, s32[256]{0:T(256)}, u32[]{:S(2)}) copy-start(s32[256]{0:T(256)} %param.11) | copy-start | bytes 3076
  308.1 37.4 %all-to-all-start.7 = ((f32[16,1,256]{2,1,0:T(1,128)}), f32[16,1,256]{2,1,0:T(1,128)S(1)}, u32[]{:S(2)}, u32[]{:S(2)}) async-start(f32[16,1,256]{2,1,0:T(1,128)} %bitcast.18), calls=%async_computation.7 | async-start | bytes 32768 | tf_op jit(solution)/shard_map/all_to_all | solution.py:392
  346.1 10.1 %all-to-all-start.6 = ((f32[16,1,512]{2,1,0:T(1,128)}), f32[16,1,512]{2,1,0:T(1,128)S(1)}, u32[]{:S(2)}, u32[]{:S(2)}) async-start(f32[16,1,512]{2,1,0:T(1,128)} %broadcast_in_dim.53), calls=%async_computation.6 | async-start | bytes 65536 | tf_op jit(solution)/shard_map/all_to_all | solution.py:321
where the time goes:
time: 362 us; the launch traced here: 361 us
  blocking collectives  131 us (36%)
  Pallas kernels  92.8 us (26%)
  starting transfers between devices  60.3 us (17%)
  waiting for transfers between devices  58.8 us (16%)
  other arithmetic  12.1 us (3%)
  local copies, waits for them, and re-layouts  4.9 us (1%)
    all_to_all x2, blocking collectives, shards(): lax.all_to_all(x, 'dp', split_axis=0, concat_axis=0, tiled=True)  115 us
    all_to_all x2, waiting for transfers between devices, shards(): lax.all_to_all(x, 'dp', split_axis=0, concat_axis=0, tiled=True)  46.4 us
    pallas_call x4, Pallas kernels, fold(): pl.pallas_call(functools.partial(fold_kernel, cap, low, part, first, last...  44.7 us
    all_to_all x1, starting transfers between devices, shards(): lax.all_to_all(partial.reshape(devices, home), 'dp', split_axis=0, concat...  30.9 us
    pallas_call x1, Pallas kernels, score(): pl.pallas_call(functools.partial(score_kernel, len(flat), cached), in_spe...  24.4 us
    all_to_all x2, starting transfers between devices, shards(): lax.all_to_all(x, 'dp', split_axis=0, concat_axis=0, tiled=True)  18.5 us
    all_to_all x1, blocking collectives, to_all(): return lax.all_to_all(rows, 'dp', split_axis=0, concat_axis=0, tiled=True)  15.8 us
    pallas_call x1, Pallas kernels, norms(): pl.pallas_call(norms_kernel, grid=(tiles // step,), in_specs=[SMEM, pl.Bl...  11.9 us
  transfers between devices with their start and end apart: 5, of which 3 were waited for; matrix products, arithmetic and copies ran while one was open for 2% of the time, Pallas kernels for 17%

commit v1 on v0

v1 whole, which is shorter than its diff:
```python
import functools
import math

import jax
import jax.numpy as jnp
import numpy as np
from jax import lax
from jax.experimental import pallas as pl
from jax.experimental.pallas import tpu as pltpu
from jax.sharding import PartitionSpec as P

K = 512
TB_OWN = 16
LANES = 128
EPSILON = 1e-06
CODE_TOP = 65535.0
CODE_SHIFT = 32768
VMEM_BYTES = 56 * 1024 * 1024
STEP_TILES = 16
PARTS = (0.0, 8 / 16, 13 / 16, 1.0)
CACHED_BLOCKS = 64
QUAD = 4
BATCH = 8
NT = (((1,), (1,)), ((), ()))
SMEM = pl.BlockSpec(memory_space=pltpu.SMEM)
VMEM = pl.BlockSpec(memory_space=pltpu.VMEM)
ANY = pl.BlockSpec(memory_space=pl.ANY)


def lane_sums(values):
    ones = jnp.ones((8, LANES), jnp.bfloat16)
    high = values.astype(jnp.bfloat16)
    low = (values - high.astype(jnp.float32)).astype(jnp.bfloat16)
    return lax.dot_general(ones, high, NT, preferred_element_type=jnp.float32) + lax.dot_general(
        ones, low, NT, preferred_element_type=jnp.float32
    )


def block_sums(square, out_ref, count):
    batch = math.gcd(BATCH, count)

    def one_batch(c, carry):
        some = square[pl.ds(c * batch, batch)].reshape((batch * LANES, LANES))
        sums = lane_sums(some)
        for j in range(batch):
            out_ref[pl.ds(c * batch + j, 1), :] += sums[:1, j * LANES : (j + 1) * LANES]
        return carry

    lax.fori_loop(0, count // batch, one_batch, 0)


def params():
    return pltpu.CompilerParams(vmem_limit_bytes=VMEM_BYTES)


def pack_kernel(cuts, place_ref, x_ref, *refs):
    parts = len(cuts) - 1
    outs = refs[:parts]
    coded, sems = refs[parts:]
    step = pl.program_id(0)
    tiles = x_ref.shape[0]

    def some_tiles(i, carry):
        first = step * tiles + i * QUAD
        for j in range(QUAD):
            x = x_ref[i * QUAD + j]
            root = x * lax.rsqrt(x)
            code = (root * CODE_TOP + 0.5).astype(jnp.int32) - CODE_SHIFT
            coded[first + j] = code.astype(jnp.int16)
        for j in range(QUAD):
            spot = place_ref[first + j]
            owner, rank = spot // cuts[-1], spot % cuts[-1]
            for q in range(parts):

                @pl.when((rank >= cuts[q]) & (rank < cuts[q + 1]))
                def _(q=q, t=first + j, owner=owner, rank=rank):
                    pltpu.make_async_copy(
                        coded.at[t], outs[q].at[owner, rank - cuts[q]], sems.at[t]
                    ).start()

        return carry

    lax.fori_loop(0, tiles // QUAD, some_tiles, 0)

    @pl.when(step == pl.num_programs(0) - 1)
    def _():
        def finish(t, carry):
            pltpu.make_async_copy(coded.at[t], outs[0].at[0, 0], sems.at[t]).wait()
            return carry

        lax.fori_loop(0, coded.shape[0], finish, 0)


def pack(tile_values, place, devices, cuts):
    tiles = tile_values.shape[0]
    step = math.gcd(STEP_TILES, tiles)
    return pl.pallas_call(
        functools.partial(pack_kernel, cuts),
        grid=(tiles // step,),
        in_specs=[SMEM, pl.BlockSpec((step, LANES, LANES), lambda i: (i, 0, 0))],
        out_specs=[ANY] * (len(cuts) - 1),
        out_shape=[
            jax.ShapeDtypeStruct((devices, high - low, LANES, LANES), jnp.int16)
            for low, high in zip(cuts, cuts[1:])
        ],
        scratch_shapes=[
            pltpu.VMEM((tiles, LANES, LANES), jnp.int16),
            pltpu.SemaphoreType.DMA((tiles,)),
        ],
        compiler_params=params(),
        cost_estimate=pl.CostEstimate(
            flops=8 * tile_values.size,
            bytes_accessed=6 * tile_values.size,
            transcendentals=tile_values.size,
        ),
        name="pack",
    )(place, tile_values)


def norms_kernel(row_ref, x_ref, sq_ref, square):
    step = pl.program_id(0)
    tiles = x_ref.shape[0]

    @pl.when(step == 0)
    def _():
        square[...] = jnp.zeros_like(square)

    def some_tiles(i, carry):
        for j in range(QUAD):
            x = x_ref[i * QUAD + j]
            square[row_ref[step * tiles + i * QUAD + j]] += x * x
        return carry

    lax.fori_loop(0, tiles // QUAD, some_tiles, 0)

    @pl.when(step == pl.num_programs(0) - 1)
    def _():
        sq_ref[...] = jnp.zeros_like(sq_ref)
        block_sums(square, sq_ref, square.shape[0])


def norms(tile_values, tile_row, blocks):
    tiles = tile_values.shape[0]
    step = math.gcd(STEP_TILES, tiles)
    return pl.pallas_call(
        norms_kernel,
        grid=(tiles // step,),
        in_specs=[SMEM, pl.BlockSpec((step, LANES, LANES), lambda i: (i, 0, 0))],
        out_specs=pl.BlockSpec((blocks, LANES), lambda i: (0, 0)),
        out_shape=jax.ShapeDtypeStruct((blocks, LANES), jnp.float32),
        scratch_shapes=[pltpu.VMEM((blocks, LANES, LANES), jnp.float32)],
        compiler_params=params(),
        cost_estimate=pl.CostEstimate(
            flops=8 * tile_values.size, bytes_accessed=4 * tile_values.size, transcendentals=0
        ),
        name="norms",
    )(tile_row, tile_values)


def stage_kernel(q, base, last, cached, fold_order, fold_bound, score_order, score_bound, meta,
                 place, done, labels, before, inv_hbm, x_hbm, hot_hbm, *refs):
    earlier, refs = refs[:q], refs[q:]
    sums_in, refs = (refs[0], refs[1:]) if q else (None, refs)
    part, sums_out, extra = refs[:3]
    inv, x, hot, sums, narrow, tiles, products, sems = refs[3:]
    fresh = tiles.at[pl.ds(base, x.shape[0])]
    needed = [
        pltpu.make_async_copy(x_hbm, x, sems.at[0]),
        pltpu.make_async_copy(inv_hbm, inv, sems.at[1]),
    ]
    if q:
        needed.append(pltpu.make_async_copy(sums_in, sums, sems.at[2]))
    later = [pltpu.make_async_copy(hot_hbm, hot, sems.at[3])] if cached else []
    spot = 0
    for e, e_hbm in enumerate(earlier):
        held = tiles.at[pl.ds(spot, e_hbm.shape[0])]
        later.append(pltpu.make_async_copy(e_hbm, held, sems.at[6 + e]))
        spot += e_hbm.shape[0]
    for copy in needed + later:
        copy.start()
    products[...] = jnp.zeros_like(products)
    part[...] = before[...]
    if not q:
        sums[...] = jnp.zeros_like(sums)
    for copy in needed:
        copy.wait()
    none = products.shape[0] - 1
    cluster = lax.broadcasted_iota(jnp.int32, (K, LANES), 0)

    def columns(sub):
        return (slice(None), pl.ds(pl.multiple_of(sub * LANES, LANES), LANES))

    def quad(order, start, end, p):
        rows, spots = [], []
        for j in range(QUAD):
            at = start + QUAD * p + j
            slot = order[jnp.where(at < end, at, start)]
            rows.append((meta[slot] // TB_OWN, at < end))
            spots.append(place[slot])
        return rows, spots

    def fold_sub(sub, carry):
        start = fold_bound[q * (TB_OWN + 1) + sub]
        end = fold_bound[q * (TB_OWN + 1) + sub + 1]

        def one_quad(p, carry):
            rows, spots = quad(fold_order, start, end, p)
            folded, picks = [], []
            for (row, held), spot in zip(rows, spots):
                root = x[spot - base].astype(jnp.int32).astype(jnp.float32) + float(CODE_SHIFT)
                tile = (root * root * inv[row]).astype(jnp.bfloat16)
                tiles[spot] = tile
                folded.append(tile)
                own = cluster == labels[pl.ds(jnp.where(held, row, none), 1), :]
                picks.append(jnp.where(own, 1.0, 0.0).astype(jnp.bfloat16))
            pick = jnp.concatenate(picks, axis=1)
            sums[columns(sub)] += jnp.dot(
                pick, jnp.concatenate(folded, axis=0), preferred_element_type=jnp.float32
            )
            return carry

        lax.fori_loop(0, (end - start + QUAD - 1) // QUAD, one_quad, 0)
        return carry

    lax.fori_loop(0, TB_OWN, fold_sub, 0)
    results = [pltpu.make_async_copy(sums, sums_out, sems.at[4])]
    if not last:
        results.append(pltpu.make_async_copy(fresh, extra, sems.at[5]))
    for copy in results:
        copy.start()
    if last:
        total = jnp.zeros((K, LANES), jnp.float32)
        for sub in range(TB_OWN):
            some = sums[:, sub * LANES : (sub + 1) * LANES]
            total = total + some * some
        extra[...] = lane_sums(total)
    for copy in later:
        copy.wait()

    def score_sub(sub, carry):
        start, end = score_bound[sub], score_bound[sub + 1]
        narrow[...] = sums[columns(sub)].astype(jnp.bfloat16)

        def one_quad(p, carry):
            rows, spots = quad(score_order, start, end, p)
            rows = [jnp.where(held, row, none) for row, held in rows]
            if cached:
                hots = [hot[row] for row in rows]
            else:
                for j, row in enumerate(rows):
                    pltpu.sync_copy(hot_hbm.at[row], hot.at[j])
                hots = [hot[j] for j in range(QUAD)]
            chosen = jnp.dot(
                jnp.concatenate(hots, axis=0), narrow[...], preferred_element_type=jnp.float32
            )
            for j in range(QUAD):
                own = chosen[j * LANES : (j + 1) * LANES]
                products[rows[j]] += own * tiles[spots[j]].astype(jnp.float32)
            return carry

        lax.fori_loop(0, (end - start + QUAD - 1) // QUAD, one_quad, 0)
        return carry

    lax.fori_loop(done[q], done[q + 1], score_sub, 0)
    block_sums(products, part, none)
    for copy in results:
        copy.wait()


def stage(q, cuts, scalars, labels, before, inverse, x, hot, normed, sums):
    devices, width = x.shape[:2]
    last = q == len(cuts) - 2
    blocks = inverse.shape[0]
    cached = blocks <= CACHED_BLOCKS
    flat = x.reshape((devices * width, LANES, LANES))
    tile_rows = devices * cuts[-1]
    wide = jax.ShapeDtypeStruct((K, TB_OWN * LANES), jnp.float32)
    return pl.pallas_call(
        functools.partial(stage_kernel, q, devices * cuts[q], last, cached),
        in_specs=[SMEM] * len(scalars) + [VMEM] * 2 + [ANY] * (3 + q + (q > 0)),
        out_specs=[VMEM, ANY, VMEM if last else ANY],
        out_shape=[
            jax.ShapeDtypeStruct((blocks, LANES), jnp.float32),
            wide,
            jax.ShapeDtypeStruct((8, K), jnp.float32)
            if last
            else jax.ShapeDtypeStruct(flat.shape, jnp.bfloat16),
        ],
        scratch_shapes=[
            pltpu.VMEM(inverse.shape, jnp.float32),
            pltpu.VMEM(flat.shape, jnp.int16),
            pltpu.VMEM(hot.shape if cached else (QUAD, LANES, K), jnp.bfloat16),
            pltpu.VMEM(wide.shape, jnp.float32),
            pltpu.VMEM((K, LANES), jnp.bfloat16),
            pltpu.VMEM((tile_rows, LANES, LANES), jnp.bfloat16),
            pltpu.VMEM((blocks + 1, LANES, LANES), jnp.float32),
            pltpu.SemaphoreType.DMA((6 + len(cuts),)),
        ],
        compiler_params=params(),
        cost_estimate=pl.CostEstimate(
            flops=x.size * K * 8,
            bytes_accessed=4 * x.size + 4 * inverse.size + 8 * K * TB_OWN * LANES,
            transcendentals=0,
        ),
        name="stage",
    )(*scalars, labels, before, inverse, flat, hot, *normed, *([sums] if q else []))


def exchange(x):
    return lax.all_to_all(x, "dp", split_axis=0, concat_axis=0, tiled=True)


def after(value, *others):
    return lax.optimization_barrier((value, *others))[0]


def sorted_slots(key, top):
    slots = jnp.arange(key.shape[0], dtype=jnp.int32)
    ahead = (key[None, :] < key[:, None]) | (
        (key[None, :] == key[:, None]) & (slots[None, :] < slots[:, None])
    )
    position = jnp.sum(ahead.astype(jnp.int32), axis=1)
    here = position[None, :] == slots[:, None]
    order = jnp.sum(jnp.where(here, slots[None, :], 0), axis=1)
    levels = jnp.arange(top + 1, dtype=jnp.int32)
    bounds = jnp.sum((key[None, :] < levels[:, None]).astype(jnp.int32), axis=1)
    return order, bounds


def ranks(group, sub):
    index = jnp.arange(sub.shape[-1], dtype=jnp.int32)
    before = (sub[..., None, :] < sub[..., :, None]) | (
        (sub[..., None, :] == sub[..., :, None]) & (index[None, :] < index[:, None])
    )
    same = group[..., None, :] == group[..., :, None]
    return jnp.sum((before & same).astype(jnp.int32), axis=-1)


def shards(tile_values, tile_row, tile_owner, tile_sub, labels):
    devices = lax.axis_size("dp")
    tiles = tile_values.shape[0]
    home = labels.shape[0]
    blocks = home // LANES * devices
    cap = max(2, 2 * tiles // devices)
    cuts = tuple(sorted({int(cap * share) for share in PARTS}))
    parts = len(cuts) - 1
    here = lax.axis_index("dp").astype(jnp.int32)
    owner = tile_owner[:, 0]

    partial_sq = norms(tile_values, tile_row, blocks)
    described = jnp.concatenate([labels, owner, tile_row * TB_OWN + tile_sub])
    told = jnp.concatenate([partial_sq.reshape(-1), described.astype(jnp.float32)])
    heard = exchange(jnp.broadcast_to(told[None], (devices, told.shape[0])))
    put = after(owner * cap + ranks(owner, tile_sub), partial_sq)
    outgoing = pack(tile_values, put, devices, cuts)
    incoming, previous = [], heard
    for x in outgoing:
        previous = exchange(after(x, previous))
        incoming.append(previous)

    row_sq = jnp.sum(heard[:, : blocks * LANES], axis=0).reshape(blocks, LANES)
    all_described = heard[:, blocks * LANES :].astype(jnp.int32)
    all_labels = all_described[:, :home].reshape(blocks, LANES)
    padded_labels = jnp.concatenate([all_labels, jnp.full((1, LANES), -1, jnp.int32)])
    hot = (padded_labels[:, :, None] == jnp.arange(K, dtype=jnp.int32)).astype(jnp.bfloat16)
    mine = all_described[:, home : home + tiles] == here
    code = all_described[:, home + tiles :]
    rank = ranks(mine.astype(jnp.int32), code % TB_OWN)
    chosen = mine[:, None, :] & (rank[:, None, :] == jnp.arange(cap)[None, :, None])
    meta = jnp.sum(jnp.where(chosen, code[:, None, :] + 1, 0), axis=2).reshape(-1) - 1
    sub = jnp.where(meta < 0, TB_OWN, meta % TB_OWN)
    slot_rank = np.arange(devices * cap) % cap
    slot_part = np.searchsorted(np.array(cuts), slot_rank, side="right") - 1
    low, high = np.array(cuts)[slot_part], np.array(cuts)[slot_part + 1]
    place = devices * low + np.arange(devices * cap) // cap * (high - low) + slot_rank - low
    fold_key = jnp.asarray(slot_part * (TB_OWN + 1), jnp.int32) + sub
    fold_order, fold_bounds = sorted_slots(fold_key, parts * (TB_OWN + 1))
    score_order, score_bounds = sorted_slots(sub, TB_OWN)
    left = np.arange(parts)[:, None] < slot_part[None, :]
    done = jnp.min(jnp.where(left, sub[None, :], TB_OWN), axis=1)
    done = jnp.concatenate([jnp.zeros((1,), jnp.int32), done])
    scalars = [
        fold_order, fold_bounds, score_order, score_bounds, meta, jnp.asarray(place, jnp.int32), done
    ]

    inverse = lax.rsqrt(row_sq + EPSILON)
    scale = jnp.broadcast_to((inverse * (1.0 / CODE_TOP**2))[:, :, None], (blocks, LANES, LANES))
    partial, sums, normed = jnp.zeros((blocks, LANES), jnp.float32), None, []
    for q in range(parts):
        partial, sums, extra = stage(
            q, cuts, scalars, padded_labels, partial, scale, incoming[q], hot, normed, sums
        )
        normed.append(extra)
    square = jnp.broadcast_to(extra[:1], (devices, K))
    back = jnp.sum(
        exchange(jnp.concatenate([partial.reshape(devices, home), square], axis=1)), axis=0
    )
    own_scale = lax.rsqrt(back[home:] + EPSILON)
    vocab_size = TB_OWN * LANES * devices
    centroid = sums * own_scale[:, None]
    centroids = (centroid * math.sqrt(vocab_size)).astype(jnp.bfloat16)
    is_label = labels[:, None] == jnp.arange(K, dtype=jnp.int32)[None, :]
    doc_scale = jnp.sum(jnp.where(is_label, own_scale[None, :], 0.0), axis=1)
    return (centroids, back[:home] * doc_scale)


def solution(mesh):
    return jax.shard_map(
        shards,
        mesh=mesh,
        in_specs=(
            P(("groups", "dp"), None, None),
            P(("groups", "dp")),
            P(("groups", "dp"), None),
            P(("groups", "dp")),
            P(("groups", "dp")),
        ),
        out_specs=(P("groups", "dp"), P(("groups", "dp"))),
        check_vma=False,
    )
```

time: 362 us -> 290 us (0.80)
  starting transfers between devices: 60.3 us -> 26.1 us
  Pallas kernels: 92.8 us -> 66.4 us
  waiting for transfers between devices: 58.8 us -> 48.7 us
  blocking collectives: 131 us -> 125 us
    all_to_all x5 -> x3, starting transfers between devices: 60.3 us -> 26.1 us  [exchange(): return lax.all_to_all(x, 'dp', split_axis=0, concat_axis=0, tiled=True)]
    pallas_call x5 -> x3, Pallas kernels: 69.1 us -> 48.8 us  [stage(): pl.pallas_call(functools.partial(stage_kernel, q, devices * cuts[q], last...]
    all_to_all x5 -> x3, waiting for transfers between devices: 58.8 us -> 48.7 us  [exchange(): return lax.all_to_all(x, 'dp', split_axis=0, concat_axis=0, tiled=True)]
    all_to_all x3 -> x2, blocking collectives: 131 us -> 125 us  [exchange(): return lax.all_to_all(x, 'dp', split_axis=0, concat_axis=0, tiled=True)]
    pallas_call x1, Pallas kernels: 11.9 us -> 7.88 us  [norms(): pl.pallas_call(norms_kernel, grid=(tiles // step,), in_specs=[SMEM, pl.Bl...]
  transfers between devices with their start and end apart: 5 -> 3, of which waited for: 3 -> 2; matrix products, arithmetic and copies ran while one was open for 2% -> 4% of each run, Pallas kernels for 17% -> 17%
where the time goes in v1:
time: 290 us; the launch traced here: 289 us
  blocking collectives  125 us (43%)
  Pallas kernels  66.4 us (23%)
  waiting for transfers between devices  48.7 us (17%)
  starting transfers between devices  26.1 us (9%)
  other arithmetic  14.6 us (5%)
  local copies, waits for them, and re-layouts  7.66 us (3%)
    all_to_all x2, blocking collectives, exchange(): return lax.all_to_all(x, 'dp', split_axis=0, concat_axis=0, tiled=True)  125 us
    pallas_call x3, Pallas kernels, stage(): pl.pallas_call(functools.partial(stage_kernel, q, devices * cuts[q], last...  48.8 us
    all_to_all x3, waiting for transfers between devices, exchange(): return lax.all_to_all(x, 'dp', split_axis=0, concat_axis=0, tiled=True)  48.7 us
    all_to_all x3, starting transfers between devices, exchange(): return lax.all_to_all(x, 'dp', split_axis=0, concat_axis=0, tiled=True)  26.1 us
    pallas_call x1, Pallas kernels, pack(): pl.pallas_call(functools.partial(pack_kernel, cuts), grid=(tiles // step,...  9.75 us
    pallas_call x1, Pallas kernels, norms(): pl.pallas_call(norms_kernel, grid=(tiles // step,), in_specs=[SMEM, pl.Bl...  7.88 us
  transfers between devices with their start and end apart: 3, of which 2 were waited for; matrix products, arithmetic and copies ran while one was open for 4% of the time, Pallas kernels for 17%

profile of v1, /device:TPU:0, one launch (start us, length us, event | category | flops | bytes accessed | tf_op | source)
XLA Modules:
  0.0 288.9 jit_solution(1013493943657175315)
XLA Ops:
  1.3 7.9 %norms.1 = f32[32,128]{1,0:T(8,128)} custom-call(s32[128]{0:T(128)} %row_ref.1, f32[128,128,128]{2,1,0:T(8,128)} %x_ref.3), custom_call_target="tpu_custom_call" | custom-call | flops 16777216 | bytes 8388608 | tf_op jit(solution)/shard_map/norms/pallas_call | solution.py:145
  9.2 0.7 pad_maximum_fusion.1
  9.9 0.9 broadcast_in_dim.56
  10.8 7.4 %all-to-all-start = ((f32[16,1,4608]{2,1,0:T(1,128)}), f32[16,1,4608]{2,1,0:T(1,128)S(1)}, u32[]{:S(2)}, u32[]{:S(2)}) async-start(f32[16,1,4608]{2,1,0:T(1,128)} %broadcast_in_dim.56), calls=%async_computation | async-start | bytes 589824 | tf_op jit(solution)/shard_map/all_to_all | solution.py:310
  18.9 9.8 %pack.1 = (s16[16,8,128,128]{3,2,1,0:T(8,128)(2,1)}, s16[16,5,128,128]{3,2,1,0:T(8,128)(2,1)}, s16[16,3,128,128]{3,2,1,0:T(8,128)(2,1)}) custom-call(s32[128]{0:T(128)} %multiply_add_fusion.place_ref, f32[128,128,128]{2,1,0:T(8,128)} %x_ref.3), custom_call_target="tpu_custom_call" | custom-call | flops 16777216 | bytes 12582912 | tf_op jit(solution)/shard_map/pack/pallas_call | solution.py:97
  28.8 98.3 %all_to_all.33 = s16[16,8,128,128]{3,2,1,0:T(8,128)(2,1)} all-to-all(s16[16,8,128,128]{3,2,1,0:T(8,128)(2,1)} %get-tuple-element.20), channel_id=1, replica_groups=mesh['groups'=2,'dp'=16] {'dp'}, dimensions={0} | all-to-all | bytes 8388608 | tf_op jit(solution)/shard_map/all_to_all | solution.py:310
  127.1 5.4 %all-to-all-start.2 = ((s16[16,5,128,128]{3,2,1,0:T(8,128)(2,1)}), s16[16,5,128,128]{3,2,1,0:T(8,128)(2,1)S(1)}, u32[]{:S(2)}, u32[]{:S(2)}) async-start(s16[16,5,128,128]{3,2,1,0:T(8,128)(2,1)} %get-tuple-element.23), calls=%async_computation.2 | async-start | bytes 5242880 | tf_op jit(solution)/shard_map/all_to_all | solution.py:310
  132.6 1.0 convert_reduce_fusion
  134.1 48.6 %all-to-all-done.2 = s16[16,5,128,128]{3,2,1,0:T(8,128)(2,1)S(1)} async-done(((s16[16,5,128,128]{3,2,1,0:T(8,128)(2,1)}), s16[16,5,128,128]{3,2,1,0:T(8,128)(2,1)S(1)}, u32[]{:S(2)}, u32[]{:S(2)}) %all-to-all-start.2) | async-done | bytes 2621472 | tf_op jit(solution)/shard_map/all_to_all | solution.py:310
  182.7 1.5 copy-done.1
  184.3 13.3 %all-to-all-start.3 = ((s16[16,3,128,128]{3,2,1,0:T(8,128)(2,1)}), s16[16,3,128,128]{3,2,1,0:T(8,128)(2,1)S(1)}, u32[]{:S(2)}, u32[]{:S(2)}) async-start(s16[16,3,128,128]{3,2,1,0:T(8,128)(2,1)} %get-tuple-element.28), calls=%async_computation.3 | async-start | bytes 3145728 | tf_op jit(solution)/shard_map/all_to_all | solution.py:310
  198.4 0.7 convert_reduce_fusion.5.score_bound
  199.0 0.7 convert_reduce_fusion.4.fold_bound
  200.0 0.7 select_reduce_fusion.1.score_order
  201.4 2.5 fusion.hot_hbm
  203.9 1.9 broadcast_in_dim.64.inv_hbm
  206.4 26.1 %stage.3 = (f32[32,128]{1,0:T(8,128)}, f32[512,2048]{1,0:T(8,128)}, bf16[128,128,128]{2,1,0:T(8,128)(2,1)}) custom-call(s32[256]{0:T(256)} %select_reduce_fusion.2.fold_order, s32[52]{0:T(128)} %convert_reduce_fusion.4.fold_bound, s32[256]{0:T(256)} %select_reduce_fusion.1.score_order, s32[17]{0:T(128)} %convert_reduce_fusion.5.score_bound, s32[256]{0:T(256)} %copy-done.3, ...), custom_call_target="tpu_custom_call" | custom-call | flops 8589934592 | bytes 18874368 | tf_op jit(solution)/shard_map/stage/pallas_call | solution.py:278
  232.5 12.2 %stage.4 = (f32[32,128]{1,0:T(8,128)}, f32[512,2048]{1,0:T(8,128)}, bf16[80,128,128]{2,1,0:T(8,128)(2,1)}) custom-call(s32[256]{0:T(256)} %select_reduce_fusion.2.fold_order, s32[52]{0:T(128)} %convert_reduce_fusion.4.fold_bound, s32[256]{0:T(256)} %select_reduce_fusion.1.score_order, s32[17]{0:T(128)} %convert_reduce_fusion.5.score_bound, s32[256]{0:T(256)} %copy-done.3, ...), custom_call_target="tpu_custom_call" | custom-call | flops 5368709120 | bytes 15728640 | tf_op jit(solution)/shard_map/stage/pallas_call | solution.py:278
  244.8 1.1 copy-done
  245.9 10.5 %stage.5 = (f32[32,128]{1,0:T(8,128)}, f32[512,2048]{1,0:T(8,128)}, f32[8,512]{1,0:T(8,128)}) custom-call(s32[256]{0:T(256)} %select_reduce_fusion.2.fold_order, s32[52]{0:T(128)} %convert_reduce_fusion.4.fold_bound, s32[256]{0:T(256)} %select_reduce_fusion.1.score_order, s32[17]{0:T(128)} %convert_reduce_fusion.5.score_bound, s32[256]{0:T(256)} %copy-done.3, ...), custom_call_target="tpu_custom_call" | custom-call | flops 3221225472 | bytes 13631488 | tf_op jit(solution)/shard_map/stage/pallas_call | solution.py:278
  256.4 0.7 slice.29
  257.1 0.7 reshape.118
  257.9 26.2 %all_to_all.34 = f32[16,1,768]{2,1,0:T(1,128)S(1)} all-to-all(f32[16,1,768]{2,1,0:T(1,128)S(1)} %all_to_all.26), channel_id=1, replica_groups=mesh['groups'=2,'dp'=16] {'dp'}, dimensions={0} | all-to-all | bytes 98304 | tf_op jit(solution)/shard_map/all_to_all | solution.py:310
  284.4 3.9 %multiply_convert_fusion = bf16[512,2048]{1,0:T(8,128)(2,1)} fusion(f32[512,2048]{1,0:T(8,128)} %get-tuple-element.31, f32[512]{0:T(512)S(1)} %add_rsqrt_fusion), kind=kLoop, calls=%fused_computation.2 | loop fusion | flops 3145728 | bytes 6293504 | tf_op jit(solution)/shard_map/convert_element_type | solution.py:401
  (48 shorter events, 5.2 us)
Async XLA Ops:
  1.3 7.9 %copy-start.4 = (s32[128,1]{0,1:T(1,128)S(1)}, s32[128,1]{0,1:T(1,128)}, u32[]{:S(2)}) copy-start(s32[128,1]{0,1:T(1,128)} %param.10) | copy-start | bytes 1540
  1.3 7.9 %copy-start.5 = (s32[256]{0:T(256)S(1)}, s32[256]{0:T(256)}, u32[]{:S(2)}) copy-start(s32[256]{0:T(256)} %param.12) | copy-start | bytes 3076
  1.3 16.9 %copy-start.6 = (s32[128]{0:T(128)S(1)}, s32[128]{0:T(128)}, u32[]{:S(2)}) copy-start(s32[128]{0:T(128)} %param.11) | copy-start | bytes 1540
  10.8 17.9 %all-to-all-start = ((f32[16,1,4608]{2,1,0:T(1,128)}), f32[16,1,4608]{2,1,0:T(1,128)S(1)}, u32[]{:S(2)}, u32[]{:S(2)}) async-start(f32[16,1,4608]{2,1,0:T(1,128)} %broadcast_in_dim.56), calls=%async_computation | async-start | bytes 589824 | tf_op jit(solution)/shard_map/all_to_all | solution.py:310
  127.1 70.5 %copy-start.8 = (s32[256]{0:T(256)S(1)}, s32[256]{0:T(256)}, u32[]{:S(2)}) copy-start(s32[256]{0:T(256)} %constant.60.clone) | copy-start | bytes 3076
  127.1 70.5 %copy-start.7 = (pred[3,256]{1,0:T(4,128)(4,1)S(1)}, pred[3,256]{1,0:T(4,128)(4,1)}, u32[]{:S(2)}) copy-start(pred[3,256]{1,0:T(4,128)(4,1)} %constant.61.clone) | copy-start | bytes 2308
  127.1 55.7 %all-to-all-start.2 = ((s16[16,5,128,128]{3,2,1,0:T(8,128)(2,1)}), s16[16,5,128,128]{3,2,1,0:T(8,128)(2,1)S(1)}, u32[]{:S(2)}, u32[]{:S(2)}) async-start(s16[16,5,128,128]{3,2,1,0:T(8,128)(2,1)} %get-tuple-element.23), calls=%async_computation.2 | async-start | bytes 5242880 | tf_op jit(solution)/shard_map/all_to_all | solution.py:310
  134.1 71.8 %copy-start.3 = (s32[256]{0:T(256)}, s32[256]{0:T(256)S(1)}, u32[]{:S(2)}) copy-start(s32[256]{0:T(256)S(1)} %sub.7.meta) | copy-start | bytes 3076
  134.1 72.3 %copy-start.2 = (s32[33,128]{1,0:T(8,128)}, s32[33,128]{1,0:T(8,128)S(1)}, u32[]{:S(2)}) copy-start(s32[33,128]{1,0:T(8,128)S(1)} %concatenate.18.labels) | copy-start | bytes 50692
  182.7 1.5 copy-start.1
  184.3 60.5 %all-to-all-start.3 = ((s16[16,3,128,128]{3,2,1,0:T(8,128)(2,1)}), s16[16,3,128,128]{3,2,1,0:T(8,128)(2,1)S(1)}, u32[]{:S(2)}, u32[]{:S(2)}) async-start(s16[16,3,128,128]{3,2,1,0:T(8,128)(2,1)} %get-tuple-element.28), calls=%async_computation.3 | async-start | bytes 3145728 | tf_op jit(solution)/shard_map/all_to_all | solution.py:310
  244.8 1.1 copy-start

commit v2 on v1

--- a/solution.py
+++ b/solution.py
@@ -17,7 +17,7 @@
 CODE_SHIFT = 32768
 VMEM_BYTES = 56 * 1024 * 1024
 STEP_TILES = 16
-PARTS = (0.0, 8 / 16, 13 / 16, 1.0)
+PARTS = (0.0, 9 / 16, 14 / 16, 1.0)
 CACHED_BLOCKS = 64
 QUAD = 4
 BATCH = 8
@@ -347,16 +347,12 @@
     here = lax.axis_index("dp").astype(jnp.int32)
     owner = tile_owner[:, 0]
 
-    partial_sq = norms(tile_values, tile_row, blocks)
+    outgoing = pack(tile_values, owner * cap + ranks(owner, tile_sub), devices, cuts)
+    incoming = [exchange(outgoing[0])]
+    partial_sq = norms(after(tile_values, outgoing[0]), tile_row, blocks)
     described = jnp.concatenate([labels, owner, tile_row * TB_OWN + tile_sub])
     told = jnp.concatenate([partial_sq.reshape(-1), described.astype(jnp.float32)])
     heard = exchange(jnp.broadcast_to(told[None], (devices, told.shape[0])))
-    put = after(owner * cap + ranks(owner, tile_sub), partial_sq)
-    outgoing = pack(tile_values, put, devices, cuts)
-    incoming, previous = [], heard
-    for x in outgoing:
-        previous = exchange(after(x, previous))
-        incoming.append(previous)
 
     row_sq = jnp.sum(heard[:, : blocks * LANES], axis=0).reshape(blocks, LANES)
     all_described = heard[:, blocks * LANES :].astype(jnp.int32)
@@ -386,10 +382,14 @@
     inverse = lax.rsqrt(row_sq + EPSILON)
     scale = jnp.broadcast_to((inverse * (1.0 / CODE_TOP**2))[:, :, None], (blocks, LANES, LANES))
     partial, sums, normed = jnp.zeros((blocks, LANES), jnp.float32), None, []
+    beside = (*scalars, padded_labels, hot, scale)
     for q in range(parts):
+        if q + 1 < parts:
+            incoming.append(exchange(after(outgoing[q + 1], incoming[q], *beside)))
         partial, sums, extra = stage(
             q, cuts, scalars, padded_labels, partial, scale, incoming[q], hot, normed, sums
         )
+        beside = (partial, sums, extra)
         normed.append(extra)
     square = jnp.broadcast_to(extra[:1], (devices, K))
     back = jnp.sum(

time: 290 us -> 281 us (0.969)
  blocking collectives: 125 us -> 36.8 us
  waiting for transfers between devices: 48.7 us -> 122 us
  starting transfers between devices: 26.1 us -> 39.7 us
  Pallas kernels: 66.4 us -> 57.3 us
    all_to_all x2, blocking collectives: 125 us -> 36.8 us  [exchange(): return lax.all_to_all(x, 'dp', split_axis=0, concat_axis=0, tiled=True)]
    all_to_all x3, waiting for transfers between devices: 48.7 us -> 122 us  [exchange(): return lax.all_to_all(x, 'dp', split_axis=0, concat_axis=0, tiled=True)]
    all_to_all x3, starting transfers between devices: 26.1 us -> 39.7 us  [exchange(): return lax.all_to_all(x, 'dp', split_axis=0, concat_axis=0, tiled=True)]
    pallas_call x3, Pallas kernels: 48.8 us -> 39.7 us  [stage(): pl.pallas_call(functools.partial(stage_kernel, q, devices * cuts[q], last...]
  transfers between devices with their start and end apart: 3 -> 3, of which waited for: 2 -> 3; matrix products, arithmetic and copies ran while one was open for 4% -> 3% of each run, Pallas kernels for 17% -> 10%
where the time goes in v2:
time: 281 us; the launch traced here: 280 us
  waiting for transfers between devices  122 us (43%)
  Pallas kernels  57.3 us (20%)
  starting transfers between devices  39.7 us (14%)
  blocking collectives  36.8 us (13%)
  other arithmetic  15.9 us (6%)
  local copies, waits for them, and re-layouts  6.78 us (2%)
    all_to_all x3, waiting for transfers between devices, exchange(): return lax.all_to_all(x, 'dp', split_axis=0, concat_axis=0, tiled=True)  122 us
    pallas_call x3, Pallas kernels, stage(): pl.pallas_call(functools.partial(stage_kernel, q, devices * cuts[q], last...  39.7 us
    all_to_all x3, starting transfers between devices, exchange(): return lax.all_to_all(x, 'dp', split_axis=0, concat_axis=0, tiled=True)  39.7 us
    all_to_all x2, blocking collectives, exchange(): return lax.all_to_all(x, 'dp', split_axis=0, concat_axis=0, tiled=True)  36.8 us
    pallas_call x1, Pallas kernels, pack(): pl.pallas_call(functools.partial(pack_kernel, cuts), grid=(tiles // step,...  9.75 us
    pallas_call x1, Pallas kernels, norms(): pl.pallas_call(norms_kernel, grid=(tiles // step,), in_specs=[SMEM, pl.Bl...  7.85 us
  transfers between devices with their start and end apart: 3, of which 3 were waited for; matrix products, arithmetic and copies ran while one was open for 3% of the time, Pallas kernels for 10%

profile of v2, /device:TPU:0, one launch (start us, length us, event | category | flops | bytes accessed | tf_op | source)
XLA Modules:
  0.0 279.6 jit_solution(4221539090722080084)
XLA Ops:
  1.3 0.9 convert_reduce_fusion.3
  2.2 1.2 multiply_add_fusion.1.place_ref
  3.4 9.8 %pack.1 = (s16[16,9,128,128]{3,2,1,0:T(8,128)(2,1)}, s16[16,5,128,128]{3,2,1,0:T(8,128)(2,1)}, s16[16,2,128,128]{3,2,1,0:T(8,128)(2,1)}) custom-call(s32[128]{0:T(128)} %multiply_add_fusion.1.place_ref, f32[128,128,128]{2,1,0:T(8,128)} %x_ref.2), custom_call_target="tpu_custom_call" | custom-call | flops 16777216 | bytes 12582912 | tf_op jit(solution)/shard_map/pack/pallas_call | solution.py:97
  13.2 7.9 %norms.1 = f32[32,128]{1,0:T(8,128)} custom-call(s32[128]{0:T(128)} %row_ref.1, f32[128,128,128]{2,1,0:T(8,128)} %x_ref.2), custom_call_target="tpu_custom_call" | custom-call | flops 16777216 | bytes 8388608 | tf_op jit(solution)/shard_map/norms/pallas_call | solution.py:145
  21.0 0.7 pad_maximum_fusion.1
  21.9 17.7 %all_to_all.33 = f32[16,1,4608]{2,1,0:T(1,128)S(1)} all-to-all(f32[16,1,4608]{2,1,0:T(1,128)S(1)} %broadcast_in_dim.56), channel_id=1, replica_groups=mesh['groups'=2,'dp'=16] {'dp'}, dimensions={0} | all-to-all | bytes 589824 | tf_op jit(solution)/shard_map/all_to_all | solution.py:310
  39.7 4.7 %all-to-all-start.1 = ((s16[16,9,128,128]{3,2,1,0:T(8,128)(2,1)}), s16[16,9,128,128]{3,2,1,0:T(8,128)(2,1)}, u32[]{:S(2)}, u32[]{:S(2)}) async-start(s16[16,9,128,128]{3,2,1,0:T(8,128)(2,1)} %get-tuple-element.17), calls=%async_computation.1 | async-start | bytes 9437184 | tf_op jit(solution)/shard_map/all_to_all | solution.py:310
  44.5 1.0 convert_reduce_fusion
  49.7 2.5 fusion.hot_hbm
  52.3 78.8 %all-to-all-done.1 = s16[16,9,128,128]{3,2,1,0:T(8,128)(2,1)} async-done(((s16[16,9,128,128]{3,2,1,0:T(8,128)(2,1)}), s16[16,9,128,128]{3,2,1,0:T(8,128)(2,1)}, u32[]{:S(2)}, u32[]{:S(2)}) %all-to-all-start.1) | async-done | bytes 4718624 | tf_op jit(solution)/shard_map/all_to_all | solution.py:310
  131.1 1.9 broadcast_in_dim.64.inv_hbm
  133.0 21.7 %all-to-all-start.2 = ((s16[16,5,128,128]{3,2,1,0:T(8,128)(2,1)}), s16[16,5,128,128]{3,2,1,0:T(8,128)(2,1)S(1)}, u32[]{:S(2)}, u32[]{:S(2)}) async-start(s16[16,5,128,128]{3,2,1,0:T(8,128)(2,1)} %get-tuple-element.21), calls=%async_computation.2 | async-start | bytes 5242880 | tf_op jit(solution)/shard_map/all_to_all | solution.py:310
  155.4 18.2 %stage.3 = (f32[32,128]{1,0:T(8,128)}, f32[512,2048]{1,0:T(8,128)}, bf16[144,128,128]{2,1,0:T(8,128)(2,1)}) custom-call(s32[256]{0:T(256)} %select_reduce_fusion.2.fold_order, s32[52]{0:T(128)} %convert_reduce_fusion.4.fold_bound, s32[256]{0:T(256)} %select_reduce_fusion.1.score_order, s32[17]{0:T(128)} %convert_reduce_fusion.5.score_bound, s32[256]{0:T(256)} %copy-done.3, ...), custom_call_target="tpu_custom_call" | custom-call | flops 9663676416 | bytes 19922944 | tf_op jit(solution)/shard_map/stage/pallas_call | solution.py:278
  173.5 31.5 %all-to-all-done.2 = s16[16,5,128,128]{3,2,1,0:T(8,128)(2,1)S(1)} async-done(((s16[16,5,128,128]{3,2,1,0:T(8,128)(2,1)}), s16[16,5,128,128]{3,2,1,0:T(8,128)(2,1)S(1)}, u32[]{:S(2)}, u32[]{:S(2)}) %all-to-all-start.2) | async-done | bytes 2621472 | tf_op jit(solution)/shard_map/all_to_all | solution.py:310
  205.0 1.5 copy-done.1
  206.5 13.3 %all-to-all-start.3 = ((s16[16,2,128,128]{3,2,1,0:T(8,128)(2,1)}), s16[16,2,128,128]{3,2,1,0:T(8,128)(2,1)S(1)}, u32[]{:S(2)}, u32[]{:S(2)}) async-start(s16[16,2,128,128]{3,2,1,0:T(8,128)(2,1)} %get-tuple-element.26), calls=%async_computation.3 | async-start | bytes 2097152 | tf_op jit(solution)/shard_map/all_to_all | solution.py:310
  219.8 11.1 %stage.4 = (f32[32,128]{1,0:T(8,128)}, f32[512,2048]{1,0:T(8,128)}, bf16[80,128,128]{2,1,0:T(8,128)(2,1)}) custom-call(s32[256]{0:T(256)} %select_reduce_fusion.2.fold_order, s32[52]{0:T(128)} %convert_reduce_fusion.4.fold_bound, s32[256]{0:T(256)} %select_reduce_fusion.1.score_order, s32[17]{0:T(128)} %convert_reduce_fusion.5.score_bound, s32[256]{0:T(256)} %copy-done.3, ...), custom_call_target="tpu_custom_call" | custom-call | flops 5368709120 | bytes 15728640 | tf_op jit(solution)/shard_map/stage/pallas_call | solution.py:278
  230.9 11.8 %all-to-all-done.3 = s16[16,2,128,128]{3,2,1,0:T(8,128)(2,1)S(1)} async-done(((s16[16,2,128,128]{3,2,1,0:T(8,128)(2,1)}), s16[16,2,128,128]{3,2,1,0:T(8,128)(2,1)S(1)}, u32[]{:S(2)}, u32[]{:S(2)}) %all-to-all-start.3) | async-done | bytes 1048608 | tf_op jit(solution)/shard_map/all_to_all | solution.py:310
  242.8 1.0 copy-done
  243.7 10.5 %stage.5 = (f32[32,128]{1,0:T(8,128)}, f32[512,2048]{1,0:T(8,128)}, f32[8,512]{1,0:T(8,128)}) custom-call(s32[256]{0:T(256)} %select_reduce_fusion.2.fold_order, s32[52]{0:T(128)} %convert_reduce_fusion.4.fold_bound, s32[256]{0:T(256)} %select_reduce_fusion.1.score_order, s32[17]{0:T(128)} %convert_reduce_fusion.5.score_bound, s32[256]{0:T(256)} %copy-done.3, ...), custom_call_target="tpu_custom_call" | custom-call | flops 2147483648 | bytes 12582912 | tf_op jit(solution)/shard_map/stage/pallas_call | solution.py:278
  254.2 0.7 slice.29
  255.0 0.7 reshape.118
  255.8 19.1 %all_to_all.34 = f32[16,1,768]{2,1,0:T(1,128)S(1)} all-to-all(f32[16,1,768]{2,1,0:T(1,128)S(1)} %all_to_all.26), channel_id=1, replica_groups=mesh['groups'=2,'dp'=16] {'dp'}, dimensions={0} | all-to-all | bytes 98304 | tf_op jit(solution)/shard_map/all_to_all | solution.py:310
  275.1 3.9 %multiply_convert_fusion = bf16[512,2048]{1,0:T(8,128)(2,1)} fusion(f32[512,2048]{1,0:T(8,128)} %get-tuple-element.29, f32[512]{0:T(512)S(1)} %add_rsqrt_fusion), kind=kLoop, calls=%fused_computation.2 | loop fusion | flops 3145728 | bytes 6293504 | tf_op jit(solution)/shard_map/convert_element_type | solution.py:401
  (46 shorter events, 6.5 us)
Async XLA Ops:
  13.2 7.9 %copy-start.4 = (s32[128,1]{0,1:T(1,128)S(1)}, s32[128,1]{0,1:T(1,128)}, u32[]{:S(2)}) copy-start(s32[128,1]{0,1:T(1,128)} %param.10) | copy-start | bytes 1540
  13.2 7.9 %copy-start.5 = (s32[256]{0:T(256)S(1)}, s32[256]{0:T(256)}, u32[]{:S(2)}) copy-start(s32[256]{0:T(256)} %param.12) | copy-start | bytes 3076
  39.7 6.3 %copy-start.7 = (s32[256]{0:T(256)S(1)}, s32[256]{0:T(256)}, u32[]{:S(2)}) copy-start(s32[256]{0:T(256)} %constant.60.clone) | copy-start | bytes 3076
  39.7 6.4 %copy-start.6 = (pred[3,256]{1,0:T(4,128)(4,1)S(1)}, pred[3,256]{1,0:T(4,128)(4,1)}, u32[]{:S(2)}) copy-start(pred[3,256]{1,0:T(4,128)(4,1)} %constant.61.clone) | copy-start | bytes 2308
  39.7 91.4 %all-to-all-start.1 = ((s16[16,9,128,128]{3,2,1,0:T(8,128)(2,1)}), s16[16,9,128,128]{3,2,1,0:T(8,128)(2,1)}, u32[]{:S(2)}, u32[]{:S(2)}) async-start(s16[16,9,128,128]{3,2,1,0:T(8,128)(2,1)} %get-tuple-element.17), calls=%async_computation.1 | async-start | bytes 9437184 | tf_op jit(solution)/shard_map/all_to_all | solution.py:310
  46.0 87.0 %copy-start.3 = (s32[256]{0:T(256)}, s32[256]{0:T(256)S(1)}, u32[]{:S(2)}) copy-start(s32[256]{0:T(256)S(1)} %sub.7.meta) | copy-start | bytes 3076
  46.0 87.0 %copy-start.2 = (s32[33,128]{1,0:T(8,128)}, s32[33,128]{1,0:T(8,128)S(1)}, u32[]{:S(2)}) copy-start(s32[33,128]{1,0:T(8,128)S(1)} %concatenate.18.labels) | copy-start | bytes 50692
  133.0 72.0 %all-to-all-start.2 = ((s16[16,5,128,128]{3,2,1,0:T(8,128)(2,1)}), s16[16,5,128,128]{3,2,1,0:T(8,128)(2,1)S(1)}, u32[]{:S(2)}, u32[]{:S(2)}) async-start(s16[16,5,128,128]{3,2,1,0:T(8,128)(2,1)} %get-tuple-element.21), calls=%async_computation.2 | async-start | bytes 5242880 | tf_op jit(solution)/shard_map/all_to_all | solution.py:310
  205.0 1.5 copy-start.1
  206.5 36.3 %all-to-all-start.3 = ((s16[16,2,128,128]{3,2,1,0:T(8,128)(2,1)}), s16[16,2,128,128]{3,2,1,0:T(8,128)(2,1)S(1)}, u32[]{:S(2)}, u32[]{:S(2)}) async-start(s16[16,2,128,128]{3,2,1,0:T(8,128)(2,1)} %get-tuple-element.26), calls=%async_computation.3 | async-start | bytes 2097152 | tf_op jit(solution)/shard_map/all_to_all | solution.py:310
  242.7 1.0 copy-start

commit v3 on v1

--- a/solution.py
+++ b/solution.py
@@ -16,8 +16,10 @@
 CODE_TOP = 65535.0
 CODE_SHIFT = 32768
 VMEM_BYTES = 56 * 1024 * 1024
-STEP_TILES = 16
-PARTS = (0.0, 8 / 16, 13 / 16, 1.0)
+STEP_TILES = 32
+PARTS = (0.0, 12 / 16, 1.0)
+FLIGHT = 6
+GROUPS = (6 / 30, 11 / 30, 15 / 30, 24 / 30, 1.0)
 CACHED_BLOCKS = 64
 QUAD = 4
 BATCH = 8
@@ -53,59 +55,58 @@
     return pltpu.CompilerParams(vmem_limit_bytes=VMEM_BYTES)
 
 
-def pack_kernel(cuts, place_ref, x_ref, *refs):
+def pack_kernel(cuts, put_ref, used_ref, x_ref, *refs):
     parts = len(cuts) - 1
-    outs = refs[:parts]
-    coded, sems = refs[parts:]
+    devices = used_ref.shape[0]
+    outs = refs[: devices * parts]
+    coded, sems = refs[devices * parts :]
     step = pl.program_id(0)
     tiles = x_ref.shape[0]
 
     def some_tiles(i, carry):
-        first = step * tiles + i * QUAD
         for j in range(QUAD):
             x = x_ref[i * QUAD + j]
             root = x * lax.rsqrt(x)
             code = (root * CODE_TOP + 0.5).astype(jnp.int32) - CODE_SHIFT
-            coded[first + j] = code.astype(jnp.int16)
-        for j in range(QUAD):
-            spot = place_ref[first + j]
-            owner, rank = spot // cuts[-1], spot % cuts[-1]
-            for q in range(parts):
-
-                @pl.when((rank >= cuts[q]) & (rank < cuts[q + 1]))
-                def _(q=q, t=first + j, owner=owner, rank=rank):
-                    pltpu.make_async_copy(
-                        coded.at[t], outs[q].at[owner, rank - cuts[q]], sems.at[t]
-                    ).start()
-
+            coded[put_ref[step * tiles + i * QUAD + j]] = code.astype(jnp.int16)
         return carry
 
     lax.fori_loop(0, tiles // QUAD, some_tiles, 0)
+
+    def each(what):
+        for q in range(parts):
+            for d in range(devices):
+
+                @pl.when(used_ref[d] > cuts[q])
+                def _(q=q, d=d):
+                    some = coded.at[pl.ds(d * cuts[-1] + cuts[q], cuts[q + 1] - cuts[q])]
+                    spot = q * devices + d
+                    what(pltpu.make_async_copy(some, outs[spot], sems.at[spot]))
 
     @pl.when(step == pl.num_programs(0) - 1)
     def _():
-        def finish(t, carry):
-            pltpu.make_async_copy(coded.at[t], outs[0].at[0, 0], sems.at[t]).wait()
-            return carry
-
-        lax.fori_loop(0, coded.shape[0], finish, 0)
-
-
-def pack(tile_values, place, devices, cuts):
+        each(lambda copy: copy.start())
+        each(lambda copy: copy.wait())
+
+
+def pack(tile_values, put, used, cuts):
     tiles = tile_values.shape[0]
+    devices = used.shape[0]
     step = math.gcd(STEP_TILES, tiles)
+    count = devices * (len(cuts) - 1)
     return pl.pallas_call(
         functools.partial(pack_kernel, cuts),
         grid=(tiles // step,),
-        in_specs=[SMEM, pl.BlockSpec((step, LANES, LANES), lambda i: (i, 0, 0))],
-        out_specs=[ANY] * (len(cuts) - 1),
+        in_specs=[SMEM, SMEM, pl.BlockSpec((step, LANES, LANES), lambda i: (i, 0, 0))],
+        out_specs=[ANY] * count,
         out_shape=[
-            jax.ShapeDtypeStruct((devices, high - low, LANES, LANES), jnp.int16)
+            jax.ShapeDtypeStruct((high - low, LANES, LANES), jnp.int16)
             for low, high in zip(cuts, cuts[1:])
+            for d in range(devices)
         ],
         scratch_shapes=[
-            pltpu.VMEM((tiles, LANES, LANES), jnp.int16),
-            pltpu.SemaphoreType.DMA((tiles,)),
+            pltpu.VMEM((devices * cuts[-1], LANES, LANES), jnp.int16),
+            pltpu.SemaphoreType.DMA((count,)),
         ],
         compiler_params=params(),
         cost_estimate=pl.CostEstimate(
@@ -114,7 +115,7 @@
             transcendentals=tile_values.size,
         ),
         name="pack",
-    )(place, tile_values)
+    )(put, used, tile_values)
 
 
 def norms_kernel(row_ref, x_ref, sq_ref, square):
@@ -157,24 +158,26 @@
     )(tile_row, tile_values)
 
 
-def stage_kernel(q, base, last, cached, fold_order, fold_bound, score_order, score_bound, meta,
-                 place, done, labels, before, inv_hbm, x_hbm, hot_hbm, *refs):
-    earlier, refs = refs[:q], refs[q:]
+def stage_kernel(q, base, width, last, cached, fold_order, fold_bound, score_order, score_bound,
+                 meta, place, done, labels, before, inv_hbm, hot_hbm, *refs):
+    x_hbms, earlier, refs = refs[:width], refs[width : width + q], refs[width + q :]
     sums_in, refs = (refs[0], refs[1:]) if q else (None, refs)
     part, sums_out, extra = refs[:3]
     inv, x, hot, sums, narrow, tiles, products, sems = refs[3:]
     fresh = tiles.at[pl.ds(base, x.shape[0])]
-    needed = [
-        pltpu.make_async_copy(x_hbm, x, sems.at[0]),
-        pltpu.make_async_copy(inv_hbm, inv, sems.at[1]),
-    ]
+    needed = [pltpu.make_async_copy(inv_hbm, inv, sems.at[1])]
     if q:
         needed.append(pltpu.make_async_copy(sums_in, sums, sems.at[2]))
+    spot = 0
+    for e, x_hbm in enumerate(x_hbms):
+        held = x.at[pl.ds(spot, x_hbm.shape[0])]
+        needed.append(pltpu.make_async_copy(x_hbm, held, sems.at[6 + e]))
+        spot += x_hbm.shape[0]
     later = [pltpu.make_async_copy(hot_hbm, hot, sems.at[3])] if cached else []
     spot = 0
     for e, e_hbm in enumerate(earlier):
         held = tiles.at[pl.ds(spot, e_hbm.shape[0])]
-        later.append(pltpu.make_async_copy(e_hbm, held, sems.at[6 + e]))
+        later.append(pltpu.make_async_copy(e_hbm, held, sems.at[6 + width + e]))
         spot += e_hbm.shape[0]
     for copy in needed + later:
         copy.start()
@@ -267,43 +270,40 @@
         copy.wait()
 
 
-def stage(q, cuts, scalars, labels, before, inverse, x, hot, normed, sums):
-    devices, width = x.shape[:2]
-    last = q == len(cuts) - 2
+def stage(q, base, slots, last, scalars, labels, before, inverse, hot, xs, normed, sums):
     blocks = inverse.shape[0]
     cached = blocks <= CACHED_BLOCKS
-    flat = x.reshape((devices * width, LANES, LANES))
-    tile_rows = devices * cuts[-1]
+    fresh = sum(x.shape[0] for x in xs)
     wide = jax.ShapeDtypeStruct((K, TB_OWN * LANES), jnp.float32)
     return pl.pallas_call(
-        functools.partial(stage_kernel, q, devices * cuts[q], last, cached),
-        in_specs=[SMEM] * len(scalars) + [VMEM] * 2 + [ANY] * (3 + q + (q > 0)),
+        functools.partial(stage_kernel, q, base, len(xs), last, cached),
+        in_specs=[SMEM] * len(scalars) + [VMEM] * 2 + [ANY] * (2 + len(xs) + q + (q > 0)),
         out_specs=[VMEM, ANY, VMEM if last else ANY],
         out_shape=[
             jax.ShapeDtypeStruct((blocks, LANES), jnp.float32),
             wide,
             jax.ShapeDtypeStruct((8, K), jnp.float32)
             if last
-            else jax.ShapeDtypeStruct(flat.shape, jnp.bfloat16),
+            else jax.ShapeDtypeStruct((fresh, LANES, LANES), jnp.bfloat16),
         ],
         scratch_shapes=[
             pltpu.VMEM(inverse.shape, jnp.float32),
-            pltpu.VMEM(flat.shape, jnp.int16),
+            pltpu.VMEM((fresh, LANES, LANES), jnp.int16),
             pltpu.VMEM(hot.shape if cached else (QUAD, LANES, K), jnp.bfloat16),
             pltpu.VMEM(wide.shape, jnp.float32),
             pltpu.VMEM((K, LANES), jnp.bfloat16),
-            pltpu.VMEM((tile_rows, LANES, LANES), jnp.bfloat16),
+            pltpu.VMEM((slots, LANES, LANES), jnp.bfloat16),
             pltpu.VMEM((blocks + 1, LANES, LANES), jnp.float32),
-            pltpu.SemaphoreType.DMA((6 + len(cuts),)),
+            pltpu.SemaphoreType.DMA((6 + len(xs) + q,)),
         ],
         compiler_params=params(),
         cost_estimate=pl.CostEstimate(
-            flops=x.size * K * 8,
-            bytes_accessed=4 * x.size + 4 * inverse.size + 8 * K * TB_OWN * LANES,
+            flops=fresh * LANES * LANES * K * 8,
+            bytes_accessed=4 * fresh * LANES * LANES + 4 * inverse.size + 8 * K * TB_OWN * LANES,
             transcendentals=0,
         ),
         name="stage",
-    )(*scalars, labels, before, inverse, flat, hot, *normed, *([sums] if q else []))
+    )(*scalars, labels, before, inverse, hot, *xs, *normed, *([sums] if q else []))
 
 
 def exchange(x):
@@ -336,13 +336,25 @@
     return jnp.sum((before & same).astype(jnp.int32), axis=-1)
 
 
+def schedule(devices, parts):
+    far, near = list(range(devices // 2, devices)), list(range(1, devices // 2))
+    order = [d for pair in zip(far, near) for d in pair] + far[len(near) :]
+    route = [(d, q) for q in range(parts) for d in [0, *order]]
+    groups, moved = {}, 0
+    for d, q in route:
+        moved += d > 0
+        share = max(moved, 1) / (parts * (devices - 1))
+        groups[d, q] = sum(share > end + 1e-9 for end in GROUPS)
+    return route, groups
+
+
 def shards(tile_values, tile_row, tile_owner, tile_sub, labels):
     devices = lax.axis_size("dp")
     tiles = tile_values.shape[0]
     home = labels.shape[0]
     blocks = home // LANES * devices
     cap = max(2, 2 * tiles // devices)
-    cuts = tuple(sorted({int(cap * share) for share in PARTS}))
+    cuts = tuple(sorted({int(cap * share) for share in PARTS})) if cap >= 8 else (0, cap)
     parts = len(cuts) - 1
     here = lax.axis_index("dp").astype(jnp.int32)
     owner = tile_owner[:, 0]
@@ -351,12 +363,11 @@
     described = jnp.concatenate([labels, owner, tile_row * TB_OWN + tile_sub])
     told = jnp.concatenate([partial_sq.reshape(-1), described.astype(jnp.float32)])
     heard = exchange(jnp.broadcast_to(told[None], (devices, told.shape[0])))
-    put = after(owner * cap + ranks(owner, tile_sub), partial_sq)
-    outgoing = pack(tile_values, put, devices, cuts)
-    incoming, previous = [], heard
-    for x in outgoing:
-        previous = exchange(after(x, previous))
-        incoming.append(previous)
+    shift = owner ^ here
+    put = after(shift * cap + ranks(owner, tile_sub), partial_sq)
+    every = jnp.arange(devices, dtype=jnp.int32)
+    used = jnp.sum((shift[None, :] == every[:, None]).astype(jnp.int32), axis=1)
+    outgoing = pack(tile_values, put, used, cuts)
 
     row_sq = jnp.sum(heard[:, : blocks * LANES], axis=0).reshape(blocks, LANES)
     all_described = heard[:, blocks * LANES :].astype(jnp.int32)
@@ -367,16 +378,26 @@
     code = all_described[:, home + tiles :]
     rank = ranks(mine.astype(jnp.int32), code % TB_OWN)
     chosen = mine[:, None, :] & (rank[:, None, :] == jnp.arange(cap)[None, :, None])
-    meta = jnp.sum(jnp.where(chosen, code[:, None, :] + 1, 0), axis=2).reshape(-1) - 1
+    meta = jnp.sum(jnp.where(chosen, code[:, None, :] + 1, 0), axis=2) - 1
+    from_shift = (every[None, :] == (every ^ here)[:, None]).astype(jnp.int32)
+    meta = jnp.sum(from_shift[:, :, None] * meta[None], axis=1).reshape(-1)
     sub = jnp.where(meta < 0, TB_OWN, meta % TB_OWN)
-    slot_rank = np.arange(devices * cap) % cap
-    slot_part = np.searchsorted(np.array(cuts), slot_rank, side="right") - 1
-    low, high = np.array(cuts)[slot_part], np.array(cuts)[slot_part + 1]
-    place = devices * low + np.arange(devices * cap) // cap * (high - low) + slot_rank - low
-    fold_key = jnp.asarray(slot_part * (TB_OWN + 1), jnp.int32) + sub
-    fold_order, fold_bounds = sorted_slots(fold_key, parts * (TB_OWN + 1))
+    route, groups = schedule(devices, parts)
+    stages = max(groups.values()) + 1
+    place, slot_group, bases, spot = np.zeros((devices, cap)), np.zeros((devices, cap), int), [], 0
+    for g in range(stages):
+        bases.append(spot)
+        for d, q in route:
+            if groups[d, q] == g:
+                some = slice(cuts[q], cuts[q + 1])
+                place[d, some] = spot + np.arange(cuts[q + 1] - cuts[q])
+                slot_group[d, some] = g
+                spot += cuts[q + 1] - cuts[q]
+    place, slot_group = place.reshape(-1), slot_group.reshape(-1)
+    fold_key = jnp.asarray(slot_group * (TB_OWN + 1), jnp.int32) + sub
+    fold_order, fold_bounds = sorted_slots(fold_key, stages * (TB_OWN + 1))
     score_order, score_bounds = sorted_slots(sub, TB_OWN)
-    left = np.arange(parts)[:, None] < slot_part[None, :]
+    left = np.arange(stages)[:, None] < slot_group[None, :]
     done = jnp.min(jnp.where(left, sub[None, :], TB_OWN), axis=1)
     done = jnp.concatenate([jnp.zeros((1,), jnp.int32), done])
     scalars = [
@@ -386,10 +407,30 @@
     inverse = lax.rsqrt(row_sq + EPSILON)
     scale = jnp.broadcast_to((inverse * (1.0 / CODE_TOP**2))[:, :, None], (blocks, LANES, LANES))
     partial, sums, normed = jnp.zeros((blocks, LANES), jnp.float32), None, []
-    for q in range(parts):
+    sent, incoming, beside = [], {}, {FLIGHT: (*scalars, padded_labels, hot, scale)}
+    moves = [key for key in route if key[0]]
+    ends = [max(i for i, key in enumerate(moves) if groups[key] == g) for g in range(stages)]
+    for g in range(stages):
+        for i, (d, q) in enumerate(moves):
+            if groups[d, q] != g:
+                continue
+            ahead = beside.get(i, ())
+            if i >= FLIGHT:
+                ahead = (sent[i - FLIGHT], *ahead)
+            x = outgoing[q * devices + d]
+            x = after(x, *ahead) if ahead else after(x, heard)
+            sent.append(lax.ppermute(x, "dp", [(j, j ^ d) for j in range(devices)]))
+            incoming[d, q] = sent[-1]
+        for q in range(parts):
+            incoming[0, q] = outgoing[q * devices]
+        xs = [incoming[key] for key in route if groups[key] == g]
         partial, sums, extra = stage(
-            q, cuts, scalars, padded_labels, partial, scale, incoming[q], hot, normed, sums
+            g, bases[g], devices * cap, g == stages - 1,
+            scalars, padded_labels, partial, scale, hot, xs, normed, sums,
         )
+        if g + 1 < stages:
+            at = ends[g + 1]
+            beside[at] = beside.get(at, ()) + (partial, sums, extra)
         normed.append(extra)
     square = jnp.broadcast_to(extra[:1], (devices, K))
     back = jnp.sum(

time: 290 us -> 280 us (0.966)
  blocking collectives: 125 us -> 16.4 us
  starting transfers between devices: 26.1 us -> 65.4 us
  waiting for transfers between devices: 48.7 us -> 86.2 us
  Pallas kernels: 66.4 us -> 85.7 us
    all_to_all x2 -> x1, blocking collectives: 125 us -> 16.4 us  [exchange(): return lax.all_to_all(x, 'dp', split_axis=0, concat_axis=0, tiled=True)]
    ppermute x0 -> x30, waiting for transfers between devices: none -> 85.7 us  [shards(): sent.append(lax.ppermute(x, 'dp', [(j, j ^ d) for j in range(devices)]))]
    ppermute x0 -> x30, starting transfers between devices: none -> 58 us  [shards(): sent.append(lax.ppermute(x, 'dp', [(j, j ^ d) for j in range(devices)]))]
    all_to_all x3 -> x1, waiting for transfers between devices: 48.7 us -> 0.51 us  [exchange(): return lax.all_to_all(x, 'dp', split_axis=0, concat_axis=0, tiled=True)]
    pallas_call x3 -> x5, Pallas kernels: 48.8 us -> 70.8 us  [stage(): pl.pallas_call(functools.partial(stage_kernel, q, base, len(xs), last, ca...]
    all_to_all x3 -> x1, starting transfers between devices: 26.1 us -> 7.36 us  [exchange(): return lax.all_to_all(x, 'dp', split_axis=0, concat_axis=0, tiled=True)]
  transfers between devices with their start and end apart: 3 -> 31, of which waited for: 2 -> 9; matrix products, arithmetic and copies ran while one was open for 4% -> 3% of each run, Pallas kernels for 17% -> 25%
where the time goes in v3:
time: 280 us; the launch traced here: 278 us
  waiting for transfers between devices  86.2 us (31%)
  Pallas kernels  85.7 us (31%)
  starting transfers between devices  65.4 us (23%)
  blocking collectives  16.4 us (6%)
  other arithmetic  15.3 us (5%)
  local copies, waits for them, and re-layouts  7.46 us (3%)
    ppermute x30, waiting for transfers between devices, shards(): sent.append(lax.ppermute(x, 'dp', [(j, j ^ d) for j in range(devices)]))  85.7 us
    pallas_call x5, Pallas kernels, stage(): pl.pallas_call(functools.partial(stage_kernel, q, base, len(xs), last, ca...  70.8 us
    ppermute x30, starting transfers between devices, shards(): sent.append(lax.ppermute(x, 'dp', [(j, j ^ d) for j in range(devices)]))  58 us
    all_to_all x1, blocking collectives, exchange(): return lax.all_to_all(x, 'dp', split_axis=0, concat_axis=0, tiled=True)  16.4 us
    pallas_call x1, Pallas kernels, pack(): pl.pallas_call(functools.partial(pack_kernel, cuts), grid=(tiles // step,...  8.59 us
    all_to_all x1, starting transfers between devices, exchange(): return lax.all_to_all(x, 'dp', split_axis=0, concat_axis=0, tiled=True)  7.36 us
    pallas_call x1, Pallas kernels, norms(): pl.pallas_call(norms_kernel, grid=(tiles // step,), in_specs=[SMEM, pl.Bl...  6.33 us
  transfers between devices with their start and end apart: 31, of which 9 were waited for; matrix products, arithmetic and copies ran while one was open for 3% of the time, Pallas kernels for 25%

profile of v3, /device:TPU:0, one launch (start us, length us, event | category | flops | bytes accessed | tf_op | source)
XLA Modules:
  0.0 277.8 jit_solution(14049323621193137538)
XLA Ops:
  1.3 6.3 %norms.1 = f32[32,128]{1,0:T(8,128)} custom-call(s32[128]{0:T(128)} %row_ref.1, f32[128,128,128]{2,1,0:T(8,128)} %x_ref.3), custom_call_target="tpu_custom_call" | custom-call | flops 16777216 | bytes 8388608 | tf_op jit(solution)/shard_map/norms/pallas_call | solution.py:146
  9.3 7.4 %all-to-all-start = ((f32[16,1,4608]{2,1,0:T(1,128)}), f32[16,1,4608]{2,1,0:T(1,128)S(1)}, u32[]{:S(2)}, u32[]{:S(2)}) async-start(f32[16,1,4608]{2,1,0:T(1,128)} %broadcast_in_dim.52), calls=%async_computation | async-start | bytes 589824 | tf_op jit(solution)/shard_map/all_to_all | solution.py:310
  17.9 8.6 %pack.1 = (s16[12,128,128]{2,1,0:T(8,128)(2,1)}, s16[12,128,128]{2,1,0:T(8,128)(2,1)}, s16[12,128,128]{2,1,0:T(8,128)(2,1)}, s16[12,128,128]{2,1,0:T(8,128)(2,1)...) custom-call(s32[128]{0:T(128)} %get-tuple-element.80.put_ref, ...), custom_call_target="tpu_custom_call" | custom-call | flops 16777216 | bytes 12582912 | tf_op jit(solution)/shard_map/pack/pallas_call | solution.py:97
  37.5 7.1 %collective-permute-done.3.refs_4_ = s16[12,128,128]{2,1,0:T(8,128)(2,1)S(1)} collective-permute-done((s16[12,128,128]{2,1,0:T(8,128)(2,1)}, s16[12,128,128]{2,1,0:T(8,128)(2,1)S(1)}, u32[]{:S(2)}, u32[]{:S(2)}) %collective-permute-start.3) | collective-permute-done | bytes 393248 | tf_op jit(solution)/shard_map/ppermute | solution.py:422
  44.6 9.7 %collective-permute-start = (s16[12,128,128]{2,1,0:T(8,128)(2,1)}, s16[12,128,128]{2,1,0:T(8,128)(2,1)S(1)}, u32[]{:S(2)}, u32[]{:S(2)}) collective-permute-start(s16[12,128,128]{2,1,0:T(8,128)(2,1)} %get-tuple-element.83), channel_id=1, source_target_pairs={{0,8},{1,9},{2,10},{3,11},{4,12},{5,13},{6,14},{7,15},{8,0},{9,1},... | collective-permute-start | bytes 1179656 | tf_op jit(solution)/shard_map/ppermute | solution.py:422
  57.3 23.2 %collective-permute-done.2.refs_3_ = s16[12,128,128]{2,1,0:T(8,128)(2,1)S(1)} collective-permute-done((s16[12,128,128]{2,1,0:T(8,128)(2,1)}, s16[12,128,128]{2,1,0:T(8,128)(2,1)S(1)}, u32[]{:S(2)}, u32[]{:S(2)}) %collective-permute-start.2) | collective-permute-done | bytes 393248 | tf_op jit(solution)/shard_map/ppermute | solution.py:422
  84.2 5.5 %collective-permute-done.refs_1_ = s16[12,128,128]{2,1,0:T(8,128)(2,1)S(1)} collective-permute-done((s16[12,128,128]{2,1,0:T(8,128)(2,1)}, s16[12,128,128]{2,1,0:T(8,128)(2,1)S(1)}, u32[]{:S(2)}, u32[]{:S(2)}) %collective-permute-start) | collective-permute-done | bytes 393248 | tf_op jit(solution)/shard_map/ppermute | solution.py:422
  95.3 13.5 %stage.5 = (f32[32,128]{1,0:T(8,128)}, f32[512,2048]{1,0:T(8,128)}, bf16[84,128,128]{2,1,0:T(8,128)(2,1)}) custom-call(s32[256]{0:T(256)} %select_reduce_fusion.2.fold_order, s32[86]{0:T(128)} %convert_reduce_fusion.3.fold_bound, s32[256]{0:T(256)} %select_reduce_fusion.1.score_order, s32[17]{0:T(128)} %convert_reduce_fusion.5.score_bound, s32[256]{0:T(256)} %copy-done.25, ...), custom_call_target="tpu_custom_call" | custom-call | flops 5637144576 | bytes 15990784 | tf_op jit(solution)/shard_map/stage/pallas_call | solution.py:278
  108.9 10.3 %collective-permute-done.7.refs_1_ = s16[12,128,128]{2,1,0:T(8,128)(2,1)S(1)} collective-permute-done((s16[12,128,128]{2,1,0:T(8,128)(2,1)S(1)}, s16[12,128,128]{2,1,0:T(8,128)(2,1)S(1)}, u32[]{:S(2)}, u32[]{:S(2)}) %collective-permute-start.7) | collective-permute-done | bytes 393248 | tf_op jit(solution)/shard_map/ppermute | solution.py:422
  119.3 12.1 %collective-permute-done.6.refs_0_ = s16[12,128,128]{2,1,0:T(8,128)(2,1)S(1)} collective-permute-done((s16[12,128,128]{2,1,0:T(8,128)(2,1)S(1)}, s16[12,128,128]{2,1,0:T(8,128)(2,1)S(1)}, u32[]{:S(2)}, u32[]{:S(2)}) %collective-permute-start.6) | collective-permute-done | bytes 393248 | tf_op jit(solution)/shard_map/ppermute | solution.py:422
  131.7 4.2 %collective-permute-start.12 = (s16[12,128,128]{2,1,0:T(8,128)(2,1)S(1)}, s16[12,128,128]{2,1,0:T(8,128)(2,1)S(1)}, u32[]{:S(2)}, u32[]{:S(2)}) collective-permute-start(s16[12,128,128]{2,1,0:T(8,128)(2,1)S(1)} %copy-done.32), channel_id=1, source_target_pairs={{0,14},{1,15},{2,12},{3,13},{4,10},{5,11},{6,8},{7,9},{8,6},{9,7},... | collective-permute-start | bytes 1179656 | tf_op jit(solution)/shard_map/ppermute | solution.py:422
  137.4 13.1 %stage.6 = (f32[32,128]{1,0:T(8,128)}, f32[512,2048]{1,0:T(8,128)}, bf16[60,128,128]{2,1,0:T(8,128)(2,1)}) custom-call(s32[256]{0:T(256)} %select_reduce_fusion.2.fold_order, s32[86]{0:T(128)} %convert_reduce_fusion.3.fold_bound, s32[256]{0:T(256)} %select_reduce_fusion.1.score_order, s32[17]{0:T(128)} %convert_reduce_fusion.5.score_bound, s32[256]{0:T(256)} %copy-done.25, ...), custom_call_target="tpu_custom_call" | custom-call | flops 4026531840 | bytes 14417920 | tf_op jit(solution)/shard_map/stage/pallas_call | solution.py:278
  152.3 4.3 %collective-permute-start.15 = (s16[4,128,128]{2,1,0:T(8,128)(2,1)S(1)}, s16[4,128,128]{2,1,0:T(8,128)(2,1)S(1)}, u32[]{:S(2)}, u32[]{:S(2)}) collective-permute-start(s16[4,128,128]{2,1,0:T(8,128)(2,1)S(1)} %copy-done.60), channel_id=1, source_target_pairs={{0,8},{1,9},{2,10},{3,11},{4,12},{5,13},{6,14},{7,15},{8,0},{9,1},... | collective-permute-start | bytes 393224 | tf_op jit(solution)/shard_map/ppermute | solution.py:422
  156.8 24.3 %collective-permute-done.15.refs_0_ = s16[4,128,128]{2,1,0:T(8,128)(2,1)S(1)} collective-permute-done((s16[4,128,128]{2,1,0:T(8,128)(2,1)S(1)}, s16[4,128,128]{2,1,0:T(8,128)(2,1)S(1)}, u32[]{:S(2)}, u32[]{:S(2)}) %collective-permute-start.15) | collective-permute-done | bytes 131104 | tf_op jit(solution)/shard_map/ppermute | solution.py:422
  181.1 3.6 %collective-permute-start.21 = (s16[4,128,128]{2,1,0:T(8,128)(2,1)S(1)}, s16[4,128,128]{2,1,0:T(8,128)(2,1)S(1)}, u32[]{:S(2)}, u32[]{:S(2)}) collective-permute-start(s16[4,128,128]{2,1,0:T(8,128)(2,1)S(1)} %copy-done.57), channel_id=1, source_target_pairs={{0,11},{1,10},{2,9},{3,8},{4,15},{5,14},{6,13},{7,12},{8,3},{9,2},... | collective-permute-start | bytes 393224 | tf_op jit(solution)/shard_map/ppermute | solution.py:422
  185.1 3.4 %collective-permute-start.19 = (s16[4,128,128]{2,1,0:T(8,128)(2,1)S(1)}, s16[4,128,128]{2,1,0:T(8,128)(2,1)S(1)}, u32[]{:S(2)}, u32[]{:S(2)}) collective-permute-start(s16[4,128,128]{2,1,0:T(8,128)(2,1)S(1)} %copy-done.55), channel_id=1, source_target_pairs={{0,10},{1,11},{2,8},{3,9},{4,14},{5,15},{6,12},{7,13},{8,2},{9,3},... | collective-permute-start | bytes 393224 | tf_op jit(solution)/shard_map/ppermute | solution.py:422
  189.7 22.9 %stage.7 = (f32[32,128]{1,0:T(8,128)}, f32[512,2048]{1,0:T(8,128)}, bf16[52,128,128]{2,1,0:T(8,128)(2,1)}) custom-call(s32[256]{0:T(256)} %select_reduce_fusion.2.fold_order, s32[86]{0:T(128)} %convert_reduce_fusion.3.fold_bound, s32[256]{0:T(256)} %select_reduce_fusion.1.score_order, s32[17]{0:T(128)} %convert_reduce_fusion.5.score_bound, s32[256]{0:T(256)} %copy-done.25, ...), custom_call_target="tpu_custom_call" | custom-call | flops 3489660928 | bytes 13893632 | tf_op jit(solution)/shard_map/stage/pallas_call | solution.py:278
  216.0 3.9 %collective-permute-start.25 = (s16[4,128,128]{2,1,0:T(8,128)(2,1)S(1)}, s16[4,128,128]{2,1,0:T(8,128)(2,1)S(1)}, u32[]{:S(2)}, u32[]{:S(2)}) collective-permute-start(s16[4,128,128]{2,1,0:T(8,128)(2,1)S(1)} %copy-done.49), channel_id=1, source_target_pairs={{0,13},{1,12},{2,15},{3,14},{4,9},{5,8},{6,11},{7,10},{8,5},{9,4},... | collective-permute-start | bytes 393224 | tf_op jit(solution)/shard_map/ppermute | solution.py:422
  220.5 3.7 %collective-permute-start.26 = (s16[4,128,128]{2,1,0:T(8,128)(2,1)S(1)}, s16[4,128,128]{2,1,0:T(8,128)(2,1)S(1)}, u32[]{:S(2)}, u32[]{:S(2)}) collective-permute-start(s16[4,128,128]{2,1,0:T(8,128)(2,1)S(1)} %copy-done.47), channel_id=1, source_target_pairs={{0,6},{1,7},{2,4},{3,5},{4,2},{5,3},{6,0},{7,1},{8,14},{9,15},{10,... | collective-permute-start | bytes 393224 | tf_op jit(solution)/shard_map/ppermute | solution.py:422
  224.2 10.7 %stage.8 = (f32[32,128]{1,0:T(8,128)}, f32[512,2048]{1,0:T(8,128)}, bf16[36,128,128]{2,1,0:T(8,128)(2,1)}) custom-call(s32[256]{0:T(256)} %select_reduce_fusion.2.fold_order, s32[86]{0:T(128)} %convert_reduce_fusion.3.fold_bound, s32[256]{0:T(256)} %select_reduce_fusion.1.score_order, s32[17]{0:T(128)} %convert_reduce_fusion.5.score_bound, s32[256]{0:T(256)} %copy-done.25, ...), custom_call_target="tpu_custom_call" | custom-call | flops 2415919104 | bytes 12845056 | tf_op jit(solution)/shard_map/stage/pallas_call | solution.py:278
  234.9 6.2 %collective-permute-start.29 = (s16[4,128,128]{2,1,0:T(8,128)(2,1)S(1)}, s16[4,128,128]{2,1,0:T(8,128)(2,1)S(1)}, u32[]{:S(2)}, u32[]{:S(2)}) collective-permute-start(s16[4,128,128]{2,1,0:T(8,128)(2,1)S(1)} %copy-done.46), channel_id=1, source_target_pairs={{0,15},{1,14},{2,13},{3,12},{4,11},{5,10},{6,9},{7,8},{8,7},{9,6},... | collective-permute-start | bytes 393224 | tf_op jit(solution)/shard_map/ppermute | solution.py:422
  244.7 10.5 %stage.9 = (f32[32,128]{1,0:T(8,128)}, f32[512,2048]{1,0:T(8,128)}, f32[8,512]{1,0:T(8,128)}) custom-call(s32[256]{0:T(256)} %select_reduce_fusion.2.fold_order, s32[86]{0:T(128)} %convert_reduce_fusion.3.fold_bound, s32[256]{0:T(256)} %select_reduce_fusion.1.score_order, s32[17]{0:T(128)} %convert_reduce_fusion.5.score_bound, s32[256]{0:T(256)} %copy-done.25, ...), custom_call_target="tpu_custom_call" | custom-call | flops 1610612736 | bytes 12058624 | tf_op jit(solution)/shard_map/stage/pallas_call | solution.py:278
  256.7 16.4 %all_to_all.18 = f32[16,1,768]{2,1,0:T(1,128)S(1)} all-to-all(f32[16,1,768]{2,1,0:T(1,128)S(1)} %all_to_all.14), channel_id=1, replica_groups=mesh['groups'=2,'dp'=16] {'dp'}, dimensions={0} | all-to-all | bytes 98304 | tf_op jit(solution)/shard_map/all_to_all | solution.py:310
  273.3 3.9 %multiply_convert_fusion = bf16[512,2048]{1,0:T(8,128)(2,1)} fusion(f32[512,2048]{1,0:T(8,128)} %get-tuple-element.155, f32[512]{0:T(512)S(1)} %add_rsqrt_fusion), kind=kLoop, calls=%fused_computation.2 | loop fusion | flops 3145728 | bytes 6293504 | tf_op jit(solution)/shard_map/convert_element_type | solution.py:442
  (213 shorter events, 41.7 us)
Async XLA Ops:
  33.4 58.4 %collective-permute-start.5 = (s16[12,128,128]{2,1,0:T(8,128)(2,1)}, s16[12,128,128]{2,1,0:T(8,128)(2,1)S(1)}, u32[]{:S(2)}, u32[]{:S(2)}) collective-permute-start(s16[12,128,128]{2,1,0:T(8,128)(2,1)} %get-tuple-element.93), channel_id=1, source_target_pairs={{0,3},{1,2},{2,1},{3,0},{4,7},{5,6},{6,5},{7,4},{8,11},{9,10},{10,... | collective-permute-start | bytes 1179656 | tf_op jit(solution)/shard_map/ppermute | solution.py:422
  33.4 61.1 %collective-permute-start.4 = (s16[12,128,128]{2,1,0:T(8,128)(2,1)}, s16[12,128,128]{2,1,0:T(8,128)(2,1)S(1)}, u32[]{:S(2)}, u32[]{:S(2)}) collective-permute-start(s16[12,128,128]{2,1,0:T(8,128)(2,1)} %get-tuple-element.91), channel_id=1, source_target_pairs={{0,10},{1,11},{2,8},{3,9},{4,14},{5,15},{6,12},{7,13},{8,2},{9,3},... | collective-permute-start | bytes 1179656 | tf_op jit(solution)/shard_map/ppermute | solution.py:422
  36.8 43.7 %collective-permute-start.2 = (s16[12,128,128]{2,1,0:T(8,128)(2,1)}, s16[12,128,128]{2,1,0:T(8,128)(2,1)S(1)}, u32[]{:S(2)}, u32[]{:S(2)}) collective-permute-start(s16[12,128,128]{2,1,0:T(8,128)(2,1)} %get-tuple-element.87), channel_id=1, source_target_pairs={{0,9},{1,8},{2,11},{3,10},{4,13},{5,12},{6,15},{7,14},{8,1},{9,0},... | collective-permute-start | bytes 1179656 | tf_op jit(solution)/shard_map/ppermute | solution.py:422
  37.3 43.9 %collective-permute-start.1 = (s16[12,128,128]{2,1,0:T(8,128)(2,1)}, s16[12,128,128]{2,1,0:T(8,128)(2,1)S(1)}, u32[]{:S(2)}, u32[]{:S(2)}) collective-permute-start(s16[12,128,128]{2,1,0:T(8,128)(2,1)} %get-tuple-element.85), channel_id=1, source_target_pairs={{0,1},{1,0},{2,3},{3,2},{4,5},{5,4},{6,7},{7,6},{8,9},{9,8},{10,11... | collective-permute-start | bytes 1179656 | tf_op jit(solution)/shard_map/ppermute | solution.py:422
  44.6 45.1 %collective-permute-start = (s16[12,128,128]{2,1,0:T(8,128)(2,1)}, s16[12,128,128]{2,1,0:T(8,128)(2,1)S(1)}, u32[]{:S(2)}, u32[]{:S(2)}) collective-permute-start(s16[12,128,128]{2,1,0:T(8,128)(2,1)} %get-tuple-element.83), channel_id=1, source_target_pairs={{0,8},{1,9},{2,10},{3,11},{4,12},{5,13},{6,14},{7,15},{8,0},{9,1},... | collective-permute-start | bytes 1179656 | tf_op jit(solution)/shard_map/ppermute | solution.py:422
  80.5 51.2 %collective-permute-start.9 = (s16[12,128,128]{2,1,0:T(8,128)(2,1)S(1)}, s16[12,128,128]{2,1,0:T(8,128)(2,1)S(1)}, u32[]{:S(2)}, u32[]{:S(2)}) collective-permute-start(s16[12,128,128]{2,1,0:T(8,128)(2,1)S(1)} %copy-done.37), channel_id=1, source_target_pairs={{0,5},{1,4},{2,7},{3,6},{4,1},{5,0},{6,3},{7,2},{8,13},{9,12},{10,... | collective-permute-start | bytes 1179656 | tf_op jit(solution)/shard_map/ppermute | solution.py:422
  81.1 54.8 %collective-permute-start.8 = (s16[12,128,128]{2,1,0:T(8,128)(2,1)S(1)}, s16[12,128,128]{2,1,0:T(8,128)(2,1)S(1)}, u32[]{:S(2)}, u32[]{:S(2)}) collective-permute-start(s16[12,128,128]{2,1,0:T(8,128)(2,1)S(1)} %copy-done.36), channel_id=1, source_target_pairs={{0,12},{1,13},{2,14},{3,15},{4,8},{5,9},{6,10},{7,11},{8,4},{9,5},... | collective-permute-start | bytes 1179656 | tf_op jit(solution)/shard_map/ppermute | solution.py:422
  89.7 29.6 %collective-permute-start.7 = (s16[12,128,128]{2,1,0:T(8,128)(2,1)S(1)}, s16[12,128,128]{2,1,0:T(8,128)(2,1)S(1)}, u32[]{:S(2)}, u32[]{:S(2)}) collective-permute-start(s16[12,128,128]{2,1,0:T(8,128)(2,1)S(1)} %copy-done.39), channel_id=1, source_target_pairs={{0,4},{1,5},{2,6},{3,7},{4,0},{5,1},{6,2},{7,3},{8,12},{9,13},{10,... | collective-permute-start | bytes 1179656 | tf_op jit(solution)/shard_map/ppermute | solution.py:422
  91.8 39.5 %collective-permute-start.6 = (s16[12,128,128]{2,1,0:T(8,128)(2,1)S(1)}, s16[12,128,128]{2,1,0:T(8,128)(2,1)S(1)}, u32[]{:S(2)}, u32[]{:S(2)}) collective-permute-start(s16[12,128,128]{2,1,0:T(8,128)(2,1)S(1)} %copy-done.38), channel_id=1, source_target_pairs={{0,11},{1,10},{2,9},{3,8},{4,15},{5,14},{6,13},{7,12},{8,3},{9,2},... | collective-permute-start | bytes 1179656 | tf_op jit(solution)/shard_map/ppermute | solution.py:422
  108.8 27.1 %collective-permute-start.10 = (s16[12,128,128]{2,1,0:T(8,128)(2,1)S(1)}, s16[12,128,128]{2,1,0:T(8,128)(2,1)S(1)}, u32[]{:S(2)}, u32[]{:S(2)}) collective-permute-start(s16[12,128,128]{2,1,0:T(8,128)(2,1)S(1)} %copy-done.35), channel_id=1, source_target_pairs={{0,13},{1,12},{2,15},{3,14},{4,9},{5,8},{6,11},{7,10},{8,5},{9,4},... | collective-permute-start | bytes 1179656 | tf_op jit(solution)/shard_map/ppermute | solution.py:422
  119.3 37.4 %collective-permute-start.11 = (s16[12,128,128]{2,1,0:T(8,128)(2,1)S(1)}, s16[12,128,128]{2,1,0:T(8,128)(2,1)S(1)}, u32[]{:S(2)}, u32[]{:S(2)}) collective-permute-start(s16[12,128,128]{2,1,0:T(8,128)(2,1)S(1)} %copy-done.34), channel_id=1, source_target_pairs={{0,6},{1,7},{2,4},{3,5},{4,2},{5,3},{6,0},{7,1},{8,14},{9,15},{10,... | collective-permute-start | bytes 1179656 | tf_op jit(solution)/shard_map/ppermute | solution.py:422
  131.4 53.3 %collective-permute-start.13 = (s16[12,128,128]{2,1,0:T(8,128)(2,1)S(1)}, s16[12,128,128]{2,1,0:T(8,128)(2,1)S(1)}, u32[]{:S(2)}, u32[]{:S(2)}) collective-permute-start(s16[12,128,128]{2,1,0:T(8,128)(2,1)S(1)} %copy-done.33), channel_id=1, source_target_pairs={{0,7},{1,6},{2,5},{3,4},{4,3},{5,2},{6,1},{7,0},{8,15},{9,14},{10,... | collective-permute-start | bytes 1179656 | tf_op jit(solution)/shard_map/ppermute | solution.py:422
  131.7 53.3 %collective-permute-start.12 = (s16[12,128,128]{2,1,0:T(8,128)(2,1)S(1)}, s16[12,128,128]{2,1,0:T(8,128)(2,1)S(1)}, u32[]{:S(2)}, u32[]{:S(2)}) collective-permute-start(s16[12,128,128]{2,1,0:T(8,128)(2,1)S(1)} %copy-done.32), channel_id=1, source_target_pairs={{0,14},{1,15},{2,12},{3,13},{4,10},{5,11},{6,8},{7,9},{8,6},{9,7},... | collective-permute-start | bytes 1179656 | tf_op jit(solution)/shard_map/ppermute | solution.py:422
  150.6 37.8 %collective-permute-start.14 = (s16[12,128,128]{2,1,0:T(8,128)(2,1)S(1)}, s16[12,128,128]{2,1,0:T(8,128)(2,1)S(1)}, u32[]{:S(2)}, u32[]{:S(2)}) collective-permute-start(s16[12,128,128]{2,1,0:T(8,128)(2,1)S(1)} %copy-done.31), channel_id=1, source_target_pairs={{0,15},{1,14},{2,13},{3,12},{4,11},{5,10},{6,9},{7,8},{8,7},{9,6},... | collective-permute-start | bytes 1179656 | tf_op jit(solution)/shard_map/ppermute | solution.py:422
  152.3 28.7 %collective-permute-start.15 = (s16[4,128,128]{2,1,0:T(8,128)(2,1)S(1)}, s16[4,128,128]{2,1,0:T(8,128)(2,1)S(1)}, u32[]{:S(2)}, u32[]{:S(2)}) collective-permute-start(s16[4,128,128]{2,1,0:T(8,128)(2,1)S(1)} %copy-done.60), channel_id=1, source_target_pairs={{0,8},{1,9},{2,10},{3,11},{4,12},{5,13},{6,14},{7,15},{8,0},{9,1},... | collective-permute-start | bytes 393224 | tf_op jit(solution)/shard_map/ppermute | solution.py:422
  156.7 24.4 %collective-permute-start.16 = (s16[4,128,128]{2,1,0:T(8,128)(2,1)S(1)}, s16[4,128,128]{2,1,0:T(8,128)(2,1)S(1)}, u32[]{:S(2)}, u32[]{:S(2)}) collective-permute-start(s16[4,128,128]{2,1,0:T(8,128)(2,1)S(1)} %copy-done.59), channel_id=1, source_target_pairs={{0,1},{1,0},{2,3},{3,2},{4,5},{5,4},{6,7},{7,6},{8,9},{9,8},{10,11... | collective-permute-start | bytes 393224 | tf_op jit(solution)/shard_map/ppermute | solution.py:422
  181.1 31.6 %collective-permute-start.17 = (s16[4,128,128]{2,1,0:T(8,128)(2,1)S(1)}, s16[4,128,128]{2,1,0:T(8,128)(2,1)S(1)}, u32[]{:S(2)}, u32[]{:S(2)}) collective-permute-start(s16[4,128,128]{2,1,0:T(8,128)(2,1)S(1)} %copy-done.58), channel_id=1, source_target_pairs={{0,9},{1,8},{2,11},{3,10},{4,13},{5,12},{6,15},{7,14},{8,1},{9,0},... | collective-permute-start | bytes 393224 | tf_op jit(solution)/shard_map/ppermute | solution.py:422
  181.1 31.6 %collective-permute-start.21 = (s16[4,128,128]{2,1,0:T(8,128)(2,1)S(1)}, s16[4,128,128]{2,1,0:T(8,128)(2,1)S(1)}, u32[]{:S(2)}, u32[]{:S(2)}) collective-permute-start(s16[4,128,128]{2,1,0:T(8,128)(2,1)S(1)} %copy-done.57), channel_id=1, source_target_pairs={{0,11},{1,10},{2,9},{3,8},{4,15},{5,14},{6,13},{7,12},{8,3},{9,2},... | collective-permute-start | bytes 393224 | tf_op jit(solution)/shard_map/ppermute | solution.py:422
  184.7 28.2 %collective-permute-start.22 = (s16[4,128,128]{2,1,0:T(8,128)(2,1)S(1)}, s16[4,128,128]{2,1,0:T(8,128)(2,1)S(1)}, u32[]{:S(2)}, u32[]{:S(2)}) collective-permute-start(s16[4,128,128]{2,1,0:T(8,128)(2,1)S(1)} %copy-done.56), channel_id=1, source_target_pairs={{0,4},{1,5},{2,6},{3,7},{4,0},{5,1},{6,2},{7,3},{8,12},{9,13},{10,... | collective-permute-start | bytes 393224 | tf_op jit(solution)/shard_map/ppermute | solution.py:422
  185.1 28.5 %collective-permute-start.19 = (s16[4,128,128]{2,1,0:T(8,128)(2,1)S(1)}, s16[4,128,128]{2,1,0:T(8,128)(2,1)S(1)}, u32[]{:S(2)}, u32[]{:S(2)}) collective-permute-start(s16[4,128,128]{2,1,0:T(8,128)(2,1)S(1)} %copy-done.55), channel_id=1, source_target_pairs={{0,10},{1,11},{2,8},{3,9},{4,14},{5,15},{6,12},{7,13},{8,2},{9,3},... | collective-permute-start | bytes 393224 | tf_op jit(solution)/shard_map/ppermute | solution.py:422
  188.4 27.6 %collective-permute-start.18 = (s16[4,128,128]{2,1,0:T(8,128)(2,1)S(1)}, s16[4,128,128]{2,1,0:T(8,128)(2,1)S(1)}, u32[]{:S(2)}, u32[]{:S(2)}) collective-permute-start(s16[4,128,128]{2,1,0:T(8,128)(2,1)S(1)} %copy-done.54), channel_id=1, source_target_pairs={{0,2},{1,3},{2,0},{3,1},{4,6},{5,7},{6,4},{7,5},{8,10},{9,11},{10,... | collective-permute-start | bytes 393224 | tf_op jit(solution)/shard_map/ppermute | solution.py:422
  212.9 22.0 %collective-permute-start.27 = (s16[4,128,128]{2,1,0:T(8,128)(2,1)S(1)}, s16[4,128,128]{2,1,0:T(8,128)(2,1)S(1)}, u32[]{:S(2)}, u32[]{:S(2)}) collective-permute-start(s16[4,128,128]{2,1,0:T(8,128)(2,1)S(1)} %copy-done.51), channel_id=1, source_target_pairs={{0,14},{1,15},{2,12},{3,13},{4,10},{5,11},{6,8},{7,9},{8,6},{9,7},... | collective-permute-start | bytes 393224 | tf_op jit(solution)/shard_map/ppermute | solution.py:422
  213.6 27.6 %collective-permute-start.28 = (s16[4,128,128]{2,1,0:T(8,128)(2,1)S(1)}, s16[4,128,128]{2,1,0:T(8,128)(2,1)S(1)}, u32[]{:S(2)}, u32[]{:S(2)}) collective-permute-start(s16[4,128,128]{2,1,0:T(8,128)(2,1)S(1)} %copy-done.50), channel_id=1, source_target_pairs={{0,7},{1,6},{2,5},{3,4},{4,3},{5,2},{6,1},{7,0},{8,15},{9,14},{10,... | collective-permute-start | bytes 393224 | tf_op jit(solution)/shard_map/ppermute | solution.py:422
  216.0 25.1 %collective-permute-start.25 = (s16[4,128,128]{2,1,0:T(8,128)(2,1)S(1)}, s16[4,128,128]{2,1,0:T(8,128)(2,1)S(1)}, u32[]{:S(2)}, u32[]{:S(2)}) collective-permute-start(s16[4,128,128]{2,1,0:T(8,128)(2,1)S(1)} %copy-done.49), channel_id=1, source_target_pairs={{0,13},{1,12},{2,15},{3,14},{4,9},{5,8},{6,11},{7,10},{8,5},{9,4},... | collective-permute-start | bytes 393224 | tf_op jit(solution)/shard_map/ppermute | solution.py:422
  (68 other events, 1468.9 us)

commit v4 on v2

--- a/solution.py
+++ b/solution.py
@@ -16,8 +16,10 @@
 CODE_TOP = 65535.0
 CODE_SHIFT = 32768
 VMEM_BYTES = 56 * 1024 * 1024
-STEP_TILES = 16
-PARTS = (0.0, 9 / 16, 14 / 16, 1.0)
+STEP_TILES = 32
+PARTS = (0.0, 13 / 16, 1.0)
+LOG_STEPS = 1800.0
+LOG_MIDDLE = -3.0
 CACHED_BLOCKS = 64
 QUAD = 4
 BATCH = 8
@@ -53,59 +55,91 @@
     return pltpu.CompilerParams(vmem_limit_bytes=VMEM_BYTES)
 
 
-def pack_kernel(cuts, place_ref, x_ref, *refs):
+def pack_kernel(cuts, put_ref, row_ref, told_ref, x_ref, *refs):
     parts = len(cuts) - 1
     outs = refs[:parts]
-    coded, sems = refs[parts:]
+    coded, square, sums, notes, held, sems = refs[parts:]
     step = pl.program_id(0)
     tiles = x_ref.shape[0]
+    devices = held.shape[0]
+    blocks = square.shape[0]
+
+    @pl.when(step == 0)
+    def _():
+        square[...] = jnp.zeros_like(square)
+
+        def clear(d, carry):
+            held[d] = 0
+            return carry
+
+        lax.fori_loop(0, devices, clear, 0)
 
     def some_tiles(i, carry):
-        first = step * tiles + i * QUAD
         for j in range(QUAD):
+            t = step * tiles + i * QUAD + j
             x = x_ref[i * QUAD + j]
             root = x * lax.rsqrt(x)
             code = (root * CODE_TOP + 0.5).astype(jnp.int32) - CODE_SHIFT
-            coded[first + j] = code.astype(jnp.int16)
-        for j in range(QUAD):
-            spot = place_ref[first + j]
-            owner, rank = spot // cuts[-1], spot % cuts[-1]
-            for q in range(parts):
-
-                @pl.when((rank >= cuts[q]) & (rank < cuts[q + 1]))
-                def _(q=q, t=first + j, owner=owner, rank=rank):
-                    pltpu.make_async_copy(
-                        coded.at[t], outs[q].at[owner, rank - cuts[q]], sems.at[t]
-                    ).start()
-
+            put = put_ref[t]
+            coded[pl.ds(pl.multiple_of(put * LANES, LANES), LANES), :] = code.astype(jnp.int16)
+            square[row_ref[t]] += x * x
+            owner = put // cuts[-1]
+            held[owner] = jnp.maximum(held[owner], put % cuts[-1] + 1)
         return carry
 
     lax.fori_loop(0, tiles // QUAD, some_tiles, 0)
+
+    def slots(q, d):
+        some = pl.ds((d * cuts[-1] + cuts[q]) * LANES, (cuts[q + 1] - cuts[q]) * LANES)
+        into = outs[q].at[d, pl.ds(0, (cuts[q + 1] - cuts[q]) * LANES)]
+        return pltpu.make_async_copy(coded.at[some], into, sems.at[q * devices + d])
+
+    def note(d):
+        into = outs[0].at[d, pl.ds((cuts[1] - cuts[0]) * LANES, notes.shape[0])]
+        return pltpu.make_async_copy(notes, into, sems.at[parts * devices + d])
+
+    def each(what):
+        for q in range(parts):
+            for d in range(devices):
+                pl.when(held[d] > cuts[q])(lambda q=q, d=d: what(slots(q, d)))
 
     @pl.when(step == pl.num_programs(0) - 1)
     def _():
-        def finish(t, carry):
-            pltpu.make_async_copy(coded.at[t], outs[0].at[0, 0], sems.at[t]).wait()
-            return carry
-
-        lax.fori_loop(0, coded.shape[0], finish, 0)
-
-
-def pack(tile_values, place, devices, cuts):
+        each(lambda copy: copy.start())
+        sums[...] = jnp.zeros_like(sums)
+        block_sums(square, sums, blocks)
+        total = sums[...]
+        level = (jnp.log2(jnp.maximum(total, 1e-30)) - LOG_MIDDLE) * LOG_STEPS
+        level = jnp.where(total > 0.0, jnp.clip(level, -32700.0, 32700.0), -32768.0)
+        level = (level + 32768.5).astype(jnp.int32) - 32768
+        notes[...] = jnp.concatenate([level, told_ref[...]], axis=0).astype(jnp.int16)
+        for d in range(devices):
+            note(d).start()
+        each(lambda copy: copy.wait())
+        for d in range(devices):
+            note(d).wait()
+
+
+def pack(tile_values, put, tile_row, told, devices, blocks, cuts):
     tiles = tile_values.shape[0]
     step = math.gcd(STEP_TILES, tiles)
+    noted = blocks + told.shape[0]
+    rows = [(high - low) * LANES for low, high in zip(cuts, cuts[1:])]
+    rows[0] += noted
     return pl.pallas_call(
         functools.partial(pack_kernel, cuts),
         grid=(tiles // step,),
-        in_specs=[SMEM, pl.BlockSpec((step, LANES, LANES), lambda i: (i, 0, 0))],
-        out_specs=[ANY] * (len(cuts) - 1),
-        out_shape=[
-            jax.ShapeDtypeStruct((devices, high - low, LANES, LANES), jnp.int16)
-            for low, high in zip(cuts, cuts[1:])
-        ],
+        in_specs=[SMEM, SMEM, pl.BlockSpec(told.shape, lambda i: (0, 0))]
+        + [pl.BlockSpec((step, LANES, LANES), lambda i: (i, 0, 0))],
+        out_specs=[ANY] * len(rows),
+        out_shape=[jax.ShapeDtypeStruct((devices, some, LANES), jnp.int16) for some in rows],
         scratch_shapes=[
-            pltpu.VMEM((tiles, LANES, LANES), jnp.int16),
-            pltpu.SemaphoreType.DMA((tiles,)),
+            pltpu.VMEM((devices * cuts[-1] * LANES, LANES), jnp.int16),
+            pltpu.VMEM((blocks, LANES, LANES), jnp.float32),
+            pltpu.VMEM((blocks, LANES), jnp.float32),
+            pltpu.VMEM((noted, LANES), jnp.int16),
+            pltpu.SMEM((devices,), jnp.int32),
+            pltpu.SemaphoreType.DMA(((len(rows) + 1) * devices,)),
         ],
         compiler_params=params(),
         cost_estimate=pl.CostEstimate(
@@ -114,58 +148,21 @@
             transcendentals=tile_values.size,
         ),
         name="pack",
-    )(place, tile_values)
-
-
-def norms_kernel(row_ref, x_ref, sq_ref, square):
-    step = pl.program_id(0)
-    tiles = x_ref.shape[0]
-
-    @pl.when(step == 0)
-    def _():
-        square[...] = jnp.zeros_like(square)
-
-    def some_tiles(i, carry):
-        for j in range(QUAD):
-            x = x_ref[i * QUAD + j]
-            square[row_ref[step * tiles + i * QUAD + j]] += x * x
-        return carry
-
-    lax.fori_loop(0, tiles // QUAD, some_tiles, 0)
-
-    @pl.when(step == pl.num_programs(0) - 1)
-    def _():
-        sq_ref[...] = jnp.zeros_like(sq_ref)
-        block_sums(square, sq_ref, square.shape[0])
-
-
-def norms(tile_values, tile_row, blocks):
-    tiles = tile_values.shape[0]
-    step = math.gcd(STEP_TILES, tiles)
-    return pl.pallas_call(
-        norms_kernel,
-        grid=(tiles // step,),
-        in_specs=[SMEM, pl.BlockSpec((step, LANES, LANES), lambda i: (i, 0, 0))],
-        out_specs=pl.BlockSpec((blocks, LANES), lambda i: (0, 0)),
-        out_shape=jax.ShapeDtypeStruct((blocks, LANES), jnp.float32),
-        scratch_shapes=[pltpu.VMEM((blocks, LANES, LANES), jnp.float32)],
-        compiler_params=params(),
-        cost_estimate=pl.CostEstimate(
-            flops=8 * tile_values.size, bytes_accessed=4 * tile_values.size, transcendentals=0
-        ),
-        name="norms",
-    )(tile_row, tile_values)
+    )(put, tile_row, told, tile_values)
 
 
 def stage_kernel(q, base, last, cached, fold_order, fold_bound, score_order, score_bound, meta,
                  place, done, labels, before, inv_hbm, x_hbm, hot_hbm, *refs):
     earlier, refs = refs[:q], refs[q:]
     sums_in, refs = (refs[0], refs[1:]) if q else (None, refs)
-    part, sums_out, extra = refs[:3]
-    inv, x, hot, sums, narrow, tiles, products, sems = refs[3:]
-    fresh = tiles.at[pl.ds(base, x.shape[0])]
+    part, sums_out, extra = (*refs[:2], None) if last else refs[:3]
+    refs = refs[2:] if last else refs[3:]
+    inv, x, hot, sums, narrow, tiles, products, scores, sems = refs
+    devices, width = x.shape[0], x.shape[1] // LANES
+    fresh = tiles.at[pl.ds(base, devices * width)]
+    from_hbm = x_hbm.at[:, pl.ds(0, width * LANES)]
     needed = [
-        pltpu.make_async_copy(x_hbm, x, sems.at[0]),
+        pltpu.make_async_copy(from_hbm, x, sems.at[0]),
         pltpu.make_async_copy(inv_hbm, inv, sems.at[1]),
     ]
     if q:
@@ -179,7 +176,7 @@
     for copy in needed + later:
         copy.start()
     products[...] = jnp.zeros_like(products)
-    part[...] = before[...]
+    scores[...] = before[...]
     if not q:
         sums[...] = jnp.zeros_like(sums)
     for copy in needed:
@@ -207,7 +204,9 @@
             rows, spots = quad(fold_order, start, end, p)
             folded, picks = [], []
             for (row, held), spot in zip(rows, spots):
-                root = x[spot - base].astype(jnp.int32).astype(jnp.float32) + float(CODE_SHIFT)
+                source, slot = (spot - base) // width, (spot - base) % width
+                raw = x[source, pl.ds(pl.multiple_of(slot * LANES, LANES), LANES), :]
+                root = raw.astype(jnp.int32).astype(jnp.float32) + float(CODE_SHIFT)
                 tile = (root * root * inv[row]).astype(jnp.bfloat16)
                 tiles[spot] = tile
                 folded.append(tile)
@@ -233,7 +232,9 @@
         for sub in range(TB_OWN):
             some = sums[:, sub * LANES : (sub + 1) * LANES]
             total = total + some * some
-        extra[...] = lane_sums(total)
+        square = lane_sums(total)[:1]
+        for d in range(devices):
+            part[d, :, part.shape[2] - K :] = square
     for copy in later:
         copy.wait()
 
@@ -262,48 +263,59 @@
         return carry
 
     lax.fori_loop(done[q], done[q + 1], score_sub, 0)
-    block_sums(products, part, none)
+    block_sums(products, scores, none)
+    if last:
+        own = none // devices
+        for d in range(devices):
+            for b in range(own):
+                at = d * own + b
+                part[d, :, b * LANES : (b + 1) * LANES] = scores[at : at + 1, :]
+    else:
+        part[...] = scores[...]
     for copy in results:
         copy.wait()
 
 
 def stage(q, cuts, scalars, labels, before, inverse, x, hot, normed, sums):
-    devices, width = x.shape[:2]
+    devices = x.shape[0]
     last = q == len(cuts) - 2
     blocks = inverse.shape[0]
     cached = blocks <= CACHED_BLOCKS
-    flat = x.reshape((devices * width, LANES, LANES))
-    tile_rows = devices * cuts[-1]
+    width = cuts[q + 1] - cuts[q]
+    home = blocks // devices * LANES
     wide = jax.ShapeDtypeStruct((K, TB_OWN * LANES), jnp.float32)
+    if last:
+        out_shape = [jax.ShapeDtypeStruct((devices, 1, home + K), jnp.float32), wide]
+    else:
+        out_shape = [
+            jax.ShapeDtypeStruct((blocks, LANES), jnp.float32),
+            wide,
+            jax.ShapeDtypeStruct((devices * width, LANES, LANES), jnp.bfloat16),
+        ]
     return pl.pallas_call(
         functools.partial(stage_kernel, q, devices * cuts[q], last, cached),
         in_specs=[SMEM] * len(scalars) + [VMEM] * 2 + [ANY] * (3 + q + (q > 0)),
-        out_specs=[VMEM, ANY, VMEM if last else ANY],
-        out_shape=[
-            jax.ShapeDtypeStruct((blocks, LANES), jnp.float32),
-            wide,
-            jax.ShapeDtypeStruct((8, K), jnp.float32)
-            if last
-            else jax.ShapeDtypeStruct(flat.shape, jnp.bfloat16),
-        ],
+        out_specs=[VMEM, ANY, ANY][: len(out_shape)],
+        out_shape=out_shape,
         scratch_shapes=[
             pltpu.VMEM(inverse.shape, jnp.float32),
-            pltpu.VMEM(flat.shape, jnp.int16),
+            pltpu.VMEM((devices, width * LANES, LANES), jnp.int16),
             pltpu.VMEM(hot.shape if cached else (QUAD, LANES, K), jnp.bfloat16),
             pltpu.VMEM(wide.shape, jnp.float32),
             pltpu.VMEM((K, LANES), jnp.bfloat16),
-            pltpu.VMEM((tile_rows, LANES, LANES), jnp.bfloat16),
+            pltpu.VMEM((devices * cuts[-1], LANES, LANES), jnp.bfloat16),
             pltpu.VMEM((blocks + 1, LANES, LANES), jnp.float32),
+            pltpu.VMEM((blocks, LANES), jnp.float32),
             pltpu.SemaphoreType.DMA((6 + len(cuts),)),
         ],
         compiler_params=params(),
         cost_estimate=pl.CostEstimate(
-            flops=x.size * K * 8,
-            bytes_accessed=4 * x.size + 4 * inverse.size + 8 * K * TB_OWN * LANES,
+            flops=devices * width * LANES * LANES * K * 8,
+            bytes_accessed=4 * devices * width * LANES * LANES + 8 * K * TB_OWN * LANES,
             transcendentals=0,
         ),
         name="stage",
-    )(*scalars, labels, before, inverse, flat, hot, *normed, *([sums] if q else []))
+    )(*scalars, labels, before, inverse, x, hot, *normed, *([sums] if q else []))
 
 
 def exchange(x):
@@ -342,25 +354,26 @@
     home = labels.shape[0]
     blocks = home // LANES * devices
     cap = max(2, 2 * tiles // devices)
-    cuts = tuple(sorted({int(cap * share) for share in PARTS}))
+    cuts = tuple(sorted({int(cap * share) for share in PARTS})) if cap >= 8 else (0, cap)
     parts = len(cuts) - 1
     here = lax.axis_index("dp").astype(jnp.int32)
     owner = tile_owner[:, 0]
 
-    outgoing = pack(tile_values, owner * cap + ranks(owner, tile_sub), devices, cuts)
+    put = owner * cap + ranks(owner, tile_sub)
+    told = jnp.concatenate([labels, owner, tile_row * TB_OWN + tile_sub]).reshape(-1, LANES)
+    told = jnp.pad(told, ((0, -(blocks + told.shape[0]) % 16), (0, 0)))
+    outgoing = pack(tile_values, put, tile_row, told, devices, blocks, cuts)
     incoming = [exchange(outgoing[0])]
-    partial_sq = norms(after(tile_values, outgoing[0]), tile_row, blocks)
-    described = jnp.concatenate([labels, owner, tile_row * TB_OWN + tile_sub])
-    told = jnp.concatenate([partial_sq.reshape(-1), described.astype(jnp.float32)])
-    heard = exchange(jnp.broadcast_to(told[None], (devices, told.shape[0])))
-
-    row_sq = jnp.sum(heard[:, : blocks * LANES], axis=0).reshape(blocks, LANES)
-    all_described = heard[:, blocks * LANES :].astype(jnp.int32)
+    heard = incoming[0][:, (cuts[1] - cuts[0]) * LANES :].astype(jnp.int32)
+    level = heard[:, :blocks]
+    partial_sq = jnp.exp2(level.astype(jnp.float32) * (1.0 / LOG_STEPS) + LOG_MIDDLE)
+    row_sq = jnp.sum(jnp.where(level > -32768, partial_sq, 0.0), axis=0)
+    all_described = heard[:, blocks:].reshape(devices, -1)
     all_labels = all_described[:, :home].reshape(blocks, LANES)
     padded_labels = jnp.concatenate([all_labels, jnp.full((1, LANES), -1, jnp.int32)])
     hot = (padded_labels[:, :, None] == jnp.arange(K, dtype=jnp.int32)).astype(jnp.bfloat16)
     mine = all_described[:, home : home + tiles] == here
-    code = all_described[:, home + tiles :]
+    code = all_described[:, home + tiles : home + 2 * tiles]
     rank = ranks(mine.astype(jnp.int32), code % TB_OWN)
     chosen = mine[:, None, :] & (rank[:, None, :] == jnp.arange(cap)[None, :, None])
     meta = jnp.sum(jnp.where(chosen, code[:, None, :] + 1, 0), axis=2).reshape(-1) - 1
@@ -385,16 +398,14 @@
     beside = (*scalars, padded_labels, hot, scale)
     for q in range(parts):
         if q + 1 < parts:
-            incoming.append(exchange(after(outgoing[q + 1], incoming[q], *beside)))
-        partial, sums, extra = stage(
+            ahead = (incoming[q], *beside) if q else (incoming[q],)
+            incoming.append(exchange(after(outgoing[q + 1], *ahead)))
+        partial, sums, *extra = stage(
             q, cuts, scalars, padded_labels, partial, scale, incoming[q], hot, normed, sums
         )
-        beside = (partial, sums, extra)
-        normed.append(extra)
-    square = jnp.broadcast_to(extra[:1], (devices, K))
-    back = jnp.sum(
-        exchange(jnp.concatenate([partial.reshape(devices, home), square], axis=1)), axis=0
-    )
+        beside = (partial, sums)
+        normed += extra
+    back = jnp.sum(exchange(partial), axis=(0, 1))
     own_scale = lax.rsqrt(back[home:] + EPSILON)
     vocab_size = TB_OWN * LANES * devices
     centroid = sums * own_scale[:, None]

time: 281 us -> 267 us (0.950)
  Pallas kernels: 57.3 us -> 44.8 us
  waiting for transfers between devices: 122 us -> 127 us
    pallas_call x1 -> x0, Pallas kernels: 7.85 us -> none  [norms(): pl.pallas_call(norms_kernel, grid=(tiles // step,), in_specs=[SMEM, pl.Bl...]
    all_to_all x3 -> x2, waiting for transfers between devices: 122 us -> 127 us  [exchange(): return lax.all_to_all(x, 'dp', split_axis=0, concat_axis=0, tiled=True)]
    pallas_call x3 -> x2, Pallas kernels: 39.7 us -> 35.4 us  [stage(): pl.pallas_call(functools.partial(stage_kernel, q, devices * cuts[q], last...]
    all_to_all x2 -> x1, blocking collectives: 36.8 us -> 35.2 us  [exchange(): return lax.all_to_all(x, 'dp', split_axis=0, concat_axis=0, tiled=True)]
    all_to_all x3 -> x2, starting transfers between devices: 39.7 us -> 38.4 us  [exchange(): return lax.all_to_all(x, 'dp', split_axis=0, concat_axis=0, tiled=True)]
  transfers between devices with their start and end apart: 3 -> 2, of which waited for: 3 -> 1; matrix products, arithmetic and copies ran while one was open for 3% -> 4% of each run, Pallas kernels for 10% -> 9%
where the time goes in v4:
time: 267 us
  waiting for transfers between devices  127 us (48%)
  Pallas kernels  44.8 us (17%)
  starting transfers between devices  38.4 us (14%)
  blocking collectives  35.2 us (13%)
  other arithmetic  16.8 us (6%)
  local copies, waits for them, and re-layouts  4.47 us (2%)
    all_to_all x2, waiting for transfers between devices, exchange(): return lax.all_to_all(x, 'dp', split_axis=0, concat_axis=0, tiled=True)  127 us
    all_to_all x2, starting transfers between devices, exchange(): return lax.all_to_all(x, 'dp', split_axis=0, concat_axis=0, tiled=True)  38.4 us
    pallas_call x2, Pallas kernels, stage(): pl.pallas_call(functools.partial(stage_kernel, q, devices * cuts[q], last...  35.4 us
    all_to_all x1, blocking collectives, exchange(): return lax.all_to_all(x, 'dp', split_axis=0, concat_axis=0, tiled=True)  35.2 us
    pallas_call x1, Pallas kernels, pack(): pl.pallas_call(functools.partial(pack_kernel, cuts), grid=(tiles // step,...  9.38 us
  transfers between devices with their start and end apart: 2, of which 1 were waited for; matrix products, arithmetic and copies ran while one was open for 4% of the time, Pallas kernels for 9%

profile of v4, /device:TPU:0, one launch (start us, length us, event | category | flops | bytes accessed | tf_op | source)
XLA Modules:
  0.0 267.2 jit_solution(6559687769876793499)
XLA Ops:
  0.6 0.7 multiply_add_fusion
  1.3 0.9 convert_reduce_fusion.3
  2.2 1.2 multiply_add_fusion.1.put_ref
  3.4 0.7 add_bitcast_fusion
  4.1 0.6 pad.5.told_ref
  4.7 9.4 %pack.1 = (s16[16,1712,128]{2,1,0:T(8,128)(2,1)}, s16[16,384,128]{2,1,0:T(8,128)(2,1)}) custom-call(s32[128]{0:T(128)} %multiply_add_fusion.1.put_ref, s32[128]{0:T(128)} %row_ref.1, s32[16,128]{1,0:T(8,128)} %pad.5.told_ref, f32[128,128,128]{2,1,0:T(8,128)} %x_ref.1), custom_call_target="tpu_custom_call" | custom-call | flops 16777216 | bytes 12582912 | tf_op jit(solution)/shard_map/pack/pallas_call | solution.py:129
  14.1 7.5 %all-to-all-start = ((s16[16,1712,128]{2,1,0:T(8,128)(2,1)}), s16[16,1712,128]{2,1,0:T(8,128)(2,1)}, u32[]{:S(2)}, u32[]{:S(2)}) async-start(s16[16,1712,128]{2,1,0:T(8,128)(2,1)} %get-tuple-element.10), calls=%async_computation | async-start | bytes 14024704 | tf_op jit(solution)/shard_map/all_to_all | solution.py:322
  21.6 126.7 %all-to-all-done.x_hbm = s16[16,1712,128]{2,1,0:T(8,128)(2,1)} async-done(((s16[16,1712,128]{2,1,0:T(8,128)(2,1)}), s16[16,1712,128]{2,1,0:T(8,128)(2,1)}, u32[]{:S(2)}, u32[]{:S(2)}) %all-to-all-start) | async-done | bytes 7012384 | tf_op jit(solution)/shard_map/all_to_all | solution.py:322
  148.3 1.0 slice_convert_fusion
  149.4 31.0 %all-to-all-start.1 = ((s16[16,384,128]{2,1,0:T(8,128)(2,1)}), s16[16,384,128]{2,1,0:T(8,128)(2,1)S(1)}, u32[]{:S(2)}, u32[]{:S(2)}) async-start(s16[16,384,128]{2,1,0:T(8,128)(2,1)} %get-tuple-element.13), calls=%async_computation.1 | async-start | bytes 3145728 | tf_op jit(solution)/shard_map/all_to_all | solution.py:322
  180.4 1.0 convert_reduce_fusion
  182.6 0.7 convert_reduce_fusion.5.score_bound
  183.3 0.6 convert_reduce_fusion.4.fold_bound
  184.2 0.7 select_reduce_fusion.2.score_order
  184.9 0.7 select_reduce_fusion.3.fold_order
  185.7 2.4 fusion.hot_hbm
  188.1 1.9 broadcast_in_dim.62.inv_hbm
  190.0 0.6 broadcast_in_dim.60.before
  190.6 24.8 %stage.2 = (f32[32,128]{1,0:T(8,128)}, f32[512,2048]{1,0:T(8,128)}, bf16[208,128,128]{2,1,0:T(8,128)(2,1)}) custom-call(s32[256]{0:T(256)} %select_reduce_fusion.3.fold_order, s32[35]{0:T(128)} %convert_reduce_fusion.4.fold_bound, s32[256]{0:T(256)} %select_reduce_fusion.2.score_order, s32[17]{0:T(128)} %convert_reduce_fusion.5.score_bound, s32[256]{0:T(256)} %copy-done.2, ...), custom_call_target="tpu_custom_call" | custom-call | flops 13958643712 | bytes 22020096 | tf_op jit(solution)/shard_map/stage/pallas_call | solution.py:295
  215.5 1.2 copy-done
  216.6 10.6 %stage.3 = (f32[16,1,768]{2,1,0:T(1,128)}, f32[512,2048]{1,0:T(8,128)}) custom-call(s32[256]{0:T(256)} %select_reduce_fusion.3.fold_order, s32[35]{0:T(128)} %convert_reduce_fusion.4.fold_bound, s32[256]{0:T(256)} %select_reduce_fusion.2.score_order, s32[17]{0:T(128)} %convert_reduce_fusion.5.score_bound, s32[256]{0:T(256)} %copy-done.2, ...), custom_call_target="tpu_custom_call" | custom-call | flops 3221225472 | bytes 11534336 | tf_op jit(solution)/shard_map/stage/pallas_call | solution.py:295
  227.3 35.2 %all_to_all.15 = f32[16,1,768]{2,1,0:T(1,128)S(1)} all-to-all(f32[16,1,768]{2,1,0:T(1,128)} %get-tuple-element.17), channel_id=1, replica_groups=mesh['groups'=2,'dp'=16] {'dp'}, dimensions={0} | all-to-all | bytes 98304 | tf_op jit(solution)/shard_map/all_to_all | solution.py:322
  262.7 3.9 %multiply_convert_fusion = bf16[512,2048]{1,0:T(8,128)(2,1)} fusion(f32[512,2048]{1,0:T(8,128)} %get-tuple-element.16, f32[512]{0:T(512)S(1)} %add_rsqrt_fusion), kind=kLoop, calls=%fused_computation.2 | loop fusion | flops 3145728 | bytes 6293504 | tf_op jit(solution)/shard_map/convert_element_type | solution.py:412
  266.6 0.6 slice_multiply_fusion
  (32 shorter events, 1.9 us)
Async XLA Ops:
  14.1 134.2 %all-to-all-start = ((s16[16,1712,128]{2,1,0:T(8,128)(2,1)}), s16[16,1712,128]{2,1,0:T(8,128)(2,1)}, u32[]{:S(2)}, u32[]{:S(2)}) async-start(s16[16,1712,128]{2,1,0:T(8,128)(2,1)} %get-tuple-element.10), calls=%async_computation | async-start | bytes 14024704 | tf_op jit(solution)/shard_map/all_to_all | solution.py:322
  21.5 160.3 %copy-start.5 = (s32[256]{0:T(256)S(1)}, s32[256]{0:T(256)}, u32[]{:S(2)}) copy-start(s32[256]{0:T(256)} %constant.68.clone) | copy-start | bytes 3076
  21.6 160.4 %copy-start.4 = (pred[2,256]{1,0:T(4,128)(4,1)S(1)}, pred[2,256]{1,0:T(4,128)(4,1)}, u32[]{:S(2)}) copy-start(pred[2,256]{1,0:T(4,128)(4,1)} %constant.69.clone) | copy-start | bytes 1540
  149.4 66.1 %all-to-all-start.1 = ((s16[16,384,128]{2,1,0:T(8,128)(2,1)}), s16[16,384,128]{2,1,0:T(8,128)(2,1)S(1)}, u32[]{:S(2)}, u32[]{:S(2)}) async-start(s16[16,384,128]{2,1,0:T(8,128)(2,1)} %get-tuple-element.13), calls=%async_computation.1 | async-start | bytes 3145728 | tf_op jit(solution)/shard_map/all_to_all | solution.py:322
  181.9 8.8 %copy-start.2 = (s32[256]{0:T(256)}, s32[256]{0:T(256)S(1)}, u32[]{:S(2)}) copy-start(s32[256]{0:T(256)S(1)} %sub.7.meta) | copy-start | bytes 3076
  181.9 8.7 %copy-start.1 = (s32[33,128]{1,0:T(8,128)}, s32[33,128]{1,0:T(8,128)S(1)}, u32[]{:S(2)}) copy-start(s32[33,128]{1,0:T(8,128)S(1)} %concatenate.11.labels) | copy-start | bytes 50692
  215.4 1.2 copy-start
  216.6 45.9 %copy-start.3 = (s32[256]{0:T(256)S(1)}, s32[256]{0:T(256)}, u32[]{:S(2)}) copy-start(s32[256]{0:T(256)} %param.12) | copy-start | bytes 3076

commit v5 on v4

--- a/solution.py
+++ b/solution.py
@@ -17,11 +17,12 @@
 CODE_SHIFT = 32768
 VMEM_BYTES = 56 * 1024 * 1024
 STEP_TILES = 32
-PARTS = (0.0, 13 / 16, 1.0)
+PARTS = (0.0, 12 / 16, 1.0)
 LOG_STEPS = 1800.0
 LOG_MIDDLE = -3.0
 CACHED_BLOCKS = 64
 QUAD = 4
+EIGHT = 8
 BATCH = 8
 NT = (((1,), (1,)), ((), ()))
 SMEM = pl.BlockSpec(memory_space=pltpu.SMEM)
@@ -55,10 +56,11 @@
     return pltpu.CompilerParams(vmem_limit_bytes=VMEM_BYTES)
 
 
-def pack_kernel(cuts, put_ref, row_ref, told_ref, x_ref, *refs):
+def pack_kernel(cuts, put_ref, row_ref, *refs):
     parts = len(cuts) - 1
+    (*told_refs, x_ref), refs = refs[:5], refs[5:]
     outs = refs[:parts]
-    coded, square, sums, notes, held, sems = refs[parts:]
+    coded, square, sums, words, notes, held, sems = refs[parts:]
     step = pl.program_id(0)
     tiles = x_ref.shape[0]
     devices = held.shape[0]
@@ -112,7 +114,14 @@
         level = (jnp.log2(jnp.maximum(total, 1e-30)) - LOG_MIDDLE) * LOG_STEPS
         level = jnp.where(total > 0.0, jnp.clip(level, -32700.0, 32700.0), -32768.0)
         level = (level + 32768.5).astype(jnp.int32) - 32768
-        notes[...] = jnp.concatenate([level, told_ref[...]], axis=0).astype(jnp.int16)
+        labels, owner, row, sub = [ref[...] for ref in told_refs]
+        words[...] = jnp.zeros_like(words)
+        words[:blocks, :] = level
+        at = blocks
+        for told in (labels, owner, row * TB_OWN + sub):
+            words[at : at + told.shape[0], :] = told
+            at += told.shape[0]
+        notes[...] = words[...].astype(jnp.int16)
         for d in range(devices):
             note(d).start()
         each(lambda copy: copy.wait())
@@ -123,13 +132,15 @@
 def pack(tile_values, put, tile_row, told, devices, blocks, cuts):
     tiles = tile_values.shape[0]
     step = math.gcd(STEP_TILES, tiles)
-    noted = blocks + told.shape[0]
+    told = [x.reshape(-1, LANES) for x in told]
+    noted = -(-(blocks + sum(x.shape[0] for x in told[:3])) // 16) * 16
     rows = [(high - low) * LANES for low, high in zip(cuts, cuts[1:])]
     rows[0] += noted
     return pl.pallas_call(
         functools.partial(pack_kernel, cuts),
         grid=(tiles // step,),
-        in_specs=[SMEM, SMEM, pl.BlockSpec(told.shape, lambda i: (0, 0))]
+        in_specs=[SMEM, SMEM]
+        + [pl.BlockSpec(x.shape, lambda i: (0, 0)) for x in told]
         + [pl.BlockSpec((step, LANES, LANES), lambda i: (i, 0, 0))],
         out_specs=[ANY] * len(rows),
         out_shape=[jax.ShapeDtypeStruct((devices, some, LANES), jnp.int16) for some in rows],
@@ -137,6 +148,7 @@
             pltpu.VMEM((devices * cuts[-1] * LANES, LANES), jnp.int16),
             pltpu.VMEM((blocks, LANES, LANES), jnp.float32),
             pltpu.VMEM((blocks, LANES), jnp.float32),
+            pltpu.VMEM((noted, LANES), jnp.int32),
             pltpu.VMEM((noted, LANES), jnp.int16),
             pltpu.SMEM((devices,), jnp.int32),
             pltpu.SemaphoreType.DMA(((len(rows) + 1) * devices,)),
@@ -148,7 +160,7 @@
             transcendentals=tile_values.size,
         ),
         name="pack",
-    )(put, tile_row, told, tile_values)
+    )(put, tile_row, *told, tile_values)
 
 
 def stage_kernel(q, base, last, cached, fold_order, fold_bound, score_order, score_bound, meta,
@@ -187,10 +199,10 @@
     def columns(sub):
         return (slice(None), pl.ds(pl.multiple_of(sub * LANES, LANES), LANES))
 
-    def quad(order, start, end, p):
+    def eight(order, start, end, p):
         rows, spots = [], []
-        for j in range(QUAD):
-            at = start + QUAD * p + j
+        for j in range(EIGHT):
+            at = start + EIGHT * p + j
             slot = order[jnp.where(at < end, at, start)]
             rows.append((meta[slot] // TB_OWN, at < end))
             spots.append(place[slot])
@@ -200,8 +212,8 @@
         start = fold_bound[q * (TB_OWN + 1) + sub]
         end = fold_bound[q * (TB_OWN + 1) + sub + 1]
 
-        def one_quad(p, carry):
-            rows, spots = quad(fold_order, start, end, p)
+        def one_eight(p, carry):
+            rows, spots = eight(fold_order, start, end, p)
             folded, picks = [], []
             for (row, held), spot in zip(rows, spots):
                 source, slot = (spot - base) // width, (spot - base) % width
@@ -218,7 +230,7 @@
             )
             return carry
 
-        lax.fori_loop(0, (end - start + QUAD - 1) // QUAD, one_quad, 0)
+        lax.fori_loop(0, (end - start + EIGHT - 1) // EIGHT, one_eight, 0)
         return carry
 
     lax.fori_loop(0, TB_OWN, fold_sub, 0)
@@ -242,24 +254,24 @@
         start, end = score_bound[sub], score_bound[sub + 1]
         narrow[...] = sums[columns(sub)].astype(jnp.bfloat16)
 
-        def one_quad(p, carry):
-            rows, spots = quad(score_order, start, end, p)
+        def one_eight(p, carry):
+            rows, spots = eight(score_order, start, end, p)
             rows = [jnp.where(held, row, none) for row, held in rows]
             if cached:
                 hots = [hot[row] for row in rows]
             else:
                 for j, row in enumerate(rows):
                     pltpu.sync_copy(hot_hbm.at[row], hot.at[j])
-                hots = [hot[j] for j in range(QUAD)]
+                hots = [hot[j] for j in range(EIGHT)]
             chosen = jnp.dot(
                 jnp.concatenate(hots, axis=0), narrow[...], preferred_element_type=jnp.float32
             )
-            for j in range(QUAD):
+            for j in range(EIGHT):
                 own = chosen[j * LANES : (j + 1) * LANES]
                 products[rows[j]] += own * tiles[spots[j]].astype(jnp.float32)
             return carry
 
-        lax.fori_loop(0, (end - start + QUAD - 1) // QUAD, one_quad, 0)
+        lax.fori_loop(0, (end - start + EIGHT - 1) // EIGHT, one_eight, 0)
         return carry
 
     lax.fori_loop(done[q], done[q + 1], score_sub, 0)
@@ -300,7 +312,7 @@
         scratch_shapes=[
             pltpu.VMEM(inverse.shape, jnp.float32),
             pltpu.VMEM((devices, width * LANES, LANES), jnp.int16),
-            pltpu.VMEM(hot.shape if cached else (QUAD, LANES, K), jnp.bfloat16),
+            pltpu.VMEM(hot.shape if cached else (EIGHT, LANES, K), jnp.bfloat16),
             pltpu.VMEM(wide.shape, jnp.float32),
             pltpu.VMEM((K, LANES), jnp.bfloat16),
             pltpu.VMEM((devices * cuts[-1], LANES, LANES), jnp.bfloat16),
@@ -360,8 +372,7 @@
     owner = tile_owner[:, 0]
 
     put = owner * cap + ranks(owner, tile_sub)
-    told = jnp.concatenate([labels, owner, tile_row * TB_OWN + tile_sub]).reshape(-1, LANES)
-    told = jnp.pad(told, ((0, -(blocks + told.shape[0]) % 16), (0, 0)))
+    told = (labels, owner, tile_row, tile_sub)
     outgoing = pack(tile_values, put, tile_row, told, devices, blocks, cuts)
     incoming = [exchange(outgoing[0])]
     heard = incoming[0][:, (cuts[1] - cuts[0]) * LANES :].astype(jnp.int32)

time: 267 us -> 252 us (0.944)
  the two profiles are of different devices: /device:TPU:0 before, /device:TPU:4 now
where the time goes in v5:
time: 252 us; the launch traced here: 253 us
  waiting for transfers between devices  120 us (48%)
  Pallas kernels  46.9 us (19%)
  starting transfers between devices  34.9 us (14%)
  blocking collectives  31.1 us (12%)
  other arithmetic  15.5 us (6%)
  local copies, waits for them, and re-layouts  4.05 us (2%)
    all_to_all x2, waiting for transfers between devices, exchange(): return lax.all_to_all(x, 'dp', split_axis=0, concat_axis=0, tiled=True)  120 us
    pallas_call x2, Pallas kernels, stage(): pl.pallas_call(functools.partial(stage_kernel, q, devices * cuts[q], last...  37.8 us
    all_to_all x2, starting transfers between devices, exchange(): return lax.all_to_all(x, 'dp', split_axis=0, concat_axis=0, tiled=True)  34.9 us
    all_to_all x1, blocking collectives, exchange(): return lax.all_to_all(x, 'dp', split_axis=0, concat_axis=0, tiled=True)  31.1 us
    pallas_call x1, Pallas kernels, pack(): pl.pallas_call(functools.partial(pack_kernel, cuts), grid=(tiles // step,...  9.03 us
  transfers between devices with their start and end apart: 2, of which 2 were waited for; matrix products, arithmetic and copies ran while one was open for 4% of the time, Pallas kernels for 11%

profile of v5, /device:TPU:4, one launch (start us, length us, event | category | flops | bytes accessed | tf_op | source)
XLA Modules:
  0.0 253.2 jit_solution(7616000733855320839)
XLA Ops:
  0.6 0.9 convert_reduce_fusion.3
  1.5 1.2 multiply_add_fusion.put_ref
  2.7 9.0 %pack.1 = (s16[16,1584,128]{2,1,0:T(8,128)(2,1)}, s16[16,512,128]{2,1,0:T(8,128)(2,1)}) custom-call(s32[128]{0:T(128)} %multiply_add_fusion.put_ref, s32[128]{0:T(128)} %row_ref.1, s32[2,128]{1,0:T(2,128)} %bitcast.17, s32[1,128]{1,0:T(1,128)} %bitcast.15, s32[1,128]{1,0:T(1,128)} %bitcast.18, s32[1,128]{1,0:T(1,128)} %bitcast.16, f32[128,128,128]{2,1,0:T(8,128)} %refs_4_.1), custom_call_target="tpu_custom_call" | custom-call | flops 16777216 | bytes 12582912 | tf_op jit(solution)/shard_map/pack/pallas_call | solution.py:139
  11.8 6.0 %all-to-all-start = ((s16[16,1584,128]{2,1,0:T(8,128)(2,1)}), s16[16,1584,128]{2,1,0:T(8,128)(2,1)}, u32[]{:S(2)}, u32[]{:S(2)}) async-start(s16[16,1584,128]{2,1,0:T(8,128)(2,1)} %get-tuple-element.10), calls=%async_computation | async-start | bytes 12976128 | tf_op jit(solution)/shard_map/all_to_all | solution.py:334
  17.8 117.6 %all-to-all-done.x_hbm = s16[16,1584,128]{2,1,0:T(8,128)(2,1)} async-done(((s16[16,1584,128]{2,1,0:T(8,128)(2,1)}), s16[16,1584,128]{2,1,0:T(8,128)(2,1)}, u32[]{:S(2)}, u32[]{:S(2)}) %all-to-all-start) | async-done | bytes 6488096 | tf_op jit(solution)/shard_map/all_to_all | solution.py:334
  135.4 28.9 %all-to-all-start.1 = ((s16[16,512,128]{2,1,0:T(8,128)(2,1)}), s16[16,512,128]{2,1,0:T(8,128)(2,1)S(1)}, u32[]{:S(2)}, u32[]{:S(2)}) async-start(s16[16,512,128]{2,1,0:T(8,128)(2,1)} %get-tuple-element.13), calls=%async_computation.1 | async-start | bytes 4194304 | tf_op jit(solution)/shard_map/all_to_all | solution.py:334
  164.3 1.0 slice_convert_fusion
  165.3 1.0 convert_reduce_fusion
  166.4 0.3 select_reduce_fusion.4
  167.0 0.7 pad_add_fusion.done
  167.7 0.7 convert_reduce_fusion.5.score_bound
  168.4 0.7 convert_reduce_fusion.4.fold_bound
  169.4 0.6 select_reduce_fusion.2.score_order
  170.0 0.7 select_reduce_fusion.3.fold_order
  170.8 2.4 fusion.hot_hbm
  173.2 2.0 broadcast_in_dim.65.inv_hbm
  175.2 0.6 broadcast_in_dim.63.before
  175.8 27.2 %stage.2 = (f32[32,128]{1,0:T(8,128)}, f32[512,2048]{1,0:T(8,128)}, bf16[192,128,128]{2,1,0:T(8,128)(2,1)}) custom-call(s32[256]{0:T(256)} %select_reduce_fusion.3.fold_order, s32[35]{0:T(128)} %convert_reduce_fusion.4.fold_bound, s32[256]{0:T(256)} %select_reduce_fusion.2.score_order, s32[17]{0:T(128)} %convert_reduce_fusion.5.score_bound, s32[256]{0:T(256)} %copy-done.2, ...), custom_call_target="tpu_custom_call" | custom-call | flops 12884901888 | bytes 20971520 | tf_op jit(solution)/shard_map/stage/pallas_call | solution.py:307
  203.0 2.4 all-to-all-done.1.x_hbm
  205.4 1.3 copy-done
  206.7 10.7 %stage.3 = (f32[16,1,768]{2,1,0:T(1,128)}, f32[512,2048]{1,0:T(8,128)}) custom-call(s32[256]{0:T(256)} %select_reduce_fusion.3.fold_order, s32[35]{0:T(128)} %convert_reduce_fusion.4.fold_bound, s32[256]{0:T(256)} %select_reduce_fusion.2.score_order, s32[17]{0:T(128)} %convert_reduce_fusion.5.score_bound, s32[256]{0:T(256)} %copy-done.2, ...), custom_call_target="tpu_custom_call" | custom-call | flops 4294967296 | bytes 12582912 | tf_op jit(solution)/shard_map/stage/pallas_call | solution.py:307
  217.3 31.1 %all_to_all.15 = f32[16,1,768]{2,1,0:T(1,128)S(1)} all-to-all(f32[16,1,768]{2,1,0:T(1,128)} %get-tuple-element.17), channel_id=1, replica_groups=mesh['groups'=2,'dp'=16] {'dp'}, dimensions={0} | all-to-all | bytes 98304 | tf_op jit(solution)/shard_map/all_to_all | solution.py:334
  248.8 3.9 %multiply_convert_fusion = bf16[512,2048]{1,0:T(8,128)(2,1)} fusion(f32[512,2048]{1,0:T(8,128)} %get-tuple-element.16, f32[512]{0:T(512)S(1)} %add_rsqrt_fusion), kind=kLoop, calls=%fused_computation.2 | loop fusion | flops 3145728 | bytes 6293504 | tf_op jit(solution)/shard_map/convert_element_type | solution.py:423
  252.7 0.6 slice_multiply_fusion
  (29 shorter events, 1.0 us)
Async XLA Ops:
  11.8 123.6 %all-to-all-start = ((s16[16,1584,128]{2,1,0:T(8,128)(2,1)}), s16[16,1584,128]{2,1,0:T(8,128)(2,1)}, u32[]{:S(2)}, u32[]{:S(2)}) async-start(s16[16,1584,128]{2,1,0:T(8,128)(2,1)} %get-tuple-element.10), calls=%async_computation | async-start | bytes 12976128 | tf_op jit(solution)/shard_map/all_to_all | solution.py:334
  17.8 149.1 %copy-start.5 = (s32[256]{0:T(256)S(1)}, s32[256]{0:T(256)}, u32[]{:S(2)}) copy-start(s32[256]{0:T(256)} %constant.68.clone) | copy-start | bytes 3076
  17.8 149.1 %copy-start.4 = (pred[2,256]{1,0:T(4,128)(4,1)S(1)}, pred[2,256]{1,0:T(4,128)(4,1)}, u32[]{:S(2)}) copy-start(pred[2,256]{1,0:T(4,128)(4,1)} %constant.69.clone) | copy-start | bytes 1540
  135.4 70.0 %all-to-all-start.1 = ((s16[16,512,128]{2,1,0:T(8,128)(2,1)}), s16[16,512,128]{2,1,0:T(8,128)(2,1)S(1)}, u32[]{:S(2)}, u32[]{:S(2)}) async-start(s16[16,512,128]{2,1,0:T(8,128)(2,1)} %get-tuple-element.13), calls=%async_computation.1 | async-start | bytes 4194304 | tf_op jit(solution)/shard_map/all_to_all | solution.py:334
  166.8 8.9 %copy-start.2 = (s32[256]{0:T(256)}, s32[256]{0:T(256)S(1)}, u32[]{:S(2)}) copy-start(s32[256]{0:T(256)S(1)} %sub.7.meta) | copy-start | bytes 3076
  166.9 8.9 %copy-start.1 = (s32[33,128]{1,0:T(8,128)}, s32[33,128]{1,0:T(8,128)S(1)}, u32[]{:S(2)}) copy-start(s32[33,128]{1,0:T(8,128)S(1)} %concatenate.7.labels) | copy-start | bytes 50692
  205.4 1.3 copy-start
  206.7 41.9 %copy-start.3 = (s32[256]{0:T(256)S(1)}, s32[256]{0:T(256)}, u32[]{:S(2)}) copy-start(s32[256]{0:T(256)} %param.12) | copy-start | bytes 3076

commit v6 on v5

--- a/solution.py
+++ b/solution.py
@@ -15,7 +15,7 @@
 EPSILON = 1e-06
 CODE_TOP = 65535.0
 CODE_SHIFT = 32768
-VMEM_BYTES = 56 * 1024 * 1024
+SPARE_BYTES = 6 * 1024 * 1024
 STEP_TILES = 32
 PARTS = (0.0, 12 / 16, 1.0)
 LOG_STEPS = 1800.0
@@ -52,8 +52,9 @@
     lax.fori_loop(0, count // batch, one_batch, 0)
 
 
-def params():
-    return pltpu.CompilerParams(vmem_limit_bytes=VMEM_BYTES)
+def params(*held):
+    need = sum(math.prod(shape) * jnp.dtype(dtype).itemsize for shape, dtype in held)
+    return pltpu.CompilerParams(vmem_limit_bytes=need + SPARE_BYTES)
 
 
 def pack_kernel(cuts, put_ref, row_ref, *refs):
@@ -153,7 +154,11 @@
             pltpu.SMEM((devices,), jnp.int32),
             pltpu.SemaphoreType.DMA(((len(rows) + 1) * devices,)),
         ],
-        compiler_params=params(),
+        compiler_params=params(
+            ((2 * step, LANES, LANES), jnp.float32),
+            ((devices * cuts[-1], LANES, LANES), jnp.int16),
+            ((blocks, LANES, LANES), jnp.float32),
+        ),
         cost_estimate=pl.CostEstimate(
             flops=8 * tile_values.size,
             bytes_accessed=6 * tile_values.size,
@@ -320,7 +325,14 @@
             pltpu.VMEM((blocks, LANES), jnp.float32),
             pltpu.SemaphoreType.DMA((6 + len(cuts),)),
         ],
-        compiler_params=params(),
+        compiler_params=params(
+            (inverse.shape, jnp.float32),
+            ((devices * width, LANES, LANES), jnp.int16),
+            (hot.shape if cached else (EIGHT, LANES, K), jnp.bfloat16),
+            (wide.shape, jnp.float32),
+            ((devices * cuts[-1], LANES, LANES), jnp.bfloat16),
+            ((blocks + 1, LANES, LANES), jnp.float32),
+        ),
         cost_estimate=pl.CostEstimate(
             flops=devices * width * LANES * LANES * K * 8,
             bytes_accessed=4 * devices * width * LANES * LANES + 8 * K * TB_OWN * LANES,

time: 252 us -> 267 us (1.060)
  the two profiles are of different devices: /device:TPU:4 before, /device:TPU:0 now
where the time goes in v6:
time: 267 us; the launch traced here: 266 us
  waiting for transfers between devices  122 us (46%)
  Pallas kernels  37.5 us (14%)
  starting transfers between devices  36.3 us (14%)
  local copies, waits for them, and re-layouts  29.6 us (11%)
  blocking collectives  29.2 us (11%)
  other arithmetic  10.7 us (4%)
    all_to_all x2, waiting for transfers between devices, exchange(): return lax.all_to_all(x, 'dp', split_axis=0, concat_axis=0, tiled=True)  122 us
    all_to_all x2, starting transfers between devices, exchange(): return lax.all_to_all(x, 'dp', split_axis=0, concat_axis=0, tiled=True)  36.3 us
    all_to_all x1, blocking collectives, exchange(): return lax.all_to_all(x, 'dp', split_axis=0, concat_axis=0, tiled=True)  29.2 us
    unnamed x41, local copies, waits for them, and re-layouts  28.9 us
    pallas_call x2, Pallas kernels, stage(): pl.pallas_call(functools.partial(stage_kernel, q, devices * cuts[q], last...  28.2 us
    pallas_call x1, Pallas kernels, pack(): pl.pallas_call(functools.partial(pack_kernel, cuts), grid=(tiles // step,...  9.38 us
  transfers between devices with their start and end apart: 2, of which 2 were waited for; matrix products, arithmetic and copies ran while one was open for 2% of the time, Pallas kernels for 9%

profile of v6, /device:TPU:0, one launch (start us, length us, event | category | flops | bytes accessed | tf_op | source)
XLA Modules:
  0.0 265.7 jit_solution(17049776074506097843)
XLA Ops:
  2.2 3.4 %copy-done.2 = f32[128,128,128]{2,1,0:T(8,128)S(1)} copy-done((f32[128,128,128]{2,1,0:T(8,128)S(1)}, f32[128,128,128]{2,1,0:T(8,128)}, u32[]{:S(2)}) %copy-start.2) | copy-done | bytes 8388632
  8.2 9.4 %pack.1 = (s16[16,1584,128]{2,1,0:T(8,128)(2,1)S(1)}, s16[16,512,128]{2,1,0:T(8,128)(2,1)S(1)}) custom-call(s32[128]{0:T(128)S(1)} %multiply_add_fusion.put_ref, s32[128]{0:T(128)S(1)} %copy-done.16, s32[2,128]{1,0:T(2,128)S(1)} %bitcast.13, s32[1,128]{1,0:T(1,128)S(1)} %bitcast.11, s32[1,128]{1,0:T(1,128)S(1)} %bitcast.14, s32[1,128]{1,0:T(1,128)S(1)} %bitcast.12, ...), custom_call_target="tpu_custom_call" | custom-call | flops 16777216 | bytes 12582912 | tf_op jit(solution)/shard_map/pack/pallas_call | solution.py:140
  17.6 2.7 %copy-done.5 = s16[16,1584,128]{2,1,0:T(8,128)(2,1)} copy-done((s16[16,1584,128]{2,1,0:T(8,128)(2,1)}, s16[16,1584,128]{2,1,0:T(8,128)(2,1)S(1)}, u32[]{:S(2)}) %copy-start.5) | copy-done | bytes 6488088
  20.3 1.3 copy-done.11
  21.6 7.4 %all-to-all-start = ((s16[16,1584,128]{2,1,0:T(8,128)(2,1)}), s16[16,1584,128]{2,1,0:T(8,128)(2,1)}, u32[]{:S(2)}, u32[]{:S(2)}) async-start(s16[16,1584,128]{2,1,0:T(8,128)(2,1)} %copy-done.5), calls=%async_computation | async-start | bytes 12976128 | tf_op jit(solution)/shard_map/all_to_all | solution.py:346
  29.1 117.6 %all-to-all-done.x_hbm = s16[16,1584,128]{2,1,0:T(8,128)(2,1)} async-done(((s16[16,1584,128]{2,1,0:T(8,128)(2,1)}), s16[16,1584,128]{2,1,0:T(8,128)(2,1)}, u32[]{:S(2)}, u32[]{:S(2)}) %all-to-all-start) | async-done | bytes 6488096 | tf_op jit(solution)/shard_map/all_to_all | solution.py:346
  146.7 28.9 %all-to-all-start.1 = ((s16[16,512,128]{2,1,0:T(8,128)(2,1)}), s16[16,512,128]{2,1,0:T(8,128)(2,1)S(1)}, u32[]{:S(2)}, u32[]{:S(2)}) async-start(s16[16,512,128]{2,1,0:T(8,128)(2,1)} %copy-done.11), calls=%async_computation.1 | async-start | bytes 4194304 | tf_op jit(solution)/shard_map/all_to_all | solution.py:346
  175.6 1.0 slice_convert_fusion
  176.6 1.0 convert_reduce_fusion
  179.2 1.0 fusion.hot_hbm
  180.9 23.7 %stage.2 = (f32[32,128]{1,0:T(8,128)S(1)}, f32[512,2048]{1,0:T(8,128)S(1)}, bf16[192,128,128]{2,1,0:T(8,128)(2,1)S(1)}) custom-call(s32[256]{0:T(256)S(1)} %select_reduce_fusion.3.fold_order, s32[35]{0:T(128)S(1)} %convert_reduce_fusion.4.fold_bound, s32[256]{0:T(256)S(1)} %select_reduce_fusion.2.score_order, s32[17]{0:T(128)S(1)} %convert_reduce_fusion.5.score_bound, ...), custom_call_target="tpu_custom_call" | custom-call | flops 12884901888 | bytes 20971520 | tf_op jit(solution)/shard_map/stage/pallas_call | solution.py:312
  204.6 2.0 copy-done
  206.7 1.3 copy-done.3
  208.0 2.7 %copy-done.6 = bf16[192,128,128]{2,1,0:T(8,128)(2,1)} copy-done((bf16[192,128,128]{2,1,0:T(8,128)(2,1)}, bf16[192,128,128]{2,1,0:T(8,128)(2,1)S(1)}, u32[]{:S(2)}) %copy-start.6) | copy-done | bytes 6291480
  210.6 2.1 copy-done.9
  212.7 4.0 %all-to-all-done.1.x_hbm = s16[16,512,128]{2,1,0:T(8,128)(2,1)S(1)} async-done(((s16[16,512,128]{2,1,0:T(8,128)(2,1)}), s16[16,512,128]{2,1,0:T(8,128)(2,1)S(1)}, u32[]{:S(2)}, u32[]{:S(2)}) %all-to-all-start.1) | async-done | bytes 2097184 | tf_op jit(solution)/shard_map/all_to_all | solution.py:346
  216.7 2.2 copy-done.1
  218.9 1.6 copy-done.4
  220.5 2.8 %copy-done.7 = bf16[192,128,128]{2,1,0:T(8,128)(2,1)S(1)} copy-done((bf16[192,128,128]{2,1,0:T(8,128)(2,1)S(1)}, bf16[192,128,128]{2,1,0:T(8,128)(2,1)}, u32[]{:S(2)}) %copy-start.7) | copy-done | bytes 6291480
  223.3 2.2 copy-done.10
  225.4 4.4 %stage.3 = (f32[16,1,768]{2,1,0:T(1,128)S(1)}, f32[512,2048]{1,0:T(8,128)S(1)}) custom-call(s32[256]{0:T(256)S(1)} %select_reduce_fusion.3.fold_order, s32[35]{0:T(128)S(1)} %convert_reduce_fusion.4.fold_bound, s32[256]{0:T(256)S(1)} %select_reduce_fusion.2.score_order, s32[17]{0:T(128)S(1)} %convert_reduce_fusion.5.score_bound, s32[256]{0:T(256)S(1)} %sub.7.meta, ...), custom_call_target="tpu_custom_call" | custom-call | flops 4294967296 | bytes 12582912 | tf_op jit(solution)/shard_map/stage/pallas_call | solution.py:312
  229.9 1.9 copy-done.8
  231.8 29.2 %all_to_all.15 = f32[16,1,768]{2,1,0:T(1,128)S(1)} all-to-all(f32[16,1,768]{2,1,0:T(1,128)S(1)} %get-tuple-element.17), channel_id=1, replica_groups=mesh['groups'=2,'dp'=16] {'dp'}, dimensions={0} | all-to-all | bytes 98304 | tf_op jit(solution)/shard_map/all_to_all | solution.py:346
  261.2 3.9 %multiply_convert_fusion = bf16[512,2048]{1,0:T(8,128)(2,1)} fusion(f32[512,2048]{1,0:T(8,128)} %copy-done.8, f32[512]{0:T(512)S(1)} %add_rsqrt_fusion), kind=kLoop, calls=%fused_computation.2 | loop fusion | flops 3145728 | bytes 6293504 | tf_op jit(solution)/shard_map/convert_element_type | solution.py:435
  (57 shorter events, 7.2 us)
Async XLA Ops:
  2.2 3.4 %copy-start.2 = (f32[128,128,128]{2,1,0:T(8,128)S(1)}, f32[128,128,128]{2,1,0:T(8,128)}, u32[]{:S(2)}) copy-start(f32[128,128,128]{2,1,0:T(8,128)} %refs_4_.1) | copy-start | bytes 25165828
  5.6 0.7 copy-start.12
  6.2 0.7 copy-start.13
  6.9 0.7 copy-start.14
  7.6 0.7 copy-start.16
  17.6 2.7 %copy-start.5 = (s16[16,1584,128]{2,1,0:T(8,128)(2,1)}, s16[16,1584,128]{2,1,0:T(8,128)(2,1)S(1)}, u32[]{:S(2)}) copy-start(s16[16,1584,128]{2,1,0:T(8,128)(2,1)S(1)} %get-tuple-element.10) | copy-start | bytes 19464196
  20.3 1.3 copy-start.11
  21.6 125.0 %all-to-all-start = ((s16[16,1584,128]{2,1,0:T(8,128)(2,1)}), s16[16,1584,128]{2,1,0:T(8,128)(2,1)}, u32[]{:S(2)}, u32[]{:S(2)}) async-start(s16[16,1584,128]{2,1,0:T(8,128)(2,1)} %copy-done.5), calls=%async_computation | async-start | bytes 12976128 | tf_op jit(solution)/shard_map/all_to_all | solution.py:346
  29.1 149.1 %copy-start.19 = (s32[256]{0:T(256)S(1)}, s32[256]{0:T(256)}, u32[]{:S(2)}) copy-start(s32[256]{0:T(256)} %constant.68.clone) | copy-start | bytes 3076
  29.1 149.1 %copy-start.18 = (pred[2,256]{1,0:T(4,128)(4,1)S(1)}, pred[2,256]{1,0:T(4,128)(4,1)}, u32[]{:S(2)}) copy-start(pred[2,256]{1,0:T(4,128)(4,1)} %constant.69.clone) | copy-start | bytes 1540
  146.7 70.0 %all-to-all-start.1 = ((s16[16,512,128]{2,1,0:T(8,128)(2,1)}), s16[16,512,128]{2,1,0:T(8,128)(2,1)S(1)}, u32[]{:S(2)}, u32[]{:S(2)}) async-start(s16[16,512,128]{2,1,0:T(8,128)(2,1)} %copy-done.11), calls=%async_computation.1 | async-start | bytes 4194304 | tf_op jit(solution)/shard_map/all_to_all | solution.py:346
  175.5 5.3 %copy-start.17 = (s32[256]{0:T(256)S(1)}, s32[256]{0:T(256)}, u32[]{:S(2)}) copy-start(s32[256]{0:T(256)} %constant.70.clone.place) | copy-start | bytes 3076
  204.6 2.1 copy-start
  206.7 1.3 copy-start.3
  208.0 2.7 %copy-start.6 = (bf16[192,128,128]{2,1,0:T(8,128)(2,1)}, bf16[192,128,128]{2,1,0:T(8,128)(2,1)S(1)}, u32[]{:S(2)}) copy-start(bf16[192,128,128]{2,1,0:T(8,128)(2,1)S(1)} %get-tuple-element.14.refs_0_) | copy-start | bytes 18874372
  210.6 2.1 copy-start.9
  216.6 2.2 copy-start.1
  218.9 1.6 copy-start.4
  220.5 2.8 %copy-start.7 = (bf16[192,128,128]{2,1,0:T(8,128)(2,1)S(1)}, bf16[192,128,128]{2,1,0:T(8,128)(2,1)}, u32[]{:S(2)}) copy-start(bf16[192,128,128]{2,1,0:T(8,128)(2,1)} %copy-done.6) | copy-start | bytes 18874372
  223.3 2.2 copy-start.10
  225.4 35.6 %copy-start.15 = (s32[256]{0:T(256)S(1)}, s32[256]{0:T(256)}, u32[]{:S(2)}) copy-start(s32[256]{0:T(256)} %param.12) | copy-start | bytes 3076
  229.9 1.9 copy-start.8

commit v7 on v5

--- a/solution.py
+++ b/solution.py
@@ -163,41 +163,89 @@
     )(put, tile_row, *told, tile_values)
 
 
-def stage_kernel(q, base, last, cached, fold_order, fold_bound, score_order, score_bound, meta,
-                 place, done, labels, before, inv_hbm, x_hbm, hot_hbm, *refs):
+def stage_kernel(q, bases, last, cached, fold_order, fold_bound, score_order, score_bound, meta,
+                 place, done, labels, before, inv_hbm, x_hbm, *refs):
+    base = bases[q]
     earlier, refs = refs[:q], refs[q:]
-    sums_in, refs = (refs[0], refs[1:]) if q else (None, refs)
-    part, sums_out, extra = (*refs[:2], None) if last else refs[:3]
-    refs = refs[2:] if last else refs[3:]
-    inv, x, hot, sums, narrow, tiles, products, scores, sems = refs
+    (sums_in, squares_in), refs = (refs[:2], refs[2:]) if q else ((None, None), refs)
+    part, sums_out, refs = refs[0], refs[1], refs[2:]
+    (squares_out, fresh_out), refs = ((None, None), refs) if last else (refs[:2], refs[2:])
+    inv, x, hot, sums, narrow, tiles, products, scores, squares, sems, sub_sems, tile_sems = refs
     devices, width = x.shape[0], x.shape[1] // LANES
-    fresh = tiles.at[pl.ds(base, devices * width)]
-    from_hbm = x_hbm.at[:, pl.ds(0, width * LANES)]
+    none = products.shape[0] - 1
+    begin, end = done[q], done[q + 1]
     needed = [
-        pltpu.make_async_copy(from_hbm, x, sems.at[0]),
+        pltpu.make_async_copy(x_hbm.at[:, pl.ds(0, width * LANES)], x, sems.at[0]),
         pltpu.make_async_copy(inv_hbm, inv, sems.at[1]),
     ]
+    for copy in needed:
+        copy.start()
+
+    def columns(sub):
+        return (slice(None), pl.ds(pl.multiple_of(sub * LANES, LANES), LANES))
+
+    def sums_read(sub):
+        return pltpu.make_async_copy(
+            sums_in.at[columns(sub)], sums.at[columns(sub)], sub_sems.at[0, sub]
+        )
+
+    def sums_write(sub):
+        return pltpu.make_async_copy(
+            sums.at[columns(sub)], sums_out.at[columns(sub)], sub_sems.at[1, sub]
+        )
+
+    def each_sub(low, high, what):
+        def one(sub, carry):
+            what(sub)
+            return carry
+
+        lax.fori_loop(low, high, one, 0)
+
+    def each_earlier(what):
+        def one(p, carry):
+            spot = place[score_order[p]]
+            for e, e_hbm in enumerate(earlier):
+                inside = (spot >= bases[e]) & (spot < bases[e + 1])
+                pl.when(inside)(
+                    lambda e=e, e_hbm=e_hbm: what(
+                        pltpu.make_async_copy(
+                            e_hbm.at[spot - bases[e]], tiles.at[spot], tile_sems.at[spot]
+                        )
+                    )
+                )
+            return carry
+
+        lax.fori_loop(score_bound[begin], score_bound[TB_OWN], one, 0)
+
     if q:
-        needed.append(pltpu.make_async_copy(sums_in, sums, sems.at[2]))
-    later = [pltpu.make_async_copy(hot_hbm, hot, sems.at[3])] if cached else []
-    spot = 0
-    for e, e_hbm in enumerate(earlier):
-        held = tiles.at[pl.ds(spot, e_hbm.shape[0])]
-        later.append(pltpu.make_async_copy(e_hbm, held, sems.at[6 + e]))
-        spot += e_hbm.shape[0]
-    for copy in needed + later:
-        copy.start()
+        each_sub(begin, TB_OWN, lambda sub: sums_read(sub).start())
+        each_earlier(lambda copy: copy.start())
+        squares[...] = squares_in[...]
+    else:
+        sums[...] = jnp.zeros_like(sums)
+        squares[...] = jnp.zeros_like(squares)
     products[...] = jnp.zeros_like(products)
     scores[...] = before[...]
-    if not q:
-        sums[...] = jnp.zeros_like(sums)
+    cluster = lax.broadcasted_iota(jnp.int32, (K, LANES), 0)
+    lane = lax.broadcasted_iota(jnp.int32, (LANES, LANES), 1)
+
+    def one_hot(row):
+        own = jnp.broadcast_to(labels[pl.ds(row, 1), :].astype(jnp.float32), (LANES, LANES))
+        own = jnp.transpose(own).astype(jnp.int32)
+        some = [jnp.where(own == lane + g, 1.0, 0.0) for g in range(0, K, LANES)]
+        return jnp.concatenate(some, axis=1).astype(jnp.bfloat16)
+
+    if cached:
+        batch = math.gcd(none + 1, 3)
+
+        def build(c, carry):
+            for j in range(batch):
+                hot[c * batch + j] = one_hot(c * batch + j)
+            return carry
+
+        lax.fori_loop(0, (none + 1) // batch, build, 0)
     for copy in needed:
         copy.wait()
-    none = products.shape[0] - 1
-    cluster = lax.broadcasted_iota(jnp.int32, (K, LANES), 0)
-
-    def columns(sub):
-        return (slice(None), pl.ds(pl.multiple_of(sub * LANES, LANES), LANES))
 
     def eight(order, start, end, p):
         rows, spots = [], []
@@ -208,9 +256,11 @@
             spots.append(place[slot])
         return rows, spots
 
-    def fold_sub(sub, carry):
+    def fold_sub(sub):
         start = fold_bound[q * (TB_OWN + 1) + sub]
         end = fold_bound[q * (TB_OWN + 1) + sub + 1]
+        if q:
+            sums_read(sub).wait()
 
         def one_eight(p, carry):
             rows, spots = eight(fold_order, start, end, p)
@@ -231,38 +281,28 @@
             return carry
 
         lax.fori_loop(0, (end - start + EIGHT - 1) // EIGHT, one_eight, 0)
-        return carry
-
-    lax.fori_loop(0, TB_OWN, fold_sub, 0)
-    results = [pltpu.make_async_copy(sums, sums_out, sems.at[4])]
+        sums_write(sub).start()
+
+    each_sub(begin, TB_OWN, fold_sub)
+    kept = []
     if not last:
-        results.append(pltpu.make_async_copy(fresh, extra, sems.at[5]))
-    for copy in results:
+        fresh = tiles.at[pl.ds(base, devices * width)]
+        kept.append(pltpu.make_async_copy(fresh, fresh_out, sems.at[2]))
+    for copy in kept:
         copy.start()
-    if last:
-        total = jnp.zeros((K, LANES), jnp.float32)
-        for sub in range(TB_OWN):
-            some = sums[:, sub * LANES : (sub + 1) * LANES]
-            total = total + some * some
-        square = lane_sums(total)[:1]
-        for d in range(devices):
-            part[d, :, part.shape[2] - K :] = square
-    for copy in later:
-        copy.wait()
-
-    def score_sub(sub, carry):
+    if q:
+        each_earlier(lambda copy: copy.wait())
+
+    def score_sub(sub):
         start, end = score_bound[sub], score_bound[sub + 1]
-        narrow[...] = sums[columns(sub)].astype(jnp.bfloat16)
+        some = sums[columns(sub)]
+        narrow[...] = some.astype(jnp.bfloat16)
+        squares[...] += some * some
 
         def one_eight(p, carry):
             rows, spots = eight(score_order, start, end, p)
             rows = [jnp.where(held, row, none) for row, held in rows]
-            if cached:
-                hots = [hot[row] for row in rows]
-            else:
-                for j, row in enumerate(rows):
-                    pltpu.sync_copy(hot_hbm.at[row], hot.at[j])
-                hots = [hot[j] for j in range(EIGHT)]
+            hots = [hot[row] if cached else one_hot(row) for row in rows]
             chosen = jnp.dot(
                 jnp.concatenate(hots, axis=0), narrow[...], preferred_element_type=jnp.float32
             )
@@ -272,23 +312,26 @@
             return carry
 
         lax.fori_loop(0, (end - start + EIGHT - 1) // EIGHT, one_eight, 0)
-        return carry
-
-    lax.fori_loop(done[q], done[q + 1], score_sub, 0)
+
+    each_sub(begin, end, score_sub)
     block_sums(products, scores, none)
     if last:
         own = none // devices
+        square = lane_sums(squares[...])[:1]
         for d in range(devices):
+            part[d, :, part.shape[2] - K :] = square
             for b in range(own):
                 at = d * own + b
                 part[d, :, b * LANES : (b + 1) * LANES] = scores[at : at + 1, :]
     else:
         part[...] = scores[...]
-    for copy in results:
+        squares_out[...] = squares[...]
+    for copy in kept:
         copy.wait()
-
-
-def stage(q, cuts, scalars, labels, before, inverse, x, hot, normed, sums):
+    each_sub(begin, TB_OWN, lambda sub: sums_write(sub).wait())
+
+
+def stage(q, cuts, scalars, labels, before, inverse, x, normed, totals):
     devices = x.shape[0]
     last = q == len(cuts) - 2
     blocks = inverse.shape[0]
@@ -302,23 +345,30 @@
         out_shape = [
             jax.ShapeDtypeStruct((blocks, LANES), jnp.float32),
             wide,
+            jax.ShapeDtypeStruct((K, LANES), jnp.float32),
             jax.ShapeDtypeStruct((devices * width, LANES, LANES), jnp.bfloat16),
         ]
+    slots = devices * cuts[-1]
+    operands = [*scalars, labels, before, inverse, x, *normed, *totals]
     return pl.pallas_call(
-        functools.partial(stage_kernel, q, devices * cuts[q], last, cached),
-        in_specs=[SMEM] * len(scalars) + [VMEM] * 2 + [ANY] * (3 + q + (q > 0)),
-        out_specs=[VMEM, ANY, ANY][: len(out_shape)],
+        functools.partial(stage_kernel, q, [devices * cut for cut in cuts], last, cached),
+        in_specs=[SMEM] * len(scalars) + [VMEM] * 2 + [ANY] * (2 + q) + [ANY, VMEM][: len(totals)],
+        out_specs=[VMEM, ANY, VMEM, ANY][: len(out_shape)],
         out_shape=out_shape,
+        input_output_aliases={len(operands) - 2: 1} if q else {},
         scratch_shapes=[
             pltpu.VMEM(inverse.shape, jnp.float32),
             pltpu.VMEM((devices, width * LANES, LANES), jnp.int16),
-            pltpu.VMEM(hot.shape if cached else (EIGHT, LANES, K), jnp.bfloat16),
+            pltpu.VMEM((blocks + 1 if cached else 1, LANES, K), jnp.bfloat16),
             pltpu.VMEM(wide.shape, jnp.float32),
             pltpu.VMEM((K, LANES), jnp.bfloat16),
-            pltpu.VMEM((devices * cuts[-1], LANES, LANES), jnp.bfloat16),
+            pltpu.VMEM((slots, LANES, LANES), jnp.bfloat16),
             pltpu.VMEM((blocks + 1, LANES, LANES), jnp.float32),
             pltpu.VMEM((blocks, LANES), jnp.float32),
-            pltpu.SemaphoreType.DMA((6 + len(cuts),)),
+            pltpu.VMEM((K, LANES), jnp.float32),
+            pltpu.SemaphoreType.DMA((3,)),
+            pltpu.SemaphoreType.DMA((2, TB_OWN)),
+            pltpu.SemaphoreType.DMA((slots,)),
         ],
         compiler_params=params(),
         cost_estimate=pl.CostEstimate(
@@ -327,7 +377,7 @@
             transcendentals=0,
         ),
         name="stage",
-    )(*scalars, labels, before, inverse, x, hot, *normed, *([sums] if q else []))
+    )(*operands)
 
 
 def exchange(x):
@@ -382,7 +432,6 @@
     all_described = heard[:, blocks:].reshape(devices, -1)
     all_labels = all_described[:, :home].reshape(blocks, LANES)
     padded_labels = jnp.concatenate([all_labels, jnp.full((1, LANES), -1, jnp.int32)])
-    hot = (padded_labels[:, :, None] == jnp.arange(K, dtype=jnp.int32)).astype(jnp.bfloat16)
     mine = all_described[:, home : home + tiles] == here
     code = all_described[:, home + tiles : home + 2 * tiles]
     rank = ranks(mine.astype(jnp.int32), code % TB_OWN)
@@ -405,17 +454,17 @@
 
     inverse = lax.rsqrt(row_sq + EPSILON)
     scale = jnp.broadcast_to((inverse * (1.0 / CODE_TOP**2))[:, :, None], (blocks, LANES, LANES))
-    partial, sums, normed = jnp.zeros((blocks, LANES), jnp.float32), None, []
-    beside = (*scalars, padded_labels, hot, scale)
+    partial, totals, normed = jnp.zeros((blocks, LANES), jnp.float32), (), []
+    beside = (*scalars, padded_labels, scale)
     for q in range(parts):
         if q + 1 < parts:
             ahead = (incoming[q], *beside) if q else (incoming[q],)
             incoming.append(exchange(after(outgoing[q + 1], *ahead)))
-        partial, sums, *extra = stage(
-            q, cuts, scalars, padded_labels, partial, scale, incoming[q], hot, normed, sums
+        partial, sums, *more = stage(
+            q, cuts, scalars, padded_labels, partial, scale, incoming[q], normed, totals
         )
         beside = (partial, sums)
-        normed += extra
+        totals, normed = (sums, *more[:1]), normed + more[1:]
     back = jnp.sum(exchange(partial), axis=(0, 1))
     own_scale = lax.rsqrt(back[home:] + EPSILON)
     vocab_size = TB_OWN * LANES * devices

time: 252 us -> 255 us (1.012)
  the two profiles are of different devices: /device:TPU:4 before, /device:TPU:0 now
where the time goes in v7:
time: 255 us; the launch traced here: 254 us
  blocking collectives  183 us (72%)
  Pallas kernels  41.5 us (16%)
  other arithmetic  13.1 us (5%)
  waiting for transfers between devices  6.7 us (3%)
  local copies, waits for them, and re-layouts  4.61 us (2%)
  starting transfers between devices  4.35 us (2%)
    all_to_all x2, blocking collectives, exchange(): return lax.all_to_all(x, 'dp', split_axis=0, concat_axis=0, tiled=True)  183 us
    pallas_call x2, Pallas kernels, stage(): pl.pallas_call(functools.partial(stage_kernel, q, [devices * cut for cut...  32.4 us
    pallas_call x1, Pallas kernels, pack(): pl.pallas_call(functools.partial(pack_kernel, cuts), grid=(tiles // step,...  9.03 us
    all_to_all x1, waiting for transfers between devices, exchange(): return lax.all_to_all(x, 'dp', split_axis=0, concat_axis=0, tiled=True)  6.7 us
  transfers between devices with their start and end apart: 1, of which 1 were waited for; matrix products, arithmetic and copies ran while one was open for 4% of the time, Pallas kernels for 10%

profile of v7, /device:TPU:0, one launch (start us, length us, event | category | flops | bytes accessed | tf_op | source)
XLA Modules:
  0.0 254.3 jit_solution(18051165287159685571)
XLA Ops:
  0.6 0.9 convert_reduce_fusion.3
  1.5 1.2 multiply_add_fusion.put_ref
  2.7 9.0 %pack.1 = (s16[16,1584,128]{2,1,0:T(8,128)(2,1)}, s16[16,512,128]{2,1,0:T(8,128)(2,1)}) custom-call(s32[128]{0:T(128)} %multiply_add_fusion.put_ref, s32[128]{0:T(128)} %row_ref.1, s32[2,128]{1,0:T(2,128)} %bitcast.17, s32[1,128]{1,0:T(1,128)} %bitcast.15, s32[1,128]{1,0:T(1,128)} %bitcast.18, s32[1,128]{1,0:T(1,128)} %bitcast.16, f32[128,128,128]{2,1,0:T(8,128)} %refs_4_.1), custom_call_target="tpu_custom_call" | custom-call | flops 16777216 | bytes 12582912 | tf_op jit(solution)/shard_map/pack/pallas_call | solution.py:139
  11.8 150.2 %all_to_all.15.x_hbm = s16[16,1584,128]{2,1,0:T(8,128)(2,1)} all-to-all(s16[16,1584,128]{2,1,0:T(8,128)(2,1)} %get-tuple-element.11), channel_id=1, replica_groups=mesh['groups'=2,'dp'=16] {'dp'}, dimensions={0} | all-to-all | bytes 12976128 | tf_op jit(solution)/shard_map/all_to_all | solution.py:384
  162.0 4.3 %all-to-all-start.1 = ((s16[16,512,128]{2,1,0:T(8,128)(2,1)}), s16[16,512,128]{2,1,0:T(8,128)(2,1)S(1)}, u32[]{:S(2)}, u32[]{:S(2)}) async-start(s16[16,512,128]{2,1,0:T(8,128)(2,1)} %get-tuple-element.14), calls=%async_computation.1 | async-start | bytes 4194304 | tf_op jit(solution)/shard_map/all_to_all | solution.py:384
  166.3 1.0 slice_convert_fusion
  167.4 1.0 convert_reduce_fusion
  168.5 0.3 select_reduce_fusion.4
  168.9 0.6 concatenate.7.labels
  169.7 0.7 pad_add_fusion.done
  170.4 0.6 convert_reduce_fusion.5.score_bound
  171.0 0.7 convert_reduce_fusion.4.fold_bound
  171.7 0.3 convert_reduce_fusion.1
  171.9 0.7 select_reduce_fusion.2.score_order
  172.6 0.7 select_reduce_fusion.3.fold_order
  173.4 1.9 broadcast_in_dim.65.inv_hbm
  175.4 0.6 broadcast_in_dim.63.before
  176.0 24.8 %stage.2 = (f32[32,128]{1,0:T(8,128)}, f32[512,2048]{1,0:T(8,128)}, f32[512,128]{1,0:T(8,128)}, bf16[192,128,128]{2,1,0:T(8,128)(2,1)}) custom-call(s32[256]{0:T(256)} %select_reduce_fusion.3.fold_order, s32[35]{0:T(128)} %convert_reduce_fusion.4.fold_bound, s32[256]{0:T(256)} %select_reduce_fusion.2.score_order, s32[17]{0:T(128)} %convert_reduce_fusion.5.score_bound, ...), custom_call_target="tpu_custom_call" | custom-call | flops 12884901888 | bytes 20971520 | tf_op jit(solution)/shard_map/stage/pallas_call | solution.py:353
  200.7 6.7 %all-to-all-done.1.x_hbm = s16[16,512,128]{2,1,0:T(8,128)(2,1)S(1)} async-done(((s16[16,512,128]{2,1,0:T(8,128)(2,1)}), s16[16,512,128]{2,1,0:T(8,128)(2,1)S(1)}, u32[]{:S(2)}, u32[]{:S(2)}) %all-to-all-start.1) | async-done | bytes 2097184 | tf_op jit(solution)/shard_map/all_to_all | solution.py:384
  207.4 1.3 copy-done
  208.7 7.7 %stage.3 = (f32[16,1,768]{2,1,0:T(1,128)}, f32[512,2048]{1,0:T(8,128)}) custom-call(s32[256]{0:T(256)} %select_reduce_fusion.3.fold_order, s32[35]{0:T(128)} %convert_reduce_fusion.4.fold_bound, s32[256]{0:T(256)} %select_reduce_fusion.2.score_order, s32[17]{0:T(128)} %convert_reduce_fusion.5.score_bound, ...), custom_call_target="tpu_custom_call", output_to_operand_aliasing={{1}: (12, {})} | custom-call | flops 4294967296 | bytes 12582912 | tf_op jit(solution)/shard_map/stage/pallas_call | solution.py:353
  216.4 33.1 %all_to_all.16 = f32[16,1,768]{2,1,0:T(1,128)S(1)} all-to-all(f32[16,1,768]{2,1,0:T(1,128)} %get-tuple-element.19), channel_id=1, replica_groups=mesh['groups'=2,'dp'=16] {'dp'}, dimensions={0} | all-to-all | bytes 98304 | tf_op jit(solution)/shard_map/all_to_all | solution.py:384
  249.8 3.9 %multiply_convert_fusion = bf16[512,2048]{1,0:T(8,128)(2,1)} fusion(f32[512,2048]{1,0:T(8,128)} %get-tuple-element.18, f32[512]{0:T(512)S(1)} %add_rsqrt_fusion), kind=kLoop, calls=%fused_computation | loop fusion | flops 3145728 | bytes 6293504 | tf_op jit(solution)/shard_map/convert_element_type | solution.py:472
  253.7 0.6 slice_multiply_fusion
  (25 shorter events, 0.7 us)
Async XLA Ops:
  162.0 7.6 %copy-start.4 = (s32[256]{0:T(256)S(1)}, s32[256]{0:T(256)}, u32[]{:S(2)}) copy-start(s32[256]{0:T(256)} %constant.68.clone) | copy-start | bytes 3076
  162.0 7.6 %copy-start.3 = (pred[2,256]{1,0:T(4,128)(4,1)S(1)}, pred[2,256]{1,0:T(4,128)(4,1)}, u32[]{:S(2)}) copy-start(pred[2,256]{1,0:T(4,128)(4,1)} %constant.69.clone) | copy-start | bytes 1540
  162.0 45.5 %all-to-all-start.1 = ((s16[16,512,128]{2,1,0:T(8,128)(2,1)}), s16[16,512,128]{2,1,0:T(8,128)(2,1)S(1)}, u32[]{:S(2)}, u32[]{:S(2)}) async-start(s16[16,512,128]{2,1,0:T(8,128)(2,1)} %get-tuple-element.14), calls=%async_computation.1 | async-start | bytes 4194304 | tf_op jit(solution)/shard_map/all_to_all | solution.py:384
  168.9 7.0 %copy-start.2 = (s32[256]{0:T(256)}, s32[256]{0:T(256)S(1)}, u32[]{:S(2)}) copy-start(s32[256]{0:T(256)S(1)} %sub.7.meta) | copy-start | bytes 3076
  207.4 1.3 copy-start
  208.7 40.9 %copy-start.1 = (s32[256]{0:T(256)S(1)}, s32[256]{0:T(256)}, u32[]{:S(2)}) copy-start(s32[256]{0:T(256)} %param.12) | copy-start | bytes 3076

commit v8 on v7

--- a/solution.py
+++ b/solution.py
@@ -201,29 +201,17 @@
 
         lax.fori_loop(low, high, one, 0)
 
-    def each_earlier(what):
-        def one(p, carry):
-            spot = place[score_order[p]]
-            for e, e_hbm in enumerate(earlier):
-                inside = (spot >= bases[e]) & (spot < bases[e + 1])
-                pl.when(inside)(
-                    lambda e=e, e_hbm=e_hbm: what(
-                        pltpu.make_async_copy(
-                            e_hbm.at[spot - bases[e]], tiles.at[spot], tile_sems.at[spot]
-                        )
-                    )
-                )
-            return carry
-
-        lax.fori_loop(score_bound[begin], score_bound[TB_OWN], one, 0)
-
     if q:
         each_sub(begin, TB_OWN, lambda sub: sums_read(sub).start())
-        each_earlier(lambda copy: copy.start())
         squares[...] = squares_in[...]
     else:
         sums[...] = jnp.zeros_like(sums)
         squares[...] = jnp.zeros_like(squares)
+    later = []
+    for e, e_hbm in enumerate(earlier):
+        held = tiles.at[pl.ds(bases[e], e_hbm.shape[0])]
+        later.append(pltpu.make_async_copy(e_hbm, held, tile_sems.at[e]))
+        later[e].start()
     products[...] = jnp.zeros_like(products)
     scores[...] = before[...]
     cluster = lax.broadcasted_iota(jnp.int32, (K, LANES), 0)
@@ -290,8 +278,8 @@
         kept.append(pltpu.make_async_copy(fresh, fresh_out, sems.at[2]))
     for copy in kept:
         copy.start()
-    if q:
-        each_earlier(lambda copy: copy.wait())
+    for copy in later:
+        copy.wait()
 
     def score_sub(sub):
         start, end = score_bound[sub], score_bound[sub + 1]
@@ -368,7 +356,7 @@
             pltpu.VMEM((K, LANES), jnp.float32),
             pltpu.SemaphoreType.DMA((3,)),
             pltpu.SemaphoreType.DMA((2, TB_OWN)),
-            pltpu.SemaphoreType.DMA((slots,)),
+            pltpu.SemaphoreType.DMA((len(cuts),)),
         ],
         compiler_params=params(),
         cost_estimate=pl.CostEstimate(

time: 255 us -> 251 us (0.984)
  blocking collectives: 183 us -> 180 us
    all_to_all x2, blocking collectives: 183 us -> 180 us  [exchange(): return lax.all_to_all(x, 'dp', split_axis=0, concat_axis=0, tiled=True)]
where the time goes in v8:
time: 251 us
  blocking collectives  180 us (72%)
  Pallas kernels  40.7 us (16%)
  other arithmetic  13.1 us (5%)
  waiting for transfers between devices  7.11 us (3%)
  local copies, waits for them, and re-layouts  4.61 us (2%)
  starting transfers between devices  4.35 us (2%)
    all_to_all x2, blocking collectives, exchange(): return lax.all_to_all(x, 'dp', split_axis=0, concat_axis=0, tiled=True)  180 us
    pallas_call x2, Pallas kernels, stage(): pl.pallas_call(functools.partial(stage_kernel, q, [devices * cut for cut...  31.6 us
    pallas_call x1, Pallas kernels, pack(): pl.pallas_call(functools.partial(pack_kernel, cuts), grid=(tiles // step,...  9.11 us
    all_to_all x1, waiting for transfers between devices, exchange(): return lax.all_to_all(x, 'dp', split_axis=0, concat_axis=0, tiled=True)  7.11 us
  transfers between devices with their start and end apart: 1, of which 1 were waited for; matrix products, arithmetic and copies ran while one was open for 4% of the time, Pallas kernels for 10%

profile of v8, /device:TPU:0, one launch (start us, length us, event | category | flops | bytes accessed | tf_op | source)
XLA Modules:
  0.0 251.0 jit_solution(99590402162860227)
XLA Ops:
  0.6 0.9 convert_reduce_fusion.3
  1.5 1.2 multiply_add_fusion.put_ref
  2.7 9.1 %pack.1 = (s16[16,1584,128]{2,1,0:T(8,128)(2,1)}, s16[16,512,128]{2,1,0:T(8,128)(2,1)}) custom-call(s32[128]{0:T(128)} %multiply_add_fusion.put_ref, s32[128]{0:T(128)} %row_ref.1, s32[2,128]{1,0:T(2,128)} %bitcast.17, s32[1,128]{1,0:T(1,128)} %bitcast.15, s32[1,128]{1,0:T(1,128)} %bitcast.18, s32[1,128]{1,0:T(1,128)} %bitcast.16, f32[128,128,128]{2,1,0:T(8,128)} %refs_4_.1), custom_call_target="tpu_custom_call" | custom-call | flops 16777216 | bytes 12582912 | tf_op jit(solution)/shard_map/pack/pallas_call | solution.py:139
  11.8 150.2 %all_to_all.15.x_hbm = s16[16,1584,128]{2,1,0:T(8,128)(2,1)} all-to-all(s16[16,1584,128]{2,1,0:T(8,128)(2,1)} %get-tuple-element.11), channel_id=1, replica_groups=mesh['groups'=2,'dp'=16] {'dp'}, dimensions={0} | all-to-all | bytes 12976128 | tf_op jit(solution)/shard_map/all_to_all | solution.py:372
  162.0 4.3 %all-to-all-start.1 = ((s16[16,512,128]{2,1,0:T(8,128)(2,1)}), s16[16,512,128]{2,1,0:T(8,128)(2,1)S(1)}, u32[]{:S(2)}, u32[]{:S(2)}) async-start(s16[16,512,128]{2,1,0:T(8,128)(2,1)} %get-tuple-element.14), calls=%async_computation.1 | async-start | bytes 4194304 | tf_op jit(solution)/shard_map/all_to_all | solution.py:372
  166.4 1.0 slice_convert_fusion
  167.5 1.0 convert_reduce_fusion
  168.5 0.3 select_reduce_fusion.4
  169.0 0.6 concatenate.7.labels
  169.7 0.7 pad_add_fusion.done
  170.4 0.6 convert_reduce_fusion.5.score_bound
  171.0 0.7 convert_reduce_fusion.4.fold_bound
  171.7 0.3 convert_reduce_fusion.1
  172.0 0.7 select_reduce_fusion.2.score_order
  172.7 0.7 select_reduce_fusion.3.fold_order
  173.5 1.9 broadcast_in_dim.65.inv_hbm
  175.4 0.6 broadcast_in_dim.63.before
  176.0 24.4 %stage.2 = (f32[32,128]{1,0:T(8,128)}, f32[512,2048]{1,0:T(8,128)}, f32[512,128]{1,0:T(8,128)}, bf16[192,128,128]{2,1,0:T(8,128)(2,1)}) custom-call(s32[256]{0:T(256)} %select_reduce_fusion.3.fold_order, s32[35]{0:T(128)} %convert_reduce_fusion.4.fold_bound, s32[256]{0:T(256)} %select_reduce_fusion.2.score_order, s32[17]{0:T(128)} %convert_reduce_fusion.5.score_bound, ...), custom_call_target="tpu_custom_call" | custom-call | flops 12884901888 | bytes 20971520 | tf_op jit(solution)/shard_map/stage/pallas_call | solution.py:341
  200.4 7.1 %all-to-all-done.1.x_hbm = s16[16,512,128]{2,1,0:T(8,128)(2,1)S(1)} async-done(((s16[16,512,128]{2,1,0:T(8,128)(2,1)}), s16[16,512,128]{2,1,0:T(8,128)(2,1)S(1)}, u32[]{:S(2)}, u32[]{:S(2)}) %all-to-all-start.1) | async-done | bytes 2097184 | tf_op jit(solution)/shard_map/all_to_all | solution.py:372
  207.5 1.3 copy-done
  208.8 7.2 %stage.3 = (f32[16,1,768]{2,1,0:T(1,128)}, f32[512,2048]{1,0:T(8,128)}) custom-call(s32[256]{0:T(256)} %select_reduce_fusion.3.fold_order, s32[35]{0:T(128)} %convert_reduce_fusion.4.fold_bound, s32[256]{0:T(256)} %select_reduce_fusion.2.score_order, s32[17]{0:T(128)} %convert_reduce_fusion.5.score_bound, ...), custom_call_target="tpu_custom_call", output_to_operand_aliasing={{1}: (12, {})} | custom-call | flops 4294967296 | bytes 12582912 | tf_op jit(solution)/shard_map/stage/pallas_call | solution.py:341
  216.0 30.2 %all_to_all.16 = f32[16,1,768]{2,1,0:T(1,128)S(1)} all-to-all(f32[16,1,768]{2,1,0:T(1,128)} %get-tuple-element.19), channel_id=1, replica_groups=mesh['groups'=2,'dp'=16] {'dp'}, dimensions={0} | all-to-all | bytes 98304 | tf_op jit(solution)/shard_map/all_to_all | solution.py:372
  246.5 3.9 %multiply_convert_fusion = bf16[512,2048]{1,0:T(8,128)(2,1)} fusion(f32[512,2048]{1,0:T(8,128)} %get-tuple-element.18, f32[512]{0:T(512)S(1)} %add_rsqrt_fusion), kind=kLoop, calls=%fused_computation | loop fusion | flops 3145728 | bytes 6293504 | tf_op jit(solution)/shard_map/convert_element_type | solution.py:460
  250.5 0.6 slice_multiply_fusion
  (25 shorter events, 0.7 us)
Async XLA Ops:
  162.0 7.6 %copy-start.4 = (s32[256]{0:T(256)S(1)}, s32[256]{0:T(256)}, u32[]{:S(2)}) copy-start(s32[256]{0:T(256)} %constant.68.clone) | copy-start | bytes 3076
  162.0 7.6 %copy-start.3 = (pred[2,256]{1,0:T(4,128)(4,1)S(1)}, pred[2,256]{1,0:T(4,128)(4,1)}, u32[]{:S(2)}) copy-start(pred[2,256]{1,0:T(4,128)(4,1)} %constant.69.clone) | copy-start | bytes 1540
  162.0 45.5 %all-to-all-start.1 = ((s16[16,512,128]{2,1,0:T(8,128)(2,1)}), s16[16,512,128]{2,1,0:T(8,128)(2,1)S(1)}, u32[]{:S(2)}, u32[]{:S(2)}) async-start(s16[16,512,128]{2,1,0:T(8,128)(2,1)} %get-tuple-element.14), calls=%async_computation.1 | async-start | bytes 4194304 | tf_op jit(solution)/shard_map/all_to_all | solution.py:372
  169.0 7.0 %copy-start.2 = (s32[256]{0:T(256)}, s32[256]{0:T(256)S(1)}, u32[]{:S(2)}) copy-start(s32[256]{0:T(256)S(1)} %sub.7.meta) | copy-start | bytes 3076
  207.5 1.3 copy-start
  208.8 37.5 %copy-start.1 = (s32[256]{0:T(256)S(1)}, s32[256]{0:T(256)}, u32[]{:S(2)}) copy-start(s32[256]{0:T(256)} %param.12) | copy-start | bytes 3076

commit v9 on v8

--- a/solution.py
+++ b/solution.py
@@ -10,6 +10,7 @@
 from jax.sharding import PartitionSpec as P
 
 K = 512
+HALF = K // 2
 TB_OWN = 16
 LANES = 128
 EPSILON = 1e-06
@@ -164,25 +165,21 @@
 
 
 def stage_kernel(q, bases, last, cached, fold_order, fold_bound, score_order, score_bound, meta,
-                 place, done, labels, before, inv_hbm, x_hbm, *refs):
+                 place, done, mods, signed, before, x_hbm, *refs):
     base = bases[q]
     earlier, refs = refs[:q], refs[q:]
     (sums_in, squares_in), refs = (refs[:2], refs[2:]) if q else ((None, None), refs)
     part, sums_out, refs = refs[0], refs[1], refs[2:]
     (squares_out, fresh_out), refs = ((None, None), refs) if last else (refs[:2], refs[2:])
-    inv, x, hot, sums, narrow, tiles, products, scores, squares, sems, sub_sems, tile_sems = refs
+    spread, x, hot, sums, narrow, tiles, products, scores, squares, sems, sub_sems, tile_sems = refs
     devices, width = x.shape[0], x.shape[1] // LANES
     none = products.shape[0] - 1
     begin, end = done[q], done[q + 1]
-    needed = [
-        pltpu.make_async_copy(x_hbm.at[:, pl.ds(0, width * LANES)], x, sems.at[0]),
-        pltpu.make_async_copy(inv_hbm, inv, sems.at[1]),
-    ]
-    for copy in needed:
-        copy.start()
+    needed = pltpu.make_async_copy(x_hbm.at[:, pl.ds(0, width * LANES)], x, sems.at[0])
+    needed.start()
 
     def columns(sub):
-        return (slice(None), pl.ds(pl.multiple_of(sub * LANES, LANES), LANES))
+        return (slice(None), pl.ds(pl.multiple_of(sub * 2 * LANES, 2 * LANES), 2 * LANES))
 
     def sums_read(sub):
         return pltpu.make_async_copy(
@@ -214,26 +211,28 @@
         later[e].start()
     products[...] = jnp.zeros_like(products)
     scores[...] = before[...]
-    cluster = lax.broadcasted_iota(jnp.int32, (K, LANES), 0)
+    cluster = lax.broadcasted_iota(jnp.int32, (HALF, LANES), 0)
     lane = lax.broadcasted_iota(jnp.int32, (LANES, LANES), 1)
 
+    def column(ref, row):
+        return jnp.transpose(jnp.broadcast_to(ref[pl.ds(row, 1), :], (LANES, LANES)))
+
     def one_hot(row):
-        own = jnp.broadcast_to(labels[pl.ds(row, 1), :].astype(jnp.float32), (LANES, LANES))
-        own = jnp.transpose(own).astype(jnp.int32)
-        some = [jnp.where(own == lane + g, 1.0, 0.0) for g in range(0, K, LANES)]
+        own = column(mods, row).astype(jnp.int32)
+        some = [jnp.where(own == lane + g, 1.0, 0.0) for g in range(0, HALF, LANES)]
         return jnp.concatenate(some, axis=1).astype(jnp.bfloat16)
 
-    if cached:
-        batch = math.gcd(none + 1, 3)
-
-        def build(c, carry):
-            for j in range(batch):
+    batch = math.gcd(none + 1, 3)
+
+    def build(c, carry):
+        for j in range(batch):
+            spread[c * batch + j] = column(signed, c * batch + j)
+            if cached:
                 hot[c * batch + j] = one_hot(c * batch + j)
-            return carry
-
-        lax.fori_loop(0, (none + 1) // batch, build, 0)
-    for copy in needed:
-        copy.wait()
+        return carry
+
+    lax.fori_loop(0, (none + 1) // batch, build, 0)
+    needed.wait()
 
     def eight(order, start, end, p):
         rows, spots = [], []
@@ -257,11 +256,13 @@
                 source, slot = (spot - base) // width, (spot - base) % width
                 raw = x[source, pl.ds(pl.multiple_of(slot * LANES, LANES), LANES), :]
                 root = raw.astype(jnp.int32).astype(jnp.float32) + float(CODE_SHIFT)
-                tile = (root * root * inv[row]).astype(jnp.bfloat16)
-                tiles[spot] = tile
-                folded.append(tile)
-                own = cluster == labels[pl.ds(jnp.where(held, row, none), 1), :]
-                picks.append(jnp.where(own, 1.0, 0.0).astype(jnp.bfloat16))
+                scale = spread[row]
+                tile = root * root * jnp.abs(scale)
+                tiles[spot] = tile.astype(jnp.bfloat16)
+                halves = [jnp.where(scale > 0.0, tile, 0.0), jnp.where(scale < 0.0, tile, 0.0)]
+                folded.append(jnp.concatenate(halves, axis=1).astype(jnp.bfloat16))
+                own = mods[pl.ds(jnp.where(held, row, none), 1), :].astype(jnp.int32)
+                picks.append(jnp.where(cluster == own, 1.0, 0.0).astype(jnp.bfloat16))
             pick = jnp.concatenate(picks, axis=1)
             sums[columns(sub)] += jnp.dot(
                 pick, jnp.concatenate(folded, axis=0), preferred_element_type=jnp.float32
@@ -295,7 +296,8 @@
                 jnp.concatenate(hots, axis=0), narrow[...], preferred_element_type=jnp.float32
             )
             for j in range(EIGHT):
-                own = chosen[j * LANES : (j + 1) * LANES]
+                both = chosen[j * LANES : (j + 1) * LANES]
+                own = jnp.where(spread[rows[j]] < 0.0, both[:, LANES:], both[:, :LANES])
                 products[rows[j]] += own * tiles[spots[j]].astype(jnp.float32)
             return carry
 
@@ -305,7 +307,8 @@
     block_sums(products, scores, none)
     if last:
         own = none // devices
-        square = lane_sums(squares[...])[:1]
+        square = [lane_sums(squares[:, h : h + LANES])[:1] for h in (0, LANES)]
+        square = jnp.concatenate(square, axis=1)
         for d in range(devices):
             part[d, :, part.shape[2] - K :] = square
             for b in range(own):
@@ -319,41 +322,42 @@
     each_sub(begin, TB_OWN, lambda sub: sums_write(sub).wait())
 
 
-def stage(q, cuts, scalars, labels, before, inverse, x, normed, totals):
+def stage(q, cuts, scalars, mods, signed, before, x, normed, totals):
     devices = x.shape[0]
     last = q == len(cuts) - 2
-    blocks = inverse.shape[0]
+    blocks = before.shape[0]
     cached = blocks <= CACHED_BLOCKS
     width = cuts[q + 1] - cuts[q]
     home = blocks // devices * LANES
-    wide = jax.ShapeDtypeStruct((K, TB_OWN * LANES), jnp.float32)
+    wide = jax.ShapeDtypeStruct((HALF, TB_OWN * 2 * LANES), jnp.float32)
+    square = jax.ShapeDtypeStruct((HALF, 2 * LANES), jnp.float32)
     if last:
         out_shape = [jax.ShapeDtypeStruct((devices, 1, home + K), jnp.float32), wide]
     else:
         out_shape = [
             jax.ShapeDtypeStruct((blocks, LANES), jnp.float32),
             wide,
-            jax.ShapeDtypeStruct((K, LANES), jnp.float32),
+            square,
             jax.ShapeDtypeStruct((devices * width, LANES, LANES), jnp.bfloat16),
         ]
     slots = devices * cuts[-1]
-    operands = [*scalars, labels, before, inverse, x, *normed, *totals]
+    operands = [*scalars, mods, signed, before, x, *normed, *totals]
     return pl.pallas_call(
         functools.partial(stage_kernel, q, [devices * cut for cut in cuts], last, cached),
-        in_specs=[SMEM] * len(scalars) + [VMEM] * 2 + [ANY] * (2 + q) + [ANY, VMEM][: len(totals)],
+        in_specs=[SMEM] * len(scalars) + [VMEM] * 3 + [ANY] * (1 + q) + [ANY, VMEM][: len(totals)],
         out_specs=[VMEM, ANY, VMEM, ANY][: len(out_shape)],
         out_shape=out_shape,
         input_output_aliases={len(operands) - 2: 1} if q else {},
         scratch_shapes=[
-            pltpu.VMEM(inverse.shape, jnp.float32),
+            pltpu.VMEM((blocks + 1, LANES, LANES), jnp.float32),
             pltpu.VMEM((devices, width * LANES, LANES), jnp.int16),
-            pltpu.VMEM((blocks + 1 if cached else 1, LANES, K), jnp.bfloat16),
+            pltpu.VMEM((blocks + 1 if cached else 1, LANES, HALF), jnp.bfloat16),
             pltpu.VMEM(wide.shape, jnp.float32),
-            pltpu.VMEM((K, LANES), jnp.bfloat16),
+            pltpu.VMEM(square.shape, jnp.bfloat16),
             pltpu.VMEM((slots, LANES, LANES), jnp.bfloat16),
             pltpu.VMEM((blocks + 1, LANES, LANES), jnp.float32),
             pltpu.VMEM((blocks, LANES), jnp.float32),
-            pltpu.VMEM((K, LANES), jnp.float32),
+            pltpu.VMEM(square.shape, jnp.float32),
             pltpu.SemaphoreType.DMA((3,)),
             pltpu.SemaphoreType.DMA((2, TB_OWN)),
             pltpu.SemaphoreType.DMA((len(cuts),)),
@@ -368,6 +372,66 @@
     )(*operands)
 
 
+def close_kernel(root, groups, labels_ref, got_ref, sums_hbm, out_hbm, similarity, sums, out, sems):
+    width = TB_OWN // groups
+    reads, writes = [], []
+    for g in range(groups):
+        some = (slice(None), pl.ds(g * width * 2 * LANES, width * 2 * LANES))
+        reads.append(pltpu.make_async_copy(sums_hbm.at[some], sums.at[some], sems.at[0, g]))
+        some = (slice(None), pl.ds(g * width * LANES, width * LANES))
+        writes.append(pltpu.make_async_copy(out.at[some], out_hbm.at[some], sems.at[1, g]))
+        reads[g].start()
+    total = jnp.sum(got_ref[...], axis=0)
+    home = total.shape[1] - K
+    own = lax.rsqrt(total[:, home:] + EPSILON)
+    columns = [
+        jnp.transpose(jnp.broadcast_to(own[:, k : k + LANES], (LANES, LANES)))
+        for k in range(0, K, LANES)
+    ]
+    cluster = lax.broadcasted_iota(jnp.int32, (LANES, LANES), 0)
+    for b in range(home // LANES):
+        found = jnp.zeros((LANES, LANES), jnp.float32)
+        for i, column in enumerate(columns):
+            found += jnp.where(cluster + i * LANES == labels_ref[b : b + 1, :], column, 0.0)
+        found = jnp.sum(found, axis=0, keepdims=True)
+        similarity[b : b + 1, :] = total[:, b * LANES : (b + 1) * LANES] * found
+    for g in range(groups):
+        reads[g].wait()
+        for sub in range(g * width, (g + 1) * width):
+            for i, column in enumerate(columns):
+                half, row = divmod(i * LANES, HALF)
+                at = (2 * sub + half) * LANES
+                some = sums[row : row + LANES, at : at + LANES]
+                done = (some * column * root).astype(jnp.bfloat16)
+                out[i * LANES : (i + 1) * LANES, sub * LANES : (sub + 1) * LANES] = done
+        writes[g].start()
+    for write in writes:
+        write.wait()
+
+
+def close(labels, got, sums, vocab_size):
+    groups = 4
+    labels = labels.reshape(-1, LANES)
+    wide = jax.ShapeDtypeStruct((K, TB_OWN * LANES), jnp.bfloat16)
+    centroids, similarity = pl.pallas_call(
+        functools.partial(close_kernel, math.sqrt(vocab_size), groups),
+        in_specs=[VMEM, VMEM, ANY],
+        out_specs=[ANY, VMEM],
+        out_shape=[wide, jax.ShapeDtypeStruct(labels.shape, jnp.float32)],
+        scratch_shapes=[
+            pltpu.VMEM(sums.shape, jnp.float32),
+            pltpu.VMEM(wide.shape, jnp.bfloat16),
+            pltpu.SemaphoreType.DMA((2, groups)),
+        ],
+        compiler_params=params(),
+        cost_estimate=pl.CostEstimate(
+            flops=2 * sums.size, bytes_accessed=6 * sums.size, transcendentals=0
+        ),
+        name="close",
+    )(labels, got, sums)
+    return centroids, similarity.reshape(-1)
+
+
 def exchange(x):
     return lax.all_to_all(x, "dp", split_axis=0, concat_axis=0, tiled=True)
 
@@ -419,7 +483,6 @@
     row_sq = jnp.sum(jnp.where(level > -32768, partial_sq, 0.0), axis=0)
     all_described = heard[:, blocks:].reshape(devices, -1)
     all_labels = all_described[:, :home].reshape(blocks, LANES)
-    padded_labels = jnp.concatenate([all_labels, jnp.full((1, LANES), -1, jnp.int32)])
     mine = all_described[:, home : home + tiles] == here
     code = all_described[:, home + tiles : home + 2 * tiles]
     rank = ranks(mine.astype(jnp.int32), code % TB_OWN)
@@ -440,27 +503,22 @@
         fold_order, fold_bounds, score_order, score_bounds, meta, jnp.asarray(place, jnp.int32), done
     ]
 
-    inverse = lax.rsqrt(row_sq + EPSILON)
-    scale = jnp.broadcast_to((inverse * (1.0 / CODE_TOP**2))[:, :, None], (blocks, LANES, LANES))
+    scale = lax.rsqrt(row_sq + EPSILON) * (1.0 / CODE_TOP**2)
+    signed = jnp.pad(jnp.where(all_labels < HALF, scale, -scale), ((0, 1), (0, 0)))
+    mods = (all_labels % HALF).astype(jnp.float32)
+    mods = jnp.pad(mods, ((0, 1), (0, 0)), constant_values=-1.0)
     partial, totals, normed = jnp.zeros((blocks, LANES), jnp.float32), (), []
-    beside = (*scalars, padded_labels, scale)
+    beside = (*scalars, mods, signed)
     for q in range(parts):
         if q + 1 < parts:
             ahead = (incoming[q], *beside) if q else (incoming[q],)
             incoming.append(exchange(after(outgoing[q + 1], *ahead)))
         partial, sums, *more = stage(
-            q, cuts, scalars, padded_labels, partial, scale, incoming[q], normed, totals
+            q, cuts, scalars, mods, signed, partial, incoming[q], normed, totals
         )
         beside = (partial, sums)
         totals, normed = (sums, *more[:1]), normed + more[1:]
-    back = jnp.sum(exchange(partial), axis=(0, 1))
-    own_scale = lax.rsqrt(back[home:] + EPSILON)
-    vocab_size = TB_OWN * LANES * devices
-    centroid = sums * own_scale[:, None]
-    centroids = (centroid * math.sqrt(vocab_size)).astype(jnp.bfloat16)
-    is_label = labels[:, None] == jnp.arange(K, dtype=jnp.int32)[None, :]
-    doc_scale = jnp.sum(jnp.where(is_label, own_scale[None, :], 0.0), axis=1)
-    return (centroids, back[:home] * doc_scale)
+    return close(labels, exchange(partial), sums, TB_OWN * LANES * devices)
 
 
 def solution(mesh):

time: 251 us -> 247 us (0.984)
  blocking collectives: 180 us -> 26.4 us
  waiting for transfers between devices: 7.11 us -> 131 us
  starting transfers between devices: 4.35 us -> 36.3 us
  other arithmetic: 13.1 us -> 8.26 us
    all_to_all x2 -> x1, blocking collectives: 180 us -> 26.4 us  [exchange(): return lax.all_to_all(x, 'dp', split_axis=0, concat_axis=0, tiled=True)]
    all_to_all x1 -> x2, waiting for transfers between devices: 7.11 us -> 131 us  [exchange(): return lax.all_to_all(x, 'dp', split_axis=0, concat_axis=0, tiled=True)]
    all_to_all x1 -> x2, starting transfers between devices: 4.35 us -> 36.3 us  [exchange(): return lax.all_to_all(x, 'dp', split_axis=0, concat_axis=0, tiled=True)]
    pallas_call x2, Pallas kernels: 31.6 us -> 26 us  [stage(): pl.pallas_call(functools.partial(stage_kernel, q, [devices * cut for cut...]
    pallas_call x0 -> x1, Pallas kernels: none -> 4.62 us  [close(): pl.pallas_call(functools.partial(close_kernel, math.sqrt(vocab_size), gro...]
    convert_element_type x1, other arithmetic: 3.92 us -> 0.01 us  [shards(): mods = (all_labels % HALF).astype(jnp.float32)]
  transfers between devices with their start and end apart: 1 -> 2, of which waited for: 1 -> 2; matrix products, arithmetic and copies ran while one was open for 4% -> 3% of each run, Pallas kernels for 10% -> 8%
where the time goes in v9:
time: 247 us; the launch traced here: 246 us
  waiting for transfers between devices  131 us (53%)
  Pallas kernels  39.7 us (16%)
  starting transfers between devices  36.3 us (15%)
  blocking collectives  26.4 us (11%)
  other arithmetic  8.26 us (3%)
  local copies, waits for them, and re-layouts  3.27 us (1%)
    all_to_all x2, waiting for transfers between devices, exchange(): return lax.all_to_all(x, 'dp', split_axis=0, concat_axis=0, tiled=True)  131 us
    all_to_all x2, starting transfers between devices, exchange(): return lax.all_to_all(x, 'dp', split_axis=0, concat_axis=0, tiled=True)  36.3 us
    all_to_all x1, blocking collectives, exchange(): return lax.all_to_all(x, 'dp', split_axis=0, concat_axis=0, tiled=True)  26.4 us
    pallas_call x2, Pallas kernels, stage(): pl.pallas_call(functools.partial(stage_kernel, q, [devices * cut for cut...  26 us
    pallas_call x1, Pallas kernels, pack(): pl.pallas_call(functools.partial(pack_kernel, cuts), grid=(tiles // step,...  9.07 us
  transfers between devices with their start and end apart: 2, of which 2 were waited for; matrix products, arithmetic and copies ran while one was open for 3% of the time, Pallas kernels for 8%

profile of v9, /device:TPU:0, one launch (start us, length us, event | category | flops | bytes accessed | tf_op | source)
XLA Modules:
  0.0 245.8 jit_solution(9874723106827968404)
XLA Ops:
  0.6 0.9 convert_reduce_fusion.3
  1.5 1.2 multiply_add_fusion.put_ref
  2.7 9.1 %pack.1 = (s16[16,1584,128]{2,1,0:T(8,128)(2,1)}, s16[16,512,128]{2,1,0:T(8,128)(2,1)}) custom-call(s32[128]{0:T(128)} %multiply_add_fusion.put_ref, s32[128]{0:T(128)} %row_ref.1, s32[2,128]{1,0:T(2,128)} %bitcast.18, s32[1,128]{1,0:T(1,128)} %bitcast.16, s32[1,128]{1,0:T(1,128)} %bitcast.20, s32[1,128]{1,0:T(1,128)} %bitcast.17, f32[128,128,128]{2,1,0:T(8,128)} %refs_4_.1), custom_call_target="tpu_custom_call" | custom-call | flops 16777216 | bytes 12582912 | tf_op jit(solution)/shard_map/pack/pallas_call | solution.py:140
  11.8 7.4 %all-to-all-start = ((s16[16,1584,128]{2,1,0:T(8,128)(2,1)}), s16[16,1584,128]{2,1,0:T(8,128)(2,1)}, u32[]{:S(2)}, u32[]{:S(2)}) async-start(s16[16,1584,128]{2,1,0:T(8,128)(2,1)} %get-tuple-element.13), calls=%async_computation | async-start | bytes 12976128 | tf_op jit(solution)/shard_map/all_to_all | solution.py:436
  19.3 117.6 %all-to-all-done.x_hbm = s16[16,1584,128]{2,1,0:T(8,128)(2,1)} async-done(((s16[16,1584,128]{2,1,0:T(8,128)(2,1)}), s16[16,1584,128]{2,1,0:T(8,128)(2,1)}, u32[]{:S(2)}, u32[]{:S(2)}) %all-to-all-start) | async-done | bytes 6488096 | tf_op jit(solution)/shard_map/all_to_all | solution.py:436
  136.9 28.9 %all-to-all-start.1 = ((s16[16,512,128]{2,1,0:T(8,128)(2,1)}), s16[16,512,128]{2,1,0:T(8,128)(2,1)S(1)}, u32[]{:S(2)}, u32[]{:S(2)}) async-start(s16[16,512,128]{2,1,0:T(8,128)(2,1)} %get-tuple-element.16), calls=%async_computation.1 | async-start | bytes 4194304 | tf_op jit(solution)/shard_map/all_to_all | solution.py:436
  165.7 1.0 slice_convert_fusion
  166.8 1.0 convert_reduce_fusion
  167.9 0.3 select_reduce_fusion.3
  168.4 0.6 pad.8.mods
  169.1 0.6 pad.9.signed
  169.8 0.6 pad_add_fusion.done
  170.4 0.6 convert_reduce_fusion.5.score_bound
  171.0 0.7 convert_reduce_fusion.4.fold_bound
  171.7 0.3 convert_reduce_fusion.1
  171.9 0.7 select_reduce_fusion.1.score_order
  172.7 0.7 select_reduce_fusion.2.fold_order
  173.3 0.6 broadcast_in_dim.54.before
  173.9 19.4 %stage.2 = (f32[32,128]{1,0:T(8,128)}, f32[256,4096]{1,0:T(8,128)}, f32[256,256]{1,0:T(8,128)}, bf16[192,128,128]{2,1,0:T(8,128)(2,1)}) custom-call(s32[256]{0:T(256)} %select_reduce_fusion.2.fold_order, s32[35]{0:T(128)} %convert_reduce_fusion.4.fold_bound, s32[256]{0:T(256)} %select_reduce_fusion.1.score_order, s32[17]{0:T(128)} %convert_reduce_fusion.5.score_bound, ...), custom_call_target="tpu_custom_call" | custom-call | flops 12884901888 | bytes 20971520 | tf_op jit(solution)/shard_map/stage/pallas_call | solution.py:345
  193.3 13.5 %all-to-all-done.1.x_hbm = s16[16,512,128]{2,1,0:T(8,128)(2,1)S(1)} async-done(((s16[16,512,128]{2,1,0:T(8,128)(2,1)}), s16[16,512,128]{2,1,0:T(8,128)(2,1)S(1)}, u32[]{:S(2)}, u32[]{:S(2)}) %all-to-all-start.1) | async-done | bytes 2097184 | tf_op jit(solution)/shard_map/all_to_all | solution.py:436
  206.8 1.3 copy-done
  208.2 6.6 %stage.3 = (f32[16,1,768]{2,1,0:T(1,128)}, f32[256,4096]{1,0:T(8,128)}) custom-call(s32[256]{0:T(256)} %select_reduce_fusion.2.fold_order, s32[35]{0:T(128)} %convert_reduce_fusion.4.fold_bound, s32[256]{0:T(256)} %select_reduce_fusion.1.score_order, s32[17]{0:T(128)} %convert_reduce_fusion.5.score_bound, ...), custom_call_target="tpu_custom_call", output_to_operand_aliasing={{1}: (12, {})} | custom-call | flops 4294967296 | bytes 12582912 | tf_op jit(solution)/shard_map/stage/pallas_call | solution.py:345
  214.8 26.4 %all_to_all.15.got_ref = f32[16,1,768]{2,1,0:T(1,128)} all-to-all(f32[16,1,768]{2,1,0:T(1,128)} %get-tuple-element.20), channel_id=1, replica_groups=mesh['groups'=2,'dp'=16] {'dp'}, dimensions={0} | all-to-all | bytes 98304 | tf_op jit(solution)/shard_map/all_to_all | solution.py:436
  241.2 4.6 %close.1 = (bf16[512,2048]{1,0:T(8,128)(2,1)}, f32[2,128]{1,0:T(2,128)}) custom-call(s32[2,128]{1,0:T(2,128)} %bitcast.19, f32[16,1,768]{2,1,0:T(1,128)} %all_to_all.15.got_ref, f32[256,4096]{1,0:T(8,128)} %get-tuple-element.21.sums_hbm), custom_call_target="tpu_custom_call" | custom-call | flops 2097152 | bytes 6291456 | tf_op jit(solution)/shard_map/close/pallas_call | solution.py:416
  (21 shorter events, 0.4 us)
Async XLA Ops:
  11.8 157.9 %copy-start.3 = (s32[256]{0:T(256)S(1)}, s32[256]{0:T(256)}, u32[]{:S(2)}) copy-start(s32[256]{0:T(256)} %constant.82.clone) | copy-start | bytes 3076
  11.8 157.9 %copy-start.2 = (pred[2,256]{1,0:T(4,128)(4,1)S(1)}, pred[2,256]{1,0:T(4,128)(4,1)}, u32[]{:S(2)}) copy-start(pred[2,256]{1,0:T(4,128)(4,1)} %constant.83.clone) | copy-start | bytes 1540
  11.8 125.0 %all-to-all-start = ((s16[16,1584,128]{2,1,0:T(8,128)(2,1)}), s16[16,1584,128]{2,1,0:T(8,128)(2,1)}, u32[]{:S(2)}, u32[]{:S(2)}) async-start(s16[16,1584,128]{2,1,0:T(8,128)(2,1)} %get-tuple-element.13), calls=%async_computation | async-start | bytes 12976128 | tf_op jit(solution)/shard_map/all_to_all | solution.py:436
  136.9 70.0 %all-to-all-start.1 = ((s16[16,512,128]{2,1,0:T(8,128)(2,1)}), s16[16,512,128]{2,1,0:T(8,128)(2,1)S(1)}, u32[]{:S(2)}, u32[]{:S(2)}) async-start(s16[16,512,128]{2,1,0:T(8,128)(2,1)} %get-tuple-element.16), calls=%async_computation.1 | async-start | bytes 4194304 | tf_op jit(solution)/shard_map/all_to_all | solution.py:436
  168.3 5.6 %copy-start.1 = (s32[256]{0:T(256)}, s32[256]{0:T(256)S(1)}, u32[]{:S(2)}) copy-start(s32[256]{0:T(256)S(1)} %sub.7.meta) | copy-start | bytes 3076
  206.8 1.3 copy-start

commit v10 on v9

--- a/solution.py
+++ b/solution.py
@@ -16,9 +16,9 @@
 EPSILON = 1e-06
 CODE_TOP = 65535.0
 CODE_SHIFT = 32768
-VMEM_BYTES = 56 * 1024 * 1024
+VMEM_BYTES = 60 * 1024 * 1024
 STEP_TILES = 32
-PARTS = (0.0, 12 / 16, 1.0)
+PARTS = (0.0, 13 / 16, 1.0)
 LOG_STEPS = 1800.0
 LOG_MIDDLE = -3.0
 CACHED_BLOCKS = 64
@@ -168,15 +168,18 @@
                  place, done, mods, signed, before, x_hbm, *refs):
     base = bases[q]
     earlier, refs = refs[:q], refs[q:]
-    (sums_in, squares_in), refs = (refs[:2], refs[2:]) if q else ((None, None), refs)
+    (sums_in, squares_in, *made_in), refs = (refs[:4], refs[4:]) if q else ((None,) * 4, refs)
     part, sums_out, refs = refs[0], refs[1], refs[2:]
-    (squares_out, fresh_out), refs = ((None, None), refs) if last else (refs[:2], refs[2:])
+    (squares_out, *made_out, fresh_out), refs = ((None,) * 4, refs) if last else (refs[:4], refs[4:])
     spread, x, hot, sums, narrow, tiles, products, scores, squares, sems, sub_sems, tile_sems = refs
     devices, width = x.shape[0], x.shape[1] // LANES
     none = products.shape[0] - 1
     begin, end = done[q], done[q + 1]
-    needed = pltpu.make_async_copy(x_hbm.at[:, pl.ds(0, width * LANES)], x, sems.at[0])
-    needed.start()
+    needed = [pltpu.make_async_copy(x_hbm.at[:, pl.ds(0, width * LANES)], x, sems.at[0])]
+    if q:
+        needed.append(pltpu.make_async_copy(made_in[0], spread, sems.at[1]))
+    for copy in needed:
+        copy.start()
 
     def columns(sub):
         return (slice(None), pl.ds(pl.multiple_of(sub * 2 * LANES, 2 * LANES), 2 * LANES))
@@ -204,11 +207,12 @@
     else:
         sums[...] = jnp.zeros_like(sums)
         squares[...] = jnp.zeros_like(squares)
-    later = []
+    later = [pltpu.make_async_copy(made_in[1], hot, sems.at[3])] if q and cached else []
     for e, e_hbm in enumerate(earlier):
         held = tiles.at[pl.ds(bases[e], e_hbm.shape[0])]
         later.append(pltpu.make_async_copy(e_hbm, held, tile_sems.at[e]))
-        later[e].start()
+    for copy in later:
+        copy.start()
     products[...] = jnp.zeros_like(products)
     scores[...] = before[...]
     cluster = lax.broadcasted_iota(jnp.int32, (HALF, LANES), 0)
@@ -231,8 +235,10 @@
                 hot[c * batch + j] = one_hot(c * batch + j)
         return carry
 
-    lax.fori_loop(0, (none + 1) // batch, build, 0)
-    needed.wait()
+    if not q:
+        lax.fori_loop(0, (none + 1) // batch, build, 0)
+    for copy in needed:
+        copy.wait()
 
     def eight(order, start, end, p):
         rows, spots = [], []
@@ -277,6 +283,8 @@
     if not last:
         fresh = tiles.at[pl.ds(base, devices * width)]
         kept.append(pltpu.make_async_copy(fresh, fresh_out, sems.at[2]))
+        kept.append(pltpu.make_async_copy(spread, made_out[0], sems.at[4]))
+        kept.append(pltpu.make_async_copy(hot, made_out[1], sems.at[5]))
     for copy in kept:
         copy.start()
     for copy in later:
@@ -338,16 +346,18 @@
             jax.ShapeDtypeStruct((blocks, LANES), jnp.float32),
             wide,
             square,
+            jax.ShapeDtypeStruct((blocks + 1, LANES, LANES), jnp.float32),
+            jax.ShapeDtypeStruct((blocks + 1 if cached else 1, LANES, HALF), jnp.bfloat16),
             jax.ShapeDtypeStruct((devices * width, LANES, LANES), jnp.bfloat16),
         ]
     slots = devices * cuts[-1]
     operands = [*scalars, mods, signed, before, x, *normed, *totals]
     return pl.pallas_call(
         functools.partial(stage_kernel, q, [devices * cut for cut in cuts], last, cached),
-        in_specs=[SMEM] * len(scalars) + [VMEM] * 3 + [ANY] * (1 + q) + [ANY, VMEM][: len(totals)],
-        out_specs=[VMEM, ANY, VMEM, ANY][: len(out_shape)],
+        in_specs=[SMEM] * len(scalars) + [VMEM] * 3 + [ANY] * (1 + q) + [ANY, VMEM, ANY, ANY][: len(totals)],
+        out_specs=[VMEM, ANY, VMEM, ANY, ANY, ANY][: len(out_shape)],
         out_shape=out_shape,
-        input_output_aliases={len(operands) - 2: 1} if q else {},
+        input_output_aliases={len(operands) - len(totals): 1} if q else {},
         scratch_shapes=[
             pltpu.VMEM((blocks + 1, LANES, LANES), jnp.float32),
             pltpu.VMEM((devices, width * LANES, LANES), jnp.int16),
@@ -358,7 +368,7 @@
             pltpu.VMEM((blocks + 1, LANES, LANES), jnp.float32),
             pltpu.VMEM((blocks, LANES), jnp.float32),
             pltpu.VMEM(square.shape, jnp.float32),
-            pltpu.SemaphoreType.DMA((3,)),
+            pltpu.SemaphoreType.DMA((6,)),
             pltpu.SemaphoreType.DMA((2, TB_OWN)),
             pltpu.SemaphoreType.DMA((len(cuts),)),
         ],
@@ -517,7 +527,7 @@
             q, cuts, scalars, mods, signed, partial, incoming[q], normed, totals
         )
         beside = (partial, sums)
-        totals, normed = (sums, *more[:1]), normed + more[1:]
+        totals, normed = (sums, *more[:3]), normed + more[3:]
     return close(labels, exchange(partial), sums, TB_OWN * LANES * devices)
 
 

time: 247 us -> 248 us (level)
  Pallas kernels: 39.7 us -> 49.1 us
  blocking collectives: 26.4 us -> 19.9 us
  waiting for transfers between devices: 131 us -> 127 us
    pallas_call x2, Pallas kernels: 26 us -> 35.3 us  [stage(): pl.pallas_call(functools.partial(stage_kernel, q, [devices * cut for cut...]
    all_to_all x1, blocking collectives: 26.4 us -> 19.9 us  [exchange(): return lax.all_to_all(x, 'dp', split_axis=0, concat_axis=0, tiled=True)]
    all_to_all x2, waiting for transfers between devices: 131 us -> 127 us  [exchange(): return lax.all_to_all(x, 'dp', split_axis=0, concat_axis=0, tiled=True)]
  transfers between devices with their start and end apart: 2 -> 2, of which waited for: 2 -> 1; matrix products, arithmetic and copies ran while one was open for 3% -> 3% of each run, Pallas kernels for 8% -> 11%
where the time goes in v10:
time: 248 us; the launch traced here: 246 us
  waiting for transfers between devices  127 us (51%)
  Pallas kernels  49.1 us (20%)
  starting transfers between devices  38.4 us (15%)
  blocking collectives  19.9 us (8%)
  other arithmetic  8.29 us (3%)
  local copies, waits for them, and re-layouts  3.09 us (1%)
    all_to_all x2, waiting for transfers between devices, exchange(): return lax.all_to_all(x, 'dp', split_axis=0, concat_axis=0, tiled=True)  127 us
    all_to_all x2, starting transfers between devices, exchange(): return lax.all_to_all(x, 'dp', split_axis=0, concat_axis=0, tiled=True)  38.4 us
    pallas_call x2, Pallas kernels, stage(): pl.pallas_call(functools.partial(stage_kernel, q, [devices * cut for cut...  35.3 us
    all_to_all x1, blocking collectives, exchange(): return lax.all_to_all(x, 'dp', split_axis=0, concat_axis=0, tiled=True)  19.9 us
    pallas_call x1, Pallas kernels, pack(): pl.pallas_call(functools.partial(pack_kernel, cuts), grid=(tiles // step,...  9.21 us
  transfers between devices with their start and end apart: 2, of which 1 were waited for; matrix products, arithmetic and copies ran while one was open for 3% of the time, Pallas kernels for 11%

profile of v10, /device:TPU:0, one launch (start us, length us, event | category | flops | bytes accessed | tf_op | source)
XLA Modules:
  0.0 246.3 jit_solution(2489934255927306775)
XLA Ops:
  0.6 0.9 convert_reduce_fusion.3
  1.5 1.2 multiply_add_fusion.put_ref
  2.7 9.2 %pack.1 = (s16[16,1712,128]{2,1,0:T(8,128)(2,1)}, s16[16,384,128]{2,1,0:T(8,128)(2,1)}) custom-call(s32[128]{0:T(128)} %multiply_add_fusion.put_ref, s32[128]{0:T(128)} %row_ref.1, s32[2,128]{1,0:T(2,128)} %bitcast.18, s32[1,128]{1,0:T(1,128)} %bitcast.16, s32[1,128]{1,0:T(1,128)} %bitcast.20, s32[1,128]{1,0:T(1,128)} %bitcast.17, f32[128,128,128]{2,1,0:T(8,128)} %refs_4_.1), custom_call_target="tpu_custom_call" | custom-call | flops 16777216 | bytes 12582912 | tf_op jit(solution)/shard_map/pack/pallas_call | solution.py:140
  11.9 7.4 %all-to-all-start = ((s16[16,1712,128]{2,1,0:T(8,128)(2,1)}), s16[16,1712,128]{2,1,0:T(8,128)(2,1)}, u32[]{:S(2)}, u32[]{:S(2)}) async-start(s16[16,1712,128]{2,1,0:T(8,128)(2,1)} %get-tuple-element.15), calls=%async_computation | async-start | bytes 14024704 | tf_op jit(solution)/shard_map/all_to_all | solution.py:446
  19.4 126.7 %all-to-all-done.x_hbm = s16[16,1712,128]{2,1,0:T(8,128)(2,1)} async-done(((s16[16,1712,128]{2,1,0:T(8,128)(2,1)}), s16[16,1712,128]{2,1,0:T(8,128)(2,1)}, u32[]{:S(2)}, u32[]{:S(2)}) %all-to-all-start) | async-done | bytes 7012384 | tf_op jit(solution)/shard_map/all_to_all | solution.py:446
  146.1 31.0 %all-to-all-start.1 = ((s16[16,384,128]{2,1,0:T(8,128)(2,1)}), s16[16,384,128]{2,1,0:T(8,128)(2,1)S(1)}, u32[]{:S(2)}, u32[]{:S(2)}) async-start(s16[16,384,128]{2,1,0:T(8,128)(2,1)} %get-tuple-element.18), calls=%async_computation.1 | async-start | bytes 3145728 | tf_op jit(solution)/shard_map/all_to_all | solution.py:446
  177.1 1.0 slice_convert_fusion
  178.1 1.0 convert_reduce_fusion
  179.2 0.3 select_reduce_fusion.3
  179.7 0.6 pad.8.mods
  180.4 0.6 pad.9.signed
  181.0 0.1 select_reduce_fusion.4
  181.1 0.6 pad_add_fusion.done
  181.7 0.7 convert_reduce_fusion.5.score_bound
  182.5 0.6 convert_reduce_fusion.4.fold_bound
  183.1 0.3 convert_reduce_fusion.1
  183.4 0.7 select_reduce_fusion.1.score_order
  184.0 0.7 select_reduce_fusion.2.fold_order
  184.7 0.6 broadcast_in_dim.54.before
  185.3 27.3 %stage.2 = (f32[32,128]{1,0:T(8,128)}, f32[256,4096]{1,0:T(8,128)}, f32[256,256]{1,0:T(8,128)}, f32[33,128,128]{2,1,0:T(8,128)}, bf16[33,128,256]{2,1,0:T(8,128)(2,1)}, /*index=5*/bf16[208,128,128]{2,1,0:T(8,128)(2,1)}) custom-call(s32[256]{0:T(256)} %select_reduce_fusion.2.fold_order, s32[35]{0:T(128)} %convert_reduce_fusion.4.fold_bound, ...), custom_call_target="tpu_custom_call" | custom-call | flops 13958643712 | bytes 22020096 | tf_op jit(solution)/shard_map/stage/pallas_call | solution.py:355
  212.7 1.1 copy-done
  213.8 7.9 %stage.3 = (f32[16,1,768]{2,1,0:T(1,128)}, f32[256,4096]{1,0:T(8,128)}) custom-call(s32[256]{0:T(256)} %select_reduce_fusion.2.fold_order, s32[35]{0:T(128)} %convert_reduce_fusion.4.fold_bound, s32[256]{0:T(256)} %select_reduce_fusion.1.score_order, s32[17]{0:T(128)} %convert_reduce_fusion.5.score_bound, ...), custom_call_target="tpu_custom_call", output_to_operand_aliasing={{1}: (12, {})} | custom-call | flops 3221225472 | bytes 11534336 | tf_op jit(solution)/shard_map/stage/pallas_call | solution.py:355
  221.7 19.9 %all_to_all.15.got_ref = f32[16,1,768]{2,1,0:T(1,128)} all-to-all(f32[16,1,768]{2,1,0:T(1,128)} %get-tuple-element.24), channel_id=1, replica_groups=mesh['groups'=2,'dp'=16] {'dp'}, dimensions={0} | all-to-all | bytes 98304 | tf_op jit(solution)/shard_map/all_to_all | solution.py:446
  241.6 4.6 %close.1 = (bf16[512,2048]{1,0:T(8,128)(2,1)}, f32[2,128]{1,0:T(2,128)}) custom-call(s32[2,128]{1,0:T(2,128)} %bitcast.19, f32[16,1,768]{2,1,0:T(1,128)} %all_to_all.15.got_ref, f32[256,4096]{1,0:T(8,128)} %get-tuple-element.25.sums_hbm), custom_call_target="tpu_custom_call" | custom-call | flops 2097152 | bytes 6291456 | tf_op jit(solution)/shard_map/close/pallas_call | solution.py:426
  (21 shorter events, 0.3 us)
Async XLA Ops:
  11.9 134.2 %all-to-all-start = ((s16[16,1712,128]{2,1,0:T(8,128)(2,1)}), s16[16,1712,128]{2,1,0:T(8,128)(2,1)}, u32[]{:S(2)}, u32[]{:S(2)}) async-start(s16[16,1712,128]{2,1,0:T(8,128)(2,1)} %get-tuple-element.15), calls=%async_computation | async-start | bytes 14024704 | tf_op jit(solution)/shard_map/all_to_all | solution.py:446
  19.3 161.6 %copy-start.3 = (s32[256]{0:T(256)S(1)}, s32[256]{0:T(256)}, u32[]{:S(2)}) copy-start(s32[256]{0:T(256)} %constant.82.clone) | copy-start | bytes 3076
  19.4 161.6 %copy-start.2 = (pred[2,256]{1,0:T(4,128)(4,1)S(1)}, pred[2,256]{1,0:T(4,128)(4,1)}, u32[]{:S(2)}) copy-start(pred[2,256]{1,0:T(4,128)(4,1)} %constant.83.clone) | copy-start | bytes 1540
  146.1 66.5 %all-to-all-start.1 = ((s16[16,384,128]{2,1,0:T(8,128)(2,1)}), s16[16,384,128]{2,1,0:T(8,128)(2,1)S(1)}, u32[]{:S(2)}, u32[]{:S(2)}) async-start(s16[16,384,128]{2,1,0:T(8,128)(2,1)} %get-tuple-element.18), calls=%async_computation.1 | async-start | bytes 3145728 | tf_op jit(solution)/shard_map/all_to_all | solution.py:446
  179.7 5.6 %copy-start.1 = (s32[256]{0:T(256)}, s32[256]{0:T(256)S(1)}, u32[]{:S(2)}) copy-start(s32[256]{0:T(256)S(1)} %sub.7.meta) | copy-start | bytes 3076
  212.6 1.1 copy-start

commit v11 on v10

--- a/solution.py
+++ b/solution.py
@@ -17,12 +17,13 @@
 CODE_TOP = 65535.0
 CODE_SHIFT = 32768
 VMEM_BYTES = 60 * 1024 * 1024
-STEP_TILES = 32
+STEP_TILES = 16
 PARTS = (0.0, 13 / 16, 1.0)
 LOG_STEPS = 1800.0
 LOG_MIDDLE = -3.0
 CACHED_BLOCKS = 64
 QUAD = 4
+PAIR = 2
 EIGHT = 8
 BATCH = 8
 NT = (((1,), (1,)), ((), ()))
@@ -57,102 +58,123 @@
     return pltpu.CompilerParams(vmem_limit_bytes=VMEM_BYTES)
 
 
-def pack_kernel(cuts, put_ref, row_ref, *refs):
+def pack_kernel(cuts, owner_ref, rank_ref, row_ref, *refs):
     parts = len(cuts) - 1
-    (*told_refs, x_ref), refs = refs[:5], refs[5:]
+    (*told_refs, x_hbm), refs = refs[:5], refs[5:]
     outs = refs[:parts]
-    coded, square, sums, words, notes, held, sems = refs[parts:]
-    step = pl.program_id(0)
-    tiles = x_ref.shape[0]
+    x, coded, square, sums, words, notes, held, tile_at, sems, x_sems = refs[parts:]
+    tiles = x.shape[0]
     devices = held.shape[0]
     blocks = square.shape[0]
-
-    @pl.when(step == 0)
-    def _():
-        square[...] = jnp.zeros_like(square)
-
-        def clear(d, carry):
-            held[d] = 0
+    step = math.gcd(STEP_TILES, tiles)
+    reads = [
+        pltpu.make_async_copy(x_hbm.at[pl.ds(i, step)], x.at[pl.ds(i, step)], x_sems.at[i // step])
+        for i in range(0, tiles, step)
+    ]
+    for read in reads:
+        read.start()
+
+    def clear(d, carry):
+        held[d] = 0
+        return carry
+
+    def list_tile(t, carry):
+        owner, rank = owner_ref[t], rank_ref[t]
+        tile_at[owner * cuts[-1] + rank] = t
+        held[owner] = jnp.maximum(held[owner], rank + 1)
+        return carry
+
+    lax.fori_loop(0, devices, clear, 0)
+    lax.fori_loop(0, tiles, list_tile, 0)
+    square[...] = jnp.zeros_like(square)
+    for i, read in enumerate(reads):
+        read.wait()
+
+        def some_squares(c, carry, first=i * step):
+            for j in range(QUAD):
+                t = first + c * QUAD + j
+                square[row_ref[t]] += x[t] * x[t]
             return carry
 
-        lax.fori_loop(0, devices, clear, 0)
-
-    def some_tiles(i, carry):
-        for j in range(QUAD):
-            t = step * tiles + i * QUAD + j
-            x = x_ref[i * QUAD + j]
-            root = x * lax.rsqrt(x)
-            code = (root * CODE_TOP + 0.5).astype(jnp.int32) - CODE_SHIFT
-            put = put_ref[t]
-            coded[pl.ds(pl.multiple_of(put * LANES, LANES), LANES), :] = code.astype(jnp.int16)
-            square[row_ref[t]] += x * x
-            owner = put // cuts[-1]
-            held[owner] = jnp.maximum(held[owner], put % cuts[-1] + 1)
-        return carry
-
-    lax.fori_loop(0, tiles // QUAD, some_tiles, 0)
+        lax.fori_loop(0, step // QUAD, some_squares, 0)
 
     def slots(q, d):
         some = pl.ds((d * cuts[-1] + cuts[q]) * LANES, (cuts[q + 1] - cuts[q]) * LANES)
         into = outs[q].at[d, pl.ds(0, (cuts[q + 1] - cuts[q]) * LANES)]
-        return pltpu.make_async_copy(coded.at[some], into, sems.at[q * devices + d])
+        return pltpu.make_async_copy(coded.at[some], into, sems.at[q, d])
 
     def note(d):
         into = outs[0].at[d, pl.ds((cuts[1] - cuts[0]) * LANES, notes.shape[0])]
-        return pltpu.make_async_copy(notes, into, sems.at[parts * devices + d])
-
-    def each(what):
+        return pltpu.make_async_copy(notes, into, sems.at[parts, d])
+
+    def one_owner(d, carry):
+        count = held[d]
+
+        def some_codes(c, carry):
+            for j in range(PAIR):
+                slot = d * cuts[-1] + jnp.minimum(c * PAIR + j, count - 1)
+                some = x[tile_at[slot]]
+                root = some * lax.rsqrt(some)
+                code = (root * CODE_TOP + 0.5).astype(jnp.int32) - CODE_SHIFT
+                at = pl.ds(pl.multiple_of(slot * LANES, LANES), LANES)
+                coded[at, :] = code.astype(jnp.int16)
+            return carry
+
+        lax.fori_loop(0, (count + PAIR - 1) // PAIR, some_codes, 0)
         for q in range(parts):
-            for d in range(devices):
-                pl.when(held[d] > cuts[q])(lambda q=q, d=d: what(slots(q, d)))
-
-    @pl.when(step == pl.num_programs(0) - 1)
-    def _():
-        each(lambda copy: copy.start())
-        sums[...] = jnp.zeros_like(sums)
-        block_sums(square, sums, blocks)
-        total = sums[...]
-        level = (jnp.log2(jnp.maximum(total, 1e-30)) - LOG_MIDDLE) * LOG_STEPS
-        level = jnp.where(total > 0.0, jnp.clip(level, -32700.0, 32700.0), -32768.0)
-        level = (level + 32768.5).astype(jnp.int32) - 32768
-        labels, owner, row, sub = [ref[...] for ref in told_refs]
-        words[...] = jnp.zeros_like(words)
-        words[:blocks, :] = level
-        at = blocks
-        for told in (labels, owner, row * TB_OWN + sub):
-            words[at : at + told.shape[0], :] = told
-            at += told.shape[0]
-        notes[...] = words[...].astype(jnp.int16)
-        for d in range(devices):
-            note(d).start()
-        each(lambda copy: copy.wait())
-        for d in range(devices):
-            note(d).wait()
-
-
-def pack(tile_values, put, tile_row, told, devices, blocks, cuts):
+            pl.when(count > cuts[q])(lambda q=q: slots(q, d).start())
+        return carry
+
+    lax.fori_loop(0, devices, one_owner, 0)
+    sums[...] = jnp.zeros_like(sums)
+    block_sums(square, sums, blocks)
+    total = sums[...]
+    level = (jnp.log2(jnp.maximum(total, 1e-30)) - LOG_MIDDLE) * LOG_STEPS
+    level = jnp.where(total > 0.0, jnp.clip(level, -32700.0, 32700.0), -32768.0)
+    level = (level + 32768.5).astype(jnp.int32) - 32768
+    labels, owner, row, sub = [ref[...] for ref in told_refs]
+    words[...] = jnp.zeros_like(words)
+    words[:blocks, :] = level
+    at = blocks
+    for told in (labels, owner, row * TB_OWN + sub):
+        words[at : at + told.shape[0], :] = told
+        at += told.shape[0]
+    notes[...] = words[...].astype(jnp.int16)
+
+    def finish(d, carry):
+        for q in range(parts):
+            pl.when(held[d] > cuts[q])(lambda q=q: slots(q, d).wait())
+        return carry
+
+    for d in range(devices):
+        note(d).start()
+    lax.fori_loop(0, devices, finish, 0)
+    for d in range(devices):
+        note(d).wait()
+
+
+def pack(tile_values, owner, rank, tile_row, told, devices, blocks, cuts):
     tiles = tile_values.shape[0]
-    step = math.gcd(STEP_TILES, tiles)
     told = [x.reshape(-1, LANES) for x in told]
     noted = -(-(blocks + sum(x.shape[0] for x in told[:3])) // 16) * 16
     rows = [(high - low) * LANES for low, high in zip(cuts, cuts[1:])]
     rows[0] += noted
     return pl.pallas_call(
         functools.partial(pack_kernel, cuts),
-        grid=(tiles // step,),
-        in_specs=[SMEM, SMEM]
-        + [pl.BlockSpec(x.shape, lambda i: (0, 0)) for x in told]
-        + [pl.BlockSpec((step, LANES, LANES), lambda i: (i, 0, 0))],
+        in_specs=[SMEM] * 3 + [VMEM] * 4 + [ANY],
         out_specs=[ANY] * len(rows),
         out_shape=[jax.ShapeDtypeStruct((devices, some, LANES), jnp.int16) for some in rows],
         scratch_shapes=[
+            pltpu.VMEM(tile_values.shape, jnp.float32),
             pltpu.VMEM((devices * cuts[-1] * LANES, LANES), jnp.int16),
             pltpu.VMEM((blocks, LANES, LANES), jnp.float32),
             pltpu.VMEM((blocks, LANES), jnp.float32),
             pltpu.VMEM((noted, LANES), jnp.int32),
             pltpu.VMEM((noted, LANES), jnp.int16),
             pltpu.SMEM((devices,), jnp.int32),
-            pltpu.SemaphoreType.DMA(((len(rows) + 1) * devices,)),
+            pltpu.SMEM((devices * cuts[-1],), jnp.int32),
+            pltpu.SemaphoreType.DMA((len(rows) + 1, devices)),
+            pltpu.SemaphoreType.DMA((tiles,)),
         ],
         compiler_params=params(),
         cost_estimate=pl.CostEstimate(
@@ -161,20 +183,22 @@
             transcendentals=tile_values.size,
         ),
         name="pack",
-    )(put, tile_row, *told, tile_values)
+    )(owner, rank, tile_row, *told, tile_values)
 
 
 def stage_kernel(q, bases, last, cached, fold_order, fold_bound, score_order, score_bound, meta,
-                 place, done, mods, signed, before, x_hbm, *refs):
+                 place, done, mods_in, signed_in, x_hbm, *refs):
     base = bases[q]
     earlier, refs = refs[:q], refs[q:]
-    (sums_in, squares_in, *made_in), refs = (refs[:4], refs[4:]) if q else ((None,) * 4, refs)
+    before, sums_in, squares_in, *made_in = refs[:5] if q else (None,) * 5
+    refs = refs[5:] if q else refs
     part, sums_out, refs = refs[0], refs[1], refs[2:]
     (squares_out, *made_out, fresh_out), refs = ((None,) * 4, refs) if last else (refs[:4], refs[4:])
-    spread, x, hot, sums, narrow, tiles, products, scores, squares, sems, sub_sems, tile_sems = refs
+    spread, x, hot, sums, narrow, tiles, products, scores, squares, mods, signed, *refs = refs
+    sems, sub_sems, tile_sems = refs
     devices, width = x.shape[0], x.shape[1] // LANES
     none = products.shape[0] - 1
-    begin, end = done[q], done[q + 1]
+    begin, end = done[q - 1] if q else 0, done[q]
     needed = [pltpu.make_async_copy(x_hbm.at[:, pl.ds(0, width * LANES)], x, sems.at[0])]
     if q:
         needed.append(pltpu.make_async_copy(made_in[0], spread, sems.at[1]))
@@ -214,7 +238,10 @@
     for copy in later:
         copy.start()
     products[...] = jnp.zeros_like(products)
-    scores[...] = before[...]
+    scores[...] = before[...] if q else jnp.zeros_like(scores)
+    for held, given, empty in ((mods, mods_in, -1.0), (signed, signed_in, 0.0)):
+        held[:none, :] = given[...]
+        held[none : none + 1, :] = jnp.full((1, LANES), empty, jnp.float32)
     cluster = lax.broadcasted_iota(jnp.int32, (HALF, LANES), 0)
     lane = lax.broadcasted_iota(jnp.int32, (LANES, LANES), 1)
 
@@ -330,10 +357,10 @@
     each_sub(begin, TB_OWN, lambda sub: sums_write(sub).wait())
 
 
-def stage(q, cuts, scalars, mods, signed, before, x, normed, totals):
+def stage(q, cuts, scalars, mods, signed, x, normed, totals):
     devices = x.shape[0]
     last = q == len(cuts) - 2
-    blocks = before.shape[0]
+    blocks = mods.shape[0]
     cached = blocks <= CACHED_BLOCKS
     width = cuts[q + 1] - cuts[q]
     home = blocks // devices * LANES
@@ -351,13 +378,13 @@
             jax.ShapeDtypeStruct((devices * width, LANES, LANES), jnp.bfloat16),
         ]
     slots = devices * cuts[-1]
-    operands = [*scalars, mods, signed, before, x, *normed, *totals]
+    operands = [*scalars, mods, signed, x, *normed, *totals]
     return pl.pallas_call(
         functools.partial(stage_kernel, q, [devices * cut for cut in cuts], last, cached),
-        in_specs=[SMEM] * len(scalars) + [VMEM] * 3 + [ANY] * (1 + q) + [ANY, VMEM, ANY, ANY][: len(totals)],
+        in_specs=[SMEM] * len(scalars) + [VMEM] * 2 + [ANY] * (1 + q) + [VMEM, ANY, VMEM, ANY, ANY][: len(totals)],
         out_specs=[VMEM, ANY, VMEM, ANY, ANY, ANY][: len(out_shape)],
         out_shape=out_shape,
-        input_output_aliases={len(operands) - len(totals): 1} if q else {},
+        input_output_aliases={len(operands) - len(totals) + 1: 1} if q else {},
         scratch_shapes=[
             pltpu.VMEM((blocks + 1, LANES, LANES), jnp.float32),
             pltpu.VMEM((devices, width * LANES, LANES), jnp.int16),
@@ -368,6 +395,8 @@
             pltpu.VMEM((blocks + 1, LANES, LANES), jnp.float32),
             pltpu.VMEM((blocks, LANES), jnp.float32),
             pltpu.VMEM(square.shape, jnp.float32),
+            pltpu.VMEM((blocks + 1, LANES), jnp.float32),
+            pltpu.VMEM((blocks + 1, LANES), jnp.float32),
             pltpu.SemaphoreType.DMA((6,)),
             pltpu.SemaphoreType.DMA((2, TB_OWN)),
             pltpu.SemaphoreType.DMA((len(cuts),)),
@@ -483,9 +512,9 @@
     here = lax.axis_index("dp").astype(jnp.int32)
     owner = tile_owner[:, 0]
 
-    put = owner * cap + ranks(owner, tile_sub)
     told = (labels, owner, tile_row, tile_sub)
-    outgoing = pack(tile_values, put, tile_row, told, devices, blocks, cuts)
+    rank = ranks(owner, tile_sub)
+    outgoing = pack(tile_values, owner, rank, tile_row, told, devices, blocks, cuts)
     incoming = [exchange(outgoing[0])]
     heard = incoming[0][:, (cuts[1] - cuts[0]) * LANES :].astype(jnp.int32)
     level = heard[:, :blocks]
@@ -508,26 +537,24 @@
     score_order, score_bounds = sorted_slots(sub, TB_OWN)
     left = np.arange(parts)[:, None] < slot_part[None, :]
     done = jnp.min(jnp.where(left, sub[None, :], TB_OWN), axis=1)
-    done = jnp.concatenate([jnp.zeros((1,), jnp.int32), done])
     scalars = [
         fold_order, fold_bounds, score_order, score_bounds, meta, jnp.asarray(place, jnp.int32), done
     ]
 
     scale = lax.rsqrt(row_sq + EPSILON) * (1.0 / CODE_TOP**2)
-    signed = jnp.pad(jnp.where(all_labels < HALF, scale, -scale), ((0, 1), (0, 0)))
+    signed = jnp.where(all_labels < HALF, scale, -scale)
     mods = (all_labels % HALF).astype(jnp.float32)
-    mods = jnp.pad(mods, ((0, 1), (0, 0)), constant_values=-1.0)
-    partial, totals, normed = jnp.zeros((blocks, LANES), jnp.float32), (), []
+    totals, normed = (), []
     beside = (*scalars, mods, signed)
     for q in range(parts):
         if q + 1 < parts:
             ahead = (incoming[q], *beside) if q else (incoming[q],)
             incoming.append(exchange(after(outgoing[q + 1], *ahead)))
         partial, sums, *more = stage(
-            q, cuts, scalars, mods, signed, partial, incoming[q], normed, totals
+            q, cuts, scalars, mods, signed, incoming[q], normed, totals
         )
         beside = (partial, sums)
-        totals, normed = (sums, *more[:3]), normed + more[3:]
+        totals, normed = (partial, sums, *more[:3]), normed + more[3:]
     return close(labels, exchange(partial), sums, TB_OWN * LANES * devices)
 
 

time: 248 us -> 248 us (level)
  blocking collectives: 19.9 us -> 22.4 us
    pallas_call x2, Pallas kernels: 35.3 us -> 31.3 us  [stage(): pl.pallas_call(functools.partial(stage_kernel, q, [devices * cut for cut...]
  transfers between devices with their start and end apart: 2 -> 2, of which waited for: 1 -> 2; matrix products, arithmetic and copies ran while one was open for 3% -> 3% of each run, Pallas kernels for 11% -> 9%
where the time goes in v11:
time: 248 us
  waiting for transfers between devices  129 us (52%)
  Pallas kernels  47.5 us (19%)
  starting transfers between devices  38.4 us (15%)
  blocking collectives  22.4 us (9%)
  other arithmetic  8.79 us (4%)
    all_to_all x2, waiting for transfers between devices, exchange(): return lax.all_to_all(x, 'dp', split_axis=0, concat_axis=0, tiled=True)  129 us
    all_to_all x2, starting transfers between devices, exchange(): return lax.all_to_all(x, 'dp', split_axis=0, concat_axis=0, tiled=True)  38.4 us
    pallas_call x2, Pallas kernels, stage(): pl.pallas_call(functools.partial(stage_kernel, q, [devices * cut for cut...  31.3 us
    all_to_all x1, blocking collectives, exchange(): return lax.all_to_all(x, 'dp', split_axis=0, concat_axis=0, tiled=True)  22.4 us
    pallas_call x1, Pallas kernels, pack(): pl.pallas_call(functools.partial(pack_kernel, cuts), in_specs=[SMEM] * 3...  11.5 us
  transfers between devices with their start and end apart: 2, of which 2 were waited for; matrix products, arithmetic and copies ran while one was open for 3% of the time, Pallas kernels for 9%

profile of v11, /device:TPU:0, one launch (start us, length us, event | category | flops | bytes accessed | tf_op | source)
XLA Modules:
  0.0 247.9 jit_solution(3271758526493187937)
XLA Ops:
  0.6 1.4 convert_reduce_fusion.3.rank_ref
  2.1 11.5 %pack.1 = (s16[16,1712,128]{2,1,0:T(8,128)(2,1)}, s16[16,384,128]{2,1,0:T(8,128)(2,1)}) custom-call(s32[128]{0:T(128)} %bitcast.15, s32[128]{0:T(128)} %convert_reduce_fusion.3.rank_ref, s32[128]{0:T(128)} %row_ref.1, s32[2,128]{1,0:T(2,128)} %bitcast.18, s32[1,128]{1,0:T(1,128)} %bitcast.16, s32[1,128]{1,0:T(1,128)} %bitcast.20, s32[1,128]{1,0:T(1,128)} %bitcast.17, ...), custom_call_target="tpu_custom_call" | custom-call | flops 16777216 | bytes 12582912 | tf_op jit(solution)/shard_map/pack/pallas_call | solution.py:162
  13.6 7.5 %all-to-all-start = ((s16[16,1712,128]{2,1,0:T(8,128)(2,1)}), s16[16,1712,128]{2,1,0:T(8,128)(2,1)}, u32[]{:S(2)}, u32[]{:S(2)}) async-start(s16[16,1712,128]{2,1,0:T(8,128)(2,1)} %get-tuple-element.15), calls=%async_computation | async-start | bytes 14024704 | tf_op jit(solution)/shard_map/all_to_all | solution.py:475
  21.1 126.7 %all-to-all-done.x_hbm = s16[16,1712,128]{2,1,0:T(8,128)(2,1)} async-done(((s16[16,1712,128]{2,1,0:T(8,128)(2,1)}), s16[16,1712,128]{2,1,0:T(8,128)(2,1)}, u32[]{:S(2)}, u32[]{:S(2)}) %all-to-all-start) | async-done | bytes 7012384 | tf_op jit(solution)/shard_map/all_to_all | solution.py:475
  147.8 1.0 slice_convert_fusion
  148.9 31.0 %all-to-all-start.1 = ((s16[16,384,128]{2,1,0:T(8,128)(2,1)}), s16[16,384,128]{2,1,0:T(8,128)(2,1)S(1)}, u32[]{:S(2)}, u32[]{:S(2)}) async-start(s16[16,384,128]{2,1,0:T(8,128)(2,1)} %get-tuple-element.17), calls=%async_computation.1 | async-start | bytes 3145728 | tf_op jit(solution)/shard_map/all_to_all | solution.py:475
  179.9 1.0 convert_reduce_fusion
  181.0 0.3 select_reduce_fusion.3
  181.3 0.1 sub.7.meta
  181.4 0.6 select_reduce_fusion.4.done
  182.1 0.7 convert_reduce_fusion.5.score_bound
  182.7 0.7 convert_reduce_fusion.4.fold_bound
  183.4 0.3 convert_reduce_fusion.1
  183.7 0.7 select_reduce_fusion.1.score_order
  184.4 0.7 select_reduce_fusion.2.fold_order
  185.1 0.1 select_reduce_fusion
  185.2 0.6 fusion.6.mods_in
  185.8 0.6 negate_select_fusion.signed_in
  186.4 23.4 %stage.2 = (f32[32,128]{1,0:T(8,128)}, f32[256,4096]{1,0:T(8,128)}, f32[256,256]{1,0:T(8,128)}, f32[33,128,128]{2,1,0:T(8,128)}, bf16[33,128,256]{2,1,0:T(8,128)(2,1)}, /*index=5*/bf16[208,128,128]{2,1,0:T(8,128)(2,1)}) custom-call(s32[256]{0:T(256)} %select_reduce_fusion.2.fold_order, s32[35]{0:T(128)} %convert_reduce_fusion.4.fold_bound, ...), custom_call_target="tpu_custom_call" | custom-call | flops 13958643712 | bytes 22020096 | tf_op jit(solution)/shard_map/stage/pallas_call | solution.py:382
  209.8 2.1 all-to-all-done.1.x_hbm
  211.9 1.1 copy-done
  213.0 7.9 %stage.3 = (f32[16,1,768]{2,1,0:T(1,128)}, f32[256,4096]{1,0:T(8,128)}) custom-call(s32[256]{0:T(256)} %select_reduce_fusion.2.fold_order, s32[35]{0:T(128)} %convert_reduce_fusion.4.fold_bound, s32[256]{0:T(256)} %select_reduce_fusion.1.score_order, s32[17]{0:T(128)} %convert_reduce_fusion.5.score_bound, ...), custom_call_target="tpu_custom_call", output_to_operand_aliasing={{1}: (12, {})} | custom-call | flops 3221225472 | bytes 11534336 | tf_op jit(solution)/shard_map/stage/pallas_call | solution.py:382
  220.9 22.4 %all_to_all.15.got_ref = f32[16,1,768]{2,1,0:T(1,128)} all-to-all(f32[16,1,768]{2,1,0:T(1,128)} %get-tuple-element.24), channel_id=1, replica_groups=mesh['groups'=2,'dp'=16] {'dp'}, dimensions={0} | all-to-all | bytes 98304 | tf_op jit(solution)/shard_map/all_to_all | solution.py:475
  243.3 4.6 %close.1 = (bf16[512,2048]{1,0:T(8,128)(2,1)}, f32[2,128]{1,0:T(2,128)}) custom-call(s32[2,128]{1,0:T(2,128)} %bitcast.19, f32[16,1,768]{2,1,0:T(1,128)} %all_to_all.15.got_ref, f32[256,4096]{1,0:T(8,128)} %get-tuple-element.25.sums_hbm), custom_call_target="tpu_custom_call" | custom-call | flops 2097152 | bytes 6291456 | tf_op jit(solution)/shard_map/close/pallas_call | solution.py:455
  (16 shorter events, 0.1 us)
Async XLA Ops:
  13.6 134.2 %all-to-all-start = ((s16[16,1712,128]{2,1,0:T(8,128)(2,1)}), s16[16,1712,128]{2,1,0:T(8,128)(2,1)}, u32[]{:S(2)}, u32[]{:S(2)}) async-start(s16[16,1712,128]{2,1,0:T(8,128)(2,1)} %get-tuple-element.15), calls=%async_computation | async-start | bytes 14024704 | tf_op jit(solution)/shard_map/all_to_all | solution.py:475
  21.1 160.3 %copy-start.3 = (s32[256]{0:T(256)S(1)}, s32[256]{0:T(256)}, u32[]{:S(2)}) copy-start(s32[256]{0:T(256)} %constant.75.clone) | copy-start | bytes 3076
  21.1 160.3 %copy-start.2 = (pred[2,256]{1,0:T(4,128)(4,1)S(1)}, pred[2,256]{1,0:T(4,128)(4,1)}, u32[]{:S(2)}) copy-start(pred[2,256]{1,0:T(4,128)(4,1)} %constant.76.clone) | copy-start | bytes 1540
  148.9 63.0 %all-to-all-start.1 = ((s16[16,384,128]{2,1,0:T(8,128)(2,1)}), s16[16,384,128]{2,1,0:T(8,128)(2,1)S(1)}, u32[]{:S(2)}, u32[]{:S(2)}) async-start(s16[16,384,128]{2,1,0:T(8,128)(2,1)} %get-tuple-element.17), calls=%async_computation.1 | async-start | bytes 3145728 | tf_op jit(solution)/shard_map/all_to_all | solution.py:475
  181.4 5.0 %copy-start.1 = (s32[256]{0:T(256)}, s32[256]{0:T(256)S(1)}, u32[]{:S(2)}) copy-start(s32[256]{0:T(256)S(1)} %sub.7.meta) | copy-start | bytes 3076
  211.9 1.1 copy-start

commit v12 on v11

--- a/solution.py
+++ b/solution.py
@@ -18,12 +18,11 @@
 CODE_SHIFT = 32768
 VMEM_BYTES = 60 * 1024 * 1024
 STEP_TILES = 16
-PARTS = (0.0, 13 / 16, 1.0)
+PARTS = (0.0, 12 / 16, 1.0)
 LOG_STEPS = 1800.0
 LOG_MIDDLE = -3.0
 CACHED_BLOCKS = 64
 QUAD = 4
-PAIR = 2
 EIGHT = 8
 BATCH = 8
 NT = (((1,), (1,)), ((), ()))
@@ -62,41 +61,40 @@
     parts = len(cuts) - 1
     (*told_refs, x_hbm), refs = refs[:5], refs[5:]
     outs = refs[:parts]
-    x, coded, square, sums, words, notes, held, tile_at, sems, x_sems = refs[parts:]
+    x, coded, square, sums, words, notes, held, sems, x_sems = refs[parts:]
     tiles = x.shape[0]
     devices = held.shape[0]
     blocks = square.shape[0]
     step = math.gcd(STEP_TILES, tiles)
-    reads = [
-        pltpu.make_async_copy(x_hbm.at[pl.ds(i, step)], x.at[pl.ds(i, step)], x_sems.at[i // step])
-        for i in range(0, tiles, step)
-    ]
-    for read in reads:
-        read.start()
+
+    def read(c):
+        some = pl.ds(c * step, step)
+        return pltpu.make_async_copy(x_hbm.at[some], x.at[some], x_sems.at[c])
 
     def clear(d, carry):
         held[d] = 0
         return carry
 
-    def list_tile(t, carry):
-        owner, rank = owner_ref[t], rank_ref[t]
-        tile_at[owner * cuts[-1] + rank] = t
-        held[owner] = jnp.maximum(held[owner], rank + 1)
+    for c in range(tiles // step):
+        read(c).start()
+    lax.fori_loop(0, devices, clear, 0)
+    square[...] = jnp.zeros_like(square)
+
+    def some_tiles(i, carry):
+        pl.when(i % (step // QUAD) == 0)(lambda: read(i // (step // QUAD)).wait())
+        for j in range(QUAD):
+            t = i * QUAD + j
+            some = x[t]
+            root = some * lax.rsqrt(some)
+            code = (root * CODE_TOP + 0.5).astype(jnp.int32) - CODE_SHIFT
+            owner, rank = owner_ref[t], rank_ref[t]
+            at = pl.ds(pl.multiple_of((owner * cuts[-1] + rank) * LANES, LANES), LANES)
+            coded[at, :] = code.astype(jnp.int16)
+            square[row_ref[t]] += some * some
+            held[owner] = jnp.maximum(held[owner], rank + 1)
         return carry
 
-    lax.fori_loop(0, devices, clear, 0)
-    lax.fori_loop(0, tiles, list_tile, 0)
-    square[...] = jnp.zeros_like(square)
-    for i, read in enumerate(reads):
-        read.wait()
-
-        def some_squares(c, carry, first=i * step):
-            for j in range(QUAD):
-                t = first + c * QUAD + j
-                square[row_ref[t]] += x[t] * x[t]
-            return carry
-
-        lax.fori_loop(0, step // QUAD, some_squares, 0)
+    lax.fori_loop(0, tiles // QUAD, some_tiles, 0)
 
     def slots(q, d):
         some = pl.ds((d * cuts[-1] + cuts[q]) * LANES, (cuts[q + 1] - cuts[q]) * LANES)
@@ -107,25 +105,15 @@
         into = outs[0].at[d, pl.ds((cuts[1] - cuts[0]) * LANES, notes.shape[0])]
         return pltpu.make_async_copy(notes, into, sems.at[parts, d])
 
-    def one_owner(d, carry):
-        count = held[d]
-
-        def some_codes(c, carry):
-            for j in range(PAIR):
-                slot = d * cuts[-1] + jnp.minimum(c * PAIR + j, count - 1)
-                some = x[tile_at[slot]]
-                root = some * lax.rsqrt(some)
-                code = (root * CODE_TOP + 0.5).astype(jnp.int32) - CODE_SHIFT
-                at = pl.ds(pl.multiple_of(slot * LANES, LANES), LANES)
-                coded[at, :] = code.astype(jnp.int16)
+    def each(what):
+        def one(d, carry):
+            for q in range(parts):
+                pl.when(held[d] > cuts[q])(lambda q=q: what(slots(q, d)))
             return carry
 
-        lax.fori_loop(0, (count + PAIR - 1) // PAIR, some_codes, 0)
-        for q in range(parts):
-            pl.when(count > cuts[q])(lambda q=q: slots(q, d).start())
-        return carry
-
-    lax.fori_loop(0, devices, one_owner, 0)
+        lax.fori_loop(0, devices, one, 0)
+
+    each(lambda copy: copy.start())
     sums[...] = jnp.zeros_like(sums)
     block_sums(square, sums, blocks)
     total = sums[...]
@@ -141,14 +129,9 @@
         at += told.shape[0]
     notes[...] = words[...].astype(jnp.int16)
 
-    def finish(d, carry):
-        for q in range(parts):
-            pl.when(held[d] > cuts[q])(lambda q=q: slots(q, d).wait())
-        return carry
-
     for d in range(devices):
         note(d).start()
-    lax.fori_loop(0, devices, finish, 0)
+    each(lambda copy: copy.wait())
     for d in range(devices):
         note(d).wait()
 
@@ -172,7 +155,6 @@
             pltpu.VMEM((noted, LANES), jnp.int32),
             pltpu.VMEM((noted, LANES), jnp.int16),
             pltpu.SMEM((devices,), jnp.int32),
-            pltpu.SMEM((devices * cuts[-1],), jnp.int32),
             pltpu.SemaphoreType.DMA((len(rows) + 1, devices)),
             pltpu.SemaphoreType.DMA((tiles,)),
         ],
@@ -436,13 +418,17 @@
         similarity[b : b + 1, :] = total[:, b * LANES : (b + 1) * LANES] * found
     for g in range(groups):
         reads[g].wait()
-        for sub in range(g * width, (g + 1) * width):
+
+        def one_sub(sub, carry):
+            to = pl.ds(pl.multiple_of(sub * LANES, LANES), LANES)
             for i, column in enumerate(columns):
                 half, row = divmod(i * LANES, HALF)
-                at = (2 * sub + half) * LANES
-                some = sums[row : row + LANES, at : at + LANES]
-                done = (some * column * root).astype(jnp.bfloat16)
-                out[i * LANES : (i + 1) * LANES, sub * LANES : (sub + 1) * LANES] = done
+                at = pl.ds(pl.multiple_of((2 * sub + half) * LANES, LANES), LANES)
+                done = sums[row : row + LANES, at] * column * root
+                out[i * LANES : (i + 1) * LANES, to] = done.astype(jnp.bfloat16)
+            return carry
+
+        lax.fori_loop(g * width, (g + 1) * width, one_sub, 0)
         writes[g].start()
     for write in writes:
         write.wait()

time: 248 us -> 249 us (level); the launches traced: 248 us -> 246 us
  blocking collectives: 22.4 us -> 168 us
  waiting for transfers between devices: 129 us -> 5.64 us
  starting transfers between devices: 38.4 us -> 4.35 us
  Pallas kernels: 47.5 us -> 57 us
    all_to_all x1 -> x2, blocking collectives: 22.4 us -> 168 us  [exchange(): return lax.all_to_all(x, 'dp', split_axis=0, concat_axis=0, tiled=True)]
    all_to_all x2 -> x1, waiting for transfers between devices: 129 us -> 5.64 us  [exchange(): return lax.all_to_all(x, 'dp', split_axis=0, concat_axis=0, tiled=True)]
    all_to_all x2 -> x1, starting transfers between devices: 38.4 us -> 4.35 us  [exchange(): return lax.all_to_all(x, 'dp', split_axis=0, concat_axis=0, tiled=True)]
    pallas_call x2, Pallas kernels: 31.3 us -> 42.8 us  [stage(): pl.pallas_call(functools.partial(stage_kernel, q, [devices * cut for cut...]
  transfers between devices with their start and end apart: 2 -> 1, of which waited for: 2 -> 1; matrix products, arithmetic and copies ran while one was open for 3% -> 3% of each run, Pallas kernels for 9% -> 11%
where the time goes in v12:
time: 249 us; the launch traced here: 246 us
  blocking collectives  168 us (67%)
  Pallas kernels  57 us (23%)
  other arithmetic  8.74 us (4%)
  waiting for transfers between devices  5.64 us (2%)
  starting transfers between devices  4.35 us (2%)
    all_to_all x2, blocking collectives, exchange(): return lax.all_to_all(x, 'dp', split_axis=0, concat_axis=0, tiled=True)  168 us
    pallas_call x2, Pallas kernels, stage(): pl.pallas_call(functools.partial(stage_kernel, q, [devices * cut for cut...  42.8 us
    pallas_call x1, Pallas kernels, pack(): pl.pallas_call(functools.partial(pack_kernel, cuts), in_specs=[SMEM] * 3...  9.56 us
    all_to_all x1, waiting for transfers between devices, exchange(): return lax.all_to_all(x, 'dp', split_axis=0, concat_axis=0, tiled=True)  5.64 us
  transfers between devices with their start and end apart: 1, of which 1 were waited for; matrix products, arithmetic and copies ran while one was open for 3% of the time, Pallas kernels for 11%

profile of v12, /device:TPU:0, one launch (start us, length us, event | category | flops | bytes accessed | tf_op | source)
XLA Modules:
  0.0 245.8 jit_solution(5858253305549572407)
XLA Ops:
  0.6 1.4 convert_reduce_fusion.3.rank_ref
  2.1 9.6 %pack.1 = (s16[16,1584,128]{2,1,0:T(8,128)(2,1)}, s16[16,512,128]{2,1,0:T(8,128)(2,1)}) custom-call(s32[128]{0:T(128)} %bitcast.15, s32[128]{0:T(128)} %convert_reduce_fusion.3.rank_ref, s32[128]{0:T(128)} %row_ref.1, s32[2,128]{1,0:T(2,128)} %bitcast.18, s32[1,128]{1,0:T(1,128)} %bitcast.16, s32[1,128]{1,0:T(1,128)} %bitcast.20, s32[1,128]{1,0:T(1,128)} %bitcast.17, ...), custom_call_target="tpu_custom_call" | custom-call | flops 16777216 | bytes 12582912 | tf_op jit(solution)/shard_map/pack/pallas_call | solution.py:145
  11.6 150.2 %all_to_all.15.x_hbm = s16[16,1584,128]{2,1,0:T(8,128)(2,1)} all-to-all(s16[16,1584,128]{2,1,0:T(8,128)(2,1)} %get-tuple-element.15), channel_id=1, replica_groups=mesh['groups'=2,'dp'=16] {'dp'}, dimensions={0} | all-to-all | bytes 12976128 | tf_op jit(solution)/shard_map/all_to_all | solution.py:461
  161.8 4.3 %all-to-all-start.1 = ((s16[16,512,128]{2,1,0:T(8,128)(2,1)}), s16[16,512,128]{2,1,0:T(8,128)(2,1)S(1)}, u32[]{:S(2)}, u32[]{:S(2)}) async-start(s16[16,512,128]{2,1,0:T(8,128)(2,1)} %get-tuple-element.17), calls=%async_computation.1 | async-start | bytes 4194304 | tf_op jit(solution)/shard_map/all_to_all | solution.py:461
  166.2 1.0 slice_convert_fusion
  167.3 1.0 convert_reduce_fusion
  168.4 0.3 select_reduce_fusion.3
  168.7 0.1 sub.7.meta
  168.9 0.0 copy-done.2
  168.9 0.6 select_reduce_fusion.4.done
  169.5 0.7 convert_reduce_fusion.5.score_bound
  170.2 0.7 convert_reduce_fusion.4.fold_bound
  170.8 0.3 convert_reduce_fusion.1
  171.1 0.7 select_reduce_fusion.1.score_order
  171.8 0.7 select_reduce_fusion.2.fold_order
  172.5 0.1 select_reduce_fusion
  172.6 0.6 fusion.6.mods_in
  173.2 0.6 negate_select_fusion.signed_in
  173.8 27.9 %stage.2 = (f32[32,128]{1,0:T(8,128)}, f32[256,4096]{1,0:T(8,128)}, f32[256,256]{1,0:T(8,128)}, f32[33,128,128]{2,1,0:T(8,128)}, bf16[33,128,256]{2,1,0:T(8,128)(2,1)}, /*index=5*/bf16[192,128,128]{2,1,0:T(8,128)(2,1)}) custom-call(s32[256]{0:T(256)} %select_reduce_fusion.2.fold_order, s32[35]{0:T(128)} %convert_reduce_fusion.4.fold_bound, ...), custom_call_target="tpu_custom_call" | custom-call | flops 12884901888 | bytes 20971520 | tf_op jit(solution)/shard_map/stage/pallas_call | solution.py:364
  201.7 5.6 %all-to-all-done.1.x_hbm = s16[16,512,128]{2,1,0:T(8,128)(2,1)S(1)} async-done(((s16[16,512,128]{2,1,0:T(8,128)(2,1)}), s16[16,512,128]{2,1,0:T(8,128)(2,1)S(1)}, u32[]{:S(2)}, u32[]{:S(2)}) %all-to-all-start.1) | async-done | bytes 2097184 | tf_op jit(solution)/shard_map/all_to_all | solution.py:461
  207.3 1.3 copy-done
  208.6 15.0 %stage.3 = (f32[16,1,768]{2,1,0:T(1,128)}, f32[256,4096]{1,0:T(8,128)}) custom-call(s32[256]{0:T(256)} %select_reduce_fusion.2.fold_order, s32[35]{0:T(128)} %convert_reduce_fusion.4.fold_bound, s32[256]{0:T(256)} %select_reduce_fusion.1.score_order, s32[17]{0:T(128)} %convert_reduce_fusion.5.score_bound, ...), custom_call_target="tpu_custom_call", output_to_operand_aliasing={{1}: (12, {})} | custom-call | flops 4294967296 | bytes 12582912 | tf_op jit(solution)/shard_map/stage/pallas_call | solution.py:364
  223.6 17.5 %all_to_all.16.got_ref = f32[16,1,768]{2,1,0:T(1,128)} all-to-all(f32[16,1,768]{2,1,0:T(1,128)} %get-tuple-element.24), channel_id=1, replica_groups=mesh['groups'=2,'dp'=16] {'dp'}, dimensions={0} | all-to-all | bytes 98304 | tf_op jit(solution)/shard_map/all_to_all | solution.py:461
  241.1 4.6 %close.1 = (bf16[512,2048]{1,0:T(8,128)(2,1)}, f32[2,128]{1,0:T(2,128)}) custom-call(s32[2,128]{1,0:T(2,128)} %bitcast.19, f32[16,1,768]{2,1,0:T(1,128)} %all_to_all.16.got_ref, f32[256,4096]{1,0:T(8,128)} %get-tuple-element.25.sums_hbm), custom_call_target="tpu_custom_call" | custom-call | flops 2097152 | bytes 6291456 | tf_op jit(solution)/shard_map/close/pallas_call | solution.py:441
  (15 shorter events, 0.1 us)
Async XLA Ops:
  161.8 7.0 %copy-start.3 = (s32[256]{0:T(256)S(1)}, s32[256]{0:T(256)}, u32[]{:S(2)}) copy-start(s32[256]{0:T(256)} %constant.75.clone) | copy-start | bytes 3076
  161.8 7.0 %copy-start.2 = (pred[2,256]{1,0:T(4,128)(4,1)S(1)}, pred[2,256]{1,0:T(4,128)(4,1)}, u32[]{:S(2)}) copy-start(pred[2,256]{1,0:T(4,128)(4,1)} %constant.76.clone) | copy-start | bytes 1540
  161.8 45.5 %all-to-all-start.1 = ((s16[16,512,128]{2,1,0:T(8,128)(2,1)}), s16[16,512,128]{2,1,0:T(8,128)(2,1)S(1)}, u32[]{:S(2)}, u32[]{:S(2)}) async-start(s16[16,512,128]{2,1,0:T(8,128)(2,1)} %get-tuple-element.17), calls=%async_computation.1 | async-start | bytes 4194304 | tf_op jit(solution)/shard_map/all_to_all | solution.py:461
  168.8 4.9 %copy-start.1 = (s32[256]{0:T(256)}, s32[256]{0:T(256)S(1)}, u32[]{:S(2)}) copy-start(s32[256]{0:T(256)S(1)} %sub.7.meta) | copy-start | bytes 3076
  207.3 1.3 copy-start

commit v13 on v12

--- a/solution.py
+++ b/solution.py
@@ -18,7 +18,7 @@
 CODE_SHIFT = 32768
 VMEM_BYTES = 60 * 1024 * 1024
 STEP_TILES = 16
-PARTS = (0.0, 12 / 16, 1.0)
+PARTS = (0.0, 13 / 16, 1.0)
 LOG_STEPS = 1800.0
 LOG_MIDDLE = -3.0
 CACHED_BLOCKS = 64
@@ -224,7 +224,9 @@
     for held, given, empty in ((mods, mods_in, -1.0), (signed, signed_in, 0.0)):
         held[:none, :] = given[...]
         held[none : none + 1, :] = jnp.full((1, LANES), empty, jnp.float32)
-    cluster = lax.broadcasted_iota(jnp.int32, (HALF, LANES), 0)
+    cluster = lax.broadcasted_iota(jnp.int32, (HALF, LANES), 0).astype(jnp.float32)
+    cluster = cluster.astype(jnp.bfloat16).reshape(HALF // 16, 16, LANES)
+    one, zero = jnp.ones((), jnp.bfloat16), jnp.zeros((), jnp.bfloat16)
     lane = lax.broadcasted_iota(jnp.int32, (LANES, LANES), 1)
 
     def column(ref, row):
@@ -272,12 +274,15 @@
                 raw = x[source, pl.ds(pl.multiple_of(slot * LANES, LANES), LANES), :]
                 root = raw.astype(jnp.int32).astype(jnp.float32) + float(CODE_SHIFT)
                 scale = spread[row]
-                tile = root * root * jnp.abs(scale)
+                square = root * root
+                tile = square * jnp.abs(scale)
+                lower = square * jnp.maximum(scale, 0.0)
                 tiles[spot] = tile.astype(jnp.bfloat16)
-                halves = [jnp.where(scale > 0.0, tile, 0.0), jnp.where(scale < 0.0, tile, 0.0)]
-                folded.append(jnp.concatenate(halves, axis=1).astype(jnp.bfloat16))
-                own = mods[pl.ds(jnp.where(held, row, none), 1), :].astype(jnp.int32)
-                picks.append(jnp.where(cluster == own, 1.0, 0.0).astype(jnp.bfloat16))
+                halves = [lower.astype(jnp.bfloat16), (tile - lower).astype(jnp.bfloat16)]
+                folded.append(jnp.concatenate(halves, axis=1))
+                own = jnp.broadcast_to(mods[pl.ds(jnp.where(held, row, none), 1), :], (16, LANES))
+                own = jnp.where(cluster == own.astype(jnp.bfloat16)[None], one, zero)
+                picks.append(own.reshape(HALF, LANES))
             pick = jnp.concatenate(picks, axis=1)
             sums[columns(sub)] += jnp.dot(
                 pick, jnp.concatenate(folded, axis=0), preferred_element_type=jnp.float32

time: 249 us -> 247 us (level); the launches traced: 246 us -> 247 us
  blocking collectives: 168 us -> 23.2 us
  waiting for transfers between devices: 5.64 us -> 133 us
  starting transfers between devices: 4.35 us -> 38.4 us
  Pallas kernels: 57 us -> 41.6 us
    all_to_all x2 -> x1, blocking collectives: 168 us -> 23.2 us  [exchange(): return lax.all_to_all(x, 'dp', split_axis=0, concat_axis=0, tiled=True)]
    all_to_all x1 -> x2, waiting for transfers between devices: 5.64 us -> 133 us  [exchange(): return lax.all_to_all(x, 'dp', split_axis=0, concat_axis=0, tiled=True)]
    all_to_all x1 -> x2, starting transfers between devices: 4.35 us -> 38.4 us  [exchange(): return lax.all_to_all(x, 'dp', split_axis=0, concat_axis=0, tiled=True)]
    pallas_call x2, Pallas kernels: 42.8 us -> 27.3 us  [stage(): pl.pallas_call(functools.partial(stage_kernel, q, [devices * cut for cut...]
  transfers between devices with their start and end apart: 1 -> 2, of which waited for: 1 -> 2; matrix products, arithmetic and copies ran while one was open for 3% -> 3% of each run, Pallas kernels for 11% -> 8%
where the time goes in v13:
time: 247 us
  waiting for transfers between devices  133 us (54%)
  Pallas kernels  41.6 us (17%)
  starting transfers between devices  38.4 us (16%)
  blocking collectives  23.2 us (9%)
  other arithmetic  8.79 us (4%)
    all_to_all x2, waiting for transfers between devices, exchange(): return lax.all_to_all(x, 'dp', split_axis=0, concat_axis=0, tiled=True)  133 us
    all_to_all x2, starting transfers between devices, exchange(): return lax.all_to_all(x, 'dp', split_axis=0, concat_axis=0, tiled=True)  38.4 us
    pallas_call x2, Pallas kernels, stage(): pl.pallas_call(functools.partial(stage_kernel, q, [devices * cut for cut...  27.3 us
    all_to_all x1, blocking collectives, exchange(): return lax.all_to_all(x, 'dp', split_axis=0, concat_axis=0, tiled=True)  23.2 us
    pallas_call x1, Pallas kernels, pack(): pl.pallas_call(functools.partial(pack_kernel, cuts), in_specs=[SMEM] * 3...  9.68 us
  transfers between devices with their start and end apart: 2, of which 2 were waited for; matrix products, arithmetic and copies ran while one was open for 3% of the time, Pallas kernels for 8%

profile of v13, /device:TPU:0, one launch (start us, length us, event | category | flops | bytes accessed | tf_op | source)
XLA Modules:
  0.0 246.9 jit_solution(15320808876519517976)
XLA Ops:
  0.6 1.4 convert_reduce_fusion.3.rank_ref
  2.1 9.7 %pack.1 = (s16[16,1712,128]{2,1,0:T(8,128)(2,1)}, s16[16,384,128]{2,1,0:T(8,128)(2,1)}) custom-call(s32[128]{0:T(128)} %bitcast.15, s32[128]{0:T(128)} %convert_reduce_fusion.3.rank_ref, s32[128]{0:T(128)} %row_ref.1, s32[2,128]{1,0:T(2,128)} %bitcast.18, s32[1,128]{1,0:T(1,128)} %bitcast.16, s32[1,128]{1,0:T(1,128)} %bitcast.20, s32[1,128]{1,0:T(1,128)} %bitcast.17, ...), custom_call_target="tpu_custom_call" | custom-call | flops 16777216 | bytes 12582912 | tf_op jit(solution)/shard_map/pack/pallas_call | solution.py:145
  11.7 7.4 %all-to-all-start = ((s16[16,1712,128]{2,1,0:T(8,128)(2,1)}), s16[16,1712,128]{2,1,0:T(8,128)(2,1)}, u32[]{:S(2)}, u32[]{:S(2)}) async-start(s16[16,1712,128]{2,1,0:T(8,128)(2,1)} %get-tuple-element.15), calls=%async_computation | async-start | bytes 14024704 | tf_op jit(solution)/shard_map/all_to_all | solution.py:466
  19.2 126.7 %all-to-all-done.x_hbm = s16[16,1712,128]{2,1,0:T(8,128)(2,1)} async-done(((s16[16,1712,128]{2,1,0:T(8,128)(2,1)}), s16[16,1712,128]{2,1,0:T(8,128)(2,1)}, u32[]{:S(2)}, u32[]{:S(2)}) %all-to-all-start) | async-done | bytes 7012384 | tf_op jit(solution)/shard_map/all_to_all | solution.py:466
  145.9 1.0 slice_convert_fusion
  147.0 31.0 %all-to-all-start.1 = ((s16[16,384,128]{2,1,0:T(8,128)(2,1)}), s16[16,384,128]{2,1,0:T(8,128)(2,1)S(1)}, u32[]{:S(2)}, u32[]{:S(2)}) async-start(s16[16,384,128]{2,1,0:T(8,128)(2,1)} %get-tuple-element.17), calls=%async_computation.1 | async-start | bytes 3145728 | tf_op jit(solution)/shard_map/all_to_all | solution.py:466
  178.0 1.0 convert_reduce_fusion
  179.1 0.3 select_reduce_fusion.3
  179.4 0.1 sub.7.meta
  179.5 0.6 select_reduce_fusion.4.done
  180.2 0.7 convert_reduce_fusion.5.score_bound
  180.8 0.7 convert_reduce_fusion.4.fold_bound
  181.5 0.3 convert_reduce_fusion.1
  181.8 0.7 select_reduce_fusion.1.score_order
  182.5 0.7 select_reduce_fusion.2.fold_order
  183.2 0.1 select_reduce_fusion
  183.3 0.6 fusion.6.mods_in
  183.9 0.6 negate_select_fusion.signed_in
  184.5 19.4 %stage.2 = (f32[32,128]{1,0:T(8,128)}, f32[256,4096]{1,0:T(8,128)}, f32[256,256]{1,0:T(8,128)}, f32[33,128,128]{2,1,0:T(8,128)}, bf16[33,128,256]{2,1,0:T(8,128)(2,1)}, /*index=5*/bf16[208,128,128]{2,1,0:T(8,128)(2,1)}) custom-call(s32[256]{0:T(256)} %select_reduce_fusion.2.fold_order, s32[35]{0:T(128)} %convert_reduce_fusion.4.fold_bound, ...), custom_call_target="tpu_custom_call" | custom-call | flops 13958643712 | bytes 22020096 | tf_op jit(solution)/shard_map/stage/pallas_call | solution.py:369
  203.9 6.1 %all-to-all-done.1.x_hbm = s16[16,384,128]{2,1,0:T(8,128)(2,1)S(1)} async-done(((s16[16,384,128]{2,1,0:T(8,128)(2,1)}), s16[16,384,128]{2,1,0:T(8,128)(2,1)S(1)}, u32[]{:S(2)}, u32[]{:S(2)}) %all-to-all-start.1) | async-done | bytes 1572896 | tf_op jit(solution)/shard_map/all_to_all | solution.py:466
  209.9 1.1 copy-done
  211.1 7.9 %stage.3 = (f32[16,1,768]{2,1,0:T(1,128)}, f32[256,4096]{1,0:T(8,128)}) custom-call(s32[256]{0:T(256)} %select_reduce_fusion.2.fold_order, s32[35]{0:T(128)} %convert_reduce_fusion.4.fold_bound, s32[256]{0:T(256)} %select_reduce_fusion.1.score_order, s32[17]{0:T(128)} %convert_reduce_fusion.5.score_bound, ...), custom_call_target="tpu_custom_call", output_to_operand_aliasing={{1}: (12, {})} | custom-call | flops 3221225472 | bytes 11534336 | tf_op jit(solution)/shard_map/stage/pallas_call | solution.py:369
  219.0 23.2 %all_to_all.15.got_ref = f32[16,1,768]{2,1,0:T(1,128)} all-to-all(f32[16,1,768]{2,1,0:T(1,128)} %get-tuple-element.24), channel_id=1, replica_groups=mesh['groups'=2,'dp'=16] {'dp'}, dimensions={0} | all-to-all | bytes 98304 | tf_op jit(solution)/shard_map/all_to_all | solution.py:466
  242.3 4.6 %close.1 = (bf16[512,2048]{1,0:T(8,128)(2,1)}, f32[2,128]{1,0:T(2,128)}) custom-call(s32[2,128]{1,0:T(2,128)} %bitcast.19, f32[16,1,768]{2,1,0:T(1,128)} %all_to_all.15.got_ref, f32[256,4096]{1,0:T(8,128)} %get-tuple-element.25.sums_hbm), custom_call_target="tpu_custom_call" | custom-call | flops 2097152 | bytes 6291456 | tf_op jit(solution)/shard_map/close/pallas_call | solution.py:446
  (16 shorter events, 0.1 us)
Async XLA Ops:
  11.7 134.2 %all-to-all-start = ((s16[16,1712,128]{2,1,0:T(8,128)(2,1)}), s16[16,1712,128]{2,1,0:T(8,128)(2,1)}, u32[]{:S(2)}, u32[]{:S(2)}) async-start(s16[16,1712,128]{2,1,0:T(8,128)(2,1)} %get-tuple-element.15), calls=%async_computation | async-start | bytes 14024704 | tf_op jit(solution)/shard_map/all_to_all | solution.py:466
  19.2 160.3 %copy-start.3 = (s32[256]{0:T(256)S(1)}, s32[256]{0:T(256)}, u32[]{:S(2)}) copy-start(s32[256]{0:T(256)} %constant.75.clone) | copy-start | bytes 3076
  19.2 160.3 %copy-start.2 = (pred[2,256]{1,0:T(4,128)(4,1)S(1)}, pred[2,256]{1,0:T(4,128)(4,1)}, u32[]{:S(2)}) copy-start(pred[2,256]{1,0:T(4,128)(4,1)} %constant.76.clone) | copy-start | bytes 1540
  147.0 63.0 %all-to-all-start.1 = ((s16[16,384,128]{2,1,0:T(8,128)(2,1)}), s16[16,384,128]{2,1,0:T(8,128)(2,1)S(1)}, u32[]{:S(2)}, u32[]{:S(2)}) async-start(s16[16,384,128]{2,1,0:T(8,128)(2,1)} %get-tuple-element.17), calls=%async_computation.1 | async-start | bytes 3145728 | tf_op jit(solution)/shard_map/all_to_all | solution.py:466
  179.5 5.0 %copy-start.1 = (s32[256]{0:T(256)}, s32[256]{0:T(256)S(1)}, u32[]{:S(2)}) copy-start(s32[256]{0:T(256)S(1)} %sub.7.meta) | copy-start | bytes 3076
  209.9 1.1 copy-start

commit v14 on v13

--- a/solution.py
+++ b/solution.py
@@ -24,6 +24,8 @@
 CACHED_BLOCKS = 64
 QUAD = 4
 EIGHT = 8
+ROW_SHIFT, SOURCE_SHIFT = 16, 8
+PLACE_MASK, SOURCE_MASK, SLOT_MASK = 0xFFFF, 0xFF, 0xFF
 BATCH = 8
 NT = (((1,), (1,)), ((), ()))
 SMEM = pl.BlockSpec(memory_space=pltpu.SMEM)
@@ -168,8 +170,8 @@
     )(owner, rank, tile_row, *told, tile_values)
 
 
-def stage_kernel(q, bases, last, cached, fold_order, fold_bound, score_order, score_bound, meta,
-                 place, done, mods_in, signed_in, x_hbm, *refs):
+def stage_kernel(q, bases, last, cached, fold_list, fold_bound, score_list, score_bound, done,
+                 mods_in, signed_in, x_hbm, *refs):
     base = bases[q]
     earlier, refs = refs[:q], refs[q:]
     before, sums_in, squares_in, *made_in = refs[:5] if q else (None,) * 5
@@ -251,14 +253,9 @@
     for copy in needed:
         copy.wait()
 
-    def eight(order, start, end, p):
-        rows, spots = [], []
-        for j in range(EIGHT):
-            at = start + EIGHT * p + j
-            slot = order[jnp.where(at < end, at, start)]
-            rows.append((meta[slot] // TB_OWN, at < end))
-            spots.append(place[slot])
-        return rows, spots
+    def eight(entries, start, end, p):
+        at = [start + EIGHT * p + j for j in range(EIGHT)]
+        return [(entries[jnp.where(spot < end, spot, start)], spot < end) for spot in at]
 
     def fold_sub(sub):
         start = fold_bound[q * (TB_OWN + 1) + sub]
@@ -267,10 +264,11 @@
             sums_read(sub).wait()
 
         def one_eight(p, carry):
-            rows, spots = eight(fold_order, start, end, p)
             folded, picks = [], []
-            for (row, held), spot in zip(rows, spots):
-                source, slot = (spot - base) // width, (spot - base) % width
+            for entry, held in eight(fold_list, start, end, p):
+                row = entry >> ROW_SHIFT
+                source, slot = (entry >> SOURCE_SHIFT) & SOURCE_MASK, entry & SLOT_MASK
+                spot = base + source * width + slot
                 raw = x[source, pl.ds(pl.multiple_of(slot * LANES, LANES), LANES), :]
                 root = raw.astype(jnp.int32).astype(jnp.float32) + float(CODE_SHIFT)
                 scale = spread[row]
@@ -311,8 +309,9 @@
         squares[...] += some * some
 
         def one_eight(p, carry):
-            rows, spots = eight(score_order, start, end, p)
-            rows = [jnp.where(held, row, none) for row, held in rows]
+            listed = eight(score_list, start, end, p)
+            rows = [jnp.where(held, entry >> ROW_SHIFT, none) for entry, held in listed]
+            spots = [entry & PLACE_MASK for entry, held in listed]
             hots = [hot[row] if cached else one_hot(row) for row in rows]
             chosen = jnp.dot(
                 jnp.concatenate(hots, axis=0), narrow[...], preferred_element_type=jnp.float32
@@ -470,17 +469,17 @@
     return lax.optimization_barrier((value, *others))[0]
 
 
-def sorted_slots(key, top):
+def sorted_slots(key, top, entries):
     slots = jnp.arange(key.shape[0], dtype=jnp.int32)
     ahead = (key[None, :] < key[:, None]) | (
         (key[None, :] == key[:, None]) & (slots[None, :] < slots[:, None])
     )
     position = jnp.sum(ahead.astype(jnp.int32), axis=1)
     here = position[None, :] == slots[:, None]
-    order = jnp.sum(jnp.where(here, slots[None, :], 0), axis=1)
+    listed = jnp.sum(jnp.where(here, entries[None, :], 0), axis=1)
     levels = jnp.arange(top + 1, dtype=jnp.int32)
     bounds = jnp.sum((key[None, :] < levels[:, None]).astype(jnp.int32), axis=1)
-    return order, bounds
+    return listed, bounds
 
 
 def ranks(group, sub):
@@ -524,13 +523,15 @@
     low, high = np.array(cuts)[slot_part], np.array(cuts)[slot_part + 1]
     place = devices * low + np.arange(devices * cap) // cap * (high - low) + slot_rank - low
     fold_key = jnp.asarray(slot_part * (TB_OWN + 1), jnp.int32) + sub
-    fold_order, fold_bounds = sorted_slots(fold_key, parts * (TB_OWN + 1))
-    score_order, score_bounds = sorted_slots(sub, TB_OWN)
+    row = (meta // TB_OWN) << ROW_SHIFT
+    from_slot = (np.arange(devices * cap) // cap << SOURCE_SHIFT) + slot_rank - low
+    fold_list, fold_bounds = sorted_slots(
+        fold_key, parts * (TB_OWN + 1), row + jnp.asarray(from_slot, jnp.int32)
+    )
+    score_list, score_bounds = sorted_slots(sub, TB_OWN, row + jnp.asarray(place, jnp.int32))
     left = np.arange(parts)[:, None] < slot_part[None, :]
     done = jnp.min(jnp.where(left, sub[None, :], TB_OWN), axis=1)
-    scalars = [
-        fold_order, fold_bounds, score_order, score_bounds, meta, jnp.asarray(place, jnp.int32), done
-    ]
+    scalars = [fold_list, fold_bounds, score_list, score_bounds, done]
 
     scale = lax.rsqrt(row_sq + EPSILON) * (1.0 / CODE_TOP**2)
     signed = jnp.where(all_labels < HALF, scale, -scale)

time: 247 us -> 246 us (level)
  blocking collectives: 23.2 us -> 20 us
    all_to_all x1, blocking collectives: 23.2 us -> 20 us  [exchange(): return lax.all_to_all(x, 'dp', split_axis=0, concat_axis=0, tiled=True)]
where the time goes in v14:
time: 246 us; the launch traced here: 244 us
  waiting for transfers between devices  133 us (54%)
  Pallas kernels  41.3 us (17%)
  starting transfers between devices  38.4 us (16%)
  blocking collectives  20 us (8%)
  other arithmetic  8.76 us (4%)
    all_to_all x2, waiting for transfers between devices, exchange(): return lax.all_to_all(x, 'dp', split_axis=0, concat_axis=0, tiled=True)  133 us
    all_to_all x2, starting transfers between devices, exchange(): return lax.all_to_all(x, 'dp', split_axis=0, concat_axis=0, tiled=True)  38.4 us
    pallas_call x2, Pallas kernels, stage(): pl.pallas_call(functools.partial(stage_kernel, q, [devices * cut for cut...  27 us
    all_to_all x1, blocking collectives, exchange(): return lax.all_to_all(x, 'dp', split_axis=0, concat_axis=0, tiled=True)  20 us
    pallas_call x1, Pallas kernels, pack(): pl.pallas_call(functools.partial(pack_kernel, cuts), in_specs=[SMEM] * 3...  9.65 us
  transfers between devices with their start and end apart: 2, of which 2 were waited for; matrix products, arithmetic and copies ran while one was open for 3% of the time, Pallas kernels for 8%

profile of v14, /device:TPU:0, one launch (start us, length us, event | category | flops | bytes accessed | tf_op | source)
XLA Modules:
  0.0 243.7 jit_solution(5292968709446352202)
XLA Ops:
  0.6 1.4 convert_reduce_fusion.3.rank_ref
  2.1 9.6 %pack.1 = (s16[16,1712,128]{2,1,0:T(8,128)(2,1)}, s16[16,384,128]{2,1,0:T(8,128)(2,1)}) custom-call(s32[128]{0:T(128)} %bitcast.15, s32[128]{0:T(128)} %convert_reduce_fusion.3.rank_ref, s32[128]{0:T(128)} %row_ref.1, s32[2,128]{1,0:T(2,128)} %bitcast.18, s32[1,128]{1,0:T(1,128)} %bitcast.16, s32[1,128]{1,0:T(1,128)} %bitcast.20, s32[1,128]{1,0:T(1,128)} %bitcast.17, ...), custom_call_target="tpu_custom_call" | custom-call | flops 16777216 | bytes 12582912 | tf_op jit(solution)/shard_map/pack/pallas_call | solution.py:147
  11.7 7.4 %all-to-all-start = ((s16[16,1712,128]{2,1,0:T(8,128)(2,1)}), s16[16,1712,128]{2,1,0:T(8,128)(2,1)}, u32[]{:S(2)}, u32[]{:S(2)}) async-start(s16[16,1712,128]{2,1,0:T(8,128)(2,1)} %get-tuple-element.15), calls=%async_computation | async-start | bytes 14024704 | tf_op jit(solution)/shard_map/all_to_all | solution.py:465
  19.2 126.7 %all-to-all-done.x_hbm = s16[16,1712,128]{2,1,0:T(8,128)(2,1)} async-done(((s16[16,1712,128]{2,1,0:T(8,128)(2,1)}), s16[16,1712,128]{2,1,0:T(8,128)(2,1)}, u32[]{:S(2)}, u32[]{:S(2)}) %all-to-all-start) | async-done | bytes 7012384 | tf_op jit(solution)/shard_map/all_to_all | solution.py:465
  145.9 1.0 slice_convert_fusion
  147.0 31.0 %all-to-all-start.1 = ((s16[16,384,128]{2,1,0:T(8,128)(2,1)}), s16[16,384,128]{2,1,0:T(8,128)(2,1)S(1)}, u32[]{:S(2)}, u32[]{:S(2)}) async-start(s16[16,384,128]{2,1,0:T(8,128)(2,1)} %get-tuple-element.17), calls=%async_computation.1 | async-start | bytes 3145728 | tf_op jit(solution)/shard_map/all_to_all | solution.py:465
  178.0 1.0 convert_reduce_fusion
  179.1 0.3 select_reduce_fusion.3
  179.4 0.1 sub.13
  179.6 0.7 select_reduce_fusion.4.done
  180.2 0.7 convert_reduce_fusion.5.score_bound
  180.9 0.6 convert_reduce_fusion.4.fold_bound
  181.5 0.2 convert_reduce_fusion.1
  181.7 0.7 select_reduce_fusion.1
  182.5 0.7 select_reduce_fusion.2.fold_list
  183.2 0.1 select_reduce_fusion
  183.3 0.6 fusion.6.mods_in
  183.9 0.6 negate_select_fusion.signed_in
  184.5 19.1 %stage.2 = (f32[32,128]{1,0:T(8,128)}, f32[256,4096]{1,0:T(8,128)}, f32[256,256]{1,0:T(8,128)}, f32[33,128,128]{2,1,0:T(8,128)}, bf16[33,128,256]{2,1,0:T(8,128)(2,1)}, /*index=5*/bf16[208,128,128]{2,1,0:T(8,128)(2,1)}) custom-call(s32[256]{0:T(256)} %select_reduce_fusion.2.fold_list, s32[35]{0:T(128)} %convert_reduce_fusion.4.fold_bound, ...), custom_call_target="tpu_custom_call" | custom-call | flops 13958643712 | bytes 22020096 | tf_op jit(solution)/shard_map/stage/pallas_call | solution.py:368
  203.5 6.4 %all-to-all-done.1.x_hbm = s16[16,384,128]{2,1,0:T(8,128)(2,1)S(1)} async-done(((s16[16,384,128]{2,1,0:T(8,128)(2,1)}), s16[16,384,128]{2,1,0:T(8,128)(2,1)S(1)}, u32[]{:S(2)}, u32[]{:S(2)}) %all-to-all-start.1) | async-done | bytes 1572896 | tf_op jit(solution)/shard_map/all_to_all | solution.py:465
  210.0 1.1 copy-done
  211.1 7.9 %stage.3 = (f32[16,1,768]{2,1,0:T(1,128)}, f32[256,4096]{1,0:T(8,128)}) custom-call(s32[256]{0:T(256)} %select_reduce_fusion.2.fold_list, s32[35]{0:T(128)} %convert_reduce_fusion.4.fold_bound, s32[256]{0:T(256)} %get-tuple-element.38.score_list, s32[17]{0:T(128)} %convert_reduce_fusion.5.score_bound, ...), custom_call_target="tpu_custom_call", output_to_operand_aliasing={{1}: (10, {})} | custom-call | flops 3221225472 | bytes 11534336 | tf_op jit(solution)/shard_map/stage/pallas_call | solution.py:368
  219.0 20.0 %all_to_all.15.got_ref = f32[16,1,768]{2,1,0:T(1,128)} all-to-all(f32[16,1,768]{2,1,0:T(1,128)} %get-tuple-element.24), channel_id=1, replica_groups=mesh['groups'=2,'dp'=16] {'dp'}, dimensions={0} | all-to-all | bytes 98304 | tf_op jit(solution)/shard_map/all_to_all | solution.py:465
  239.0 4.6 %close.1 = (bf16[512,2048]{1,0:T(8,128)(2,1)}, f32[2,128]{1,0:T(2,128)}) custom-call(s32[2,128]{1,0:T(2,128)} %bitcast.19, f32[16,1,768]{2,1,0:T(1,128)} %all_to_all.15.got_ref, f32[256,4096]{1,0:T(8,128)} %get-tuple-element.25.sums_hbm), custom_call_target="tpu_custom_call" | custom-call | flops 2097152 | bytes 6291456 | tf_op jit(solution)/shard_map/close/pallas_call | solution.py:445
  (19 shorter events, 0.1 us)
Async XLA Ops:
  11.7 134.2 %all-to-all-start = ((s16[16,1712,128]{2,1,0:T(8,128)(2,1)}), s16[16,1712,128]{2,1,0:T(8,128)(2,1)}, u32[]{:S(2)}, u32[]{:S(2)}) async-start(s16[16,1712,128]{2,1,0:T(8,128)(2,1)} %get-tuple-element.15), calls=%async_computation | async-start | bytes 14024704 | tf_op jit(solution)/shard_map/all_to_all | solution.py:465
  19.2 160.3 %copy-start.2 = (s32[256]{0:T(256)S(1)}, s32[256]{0:T(256)}, u32[]{:S(2)}) copy-start(s32[256]{0:T(256)} %constant.91.clone) | copy-start | bytes 3076
  19.2 160.3 %copy-start.3 = (s32[256]{0:T(256)S(1)}, s32[256]{0:T(256)}, u32[]{:S(2)}) copy-start(s32[256]{0:T(256)} %constant.89.clone) | copy-start | bytes 3076
  19.2 160.3 %copy-start.1 = (s32[256]{0:T(256)S(1)}, s32[256]{0:T(256)}, u32[]{:S(2)}) copy-start(s32[256]{0:T(256)} %constant.90.clone) | copy-start | bytes 3076
  19.2 160.3 %copy-start.4 = (pred[2,256]{1,0:T(4,128)(4,1)S(1)}, pred[2,256]{1,0:T(4,128)(4,1)}, u32[]{:S(2)}) copy-start(pred[2,256]{1,0:T(4,128)(4,1)} %constant.92.clone) | copy-start | bytes 1540
  147.0 63.0 %all-to-all-start.1 = ((s16[16,384,128]{2,1,0:T(8,128)(2,1)}), s16[16,384,128]{2,1,0:T(8,128)(2,1)S(1)}, u32[]{:S(2)}, u32[]{:S(2)}) async-start(s16[16,384,128]{2,1,0:T(8,128)(2,1)} %get-tuple-element.17), calls=%async_computation.1 | async-start | bytes 3145728 | tf_op jit(solution)/shard_map/all_to_all | solution.py:465
  209.9 1.1 copy-start

commit v15 on v14

--- a/solution.py
+++ b/solution.py
@@ -34,12 +34,11 @@
 
 
 def lane_sums(values):
-    ones = jnp.ones((8, LANES), jnp.bfloat16)
+    ones = jnp.ones((8, 2 * LANES), jnp.bfloat16)
     high = values.astype(jnp.bfloat16)
     low = (values - high.astype(jnp.float32)).astype(jnp.bfloat16)
-    return lax.dot_general(ones, high, NT, preferred_element_type=jnp.float32) + lax.dot_general(
-        ones, low, NT, preferred_element_type=jnp.float32
-    )
+    both = jnp.concatenate([high, low], axis=1)
+    return lax.dot_general(ones, both, NT, preferred_element_type=jnp.float32)
 
 
 def block_sums(square, out_ref, count):
@@ -170,7 +169,7 @@
     )(owner, rank, tile_row, *told, tile_values)
 
 
-def stage_kernel(q, bases, last, cached, fold_list, fold_bound, score_list, score_bound, done,
+def stage_kernel(q, bases, last, cached, fold_list, fold_bound, score_list,
                  mods_in, signed_in, x_hbm, *refs):
     base = bases[q]
     earlier, refs = refs[:q], refs[q:]
@@ -182,7 +181,23 @@
     sems, sub_sems, tile_sems = refs
     devices, width = x.shape[0], x.shape[1] // LANES
     none = products.shape[0] - 1
-    begin, end = done[q - 1] if q else 0, done[q]
+    parts = len(bases) - 1
+
+    def bound(p, sub):
+        return fold_bound[p * (TB_OWN + 1) + sub]
+
+    def score_bound(sub):
+        return sum(bound(p, sub) - bound(p, 0) for p in range(parts))
+
+    def complete(arrived):
+        def one(i, least):
+            sub = TB_OWN - 1 - i
+            waits = [bound(p, sub + 1) > bound(p, sub) for p in range(arrived, parts)]
+            return jnp.where(functools.reduce(jnp.logical_or, waits), sub, least)
+
+        return lax.fori_loop(0, TB_OWN, one, TB_OWN) if arrived < parts else TB_OWN
+
+    begin, end = complete(q) if q else 0, complete(q + 1)
     needed = [pltpu.make_async_copy(x_hbm.at[:, pl.ds(0, width * LANES)], x, sems.at[0])]
     if q:
         needed.append(pltpu.make_async_copy(made_in[0], spread, sems.at[1]))
@@ -219,8 +234,6 @@
     for e, e_hbm in enumerate(earlier):
         held = tiles.at[pl.ds(bases[e], e_hbm.shape[0])]
         later.append(pltpu.make_async_copy(e_hbm, held, tile_sems.at[e]))
-    for copy in later:
-        copy.start()
     products[...] = jnp.zeros_like(products)
     scores[...] = before[...] if q else jnp.zeros_like(scores)
     for held, given, empty in ((mods, mods_in, -1.0), (signed, signed_in, 0.0)):
@@ -252,14 +265,15 @@
         lax.fori_loop(0, (none + 1) // batch, build, 0)
     for copy in needed:
         copy.wait()
+    for copy in later:
+        copy.start()
 
     def eight(entries, start, end, p):
         at = [start + EIGHT * p + j for j in range(EIGHT)]
         return [(entries[jnp.where(spot < end, spot, start)], spot < end) for spot in at]
 
     def fold_sub(sub):
-        start = fold_bound[q * (TB_OWN + 1) + sub]
-        end = fold_bound[q * (TB_OWN + 1) + sub + 1]
+        start, end = bound(q, sub), bound(q, sub + 1)
         if q:
             sums_read(sub).wait()
 
@@ -303,7 +317,7 @@
         copy.wait()
 
     def score_sub(sub):
-        start, end = score_bound[sub], score_bound[sub + 1]
+        start, end = score_bound(sub), score_bound(sub + 1)
         some = sums[columns(sub)]
         narrow[...] = some.astype(jnp.bfloat16)
         squares[...] += some * some
@@ -528,10 +542,8 @@
     fold_list, fold_bounds = sorted_slots(
         fold_key, parts * (TB_OWN + 1), row + jnp.asarray(from_slot, jnp.int32)
     )
-    score_list, score_bounds = sorted_slots(sub, TB_OWN, row + jnp.asarray(place, jnp.int32))
-    left = np.arange(parts)[:, None] < slot_part[None, :]
-    done = jnp.min(jnp.where(left, sub[None, :], TB_OWN), axis=1)
-    scalars = [fold_list, fold_bounds, score_list, score_bounds, done]
+    score_list, _ = sorted_slots(sub, TB_OWN, row + jnp.asarray(place, jnp.int32))
+    scalars = [fold_list, fold_bounds, score_list]
 
     scale = lax.rsqrt(row_sq + EPSILON) * (1.0 / CODE_TOP**2)
     signed = jnp.where(all_labels < HALF, scale, -scale)

time: 246 us -> 245 us (level); the launches traced: 244 us -> 245 us
  transfers between devices with their start and end apart: 2 -> 2, of which waited for: 2 -> 2; matrix products, arithmetic and copies ran while one was open for 3% -> 2% of each run, Pallas kernels for 8% -> 8%
where the time goes in v15:
time: 245 us
  waiting for transfers between devices  133 us (54%)
  Pallas kernels  42.5 us (17%)
  starting transfers between devices  38.3 us (16%)
  blocking collectives  21.7 us (9%)
  other arithmetic  7.4 us (3%)
    all_to_all x2, waiting for transfers between devices, exchange(): return lax.all_to_all(x, 'dp', split_axis=0, concat_axis=0, tiled=True)  133 us
    all_to_all x2, starting transfers between devices, exchange(): return lax.all_to_all(x, 'dp', split_axis=0, concat_axis=0, tiled=True)  38.3 us
    pallas_call x2, Pallas kernels, stage(): pl.pallas_call(functools.partial(stage_kernel, q, [devices * cut for cut...  28.2 us
    all_to_all x1, blocking collectives, exchange(): return lax.all_to_all(x, 'dp', split_axis=0, concat_axis=0, tiled=True)  21.7 us
    pallas_call x1, Pallas kernels, pack(): pl.pallas_call(functools.partial(pack_kernel, cuts), in_specs=[SMEM] * 3...  9.68 us
  transfers between devices with their start and end apart: 2, of which 2 were waited for; matrix products, arithmetic and copies ran while one was open for 2% of the time, Pallas kernels for 8%

profile of v15, /device:TPU:0, one launch (start us, length us, event | category | flops | bytes accessed | tf_op | source)
XLA Modules:
  0.0 245.4 jit_solution(16671095953915443397)
XLA Ops:
  0.6 1.4 convert_reduce_fusion.3.rank_ref
  2.1 9.7 %pack.1 = (s16[16,1712,128]{2,1,0:T(8,128)(2,1)}, s16[16,384,128]{2,1,0:T(8,128)(2,1)}) custom-call(s32[128]{0:T(128)} %bitcast.15, s32[128]{0:T(128)} %convert_reduce_fusion.3.rank_ref, s32[128]{0:T(128)} %row_ref.1, s32[2,128]{1,0:T(2,128)} %bitcast.18, s32[1,128]{1,0:T(1,128)} %bitcast.16, s32[1,128]{1,0:T(1,128)} %bitcast.20, s32[1,128]{1,0:T(1,128)} %bitcast.17, ...), custom_call_target="tpu_custom_call" | custom-call | flops 16777216 | bytes 12582912 | tf_op jit(solution)/shard_map/pack/pallas_call | solution.py:146
  11.7 7.4 %all-to-all-start = ((s16[16,1712,128]{2,1,0:T(8,128)(2,1)}), s16[16,1712,128]{2,1,0:T(8,128)(2,1)}, u32[]{:S(2)}, u32[]{:S(2)}) async-start(s16[16,1712,128]{2,1,0:T(8,128)(2,1)} %get-tuple-element.15), calls=%async_computation | async-start | bytes 14024704 | tf_op jit(solution)/shard_map/all_to_all | solution.py:479
  19.1 0.0 copy-start.2
  19.2 0.0 copy-start.3
  19.2 126.7 %all-to-all-done.x_hbm = s16[16,1712,128]{2,1,0:T(8,128)(2,1)} async-done(((s16[16,1712,128]{2,1,0:T(8,128)(2,1)}), s16[16,1712,128]{2,1,0:T(8,128)(2,1)}, u32[]{:S(2)}, u32[]{:S(2)}) %all-to-all-start) | async-done | bytes 7012384 | tf_op jit(solution)/shard_map/all_to_all | solution.py:479
  145.9 31.0 %all-to-all-start.1 = ((s16[16,384,128]{2,1,0:T(8,128)(2,1)}), s16[16,384,128]{2,1,0:T(8,128)(2,1)S(1)}, u32[]{:S(2)}, u32[]{:S(2)}) async-start(s16[16,384,128]{2,1,0:T(8,128)(2,1)} %get-tuple-element.17), calls=%async_computation.1 | async-start | bytes 3145728 | tf_op jit(solution)/shard_map/all_to_all | solution.py:479
  176.9 1.0 slice_convert_fusion
  177.9 1.0 convert_reduce_fusion
  179.0 0.3 select_reduce_fusion.3
  179.4 0.1 sub.13
  179.5 0.6 convert_reduce_fusion.4.fold_bound
  180.1 0.2 convert_reduce_fusion.1
  180.3 0.7 select_reduce_fusion.1
  181.1 0.7 select_reduce_fusion.2.fold_list
  181.8 0.1 select_reduce_fusion
  181.8 0.6 fusion.6.mods_in
  182.5 0.6 negate_select_fusion.signed_in
  183.1 19.2 %stage.2 = (f32[32,128]{1,0:T(8,128)}, f32[256,4096]{1,0:T(8,128)}, f32[256,256]{1,0:T(8,128)}, f32[33,128,128]{2,1,0:T(8,128)}, bf16[33,128,256]{2,1,0:T(8,128)(2,1)}, /*index=5*/bf16[208,128,128]{2,1,0:T(8,128)(2,1)}) custom-call(s32[256]{0:T(256)} %select_reduce_fusion.2.fold_list, s32[35]{0:T(128)} %convert_reduce_fusion.4.fold_bound, ...), custom_call_target="tpu_custom_call" | custom-call | flops 13958643712 | bytes 22020096 | tf_op jit(solution)/shard_map/stage/pallas_call | solution.py:382
  202.2 6.6 %all-to-all-done.1.x_hbm = s16[16,384,128]{2,1,0:T(8,128)(2,1)S(1)} async-done(((s16[16,384,128]{2,1,0:T(8,128)(2,1)}), s16[16,384,128]{2,1,0:T(8,128)(2,1)S(1)}, u32[]{:S(2)}, u32[]{:S(2)}) %all-to-all-start.1) | async-done | bytes 1572896 | tf_op jit(solution)/shard_map/all_to_all | solution.py:479
  208.8 1.1 copy-done
  210.0 9.0 %stage.3 = (f32[16,1,768]{2,1,0:T(1,128)}, f32[256,4096]{1,0:T(8,128)}) custom-call(s32[256]{0:T(256)} %select_reduce_fusion.2.fold_list, s32[35]{0:T(128)} %convert_reduce_fusion.4.fold_bound, s32[256]{0:T(256)} %get-tuple-element.38.score_list, f32[32,128]{1,0:T(8,128)} %fusion.6.mods_in, ...), custom_call_target="tpu_custom_call", output_to_operand_aliasing={{1}: (8, {})} | custom-call | flops 3221225472 | bytes 11534336 | tf_op jit(solution)/shard_map/stage/pallas_call | solution.py:382
  219.0 21.7 %all_to_all.15.got_ref = f32[16,1,768]{2,1,0:T(1,128)} all-to-all(f32[16,1,768]{2,1,0:T(1,128)} %get-tuple-element.24), channel_id=1, replica_groups=mesh['groups'=2,'dp'=16] {'dp'}, dimensions={0} | all-to-all | bytes 98304 | tf_op jit(solution)/shard_map/all_to_all | solution.py:479
  240.7 4.6 %close.1 = (bf16[512,2048]{1,0:T(8,128)(2,1)}, f32[2,128]{1,0:T(2,128)}) custom-call(s32[2,128]{1,0:T(2,128)} %bitcast.19, f32[16,1,768]{2,1,0:T(1,128)} %all_to_all.15.got_ref, f32[256,4096]{1,0:T(8,128)} %get-tuple-element.25.sums_hbm), custom_call_target="tpu_custom_call" | custom-call | flops 2097152 | bytes 6291456 | tf_op jit(solution)/shard_map/close/pallas_call | solution.py:459
  (15 shorter events, 0.1 us)
Async XLA Ops:
  11.7 134.1 %all-to-all-start = ((s16[16,1712,128]{2,1,0:T(8,128)(2,1)}), s16[16,1712,128]{2,1,0:T(8,128)(2,1)}, u32[]{:S(2)}, u32[]{:S(2)}) async-start(s16[16,1712,128]{2,1,0:T(8,128)(2,1)} %get-tuple-element.15), calls=%async_computation | async-start | bytes 14024704 | tf_op jit(solution)/shard_map/all_to_all | solution.py:479
  19.1 160.3 %copy-start.2 = (s32[256]{0:T(256)S(1)}, s32[256]{0:T(256)}, u32[]{:S(2)}) copy-start(s32[256]{0:T(256)} %constant.87.clone) | copy-start | bytes 3076
  19.2 160.3 %copy-start.3 = (s32[256]{0:T(256)S(1)}, s32[256]{0:T(256)}, u32[]{:S(2)}) copy-start(s32[256]{0:T(256)} %constant.85.clone) | copy-start | bytes 3076
  19.2 160.3 %copy-start.1 = (s32[256]{0:T(256)S(1)}, s32[256]{0:T(256)}, u32[]{:S(2)}) copy-start(s32[256]{0:T(256)} %constant.86.clone) | copy-start | bytes 3076
  145.9 62.9 %all-to-all-start.1 = ((s16[16,384,128]{2,1,0:T(8,128)(2,1)}), s16[16,384,128]{2,1,0:T(8,128)(2,1)S(1)}, u32[]{:S(2)}, u32[]{:S(2)}) async-start(s16[16,384,128]{2,1,0:T(8,128)(2,1)} %get-tuple-element.17), calls=%async_computation.1 | async-start | bytes 3145728 | tf_op jit(solution)/shard_map/all_to_all | solution.py:479
  208.8 1.1 copy-start

commit v16 on v15

--- a/solution.py
+++ b/solution.py
@@ -24,6 +24,7 @@
 CACHED_BLOCKS = 64
 QUAD = 4
 EIGHT = 8
+CHUNK = 16
 ROW_SHIFT, SOURCE_SHIFT = 16, 8
 PLACE_MASK, SOURCE_MASK, SLOT_MASK = 0xFFFF, 0xFF, 0xFF
 BATCH = 8
@@ -58,11 +59,11 @@
     return pltpu.CompilerParams(vmem_limit_bytes=VMEM_BYTES)
 
 
-def pack_kernel(cuts, owner_ref, rank_ref, row_ref, *refs):
+def pack_kernel(cuts, owner_ref, row_ref, *refs):
     parts = len(cuts) - 1
     (*told_refs, x_hbm), refs = refs[:5], refs[5:]
     outs = refs[:parts]
-    x, coded, square, sums, words, notes, held, sems, x_sems = refs[parts:]
+    x, coded, square, sums, words, notes, held, rank_row, rank_ref, sems, x_sems = refs[parts:]
     tiles = x.shape[0]
     devices = held.shape[0]
     blocks = square.shape[0]
@@ -78,6 +79,14 @@
 
     for c in range(tiles // step):
         read(c).start()
+    labels, owner, row, sub = [ref[...] for ref in told_refs]
+    own, sub_own = [jnp.broadcast_to(v.astype(jnp.float32), (tiles, tiles)) for v in (owner, sub)]
+    other, sub_other = jnp.transpose(own), jnp.transpose(sub_own)
+    index = [lax.broadcasted_iota(jnp.int32, (tiles, tiles), d) for d in (0, 1)]
+    ahead = (sub_other < sub_own) | ((sub_other == sub_own) & (index[0] < index[1]))
+    ahead = jnp.where(ahead & (other == own), 1.0, 0.0)
+    rank_row[...] = jnp.sum(ahead, axis=0, keepdims=True).astype(jnp.int32)
+    pltpu.sync_copy(rank_row, rank_ref)
     lax.fori_loop(0, devices, clear, 0)
     square[...] = jnp.zeros_like(square)
 
@@ -88,7 +97,7 @@
             some = x[t]
             root = some * lax.rsqrt(some)
             code = (root * CODE_TOP + 0.5).astype(jnp.int32) - CODE_SHIFT
-            owner, rank = owner_ref[t], rank_ref[t]
+            owner, rank = owner_ref[t], rank_ref[0, t]
             at = pl.ds(pl.multiple_of((owner * cuts[-1] + rank) * LANES, LANES), LANES)
             coded[at, :] = code.astype(jnp.int16)
             square[row_ref[t]] += some * some
@@ -121,7 +130,6 @@
     level = (jnp.log2(jnp.maximum(total, 1e-30)) - LOG_MIDDLE) * LOG_STEPS
     level = jnp.where(total > 0.0, jnp.clip(level, -32700.0, 32700.0), -32768.0)
     level = (level + 32768.5).astype(jnp.int32) - 32768
-    labels, owner, row, sub = [ref[...] for ref in told_refs]
     words[...] = jnp.zeros_like(words)
     words[:blocks, :] = level
     at = blocks
@@ -137,7 +145,7 @@
         note(d).wait()
 
 
-def pack(tile_values, owner, rank, tile_row, told, devices, blocks, cuts):
+def pack(tile_values, owner, tile_row, told, devices, blocks, cuts):
     tiles = tile_values.shape[0]
     told = [x.reshape(-1, LANES) for x in told]
     noted = -(-(blocks + sum(x.shape[0] for x in told[:3])) // 16) * 16
@@ -145,7 +153,7 @@
     rows[0] += noted
     return pl.pallas_call(
         functools.partial(pack_kernel, cuts),
-        in_specs=[SMEM] * 3 + [VMEM] * 4 + [ANY],
+        in_specs=[SMEM] * 2 + [VMEM] * 4 + [ANY],
         out_specs=[ANY] * len(rows),
         out_shape=[jax.ShapeDtypeStruct((devices, some, LANES), jnp.int16) for some in rows],
         scratch_shapes=[
@@ -156,6 +164,8 @@
             pltpu.VMEM((noted, LANES), jnp.int32),
             pltpu.VMEM((noted, LANES), jnp.int16),
             pltpu.SMEM((devices,), jnp.int32),
+            pltpu.VMEM((1, tiles), jnp.int32),
+            pltpu.SMEM((1, tiles), jnp.int32),
             pltpu.SemaphoreType.DMA((len(rows) + 1, devices)),
             pltpu.SemaphoreType.DMA((tiles,)),
         ],
@@ -166,7 +176,7 @@
             transcendentals=tile_values.size,
         ),
         name="pack",
-    )(owner, rank, tile_row, *told, tile_values)
+    )(owner, tile_row, *told, tile_values)
 
 
 def stage_kernel(q, bases, last, cached, fold_list, fold_bound, score_list,
@@ -231,9 +241,26 @@
         sums[...] = jnp.zeros_like(sums)
         squares[...] = jnp.zeros_like(squares)
     later = [pltpu.make_async_copy(made_in[1], hot, sems.at[3])] if q and cached else []
-    for e, e_hbm in enumerate(earlier):
-        held = tiles.at[pl.ds(bases[e], e_hbm.shape[0])]
-        later.append(pltpu.make_async_copy(e_hbm, held, tile_sems.at[e]))
+
+    def each_chunk(p, outside, write, sub, what):
+        count = math.gcd(CHUNK, bases[p + 1] - bases[p])
+
+        def one(c, carry):
+            away, own = outside.at[pl.ds(c * count, count)], tiles.at[pl.ds(bases[p] + c * count, count)]
+            some = (own, away) if write else (away, own)
+            what(pltpu.make_async_copy(*some, tile_sems.at[p, c]))
+            return carry
+
+        first, stop = bound(p, sub) - bases[p], bound(p, TB_OWN) - bases[p]
+        lax.fori_loop(first // count, (stop + count - 1) // count, one, 0)
+
+    def each_earlier(what):
+        for copy in later:
+            what(copy)
+        for e, e_hbm in enumerate(earlier):
+            each_chunk(e, e_hbm, False, begin, what)
+
+    each_earlier(lambda copy: copy.start())
     products[...] = jnp.zeros_like(products)
     scores[...] = before[...] if q else jnp.zeros_like(scores)
     for held, given, empty in ((mods, mods_in, -1.0), (signed, signed_in, 0.0)):
@@ -265,12 +292,11 @@
         lax.fori_loop(0, (none + 1) // batch, build, 0)
     for copy in needed:
         copy.wait()
-    for copy in later:
-        copy.start()
 
     def eight(entries, start, end, p):
         at = [start + EIGHT * p + j for j in range(EIGHT)]
-        return [(entries[jnp.where(spot < end, spot, start)], spot < end) for spot in at]
+        at = [(jnp.where(spot < end, spot, start), spot < end) for spot in at]
+        return [(entries[spot], spot, held) for spot, held in at]
 
     def fold_sub(sub):
         start, end = bound(q, sub), bound(q, sub + 1)
@@ -279,10 +305,9 @@
 
         def one_eight(p, carry):
             folded, picks = [], []
-            for entry, held in eight(fold_list, start, end, p):
+            for entry, spot, held in eight(fold_list, start, end, p):
                 row = entry >> ROW_SHIFT
                 source, slot = (entry >> SOURCE_SHIFT) & SOURCE_MASK, entry & SLOT_MASK
-                spot = base + source * width + slot
                 raw = x[source, pl.ds(pl.multiple_of(slot * LANES, LANES), LANES), :]
                 root = raw.astype(jnp.int32).astype(jnp.float32) + float(CODE_SHIFT)
                 scale = spread[row]
@@ -307,14 +332,12 @@
     each_sub(begin, TB_OWN, fold_sub)
     kept = []
     if not last:
-        fresh = tiles.at[pl.ds(base, devices * width)]
-        kept.append(pltpu.make_async_copy(fresh, fresh_out, sems.at[2]))
+        each_chunk(q, fresh_out, True, end, lambda copy: copy.start())
         kept.append(pltpu.make_async_copy(spread, made_out[0], sems.at[4]))
         kept.append(pltpu.make_async_copy(hot, made_out[1], sems.at[5]))
     for copy in kept:
         copy.start()
-    for copy in later:
-        copy.wait()
+    each_earlier(lambda copy: copy.wait())
 
     def score_sub(sub):
         start, end = score_bound(sub), score_bound(sub + 1)
@@ -324,8 +347,8 @@
 
         def one_eight(p, carry):
             listed = eight(score_list, start, end, p)
-            rows = [jnp.where(held, entry >> ROW_SHIFT, none) for entry, held in listed]
-            spots = [entry & PLACE_MASK for entry, held in listed]
+            rows = [jnp.where(held, entry >> ROW_SHIFT, none) for entry, spot, held in listed]
+            spots = [entry & PLACE_MASK for entry, spot, held in listed]
             hots = [hot[row] if cached else one_hot(row) for row in rows]
             chosen = jnp.dot(
                 jnp.concatenate(hots, axis=0), narrow[...], preferred_element_type=jnp.float32
@@ -354,6 +377,8 @@
         squares_out[...] = squares[...]
     for copy in kept:
         copy.wait()
+    if not last:
+        each_chunk(q, fresh_out, True, end, lambda copy: copy.wait())
     each_sub(begin, TB_OWN, lambda sub: sums_write(sub).wait())
 
 
@@ -399,7 +424,7 @@
             pltpu.VMEM((blocks + 1, LANES), jnp.float32),
             pltpu.SemaphoreType.DMA((6,)),
             pltpu.SemaphoreType.DMA((2, TB_OWN)),
-            pltpu.SemaphoreType.DMA((len(cuts),)),
+            pltpu.SemaphoreType.DMA((len(cuts), slots)),
         ],
         compiler_params=params(),
         cost_estimate=pl.CostEstimate(
@@ -493,7 +518,7 @@
     listed = jnp.sum(jnp.where(here, entries[None, :], 0), axis=1)
     levels = jnp.arange(top + 1, dtype=jnp.int32)
     bounds = jnp.sum((key[None, :] < levels[:, None]).astype(jnp.int32), axis=1)
-    return listed, bounds
+    return listed, bounds, position
 
 
 def ranks(group, sub):
@@ -517,8 +542,7 @@
     owner = tile_owner[:, 0]
 
     told = (labels, owner, tile_row, tile_sub)
-    rank = ranks(owner, tile_sub)
-    outgoing = pack(tile_values, owner, rank, tile_row, told, devices, blocks, cuts)
+    outgoing = pack(tile_values, owner, tile_row, told, devices, blocks, cuts)
     incoming = [exchange(outgoing[0])]
     heard = incoming[0][:, (cuts[1] - cuts[0]) * LANES :].astype(jnp.int32)
     level = heard[:, :blocks]
@@ -534,15 +558,14 @@
     sub = jnp.where(meta < 0, TB_OWN, meta % TB_OWN)
     slot_rank = np.arange(devices * cap) % cap
     slot_part = np.searchsorted(np.array(cuts), slot_rank, side="right") - 1
-    low, high = np.array(cuts)[slot_part], np.array(cuts)[slot_part + 1]
-    place = devices * low + np.arange(devices * cap) // cap * (high - low) + slot_rank - low
+    low = np.array(cuts)[slot_part]
     fold_key = jnp.asarray(slot_part * (TB_OWN + 1), jnp.int32) + sub
     row = (meta // TB_OWN) << ROW_SHIFT
     from_slot = (np.arange(devices * cap) // cap << SOURCE_SHIFT) + slot_rank - low
-    fold_list, fold_bounds = sorted_slots(
+    fold_list, fold_bounds, position = sorted_slots(
         fold_key, parts * (TB_OWN + 1), row + jnp.asarray(from_slot, jnp.int32)
     )
-    score_list, _ = sorted_slots(sub, TB_OWN, row + jnp.asarray(place, jnp.int32))
+    score_list, *_ = sorted_slots(sub, TB_OWN, row + position)
     scalars = [fold_list, fold_bounds, score_list]
 
     scale = lax.rsqrt(row_sq + EPSILON) * (1.0 / CODE_TOP**2)

time: 245 us -> 256 us (1.045)
  Pallas kernels: 42.5 us -> 70.6 us
  blocking collectives: 21.7 us -> 10.9 us
  waiting for transfers between devices: 133 us -> 127 us
    pallas_call x2, Pallas kernels: 28.2 us -> 56.3 us  [stage(): pl.pallas_call(functools.partial(stage_kernel, q, [devices * cut for cut...]
    all_to_all x1, blocking collectives: 21.7 us -> 10.9 us  [exchange(): return lax.all_to_all(x, 'dp', split_axis=0, concat_axis=0, tiled=True)]
    all_to_all x2, waiting for transfers between devices: 133 us -> 127 us  [exchange(): return lax.all_to_all(x, 'dp', split_axis=0, concat_axis=0, tiled=True)]
  transfers between devices with their start and end apart: 2 -> 2, of which waited for: 2 -> 1; matrix products, arithmetic and copies ran while one was open for 2% -> 2% of each run, Pallas kernels for 8% -> 13%
where the time goes in v16:
time: 256 us; the launch traced here: 255 us
  waiting for transfers between devices  127 us (50%)
  Pallas kernels  70.6 us (28%)
  starting transfers between devices  38.4 us (15%)
  blocking collectives  10.9 us (4%)
  other arithmetic  6.01 us (2%)
    all_to_all x2, waiting for transfers between devices, exchange(): return lax.all_to_all(x, 'dp', split_axis=0, concat_axis=0, tiled=True)  127 us
    pallas_call x2, Pallas kernels, stage(): pl.pallas_call(functools.partial(stage_kernel, q, [devices * cut for cut...  56.3 us
    all_to_all x2, starting transfers between devices, exchange(): return lax.all_to_all(x, 'dp', split_axis=0, concat_axis=0, tiled=True)  38.4 us
    all_to_all x1, blocking collectives, exchange(): return lax.all_to_all(x, 'dp', split_axis=0, concat_axis=0, tiled=True)  10.9 us
    pallas_call x1, Pallas kernels, pack(): pl.pallas_call(functools.partial(pack_kernel, cuts), in_specs=[SMEM] * 2...  9.66 us
  transfers between devices with their start and end apart: 2, of which 1 were waited for; matrix products, arithmetic and copies ran while one was open for 2% of the time, Pallas kernels for 13%

profile of v16, /device:TPU:0, one launch (start us, length us, event | category | flops | bytes accessed | tf_op | source)
XLA Modules:
  0.0 254.7 jit_solution(1994567241413527021)
XLA Ops:
  0.6 9.7 %pack.1 = (s16[16,1712,128]{2,1,0:T(8,128)(2,1)}, s16[16,384,128]{2,1,0:T(8,128)(2,1)}) custom-call(s32[128]{0:T(128)} %bitcast.16, s32[128]{0:T(128)} %row_ref.1, s32[2,128]{1,0:T(2,128)} %bitcast.14, s32[1,128]{1,0:T(1,128)} %bitcast.17, s32[1,128]{1,0:T(1,128)} %bitcast.18, s32[1,128]{1,0:T(1,128)} %bitcast.19, f32[128,128,128]{2,1,0:T(8,128)} %refs_4_.1), custom_call_target="tpu_custom_call" | custom-call | flops 16777216 | bytes 12582912 | tf_op jit(solution)/shard_map/pack/pallas_call | solution.py:154
  10.3 7.4 %all-to-all-start = ((s16[16,1712,128]{2,1,0:T(8,128)(2,1)}), s16[16,1712,128]{2,1,0:T(8,128)(2,1)}, u32[]{:S(2)}, u32[]{:S(2)}) async-start(s16[16,1712,128]{2,1,0:T(8,128)(2,1)} %get-tuple-element.15), calls=%async_computation | async-start | bytes 14024704 | tf_op jit(solution)/shard_map/all_to_all | solution.py:504
  17.7 0.0 copy-start.2
  17.7 0.0 copy-start.1
  17.8 126.7 %all-to-all-done.x_hbm = s16[16,1712,128]{2,1,0:T(8,128)(2,1)} async-done(((s16[16,1712,128]{2,1,0:T(8,128)(2,1)}), s16[16,1712,128]{2,1,0:T(8,128)(2,1)}, u32[]{:S(2)}, u32[]{:S(2)}) %all-to-all-start) | async-done | bytes 7012384 | tf_op jit(solution)/shard_map/all_to_all | solution.py:504
  144.5 1.0 slice_convert_fusion
  145.5 31.0 %all-to-all-start.1 = ((s16[16,384,128]{2,1,0:T(8,128)(2,1)}), s16[16,384,128]{2,1,0:T(8,128)(2,1)S(1)}, u32[]{:S(2)}, u32[]{:S(2)}) async-start(s16[16,384,128]{2,1,0:T(8,128)(2,1)} %get-tuple-element.17), calls=%async_computation.1 | async-start | bytes 3145728 | tf_op jit(solution)/shard_map/all_to_all | solution.py:504
  176.6 1.0 convert_reduce_fusion
  177.6 0.3 select_reduce_fusion.3
  178.0 0.1 sub.13
  178.1 0.3 convert_reduce_fusion.1
  178.4 0.6 convert_reduce_fusion.3.fold_bound
  179.0 0.7 select_reduce_fusion.2.fold_list
  179.7 0.7 select_reduce_fusion.1.score_list
  180.4 0.1 select_reduce_fusion
  180.5 0.6 fusion.6.mods_in
  181.1 0.6 negate_select_fusion.signed_in
  181.7 33.8 %stage.2 = (f32[32,128]{1,0:T(8,128)}, f32[256,4096]{1,0:T(8,128)}, f32[256,256]{1,0:T(8,128)}, f32[33,128,128]{2,1,0:T(8,128)}, bf16[33,128,256]{2,1,0:T(8,128)(2,1)}, /*index=5*/bf16[208,128,128]{2,1,0:T(8,128)(2,1)}) custom-call(s32[256]{0:T(256)} %select_reduce_fusion.2.fold_list, s32[35]{0:T(128)} %convert_reduce_fusion.3.fold_bound, ...), custom_call_target="tpu_custom_call" | custom-call | flops 13958643712 | bytes 22020096 | tf_op jit(solution)/shard_map/stage/pallas_call | solution.py:407
  215.5 0.0 all-to-all-done.1.x_hbm
  215.5 0.0 copy-start
  215.5 1.1 copy-done
  216.7 22.4 %stage.3 = (f32[16,1,768]{2,1,0:T(1,128)}, f32[256,4096]{1,0:T(8,128)}) custom-call(s32[256]{0:T(256)} %select_reduce_fusion.2.fold_list, s32[35]{0:T(128)} %convert_reduce_fusion.3.fold_bound, s32[256]{0:T(256)} %select_reduce_fusion.1.score_list, f32[32,128]{1,0:T(8,128)} %fusion.6.mods_in, ...), custom_call_target="tpu_custom_call", output_to_operand_aliasing={{1}: (8, {})} | custom-call | flops 3221225472 | bytes 11534336 | tf_op jit(solution)/shard_map/stage/pallas_call | solution.py:407
  239.1 10.9 %all_to_all.15.got_ref = f32[16,1,768]{2,1,0:T(1,128)} all-to-all(f32[16,1,768]{2,1,0:T(1,128)} %get-tuple-element.24), channel_id=1, replica_groups=mesh['groups'=2,'dp'=16] {'dp'}, dimensions={0} | all-to-all | bytes 98304 | tf_op jit(solution)/shard_map/all_to_all | solution.py:504
  250.1 4.6 %close.1 = (bf16[512,2048]{1,0:T(8,128)(2,1)}, f32[2,128]{1,0:T(2,128)}) custom-call(s32[2,128]{1,0:T(2,128)} %bitcast.15, f32[16,1,768]{2,1,0:T(1,128)} %all_to_all.15.got_ref, f32[256,4096]{1,0:T(8,128)} %get-tuple-element.25.sums_hbm), custom_call_target="tpu_custom_call" | custom-call | flops 2097152 | bytes 6291456 | tf_op jit(solution)/shard_map/close/pallas_call | solution.py:484
  (13 shorter events, 0.1 us)
Async XLA Ops:
  10.3 134.2 %all-to-all-start = ((s16[16,1712,128]{2,1,0:T(8,128)(2,1)}), s16[16,1712,128]{2,1,0:T(8,128)(2,1)}, u32[]{:S(2)}, u32[]{:S(2)}) async-start(s16[16,1712,128]{2,1,0:T(8,128)(2,1)} %get-tuple-element.15), calls=%async_computation | async-start | bytes 14024704 | tf_op jit(solution)/shard_map/all_to_all | solution.py:504
  17.7 160.3 %copy-start.2 = (s32[256]{0:T(256)S(1)}, s32[256]{0:T(256)}, u32[]{:S(2)}) copy-start(s32[256]{0:T(256)} %constant.83.clone) | copy-start | bytes 3076
  17.7 160.6 %copy-start.1 = (s32[256]{0:T(256)S(1)}, s32[256]{0:T(256)}, u32[]{:S(2)}) copy-start(s32[256]{0:T(256)} %constant.84.clone) | copy-start | bytes 3076
  145.5 70.0 %all-to-all-start.1 = ((s16[16,384,128]{2,1,0:T(8,128)(2,1)}), s16[16,384,128]{2,1,0:T(8,128)(2,1)S(1)}, u32[]{:S(2)}, u32[]{:S(2)}) async-start(s16[16,384,128]{2,1,0:T(8,128)(2,1)} %get-tuple-element.17), calls=%async_computation.1 | async-start | bytes 3145728 | tf_op jit(solution)/shard_map/all_to_all | solution.py:504
  215.5 1.1 copy-start

commit v17 on v16

--- a/solution.py
+++ b/solution.py
@@ -167,7 +167,7 @@
             pltpu.VMEM((1, tiles), jnp.int32),
             pltpu.SMEM((1, tiles), jnp.int32),
             pltpu.SemaphoreType.DMA((len(rows) + 1, devices)),
-            pltpu.SemaphoreType.DMA((tiles,)),
+            pltpu.SemaphoreType.DMA((tiles // math.gcd(STEP_TILES, tiles),)),
         ],
         compiler_params=params(),
         cost_estimate=pl.CostEstimate(
@@ -248,7 +248,7 @@
         def one(c, carry):
             away, own = outside.at[pl.ds(c * count, count)], tiles.at[pl.ds(bases[p] + c * count, count)]
             some = (own, away) if write else (away, own)
-            what(pltpu.make_async_copy(*some, tile_sems.at[p, c]))
+            what(pltpu.make_async_copy(*some, tile_sems.at[0 if write else p, c]))
             return carry
 
         first, stop = bound(p, sub) - bases[p], bound(p, TB_OWN) - bases[p]
@@ -403,6 +403,8 @@
             jax.ShapeDtypeStruct((devices * width, LANES, LANES), jnp.bfloat16),
         ]
     slots = devices * cuts[-1]
+    sizes = [devices * (high - low) for low, high in zip(cuts, cuts[1:])]
+    chunks = max(size // math.gcd(CHUNK, size) for size in sizes)
     operands = [*scalars, mods, signed, x, *normed, *totals]
     return pl.pallas_call(
         functools.partial(stage_kernel, q, [devices * cut for cut in cuts], last, cached),
@@ -424,7 +426,7 @@
             pltpu.VMEM((blocks + 1, LANES), jnp.float32),
             pltpu.SemaphoreType.DMA((6,)),
             pltpu.SemaphoreType.DMA((2, TB_OWN)),
-            pltpu.SemaphoreType.DMA((len(cuts), slots)),
+            pltpu.SemaphoreType.DMA((max(q, 1), chunks)),
         ],
         compiler_params=params(),
         cost_estimate=pl.CostEstimate(

time: 256 us -> 245 us (0.957)
  Pallas kernels: 70.6 us -> 38.1 us
  blocking collectives: 10.9 us -> 24.7 us
  waiting for transfers between devices: 127 us -> 135 us
    pallas_call x2, Pallas kernels: 56.3 us -> 24.9 us  [stage(): pl.pallas_call(functools.partial(stage_kernel, q, [devices * cut for cut...]
    all_to_all x1, blocking collectives: 10.9 us -> 24.7 us  [exchange(): return lax.all_to_all(x, 'dp', split_axis=0, concat_axis=0, tiled=True)]
    all_to_all x2, waiting for transfers between devices: 127 us -> 135 us  [exchange(): return lax.all_to_all(x, 'dp', split_axis=0, concat_axis=0, tiled=True)]
  transfers between devices with their start and end apart: 2 -> 2, of which waited for: 1 -> 2; matrix products, arithmetic and copies ran while one was open for 2% -> 2% of each run, Pallas kernels for 13% -> 8%
where the time goes in v17:
time: 245 us; the launch traced here: 244 us
  waiting for transfers between devices  135 us (55%)
  starting transfers between devices  38.4 us (16%)
  Pallas kernels  38.1 us (16%)
  blocking collectives  24.7 us (10%)
  other arithmetic  6.01 us (2%)
    all_to_all x2, waiting for transfers between devices, exchange(): return lax.all_to_all(x, 'dp', split_axis=0, concat_axis=0, tiled=True)  135 us
    all_to_all x2, starting transfers between devices, exchange(): return lax.all_to_all(x, 'dp', split_axis=0, concat_axis=0, tiled=True)  38.4 us
    pallas_call x2, Pallas kernels, stage(): pl.pallas_call(functools.partial(stage_kernel, q, [devices * cut for cut...  24.9 us
    all_to_all x1, blocking collectives, exchange(): return lax.all_to_all(x, 'dp', split_axis=0, concat_axis=0, tiled=True)  24.7 us
    pallas_call x1, Pallas kernels, pack(): pl.pallas_call(functools.partial(pack_kernel, cuts), in_specs=[SMEM] * 2...  8.59 us
  transfers between devices with their start and end apart: 2, of which 2 were waited for; matrix products, arithmetic and copies ran while one was open for 2% of the time, Pallas kernels for 8%

profile of v17, /device:TPU:0, one launch (start us, length us, event | category | flops | bytes accessed | tf_op | source)
XLA Modules:
  0.0 244.1 jit_solution(15136729289919889109)
XLA Ops:
  0.6 8.6 %pack.1 = (s16[16,1712,128]{2,1,0:T(8,128)(2,1)}, s16[16,384,128]{2,1,0:T(8,128)(2,1)}) custom-call(s32[128]{0:T(128)} %bitcast.16, s32[128]{0:T(128)} %row_ref.1, s32[2,128]{1,0:T(2,128)} %bitcast.14, s32[1,128]{1,0:T(1,128)} %bitcast.17, s32[1,128]{1,0:T(1,128)} %bitcast.18, s32[1,128]{1,0:T(1,128)} %bitcast.19, f32[128,128,128]{2,1,0:T(8,128)} %refs_4_.1), custom_call_target="tpu_custom_call" | custom-call | flops 16777216 | bytes 12582912 | tf_op jit(solution)/shard_map/pack/pallas_call | solution.py:154
  9.2 7.4 %all-to-all-start = ((s16[16,1712,128]{2,1,0:T(8,128)(2,1)}), s16[16,1712,128]{2,1,0:T(8,128)(2,1)}, u32[]{:S(2)}, u32[]{:S(2)}) async-start(s16[16,1712,128]{2,1,0:T(8,128)(2,1)} %get-tuple-element.15), calls=%async_computation | async-start | bytes 14024704 | tf_op jit(solution)/shard_map/all_to_all | solution.py:506
  16.7 0.0 copy-start.2
  16.7 0.0 copy-start.1
  16.7 126.7 %all-to-all-done.x_hbm = s16[16,1712,128]{2,1,0:T(8,128)(2,1)} async-done(((s16[16,1712,128]{2,1,0:T(8,128)(2,1)}), s16[16,1712,128]{2,1,0:T(8,128)(2,1)}, u32[]{:S(2)}, u32[]{:S(2)}) %all-to-all-start) | async-done | bytes 7012384 | tf_op jit(solution)/shard_map/all_to_all | solution.py:506
  143.4 1.0 slice_convert_fusion
  144.5 31.0 %all-to-all-start.1 = ((s16[16,384,128]{2,1,0:T(8,128)(2,1)}), s16[16,384,128]{2,1,0:T(8,128)(2,1)S(1)}, u32[]{:S(2)}, u32[]{:S(2)}) async-start(s16[16,384,128]{2,1,0:T(8,128)(2,1)} %get-tuple-element.17), calls=%async_computation.1 | async-start | bytes 3145728 | tf_op jit(solution)/shard_map/all_to_all | solution.py:506
  175.5 1.0 convert_reduce_fusion
  176.6 0.3 select_reduce_fusion.3
  176.9 0.1 sub.13
  177.0 0.3 convert_reduce_fusion.1
  177.3 0.0 copy-done.1
  177.3 0.6 convert_reduce_fusion.3.fold_bound
  178.0 0.7 select_reduce_fusion.2.fold_list
  178.6 0.7 select_reduce_fusion.1.score_list
  179.3 0.1 select_reduce_fusion
  179.4 0.6 fusion.6.mods_in
  180.0 0.6 negate_select_fusion.signed_in
  180.6 18.7 %stage.2 = (f32[32,128]{1,0:T(8,128)}, f32[256,4096]{1,0:T(8,128)}, f32[256,256]{1,0:T(8,128)}, f32[33,128,128]{2,1,0:T(8,128)}, bf16[33,128,256]{2,1,0:T(8,128)(2,1)}, /*index=5*/bf16[208,128,128]{2,1,0:T(8,128)(2,1)}) custom-call(s32[256]{0:T(256)} %select_reduce_fusion.2.fold_list, s32[35]{0:T(128)} %convert_reduce_fusion.3.fold_bound, ...), custom_call_target="tpu_custom_call" | custom-call | flops 13958643712 | bytes 22020096 | tf_op jit(solution)/shard_map/stage/pallas_call | solution.py:409
  199.4 8.1 %all-to-all-done.1.x_hbm = s16[16,384,128]{2,1,0:T(8,128)(2,1)S(1)} async-done(((s16[16,384,128]{2,1,0:T(8,128)(2,1)}), s16[16,384,128]{2,1,0:T(8,128)(2,1)S(1)}, u32[]{:S(2)}, u32[]{:S(2)}) %all-to-all-start.1) | async-done | bytes 1572896 | tf_op jit(solution)/shard_map/all_to_all | solution.py:506
  207.5 1.1 copy-done
  208.6 6.2 %stage.3 = (f32[16,1,768]{2,1,0:T(1,128)}, f32[256,4096]{1,0:T(8,128)}) custom-call(s32[256]{0:T(256)} %select_reduce_fusion.2.fold_list, s32[35]{0:T(128)} %convert_reduce_fusion.3.fold_bound, s32[256]{0:T(256)} %select_reduce_fusion.1.score_list, f32[32,128]{1,0:T(8,128)} %fusion.6.mods_in, ...), custom_call_target="tpu_custom_call", output_to_operand_aliasing={{1}: (8, {})} | custom-call | flops 3221225472 | bytes 11534336 | tf_op jit(solution)/shard_map/stage/pallas_call | solution.py:409
  214.8 24.7 %all_to_all.15.got_ref = f32[16,1,768]{2,1,0:T(1,128)} all-to-all(f32[16,1,768]{2,1,0:T(1,128)} %get-tuple-element.24), channel_id=1, replica_groups=mesh['groups'=2,'dp'=16] {'dp'}, dimensions={0} | all-to-all | bytes 98304 | tf_op jit(solution)/shard_map/all_to_all | solution.py:506
  239.5 4.6 %close.1 = (bf16[512,2048]{1,0:T(8,128)(2,1)}, f32[2,128]{1,0:T(2,128)}) custom-call(s32[2,128]{1,0:T(2,128)} %bitcast.15, f32[16,1,768]{2,1,0:T(1,128)} %all_to_all.15.got_ref, f32[256,4096]{1,0:T(8,128)} %get-tuple-element.25.sums_hbm), custom_call_target="tpu_custom_call" | custom-call | flops 2097152 | bytes 6291456 | tf_op jit(solution)/shard_map/close/pallas_call | solution.py:486
  (13 shorter events, 0.1 us)
Async XLA Ops:
  9.2 134.2 %all-to-all-start = ((s16[16,1712,128]{2,1,0:T(8,128)(2,1)}), s16[16,1712,128]{2,1,0:T(8,128)(2,1)}, u32[]{:S(2)}, u32[]{:S(2)}) async-start(s16[16,1712,128]{2,1,0:T(8,128)(2,1)} %get-tuple-element.15), calls=%async_computation | async-start | bytes 14024704 | tf_op jit(solution)/shard_map/all_to_all | solution.py:506
  16.7 160.3 %copy-start.2 = (s32[256]{0:T(256)S(1)}, s32[256]{0:T(256)}, u32[]{:S(2)}) copy-start(s32[256]{0:T(256)} %constant.83.clone) | copy-start | bytes 3076
  16.7 160.6 %copy-start.1 = (s32[256]{0:T(256)S(1)}, s32[256]{0:T(256)}, u32[]{:S(2)}) copy-start(s32[256]{0:T(256)} %constant.84.clone) | copy-start | bytes 3076
  144.5 63.0 %all-to-all-start.1 = ((s16[16,384,128]{2,1,0:T(8,128)(2,1)}), s16[16,384,128]{2,1,0:T(8,128)(2,1)S(1)}, u32[]{:S(2)}, u32[]{:S(2)}) async-start(s16[16,384,128]{2,1,0:T(8,128)(2,1)} %get-tuple-element.17), calls=%async_computation.1 | async-start | bytes 3145728 | tf_op jit(solution)/shard_map/all_to_all | solution.py:506
  207.5 1.1 copy-start

commit v18 on v17

--- a/solution.py
+++ b/solution.py
@@ -25,6 +25,7 @@
 QUAD = 4
 EIGHT = 8
 CHUNK = 16
+BLOCKS = 4
 ROW_SHIFT, SOURCE_SHIFT = 16, 8
 PLACE_MASK, SOURCE_MASK, SLOT_MASK = 0xFFFF, 0xFF, 0xFF
 BATCH = 8
@@ -63,19 +64,15 @@
     parts = len(cuts) - 1
     (*told_refs, x_hbm), refs = refs[:5], refs[5:]
     outs = refs[:parts]
-    x, coded, square, sums, words, notes, held, rank_row, rank_ref, sems, x_sems = refs[parts:]
+    x, coded, square, sums, words, notes, rank_row, rank_ref, sems, x_sems = refs[parts:]
     tiles = x.shape[0]
-    devices = held.shape[0]
+    devices = coded.shape[0]
     blocks = square.shape[0]
     step = math.gcd(STEP_TILES, tiles)
 
     def read(c):
         some = pl.ds(c * step, step)
         return pltpu.make_async_copy(x_hbm.at[some], x.at[some], x_sems.at[c])
-
-    def clear(d, carry):
-        held[d] = 0
-        return carry
 
     for c in range(tiles // step):
         read(c).start()
@@ -87,7 +84,6 @@
     ahead = jnp.where(ahead & (other == own), 1.0, 0.0)
     rank_row[...] = jnp.sum(ahead, axis=0, keepdims=True).astype(jnp.int32)
     pltpu.sync_copy(rank_row, rank_ref)
-    lax.fori_loop(0, devices, clear, 0)
     square[...] = jnp.zeros_like(square)
 
     def some_tiles(i, carry):
@@ -98,32 +94,22 @@
             root = some * lax.rsqrt(some)
             code = (root * CODE_TOP + 0.5).astype(jnp.int32) - CODE_SHIFT
             owner, rank = owner_ref[t], rank_ref[0, t]
-            at = pl.ds(pl.multiple_of((owner * cuts[-1] + rank) * LANES, LANES), LANES)
-            coded[at, :] = code.astype(jnp.int16)
+            at = pl.ds(pl.multiple_of(rank * LANES, LANES), LANES)
+            coded[owner, at, :] = code.astype(jnp.int16)
             square[row_ref[t]] += some * some
-            held[owner] = jnp.maximum(held[owner], rank + 1)
         return carry
 
     lax.fori_loop(0, tiles // QUAD, some_tiles, 0)
 
-    def slots(q, d):
-        some = pl.ds((d * cuts[-1] + cuts[q]) * LANES, (cuts[q + 1] - cuts[q]) * LANES)
-        into = outs[q].at[d, pl.ds(0, (cuts[q + 1] - cuts[q]) * LANES)]
-        return pltpu.make_async_copy(coded.at[some], into, sems.at[q, d])
-
-    def note(d):
-        into = outs[0].at[d, pl.ds((cuts[1] - cuts[0]) * LANES, notes.shape[0])]
-        return pltpu.make_async_copy(notes, into, sems.at[parts, d])
-
-    def each(what):
-        def one(d, carry):
-            for q in range(parts):
-                pl.when(held[d] > cuts[q])(lambda q=q: what(slots(q, d)))
-            return carry
-
-        lax.fori_loop(0, devices, one, 0)
-
-    each(lambda copy: copy.start())
+    copies = []
+    for q in range(parts):
+        rows, count = (cuts[q + 1] - cuts[q]) * LANES, devices // (1 if q else math.gcd(4, devices))
+        for d in range(0, devices, count):
+            from_ref = coded.at[pl.ds(d, count), pl.ds(cuts[q] * LANES, rows)]
+            into = outs[q].at[pl.ds(d, count), pl.ds(0, rows)]
+            copies.append(pltpu.make_async_copy(from_ref, into, sems.at[len(copies)]))
+    for copy in copies:
+        copy.start()
     sums[...] = jnp.zeros_like(sums)
     block_sums(square, sums, blocks)
     total = sums[...]
@@ -136,13 +122,12 @@
     for told in (labels, owner, row * TB_OWN + sub):
         words[at : at + told.shape[0], :] = told
         at += told.shape[0]
-    notes[...] = words[...].astype(jnp.int16)
-
-    for d in range(devices):
-        note(d).start()
-    each(lambda copy: copy.wait())
-    for d in range(devices):
-        note(d).wait()
+    notes[...] = jnp.broadcast_to(words[...].astype(jnp.int16)[None], notes.shape)
+    into = outs[0].at[:, pl.ds((cuts[1] - cuts[0]) * LANES, notes.shape[1])]
+    copies.append(pltpu.make_async_copy(notes, into, sems.at[len(copies)]))
+    copies[-1].start()
+    for copy in copies:
+        copy.wait()
 
 
 def pack(tile_values, owner, tile_row, told, devices, blocks, cuts):
@@ -158,15 +143,14 @@
         out_shape=[jax.ShapeDtypeStruct((devices, some, LANES), jnp.int16) for some in rows],
         scratch_shapes=[
             pltpu.VMEM(tile_values.shape, jnp.float32),
-            pltpu.VMEM((devices * cuts[-1] * LANES, LANES), jnp.int16),
+            pltpu.VMEM((devices, cuts[-1] * LANES, LANES), jnp.int16),
             pltpu.VMEM((blocks, LANES, LANES), jnp.float32),
             pltpu.VMEM((blocks, LANES), jnp.float32),
             pltpu.VMEM((noted, LANES), jnp.int32),
-            pltpu.VMEM((noted, LANES), jnp.int16),
-            pltpu.SMEM((devices,), jnp.int32),
+            pltpu.VMEM((devices, noted, LANES), jnp.int16),
             pltpu.VMEM((1, tiles), jnp.int32),
             pltpu.SMEM((1, tiles), jnp.int32),
-            pltpu.SemaphoreType.DMA((len(rows) + 1, devices)),
+            pltpu.SemaphoreType.DMA((len(rows) + 4,)),
             pltpu.SemaphoreType.DMA((tiles // math.gcd(STEP_TILES, tiles),)),
         ],
         compiler_params=params(),
@@ -217,15 +201,15 @@
     def columns(sub):
         return (slice(None), pl.ds(pl.multiple_of(sub * 2 * LANES, 2 * LANES), 2 * LANES))
 
-    def sums_read(sub):
-        return pltpu.make_async_copy(
-            sums_in.at[columns(sub)], sums.at[columns(sub)], sub_sems.at[0, sub]
-        )
-
-    def sums_write(sub):
-        return pltpu.make_async_copy(
-            sums.at[columns(sub)], sums_out.at[columns(sub)], sub_sems.at[1, sub]
-        )
+    def group(g):
+        size = BLOCKS * 2 * LANES
+        return (slice(None), pl.ds(pl.multiple_of(g * size, size), size))
+
+    def sums_read(g):
+        return pltpu.make_async_copy(sums_in.at[group(g)], sums.at[group(g)], sub_sems.at[0, g])
+
+    def sums_write(g):
+        return pltpu.make_async_copy(sums.at[group(g)], sums_out.at[group(g)], sub_sems.at[1, g])
 
     def each_sub(low, high, what):
         def one(sub, carry):
@@ -235,7 +219,7 @@
         lax.fori_loop(low, high, one, 0)
 
     if q:
-        each_sub(begin, TB_OWN, lambda sub: sums_read(sub).start())
+        each_sub(begin // BLOCKS, TB_OWN // BLOCKS, lambda g: sums_read(g).start())
         squares[...] = squares_in[...]
     else:
         sums[...] = jnp.zeros_like(sums)
@@ -292,6 +276,8 @@
         lax.fori_loop(0, (none + 1) // batch, build, 0)
     for copy in needed:
         copy.wait()
+    if q:
+        each_sub(begin // BLOCKS, TB_OWN // BLOCKS, lambda g: sums_read(g).wait())
 
     def eight(entries, start, end, p):
         at = [start + EIGHT * p + j for j in range(EIGHT)]
@@ -300,9 +286,6 @@
 
     def fold_sub(sub):
         start, end = bound(q, sub), bound(q, sub + 1)
-        if q:
-            sums_read(sub).wait()
-
         def one_eight(p, carry):
             folded, picks = [], []
             for entry, spot, held in eight(fold_list, start, end, p):
@@ -327,9 +310,12 @@
             return carry
 
         lax.fori_loop(0, (end - start + EIGHT - 1) // EIGHT, one_eight, 0)
-        sums_write(sub).start()
-
-    each_sub(begin, TB_OWN, fold_sub)
+
+    def fold_group(g):
+        each_sub(jnp.maximum(begin, g * BLOCKS), (g + 1) * BLOCKS, fold_sub)
+        sums_write(g).start()
+
+    each_sub(begin // BLOCKS, TB_OWN // BLOCKS, fold_group)
     kept = []
     if not last:
         each_chunk(q, fresh_out, True, end, lambda copy: copy.start())
@@ -379,7 +365,7 @@
         copy.wait()
     if not last:
         each_chunk(q, fresh_out, True, end, lambda copy: copy.wait())
-    each_sub(begin, TB_OWN, lambda sub: sums_write(sub).wait())
+    each_sub(begin // BLOCKS, TB_OWN // BLOCKS, lambda g: sums_write(g).wait())
 
 
 def stage(q, cuts, scalars, mods, signed, x, normed, totals):
@@ -425,7 +411,7 @@
             pltpu.VMEM((blocks + 1, LANES), jnp.float32),
             pltpu.VMEM((blocks + 1, LANES), jnp.float32),
             pltpu.SemaphoreType.DMA((6,)),
-            pltpu.SemaphoreType.DMA((2, TB_OWN)),
+            pltpu.SemaphoreType.DMA((2, TB_OWN // BLOCKS)),
             pltpu.SemaphoreType.DMA((max(q, 1), chunks)),
         ],
         compiler_params=params(),

time: 245 us -> 244 us (level)
  no operation moved by 1% of the time
where the time goes in v18:
time: 244 us; the launch traced here: 242 us
  waiting for transfers between devices  135 us (55%)
  starting transfers between devices  38.4 us (16%)
  Pallas kernels  37.6 us (15%)
  blocking collectives  23.1 us (9%)
  other arithmetic  6.01 us (2%)
    all_to_all x2, waiting for transfers between devices, exchange(): return lax.all_to_all(x, 'dp', split_axis=0, concat_axis=0, tiled=True)  135 us
    all_to_all x2, starting transfers between devices, exchange(): return lax.all_to_all(x, 'dp', split_axis=0, concat_axis=0, tiled=True)  38.4 us
    pallas_call x2, Pallas kernels, stage(): pl.pallas_call(functools.partial(stage_kernel, q, [devices * cut for cut...  24.3 us
    all_to_all x1, blocking collectives, exchange(): return lax.all_to_all(x, 'dp', split_axis=0, concat_axis=0, tiled=True)  23.1 us
    pallas_call x1, Pallas kernels, pack(): pl.pallas_call(functools.partial(pack_kernel, cuts), in_specs=[SMEM] * 2...  8.65 us
  transfers between devices with their start and end apart: 2, of which 2 were waited for; matrix products, arithmetic and copies ran while one was open for 2% of the time, Pallas kernels for 8%

profile of v18, /device:TPU:0, one launch (start us, length us, event | category | flops | bytes accessed | tf_op | source)
XLA Modules:
  0.0 242.4 jit_solution(5376489029030767017)
XLA Ops:
  0.6 8.6 %pack.1 = (s16[16,1712,128]{2,1,0:T(8,128)(2,1)}, s16[16,384,128]{2,1,0:T(8,128)(2,1)}) custom-call(s32[128]{0:T(128)} %bitcast.16, s32[128]{0:T(128)} %row_ref.1, s32[2,128]{1,0:T(2,128)} %bitcast.14, s32[1,128]{1,0:T(1,128)} %bitcast.17, s32[1,128]{1,0:T(1,128)} %bitcast.18, s32[1,128]{1,0:T(1,128)} %bitcast.19, f32[128,128,128]{2,1,0:T(8,128)} %refs_4_.1), custom_call_target="tpu_custom_call" | custom-call | flops 16777216 | bytes 12582912 | tf_op jit(solution)/shard_map/pack/pallas_call | solution.py:139
  9.3 7.4 %all-to-all-start = ((s16[16,1712,128]{2,1,0:T(8,128)(2,1)}), s16[16,1712,128]{2,1,0:T(8,128)(2,1)}, u32[]{:S(2)}, u32[]{:S(2)}) async-start(s16[16,1712,128]{2,1,0:T(8,128)(2,1)} %get-tuple-element.15), calls=%async_computation | async-start | bytes 14024704 | tf_op jit(solution)/shard_map/all_to_all | solution.py:492
  16.7 0.0 copy-start.2
  16.7 0.0 copy-start.1
  16.8 126.7 %all-to-all-done.x_hbm = s16[16,1712,128]{2,1,0:T(8,128)(2,1)} async-done(((s16[16,1712,128]{2,1,0:T(8,128)(2,1)}), s16[16,1712,128]{2,1,0:T(8,128)(2,1)}, u32[]{:S(2)}, u32[]{:S(2)}) %all-to-all-start) | async-done | bytes 7012384 | tf_op jit(solution)/shard_map/all_to_all | solution.py:492
  143.5 1.0 slice_convert_fusion
  144.5 31.0 %all-to-all-start.1 = ((s16[16,384,128]{2,1,0:T(8,128)(2,1)}), s16[16,384,128]{2,1,0:T(8,128)(2,1)S(1)}, u32[]{:S(2)}, u32[]{:S(2)}) async-start(s16[16,384,128]{2,1,0:T(8,128)(2,1)} %get-tuple-element.17), calls=%async_computation.1 | async-start | bytes 3145728 | tf_op jit(solution)/shard_map/all_to_all | solution.py:492
  175.5 1.0 convert_reduce_fusion
  176.6 0.3 select_reduce_fusion.3
  177.0 0.1 sub.13
  177.0 0.0 copy-done.2
  177.1 0.3 convert_reduce_fusion.1
  177.4 0.6 convert_reduce_fusion.3.fold_bound
  178.0 0.7 select_reduce_fusion.2.fold_list
  178.7 0.7 select_reduce_fusion.1.score_list
  179.4 0.1 select_reduce_fusion
  179.5 0.6 fusion.6.mods_in
  180.1 0.6 negate_select_fusion.signed_in
  180.7 18.4 %stage.2 = (f32[32,128]{1,0:T(8,128)}, f32[256,4096]{1,0:T(8,128)}, f32[256,256]{1,0:T(8,128)}, f32[33,128,128]{2,1,0:T(8,128)}, bf16[33,128,256]{2,1,0:T(8,128)(2,1)}, /*index=5*/bf16[208,128,128]{2,1,0:T(8,128)(2,1)}) custom-call(s32[256]{0:T(256)} %select_reduce_fusion.2.fold_list, s32[35]{0:T(128)} %convert_reduce_fusion.3.fold_bound, ...), custom_call_target="tpu_custom_call" | custom-call | flops 13958643712 | bytes 22020096 | tf_op jit(solution)/shard_map/stage/pallas_call | solution.py:395
  199.0 8.4 %all-to-all-done.1.x_hbm = s16[16,384,128]{2,1,0:T(8,128)(2,1)S(1)} async-done(((s16[16,384,128]{2,1,0:T(8,128)(2,1)}), s16[16,384,128]{2,1,0:T(8,128)(2,1)S(1)}, u32[]{:S(2)}, u32[]{:S(2)}) %all-to-all-start.1) | async-done | bytes 1572896 | tf_op jit(solution)/shard_map/all_to_all | solution.py:492
  207.5 1.1 copy-done
  208.6 6.0 %stage.3 = (f32[16,1,768]{2,1,0:T(1,128)}, f32[256,4096]{1,0:T(8,128)}) custom-call(s32[256]{0:T(256)} %select_reduce_fusion.2.fold_list, s32[35]{0:T(128)} %convert_reduce_fusion.3.fold_bound, s32[256]{0:T(256)} %select_reduce_fusion.1.score_list, f32[32,128]{1,0:T(8,128)} %fusion.6.mods_in, ...), custom_call_target="tpu_custom_call", output_to_operand_aliasing={{1}: (8, {})} | custom-call | flops 3221225472 | bytes 11534336 | tf_op jit(solution)/shard_map/stage/pallas_call | solution.py:395
  214.6 23.1 %all_to_all.15.got_ref = f32[16,1,768]{2,1,0:T(1,128)} all-to-all(f32[16,1,768]{2,1,0:T(1,128)} %get-tuple-element.24), channel_id=1, replica_groups=mesh['groups'=2,'dp'=16] {'dp'}, dimensions={0} | all-to-all | bytes 98304 | tf_op jit(solution)/shard_map/all_to_all | solution.py:492
  237.8 4.6 %close.1 = (bf16[512,2048]{1,0:T(8,128)(2,1)}, f32[2,128]{1,0:T(2,128)}) custom-call(s32[2,128]{1,0:T(2,128)} %bitcast.15, f32[16,1,768]{2,1,0:T(1,128)} %all_to_all.15.got_ref, f32[256,4096]{1,0:T(8,128)} %get-tuple-element.25.sums_hbm), custom_call_target="tpu_custom_call" | custom-call | flops 2097152 | bytes 6291456 | tf_op jit(solution)/shard_map/close/pallas_call | solution.py:472
  (13 shorter events, 0.1 us)
Async XLA Ops:
  9.3 134.2 %all-to-all-start = ((s16[16,1712,128]{2,1,0:T(8,128)(2,1)}), s16[16,1712,128]{2,1,0:T(8,128)(2,1)}, u32[]{:S(2)}, u32[]{:S(2)}) async-start(s16[16,1712,128]{2,1,0:T(8,128)(2,1)} %get-tuple-element.15), calls=%async_computation | async-start | bytes 14024704 | tf_op jit(solution)/shard_map/all_to_all | solution.py:492
  16.7 160.3 %copy-start.2 = (s32[256]{0:T(256)S(1)}, s32[256]{0:T(256)}, u32[]{:S(2)}) copy-start(s32[256]{0:T(256)} %constant.83.clone) | copy-start | bytes 3076
  16.7 160.6 %copy-start.1 = (s32[256]{0:T(256)S(1)}, s32[256]{0:T(256)}, u32[]{:S(2)}) copy-start(s32[256]{0:T(256)} %constant.84.clone) | copy-start | bytes 3076
  144.5 63.0 %all-to-all-start.1 = ((s16[16,384,128]{2,1,0:T(8,128)(2,1)}), s16[16,384,128]{2,1,0:T(8,128)(2,1)S(1)}, u32[]{:S(2)}, u32[]{:S(2)}) async-start(s16[16,384,128]{2,1,0:T(8,128)(2,1)} %get-tuple-element.17), calls=%async_computation.1 | async-start | bytes 3145728 | tf_op jit(solution)/shard_map/all_to_all | solution.py:492
  207.5 1.1 copy-start

commit v19 on v18

--- a/solution.py
+++ b/solution.py
@@ -24,6 +24,7 @@
 CACHED_BLOCKS = 64
 QUAD = 4
 EIGHT = 8
+WIDE_SHIFT = 4
 CHUNK = 16
 BLOCKS = 4
 ROW_SHIFT, SOURCE_SHIFT = 16, 8
@@ -279,16 +280,27 @@
     if q:
         each_sub(begin // BLOCKS, TB_OWN // BLOCKS, lambda g: sums_read(g).wait())
 
-    def eight(entries, start, end, p):
-        at = [start + EIGHT * p + j for j in range(EIGHT)]
+    def steps(start, end, work):
+        wide = 2 * EIGHT
+        count = (end - start + EIGHT - 1) >> WIDE_SHIFT
+
+        def one(p, carry):
+            work(start + wide * p, wide)
+            return carry
+
+        lax.fori_loop(0, count, one, 0)
+        pl.when(start + wide * count < end)(lambda: work(start + wide * count, EIGHT))
+
+    def some(entries, start, end, count):
+        at = [start + j for j in range(count)]
         at = [(jnp.where(spot < end, spot, start), spot < end) for spot in at]
         return [(entries[spot], spot, held) for spot, held in at]
 
     def fold_sub(sub):
         start, end = bound(q, sub), bound(q, sub + 1)
-        def one_eight(p, carry):
+        def fold_some(first, count):
             folded, picks = [], []
-            for entry, spot, held in eight(fold_list, start, end, p):
+            for entry, spot, held in some(fold_list, first, end, count):
                 row = entry >> ROW_SHIFT
                 source, slot = (entry >> SOURCE_SHIFT) & SOURCE_MASK, entry & SLOT_MASK
                 raw = x[source, pl.ds(pl.multiple_of(slot * LANES, LANES), LANES), :]
@@ -307,9 +319,8 @@
             sums[columns(sub)] += jnp.dot(
                 pick, jnp.concatenate(folded, axis=0), preferred_element_type=jnp.float32
             )
-            return carry
-
-        lax.fori_loop(0, (end - start + EIGHT - 1) // EIGHT, one_eight, 0)
+
+        steps(start, end, fold_some)
 
     def fold_group(g):
         each_sub(jnp.maximum(begin, g * BLOCKS), (g + 1) * BLOCKS, fold_sub)
@@ -327,25 +338,24 @@
 
     def score_sub(sub):
         start, end = score_bound(sub), score_bound(sub + 1)
-        some = sums[columns(sub)]
-        narrow[...] = some.astype(jnp.bfloat16)
-        squares[...] += some * some
-
-        def one_eight(p, carry):
-            listed = eight(score_list, start, end, p)
+        own_sums = sums[columns(sub)]
+        narrow[...] = own_sums.astype(jnp.bfloat16)
+        squares[...] += own_sums * own_sums
+
+        def score_some(first, count):
+            listed = some(score_list, first, end, count)
             rows = [jnp.where(held, entry >> ROW_SHIFT, none) for entry, spot, held in listed]
             spots = [entry & PLACE_MASK for entry, spot, held in listed]
             hots = [hot[row] if cached else one_hot(row) for row in rows]
             chosen = jnp.dot(
                 jnp.concatenate(hots, axis=0), narrow[...], preferred_element_type=jnp.float32
             )
-            for j in range(EIGHT):
+            for j in range(count):
                 both = chosen[j * LANES : (j + 1) * LANES]
                 own = jnp.where(spread[rows[j]] < 0.0, both[:, LANES:], both[:, :LANES])
                 products[rows[j]] += own * tiles[spots[j]].astype(jnp.float32)
-            return carry
-
-        lax.fori_loop(0, (end - start + EIGHT - 1) // EIGHT, one_eight, 0)
+
+        steps(start, end, score_some)
 
     each_sub(begin, end, score_sub)
     block_sums(products, scores, none)

time: 244 us -> 242 us (level)
  Pallas kernels: 37.6 us -> 44.7 us
  waiting for transfers between devices: 135 us -> 128 us
    all_to_all x2, waiting for transfers between devices: 135 us -> 128 us  [exchange(): return lax.all_to_all(x, 'dp', split_axis=0, concat_axis=0, tiled=True)]
    pallas_call x2, Pallas kernels: 24.3 us -> 31.4 us  [stage(): pl.pallas_call(functools.partial(stage_kernel, q, [devices * cut for cut...]
  transfers between devices with their start and end apart: 2 -> 2, of which waited for: 2 -> 2; matrix products, arithmetic and copies ran while one was open for 2% -> 2% of each run, Pallas kernels for 8% -> 11%
where the time goes in v19:
time: 242 us; the launch traced here: 241 us
  waiting for transfers between devices  128 us (53%)
  Pallas kernels  44.7 us (18%)
  starting transfers between devices  38.4 us (16%)
  blocking collectives  21.3 us (9%)
  other arithmetic  6.01 us (2%)
    all_to_all x2, waiting for transfers between devices, exchange(): return lax.all_to_all(x, 'dp', split_axis=0, concat_axis=0, tiled=True)  128 us
    all_to_all x2, starting transfers between devices, exchange(): return lax.all_to_all(x, 'dp', split_axis=0, concat_axis=0, tiled=True)  38.4 us
    pallas_call x2, Pallas kernels, stage(): pl.pallas_call(functools.partial(stage_kernel, q, [devices * cut for cut...  31.4 us
    all_to_all x1, blocking collectives, exchange(): return lax.all_to_all(x, 'dp', split_axis=0, concat_axis=0, tiled=True)  21.3 us
    pallas_call x1, Pallas kernels, pack(): pl.pallas_call(functools.partial(pack_kernel, cuts), in_specs=[SMEM] * 2...  8.65 us
  transfers between devices with their start and end apart: 2, of which 2 were waited for; matrix products, arithmetic and copies ran while one was open for 2% of the time, Pallas kernels for 11%

profile of v19, /device:TPU:0, one launch (start us, length us, event | category | flops | bytes accessed | tf_op | source)
XLA Modules:
  0.0 240.5 jit_solution(8932770655958724484)
XLA Ops:
  0.6 8.6 %pack.1 = (s16[16,1712,128]{2,1,0:T(8,128)(2,1)}, s16[16,384,128]{2,1,0:T(8,128)(2,1)}) custom-call(s32[128]{0:T(128)} %bitcast.16, s32[128]{0:T(128)} %row_ref.1, s32[2,128]{1,0:T(2,128)} %bitcast.14, s32[1,128]{1,0:T(1,128)} %bitcast.17, s32[1,128]{1,0:T(1,128)} %bitcast.18, s32[1,128]{1,0:T(1,128)} %bitcast.19, f32[128,128,128]{2,1,0:T(8,128)} %refs_4_.1), custom_call_target="tpu_custom_call" | custom-call | flops 16777216 | bytes 12582912 | tf_op jit(solution)/shard_map/pack/pallas_call | solution.py:140
  9.3 7.4 %all-to-all-start = ((s16[16,1712,128]{2,1,0:T(8,128)(2,1)}), s16[16,1712,128]{2,1,0:T(8,128)(2,1)}, u32[]{:S(2)}, u32[]{:S(2)}) async-start(s16[16,1712,128]{2,1,0:T(8,128)(2,1)} %get-tuple-element.15), calls=%async_computation | async-start | bytes 14024704 | tf_op jit(solution)/shard_map/all_to_all | solution.py:502
  16.7 0.0 copy-start.2
  16.7 0.0 copy-start.1
  16.8 126.7 %all-to-all-done.x_hbm = s16[16,1712,128]{2,1,0:T(8,128)(2,1)} async-done(((s16[16,1712,128]{2,1,0:T(8,128)(2,1)}), s16[16,1712,128]{2,1,0:T(8,128)(2,1)}, u32[]{:S(2)}, u32[]{:S(2)}) %all-to-all-start) | async-done | bytes 7012384 | tf_op jit(solution)/shard_map/all_to_all | solution.py:502
  143.5 1.0 slice_convert_fusion
  144.5 31.0 %all-to-all-start.1 = ((s16[16,384,128]{2,1,0:T(8,128)(2,1)}), s16[16,384,128]{2,1,0:T(8,128)(2,1)S(1)}, u32[]{:S(2)}, u32[]{:S(2)}) async-start(s16[16,384,128]{2,1,0:T(8,128)(2,1)} %get-tuple-element.17), calls=%async_computation.1 | async-start | bytes 3145728 | tf_op jit(solution)/shard_map/all_to_all | solution.py:502
  175.5 1.0 convert_reduce_fusion
  176.6 0.3 select_reduce_fusion.3
  177.0 0.1 sub.13
  177.0 0.0 copy-done.2
  177.1 0.3 convert_reduce_fusion.1
  177.4 0.6 convert_reduce_fusion.3.fold_bound
  178.0 0.7 select_reduce_fusion.2.fold_list
  178.7 0.7 select_reduce_fusion.1.score_list
  179.4 0.1 select_reduce_fusion
  179.5 0.6 fusion.6.mods_in
  180.1 0.6 negate_select_fusion.signed_in
  180.7 25.4 %stage.2 = (f32[32,128]{1,0:T(8,128)}, f32[256,4096]{1,0:T(8,128)}, f32[256,256]{1,0:T(8,128)}, f32[33,128,128]{2,1,0:T(8,128)}, bf16[33,128,256]{2,1,0:T(8,128)(2,1)}, /*index=5*/bf16[208,128,128]{2,1,0:T(8,128)(2,1)}) custom-call(s32[256]{0:T(256)} %select_reduce_fusion.2.fold_list, s32[35]{0:T(128)} %convert_reduce_fusion.3.fold_bound, ...), custom_call_target="tpu_custom_call" | custom-call | flops 13958643712 | bytes 22020096 | tf_op jit(solution)/shard_map/stage/pallas_call | solution.py:405
  206.1 1.4 all-to-all-done.1.x_hbm
  207.5 1.1 copy-done
  208.6 6.0 %stage.3 = (f32[16,1,768]{2,1,0:T(1,128)}, f32[256,4096]{1,0:T(8,128)}) custom-call(s32[256]{0:T(256)} %select_reduce_fusion.2.fold_list, s32[35]{0:T(128)} %convert_reduce_fusion.3.fold_bound, s32[256]{0:T(256)} %select_reduce_fusion.1.score_list, f32[32,128]{1,0:T(8,128)} %fusion.6.mods_in, ...), custom_call_target="tpu_custom_call", output_to_operand_aliasing={{1}: (8, {})} | custom-call | flops 3221225472 | bytes 11534336 | tf_op jit(solution)/shard_map/stage/pallas_call | solution.py:405
  214.6 21.3 %all_to_all.15.got_ref = f32[16,1,768]{2,1,0:T(1,128)} all-to-all(f32[16,1,768]{2,1,0:T(1,128)} %get-tuple-element.24), channel_id=1, replica_groups=mesh['groups'=2,'dp'=16] {'dp'}, dimensions={0} | all-to-all | bytes 98304 | tf_op jit(solution)/shard_map/all_to_all | solution.py:502
  235.9 4.6 %close.1 = (bf16[512,2048]{1,0:T(8,128)(2,1)}, f32[2,128]{1,0:T(2,128)}) custom-call(s32[2,128]{1,0:T(2,128)} %bitcast.15, f32[16,1,768]{2,1,0:T(1,128)} %all_to_all.15.got_ref, f32[256,4096]{1,0:T(8,128)} %get-tuple-element.25.sums_hbm), custom_call_target="tpu_custom_call" | custom-call | flops 2097152 | bytes 6291456 | tf_op jit(solution)/shard_map/close/pallas_call | solution.py:482
  (13 shorter events, 0.1 us)
Async XLA Ops:
  9.3 134.2 %all-to-all-start = ((s16[16,1712,128]{2,1,0:T(8,128)(2,1)}), s16[16,1712,128]{2,1,0:T(8,128)(2,1)}, u32[]{:S(2)}, u32[]{:S(2)}) async-start(s16[16,1712,128]{2,1,0:T(8,128)(2,1)} %get-tuple-element.15), calls=%async_computation | async-start | bytes 14024704 | tf_op jit(solution)/shard_map/all_to_all | solution.py:502
  16.7 160.3 %copy-start.2 = (s32[256]{0:T(256)S(1)}, s32[256]{0:T(256)}, u32[]{:S(2)}) copy-start(s32[256]{0:T(256)} %constant.83.clone) | copy-start | bytes 3076
  16.7 160.6 %copy-start.1 = (s32[256]{0:T(256)S(1)}, s32[256]{0:T(256)}, u32[]{:S(2)}) copy-start(s32[256]{0:T(256)} %constant.84.clone) | copy-start | bytes 3076
  144.5 63.0 %all-to-all-start.1 = ((s16[16,384,128]{2,1,0:T(8,128)(2,1)}), s16[16,384,128]{2,1,0:T(8,128)(2,1)S(1)}, u32[]{:S(2)}, u32[]{:S(2)}) async-start(s16[16,384,128]{2,1,0:T(8,128)(2,1)} %get-tuple-element.17), calls=%async_computation.1 | async-start | bytes 3145728 | tf_op jit(solution)/shard_map/all_to_all | solution.py:502
  207.5 1.1 copy-start

commit v20 on v19

--- a/solution.py
+++ b/solution.py
@@ -426,9 +426,7 @@
         ],
         compiler_params=params(),
         cost_estimate=pl.CostEstimate(
-            flops=devices * width * LANES * LANES * K * 8,
-            bytes_accessed=4 * devices * width * LANES * LANES + 8 * K * TB_OWN * LANES,
-            transcendentals=0,
+            flops=devices * width * LANES * LANES * K, bytes_accessed=wide.size, transcendentals=0
         ),
         name="stage",
     )(*operands)
@@ -476,7 +474,7 @@
 
 
 def close(labels, got, sums, vocab_size):
-    groups = 4
+    groups = 8
     labels = labels.reshape(-1, LANES)
     wide = jax.ShapeDtypeStruct((K, TB_OWN * LANES), jnp.bfloat16)
     centroids, similarity = pl.pallas_call(

time: 242 us -> 241 us (level)
  Pallas kernels: 44.7 us -> 39 us
  waiting for transfers between devices: 128 us -> 133 us
    pallas_call x2, Pallas kernels: 31.4 us -> 25.6 us  [stage(): pl.pallas_call(functools.partial(stage_kernel, q, [devices * cut for cut...]
    all_to_all x2, waiting for transfers between devices: 128 us -> 133 us  [exchange(): return lax.all_to_all(x, 'dp', split_axis=0, concat_axis=0, tiled=True)]
  transfers between devices with their start and end apart: 2 -> 2, of which waited for: 2 -> 2; matrix products, arithmetic and copies ran while one was open for 2% -> 3% of each run, Pallas kernels for 11% -> 8%
where the time goes in v20:
time: 241 us
  waiting for transfers between devices  133 us (55%)
  Pallas kernels  39 us (16%)
  starting transfers between devices  38.4 us (16%)
  blocking collectives  22.3 us (9%)
  other arithmetic  6.01 us (2%)
    all_to_all x2, waiting for transfers between devices, exchange(): return lax.all_to_all(x, 'dp', split_axis=0, concat_axis=0, tiled=True)  133 us
    all_to_all x2, starting transfers between devices, exchange(): return lax.all_to_all(x, 'dp', split_axis=0, concat_axis=0, tiled=True)  38.4 us
    pallas_call x2, Pallas kernels, stage(): pl.pallas_call(functools.partial(stage_kernel, q, [devices * cut for cut...  25.6 us
    all_to_all x1, blocking collectives, exchange(): return lax.all_to_all(x, 'dp', split_axis=0, concat_axis=0, tiled=True)  22.3 us
    pallas_call x1, Pallas kernels, pack(): pl.pallas_call(functools.partial(pack_kernel, cuts), in_specs=[SMEM] * 2...  8.65 us
  transfers between devices with their start and end apart: 2, of which 2 were waited for; matrix products, arithmetic and copies ran while one was open for 3% of the time, Pallas kernels for 8%

profile of v20, /device:TPU:0, one launch (start us, length us, event | category | flops | bytes accessed | tf_op | source)
XLA Modules:
  0.0 240.6 jit_solution(5440509283020280780)
XLA Ops:
  0.6 8.6 %pack.1 = (s16[16,1712,128]{2,1,0:T(8,128)(2,1)}, s16[16,384,128]{2,1,0:T(8,128)(2,1)}) custom-call(s32[128]{0:T(128)} %bitcast.16, s32[128]{0:T(128)} %row_ref.1, s32[2,128]{1,0:T(2,128)} %bitcast.14, s32[1,128]{1,0:T(1,128)} %bitcast.17, s32[1,128]{1,0:T(1,128)} %bitcast.18, s32[1,128]{1,0:T(1,128)} %bitcast.19, f32[128,128,128]{2,1,0:T(8,128)} %refs_4_.1), custom_call_target="tpu_custom_call" | custom-call | flops 16777216 | bytes 12582912 | tf_op jit(solution)/shard_map/pack/pallas_call | solution.py:140
  9.3 7.4 %all-to-all-start = ((s16[16,1712,128]{2,1,0:T(8,128)(2,1)}), s16[16,1712,128]{2,1,0:T(8,128)(2,1)}, u32[]{:S(2)}, u32[]{:S(2)}) async-start(s16[16,1712,128]{2,1,0:T(8,128)(2,1)} %get-tuple-element.15), calls=%async_computation | async-start | bytes 14024704 | tf_op jit(solution)/shard_map/all_to_all | solution.py:500
  16.7 0.0 copy-start.2
  16.7 0.0 copy-start.1
  16.7 126.7 %all-to-all-done.x_hbm = s16[16,1712,128]{2,1,0:T(8,128)(2,1)} async-done(((s16[16,1712,128]{2,1,0:T(8,128)(2,1)}), s16[16,1712,128]{2,1,0:T(8,128)(2,1)}, u32[]{:S(2)}, u32[]{:S(2)}) %all-to-all-start) | async-done | bytes 7012384 | tf_op jit(solution)/shard_map/all_to_all | solution.py:500
  143.5 31.0 %all-to-all-start.1 = ((s16[16,384,128]{2,1,0:T(8,128)(2,1)}), s16[16,384,128]{2,1,0:T(8,128)(2,1)S(1)}, u32[]{:S(2)}, u32[]{:S(2)}) async-start(s16[16,384,128]{2,1,0:T(8,128)(2,1)} %get-tuple-element.17), calls=%async_computation.1 | async-start | bytes 3145728 | tf_op jit(solution)/shard_map/all_to_all | solution.py:500
  174.4 1.0 slice_convert_fusion
  175.6 1.0 convert_reduce_fusion
  176.6 0.3 select_reduce_fusion.3
  177.0 0.1 sub.13
  177.1 0.3 convert_reduce_fusion.1
  177.4 0.0 copy-done.1
  177.4 0.6 convert_reduce_fusion.3.fold_bound
  178.0 0.7 select_reduce_fusion.2.fold_list
  178.7 0.7 select_reduce_fusion.1.score_list
  179.4 0.1 select_reduce_fusion
  179.5 0.6 fusion.6.mods_in
  180.1 0.6 negate_select_fusion.signed_in
  180.7 19.7 %stage.2 = (f32[32,128]{1,0:T(8,128)}, f32[256,4096]{1,0:T(8,128)}, f32[256,256]{1,0:T(8,128)}, f32[33,128,128]{2,1,0:T(8,128)}, bf16[33,128,256]{2,1,0:T(8,128)(2,1)}, /*index=5*/bf16[208,128,128]{2,1,0:T(8,128)(2,1)}) custom-call(s32[256]{0:T(256)} %select_reduce_fusion.2.fold_list, s32[35]{0:T(128)} %convert_reduce_fusion.3.fold_bound, ...), custom_call_target="tpu_custom_call" | custom-call | flops 1744830464 | bytes 1048576 | tf_op jit(solution)/shard_map/stage/pallas_call | solution.py:405
  200.4 6.0 %all-to-all-done.1.x_hbm = s16[16,384,128]{2,1,0:T(8,128)(2,1)S(1)} async-done(((s16[16,384,128]{2,1,0:T(8,128)(2,1)}), s16[16,384,128]{2,1,0:T(8,128)(2,1)S(1)}, u32[]{:S(2)}, u32[]{:S(2)}) %all-to-all-start.1) | async-done | bytes 1572896 | tf_op jit(solution)/shard_map/all_to_all | solution.py:500
  206.4 1.1 copy-done
  207.5 6.0 %stage.3 = (f32[16,1,768]{2,1,0:T(1,128)}, f32[256,4096]{1,0:T(8,128)}) custom-call(s32[256]{0:T(256)} %select_reduce_fusion.2.fold_list, s32[35]{0:T(128)} %convert_reduce_fusion.3.fold_bound, s32[256]{0:T(256)} %select_reduce_fusion.1.score_list, f32[32,128]{1,0:T(8,128)} %fusion.6.mods_in, ...), custom_call_target="tpu_custom_call", output_to_operand_aliasing={{1}: (8, {})} | custom-call | flops 402653184 | bytes 1048576 | tf_op jit(solution)/shard_map/stage/pallas_call | solution.py:405
  213.5 22.3 %all_to_all.15.got_ref = f32[16,1,768]{2,1,0:T(1,128)} all-to-all(f32[16,1,768]{2,1,0:T(1,128)} %get-tuple-element.24), channel_id=1, replica_groups=mesh['groups'=2,'dp'=16] {'dp'}, dimensions={0} | all-to-all | bytes 98304 | tf_op jit(solution)/shard_map/all_to_all | solution.py:500
  235.9 4.7 %close.1 = (bf16[512,2048]{1,0:T(8,128)(2,1)}, f32[2,128]{1,0:T(2,128)}) custom-call(s32[2,128]{1,0:T(2,128)} %bitcast.15, f32[16,1,768]{2,1,0:T(1,128)} %all_to_all.15.got_ref, f32[256,4096]{1,0:T(8,128)} %get-tuple-element.25.sums_hbm), custom_call_target="tpu_custom_call" | custom-call | flops 2097152 | bytes 6291456 | tf_op jit(solution)/shard_map/close/pallas_call | solution.py:480
  (13 shorter events, 0.1 us)
Async XLA Ops:
  9.3 134.2 %all-to-all-start = ((s16[16,1712,128]{2,1,0:T(8,128)(2,1)}), s16[16,1712,128]{2,1,0:T(8,128)(2,1)}, u32[]{:S(2)}, u32[]{:S(2)}) async-start(s16[16,1712,128]{2,1,0:T(8,128)(2,1)} %get-tuple-element.15), calls=%async_computation | async-start | bytes 14024704 | tf_op jit(solution)/shard_map/all_to_all | solution.py:500
  16.7 160.3 %copy-start.2 = (s32[256]{0:T(256)S(1)}, s32[256]{0:T(256)}, u32[]{:S(2)}) copy-start(s32[256]{0:T(256)} %constant.83.clone) | copy-start | bytes 3076
  16.7 160.6 %copy-start.1 = (s32[256]{0:T(256)S(1)}, s32[256]{0:T(256)}, u32[]{:S(2)}) copy-start(s32[256]{0:T(256)} %constant.84.clone) | copy-start | bytes 3076
  143.5 62.9 %all-to-all-start.1 = ((s16[16,384,128]{2,1,0:T(8,128)(2,1)}), s16[16,384,128]{2,1,0:T(8,128)(2,1)S(1)}, u32[]{:S(2)}, u32[]{:S(2)}) async-start(s16[16,384,128]{2,1,0:T(8,128)(2,1)} %get-tuple-element.17), calls=%async_computation.1 | async-start | bytes 3145728 | tf_op jit(solution)/shard_map/all_to_all | solution.py:500
  206.4 1.1 copy-start

commit v21 on v20

--- a/solution.py
+++ b/solution.py
@@ -61,11 +61,12 @@
     return pltpu.CompilerParams(vmem_limit_bytes=VMEM_BYTES)
 
 
-def pack_kernel(cuts, owner_ref, row_ref, *refs):
+def pack_kernel(cuts, owner_hbm, row_hbm, *refs):
     parts = len(cuts) - 1
-    (*told_refs, x_hbm), refs = refs[:5], refs[5:]
+    (*told_hbms, x_hbm), refs = refs[:5], refs[5:]
     outs = refs[:parts]
-    x, coded, square, sums, words, notes, rank_row, rank_ref, sems, x_sems = refs[parts:]
+    x, coded, square, sums, words, notes, rank_row, rank_ref, *refs = refs[parts:]
+    owner_ref, row_ref, *told_refs, sems, x_sems, small_sems = refs
     tiles = x.shape[0]
     devices = coded.shape[0]
     blocks = square.shape[0]
@@ -77,6 +78,12 @@
 
     for c in range(tiles // step):
         read(c).start()
+    pairs = zip((owner_hbm, row_hbm, *told_hbms), (owner_ref, row_ref, *told_refs))
+    small = [pltpu.make_async_copy(*pair, small_sems.at[i]) for i, pair in enumerate(pairs)]
+    for copy in small:
+        copy.start()
+    for copy in small:
+        copy.wait()
     labels, owner, row, sub = [ref[...] for ref in told_refs]
     own, sub_own = [jnp.broadcast_to(v.astype(jnp.float32), (tiles, tiles)) for v in (owner, sub)]
     other, sub_other = jnp.transpose(own), jnp.transpose(sub_own)
@@ -139,7 +146,7 @@
     rows[0] += noted
     return pl.pallas_call(
         functools.partial(pack_kernel, cuts),
-        in_specs=[SMEM] * 2 + [VMEM] * 4 + [ANY],
+        in_specs=[ANY] * 7,
         out_specs=[ANY] * len(rows),
         out_shape=[jax.ShapeDtypeStruct((devices, some, LANES), jnp.int16) for some in rows],
         scratch_shapes=[
@@ -151,8 +158,12 @@
             pltpu.VMEM((devices, noted, LANES), jnp.int16),
             pltpu.VMEM((1, tiles), jnp.int32),
             pltpu.SMEM((1, tiles), jnp.int32),
+            pltpu.SMEM((tiles,), jnp.int32),
+            pltpu.SMEM((tiles,), jnp.int32),
+            *[pltpu.VMEM(some.shape, jnp.int32) for some in told],
             pltpu.SemaphoreType.DMA((len(rows) + 4,)),
             pltpu.SemaphoreType.DMA((tiles // math.gcd(STEP_TILES, tiles),)),
+            pltpu.SemaphoreType.DMA((6,)),
         ],
         compiler_params=params(),
         cost_estimate=pl.CostEstimate(
@@ -164,7 +175,7 @@
     )(owner, tile_row, *told, tile_values)
 
 
-def stage_kernel(q, bases, last, cached, fold_list, fold_bound, score_list,
+def stage_kernel(q, bases, last, cached, fold_list_in, fold_bound_in, score_list_in,
                  mods_in, signed_in, x_hbm, *refs):
     base = bases[q]
     earlier, refs = refs[:q], refs[q:]
@@ -173,9 +184,24 @@
     part, sums_out, refs = refs[0], refs[1], refs[2:]
     (squares_out, *made_out, fresh_out), refs = ((None,) * 4, refs) if last else (refs[:4], refs[4:])
     spread, x, hot, sums, narrow, tiles, products, scores, squares, mods, signed, *refs = refs
-    sems, sub_sems, tile_sems = refs
+    fold_list, fold_bound, score_list, sems, sub_sems, tile_sems, small_sems = refs
     devices, width = x.shape[0], x.shape[1] // LANES
     none = products.shape[0] - 1
+    needed = [pltpu.make_async_copy(x_hbm.at[:, pl.ds(0, width * LANES)], x, sems.at[0])]
+    if q:
+        needed.append(pltpu.make_async_copy(made_in[0], spread, sems.at[1]))
+    for copy in needed:
+        copy.start()
+    for held, empty in ((mods, -1.0), (signed, 0.0)):
+        held[none : none + 1, :] = jnp.full((1, LANES), empty, jnp.float32)
+    pairs = [(fold_list_in, fold_list), (fold_bound_in, fold_bound), (score_list_in, score_list)]
+    pairs += [(mods_in, mods.at[pl.ds(0, none)]), (signed_in, signed.at[pl.ds(0, none)])]
+    pairs += [(before, scores), (squares_in, squares)] if q else []
+    small = [pltpu.make_async_copy(*pair, small_sems.at[i]) for i, pair in enumerate(pairs)]
+    for copy in small:
+        copy.start()
+    for copy in small:
+        copy.wait()
     parts = len(bases) - 1
 
     def bound(p, sub):
@@ -193,11 +219,6 @@
         return lax.fori_loop(0, TB_OWN, one, TB_OWN) if arrived < parts else TB_OWN
 
     begin, end = complete(q) if q else 0, complete(q + 1)
-    needed = [pltpu.make_async_copy(x_hbm.at[:, pl.ds(0, width * LANES)], x, sems.at[0])]
-    if q:
-        needed.append(pltpu.make_async_copy(made_in[0], spread, sems.at[1]))
-    for copy in needed:
-        copy.start()
 
     def columns(sub):
         return (slice(None), pl.ds(pl.multiple_of(sub * 2 * LANES, 2 * LANES), 2 * LANES))
@@ -221,8 +242,8 @@
 
     if q:
         each_sub(begin // BLOCKS, TB_OWN // BLOCKS, lambda g: sums_read(g).start())
-        squares[...] = squares_in[...]
     else:
+        scores[...] = jnp.zeros_like(scores)
         sums[...] = jnp.zeros_like(sums)
         squares[...] = jnp.zeros_like(squares)
     later = [pltpu.make_async_copy(made_in[1], hot, sems.at[3])] if q and cached else []
@@ -247,10 +268,6 @@
 
     each_earlier(lambda copy: copy.start())
     products[...] = jnp.zeros_like(products)
-    scores[...] = before[...] if q else jnp.zeros_like(scores)
-    for held, given, empty in ((mods, mods_in, -1.0), (signed, signed_in, 0.0)):
-        held[:none, :] = given[...]
-        held[none : none + 1, :] = jnp.full((1, LANES), empty, jnp.float32)
     cluster = lax.broadcasted_iota(jnp.int32, (HALF, LANES), 0).astype(jnp.float32)
     cluster = cluster.astype(jnp.bfloat16).reshape(HALF // 16, 16, LANES)
     one, zero = jnp.ones((), jnp.bfloat16), jnp.zeros((), jnp.bfloat16)
@@ -404,7 +421,7 @@
     operands = [*scalars, mods, signed, x, *normed, *totals]
     return pl.pallas_call(
         functools.partial(stage_kernel, q, [devices * cut for cut in cuts], last, cached),
-        in_specs=[SMEM] * len(scalars) + [VMEM] * 2 + [ANY] * (1 + q) + [VMEM, ANY, VMEM, ANY, ANY][: len(totals)],
+        in_specs=[ANY] * len(operands),
         out_specs=[VMEM, ANY, VMEM, ANY, ANY, ANY][: len(out_shape)],
         out_shape=out_shape,
         input_output_aliases={len(operands) - len(totals) + 1: 1} if q else {},
@@ -420,9 +437,11 @@
             pltpu.VMEM(square.shape, jnp.float32),
             pltpu.VMEM((blocks + 1, LANES), jnp.float32),
             pltpu.VMEM((blocks + 1, LANES), jnp.float32),
+            *[pltpu.SMEM(some.shape, jnp.int32) for some in scalars],
             pltpu.SemaphoreType.DMA((6,)),
             pltpu.SemaphoreType.DMA((2, TB_OWN // BLOCKS)),
             pltpu.SemaphoreType.DMA((max(q, 1), chunks)),
+            pltpu.SemaphoreType.DMA((7,)),
         ],
         compiler_params=params(),
         cost_estimate=pl.CostEstimate(
@@ -432,15 +451,24 @@
     )(*operands)
 
 
-def close_kernel(root, groups, labels_ref, got_ref, sums_hbm, out_hbm, similarity, sums, out, sems):
+def close_kernel(root, groups, labels_hbm, got_hbm, sums_hbm, out_hbm, similarity_hbm, labels_ref,
+                 got_ref, similarity, sums, out, sems, small_sems):
     width = TB_OWN // groups
     reads, writes = [], []
+    small = [
+        pltpu.make_async_copy(got_hbm, got_ref, small_sems.at[0]),
+        pltpu.make_async_copy(labels_hbm, labels_ref, small_sems.at[1]),
+    ]
+    for copy in small:
+        copy.start()
     for g in range(groups):
         some = (slice(None), pl.ds(g * width * 2 * LANES, width * 2 * LANES))
         reads.append(pltpu.make_async_copy(sums_hbm.at[some], sums.at[some], sems.at[0, g]))
         some = (slice(None), pl.ds(g * width * LANES, width * LANES))
         writes.append(pltpu.make_async_copy(out.at[some], out_hbm.at[some], sems.at[1, g]))
         reads[g].start()
+    for copy in small:
+        copy.wait()
     total = jnp.sum(got_ref[...], axis=0)
     home = total.shape[1] - K
     own = lax.rsqrt(total[:, home:] + EPSILON)
@@ -455,6 +483,8 @@
             found += jnp.where(cluster + i * LANES == labels_ref[b : b + 1, :], column, 0.0)
         found = jnp.sum(found, axis=0, keepdims=True)
         similarity[b : b + 1, :] = total[:, b * LANES : (b + 1) * LANES] * found
+    writes.append(pltpu.make_async_copy(similarity, similarity_hbm, small_sems.at[2]))
+    writes[-1].start()
     for g in range(groups):
         reads[g].wait()
 
@@ -474,18 +504,22 @@
 
 
 def close(labels, got, sums, vocab_size):
-    groups = 8
+    groups = 4
     labels = labels.reshape(-1, LANES)
     wide = jax.ShapeDtypeStruct((K, TB_OWN * LANES), jnp.bfloat16)
     centroids, similarity = pl.pallas_call(
         functools.partial(close_kernel, math.sqrt(vocab_size), groups),
-        in_specs=[VMEM, VMEM, ANY],
-        out_specs=[ANY, VMEM],
+        in_specs=[ANY] * 3,
+        out_specs=[ANY] * 2,
         out_shape=[wide, jax.ShapeDtypeStruct(labels.shape, jnp.float32)],
         scratch_shapes=[
+            pltpu.VMEM(labels.shape, jnp.int32),
+            pltpu.VMEM(got.shape, jnp.float32),
+            pltpu.VMEM(labels.shape, jnp.float32),
             pltpu.VMEM(sums.shape, jnp.float32),
             pltpu.VMEM(wide.shape, jnp.bfloat16),
             pltpu.SemaphoreType.DMA((2, groups)),
+            pltpu.SemaphoreType.DMA((3,)),
         ],
         compiler_params=params(),
         cost_estimate=pl.CostEstimate(
@@ -512,7 +546,7 @@
     position = jnp.sum(ahead.astype(jnp.int32), axis=1)
     here = position[None, :] == slots[:, None]
     listed = jnp.sum(jnp.where(here, entries[None, :], 0), axis=1)
-    levels = jnp.arange(top + 1, dtype=jnp.int32)
+    levels = jnp.arange(-(-(top + 1) // LANES) * LANES, dtype=jnp.int32)
     bounds = jnp.sum((key[None, :] < levels[:, None]).astype(jnp.int32), axis=1)
     return listed, bounds, position
 

time: 241 us -> 242 us (level)
  transfers between devices with their start and end apart: 2 -> 2, of which waited for: 2 -> 2; matrix products, arithmetic and copies ran while one was open for 3% -> 3% of each run, Pallas kernels for 8% -> 9%
where the time goes in v21:
time: 242 us; the launch traced here: 241 us
  waiting for transfers between devices  132 us (55%)
  Pallas kernels  40.7 us (17%)
  starting transfers between devices  38.4 us (16%)
  blocking collectives  21.8 us (9%)
  other arithmetic  6.01 us (2%)
    all_to_all x2, waiting for transfers between devices, exchange(): return lax.all_to_all(x, 'dp', split_axis=0, concat_axis=0, tiled=True)  132 us
    all_to_all x2, starting transfers between devices, exchange(): return lax.all_to_all(x, 'dp', split_axis=0, concat_axis=0, tiled=True)  38.4 us
    pallas_call x2, Pallas kernels, stage(): pl.pallas_call(functools.partial(stage_kernel, q, [devices * cut for cut...  26.5 us
    all_to_all x1, blocking collectives, exchange(): return lax.all_to_all(x, 'dp', split_axis=0, concat_axis=0, tiled=True)  21.8 us
    pallas_call x1, Pallas kernels, pack(): pl.pallas_call(functools.partial(pack_kernel, cuts), in_specs=[ANY] * 7,...  10.6 us
  transfers between devices with their start and end apart: 2, of which 2 were waited for; matrix products, arithmetic and copies ran while one was open for 3% of the time, Pallas kernels for 9%

profile of v21, /device:TPU:0, one launch (start us, length us, event | category | flops | bytes accessed | tf_op | source)
XLA Modules:
  0.0 240.8 jit_solution(10382979649119915582)
XLA Ops:
  0.6 10.6 %pack.1 = (s16[16,1712,128]{2,1,0:T(8,128)(2,1)}, s16[16,384,128]{2,1,0:T(8,128)(2,1)}) custom-call(s32[128]{0:T(128)} %bitcast.16, s32[128]{0:T(128)} %row_hbm.1, s32[2,128]{1,0:T(2,128)} %bitcast.14, s32[1,128]{1,0:T(1,128)} %bitcast.17, s32[1,128]{1,0:T(1,128)} %bitcast.18, s32[1,128]{1,0:T(1,128)} %bitcast.19, f32[128,128,128]{2,1,0:T(8,128)} %refs_4_.1), custom_call_target="tpu_custom_call" | custom-call | flops 16777216 | bytes 12582912 | tf_op jit(solution)/shard_map/pack/pallas_call | solution.py:147
  11.3 7.4 %all-to-all-start = ((s16[16,1712,128]{2,1,0:T(8,128)(2,1)}), s16[16,1712,128]{2,1,0:T(8,128)(2,1)}, u32[]{:S(2)}, u32[]{:S(2)}) async-start(s16[16,1712,128]{2,1,0:T(8,128)(2,1)} %get-tuple-element.15), calls=%async_computation | async-start | bytes 14024704 | tf_op jit(solution)/shard_map/all_to_all | solution.py:534
  18.7 0.0 copy-start.2
  18.7 0.0 copy-start.1
  18.7 126.7 %all-to-all-done.x_hbm = s16[16,1712,128]{2,1,0:T(8,128)(2,1)} async-done(((s16[16,1712,128]{2,1,0:T(8,128)(2,1)}), s16[16,1712,128]{2,1,0:T(8,128)(2,1)}, u32[]{:S(2)}, u32[]{:S(2)}) %all-to-all-start) | async-done | bytes 7012384 | tf_op jit(solution)/shard_map/all_to_all | solution.py:534
  145.4 31.0 %all-to-all-start.1 = ((s16[16,384,128]{2,1,0:T(8,128)(2,1)}), s16[16,384,128]{2,1,0:T(8,128)(2,1)S(1)}, u32[]{:S(2)}, u32[]{:S(2)}) async-start(s16[16,384,128]{2,1,0:T(8,128)(2,1)} %get-tuple-element.17), calls=%async_computation.1 | async-start | bytes 3145728 | tf_op jit(solution)/shard_map/all_to_all | solution.py:534
  176.4 1.0 slice_convert_fusion
  177.5 1.0 convert_reduce_fusion
  178.6 0.3 select_reduce_fusion.3
  178.9 0.1 sub.13
  179.0 0.3 convert_reduce_fusion.1
  179.3 0.0 copy-done.1
  179.4 0.6 convert_reduce_fusion.3.fold_bound_in
  180.0 0.7 select_reduce_fusion.2.fold_list_in
  180.7 0.7 select_reduce_fusion.1.score_list_in
  181.4 0.1 select_reduce_fusion
  181.4 0.6 fusion.6.mods_in
  182.1 0.6 negate_select_fusion.signed_in
  182.7 20.6 %stage.2 = (f32[32,128]{1,0:T(8,128)}, f32[256,4096]{1,0:T(8,128)}, f32[256,256]{1,0:T(8,128)}, f32[33,128,128]{2,1,0:T(8,128)}, bf16[33,128,256]{2,1,0:T(8,128)(2,1)}, /*index=5*/bf16[208,128,128]{2,1,0:T(8,128)(2,1)}) custom-call(s32[256]{0:T(256)} %select_reduce_fusion.2.fold_list_in, s32[128]{0:T(128)} %convert_reduce_fusion.3.fold_bound_in, ...), custom_call_target="tpu_custom_call" | custom-call | flops 1744830464 | bytes 1048576 | tf_op jit(solution)/shard_map/stage/pallas_call | solution.py:422
  203.3 5.1 %all-to-all-done.1.x_hbm = s16[16,384,128]{2,1,0:T(8,128)(2,1)S(1)} async-done(((s16[16,384,128]{2,1,0:T(8,128)(2,1)}), s16[16,384,128]{2,1,0:T(8,128)(2,1)S(1)}, u32[]{:S(2)}, u32[]{:S(2)}) %all-to-all-start.1) | async-done | bytes 1572896 | tf_op jit(solution)/shard_map/all_to_all | solution.py:534
  208.4 1.1 copy-done
  209.5 5.9 %stage.3 = (f32[16,1,768]{2,1,0:T(1,128)}, f32[256,4096]{1,0:T(8,128)}) custom-call(s32[256]{0:T(256)} %select_reduce_fusion.2.fold_list_in, s32[128]{0:T(128)} %convert_reduce_fusion.3.fold_bound_in, s32[256]{0:T(256)} %select_reduce_fusion.1.score_list_in, f32[32,128]{1,0:T(8,128)} %fusion.6.mods_in, ...), custom_call_target="tpu_custom_call", output_to_operand_aliasing={{1}: (8, {})} | custom-call | flops 402653184 | bytes 1048576 | tf_op jit(solution)/shard_map/stage/pallas_call | solution.py:422
  215.5 21.8 %all_to_all.15.got_hbm = f32[16,1,768]{2,1,0:T(1,128)} all-to-all(f32[16,1,768]{2,1,0:T(1,128)} %get-tuple-element.24), channel_id=1, replica_groups=mesh['groups'=2,'dp'=16] {'dp'}, dimensions={0} | all-to-all | bytes 98304 | tf_op jit(solution)/shard_map/all_to_all | solution.py:534
  237.3 3.5 %close.1 = (bf16[512,2048]{1,0:T(8,128)(2,1)}, f32[2,128]{1,0:T(2,128)}) custom-call(s32[2,128]{1,0:T(2,128)} %bitcast.15, f32[16,1,768]{2,1,0:T(1,128)} %all_to_all.15.got_hbm, f32[256,4096]{1,0:T(8,128)} %get-tuple-element.25.sums_hbm), custom_call_target="tpu_custom_call" | custom-call | flops 2097152 | bytes 6291456 | tf_op jit(solution)/shard_map/close/pallas_call | solution.py:510
  (13 shorter events, 0.1 us)
Async XLA Ops:
  11.3 134.2 %all-to-all-start = ((s16[16,1712,128]{2,1,0:T(8,128)(2,1)}), s16[16,1712,128]{2,1,0:T(8,128)(2,1)}, u32[]{:S(2)}, u32[]{:S(2)}) async-start(s16[16,1712,128]{2,1,0:T(8,128)(2,1)} %get-tuple-element.15), calls=%async_computation | async-start | bytes 14024704 | tf_op jit(solution)/shard_map/all_to_all | solution.py:534
  18.7 160.3 %copy-start.2 = (s32[256]{0:T(256)S(1)}, s32[256]{0:T(256)}, u32[]{:S(2)}) copy-start(s32[256]{0:T(256)} %constant.83.clone) | copy-start | bytes 3076
  18.7 160.6 %copy-start.1 = (s32[256]{0:T(256)S(1)}, s32[256]{0:T(256)}, u32[]{:S(2)}) copy-start(s32[256]{0:T(256)} %constant.84.clone) | copy-start | bytes 3076
  145.4 62.9 %all-to-all-start.1 = ((s16[16,384,128]{2,1,0:T(8,128)(2,1)}), s16[16,384,128]{2,1,0:T(8,128)(2,1)S(1)}, u32[]{:S(2)}, u32[]{:S(2)}) async-start(s16[16,384,128]{2,1,0:T(8,128)(2,1)} %get-tuple-element.17), calls=%async_computation.1 | async-start | bytes 3145728 | tf_op jit(solution)/shard_map/all_to_all | solution.py:534
  208.4 1.1 copy-start

commit v22 on v20

--- a/solution.py
+++ b/solution.py
@@ -432,15 +432,24 @@
     )(*operands)
 
 
-def close_kernel(root, groups, labels_ref, got_ref, sums_hbm, out_hbm, similarity, sums, out, sems):
+def close_kernel(root, groups, labels_hbm, got_hbm, sums_hbm, out_hbm, similarity_hbm, labels_ref,
+                 got_ref, similarity, sums, out, sems, small_sems):
     width = TB_OWN // groups
     reads, writes = [], []
+    small = [
+        pltpu.make_async_copy(got_hbm, got_ref, small_sems.at[0]),
+        pltpu.make_async_copy(labels_hbm, labels_ref, small_sems.at[1]),
+    ]
+    for copy in small:
+        copy.start()
     for g in range(groups):
         some = (slice(None), pl.ds(g * width * 2 * LANES, width * 2 * LANES))
         reads.append(pltpu.make_async_copy(sums_hbm.at[some], sums.at[some], sems.at[0, g]))
         some = (slice(None), pl.ds(g * width * LANES, width * LANES))
         writes.append(pltpu.make_async_copy(out.at[some], out_hbm.at[some], sems.at[1, g]))
         reads[g].start()
+    for copy in small:
+        copy.wait()
     total = jnp.sum(got_ref[...], axis=0)
     home = total.shape[1] - K
     own = lax.rsqrt(total[:, home:] + EPSILON)
@@ -455,6 +464,8 @@
             found += jnp.where(cluster + i * LANES == labels_ref[b : b + 1, :], column, 0.0)
         found = jnp.sum(found, axis=0, keepdims=True)
         similarity[b : b + 1, :] = total[:, b * LANES : (b + 1) * LANES] * found
+    writes.append(pltpu.make_async_copy(similarity, similarity_hbm, small_sems.at[2]))
+    writes[-1].start()
     for g in range(groups):
         reads[g].wait()
 
@@ -474,18 +485,22 @@
 
 
 def close(labels, got, sums, vocab_size):
-    groups = 8
+    groups = 4
     labels = labels.reshape(-1, LANES)
     wide = jax.ShapeDtypeStruct((K, TB_OWN * LANES), jnp.bfloat16)
     centroids, similarity = pl.pallas_call(
         functools.partial(close_kernel, math.sqrt(vocab_size), groups),
-        in_specs=[VMEM, VMEM, ANY],
-        out_specs=[ANY, VMEM],
+        in_specs=[ANY] * 3,
+        out_specs=[ANY] * 2,
         out_shape=[wide, jax.ShapeDtypeStruct(labels.shape, jnp.float32)],
         scratch_shapes=[
+            pltpu.VMEM(labels.shape, jnp.int32),
+            pltpu.VMEM(got.shape, jnp.float32),
+            pltpu.VMEM(labels.shape, jnp.float32),
             pltpu.VMEM(sums.shape, jnp.float32),
             pltpu.VMEM(wide.shape, jnp.bfloat16),
             pltpu.SemaphoreType.DMA((2, groups)),
+            pltpu.SemaphoreType.DMA((3,)),
         ],
         compiler_params=params(),
         cost_estimate=pl.CostEstimate(

time: 241 us -> 240 us (level)
  no operation moved by 1% of the time
where the time goes in v22:
time: 240 us; the launch traced here: 239 us
  waiting for transfers between devices  132 us (55%)
  starting transfers between devices  38.4 us (16%)
  Pallas kernels  38.2 us (16%)
  blocking collectives  21.7 us (9%)
  other arithmetic  6.01 us (3%)
    all_to_all x2, waiting for transfers between devices, exchange(): return lax.all_to_all(x, 'dp', split_axis=0, concat_axis=0, tiled=True)  132 us
    all_to_all x2, starting transfers between devices, exchange(): return lax.all_to_all(x, 'dp', split_axis=0, concat_axis=0, tiled=True)  38.4 us
    pallas_call x2, Pallas kernels, stage(): pl.pallas_call(functools.partial(stage_kernel, q, [devices * cut for cut...  26 us
    all_to_all x1, blocking collectives, exchange(): return lax.all_to_all(x, 'dp', split_axis=0, concat_axis=0, tiled=True)  21.7 us
    pallas_call x1, Pallas kernels, pack(): pl.pallas_call(functools.partial(pack_kernel, cuts), in_specs=[SMEM] * 2...  8.65 us
  transfers between devices with their start and end apart: 2, of which 2 were waited for; matrix products, arithmetic and copies ran while one was open for 3% of the time, Pallas kernels for 8%

profile of v22, /device:TPU:0, one launch (start us, length us, event | category | flops | bytes accessed | tf_op | source)
XLA Modules:
  0.0 238.7 jit_solution(16423686549466659571)
XLA Ops:
  0.6 8.6 %pack.1 = (s16[16,1712,128]{2,1,0:T(8,128)(2,1)}, s16[16,384,128]{2,1,0:T(8,128)(2,1)}) custom-call(s32[128]{0:T(128)} %bitcast.16, s32[128]{0:T(128)} %row_ref.1, s32[2,128]{1,0:T(2,128)} %bitcast.14, s32[1,128]{1,0:T(1,128)} %bitcast.17, s32[1,128]{1,0:T(1,128)} %bitcast.18, s32[1,128]{1,0:T(1,128)} %bitcast.19, f32[128,128,128]{2,1,0:T(8,128)} %refs_4_.1), custom_call_target="tpu_custom_call" | custom-call | flops 16777216 | bytes 12582912 | tf_op jit(solution)/shard_map/pack/pallas_call | solution.py:140
  9.3 7.4 %all-to-all-start = ((s16[16,1712,128]{2,1,0:T(8,128)(2,1)}), s16[16,1712,128]{2,1,0:T(8,128)(2,1)}, u32[]{:S(2)}, u32[]{:S(2)}) async-start(s16[16,1712,128]{2,1,0:T(8,128)(2,1)} %get-tuple-element.15), calls=%async_computation | async-start | bytes 14024704 | tf_op jit(solution)/shard_map/all_to_all | solution.py:515
  16.7 0.0 copy-start.2
  16.7 0.0 copy-start.1
  16.7 126.7 %all-to-all-done.x_hbm = s16[16,1712,128]{2,1,0:T(8,128)(2,1)} async-done(((s16[16,1712,128]{2,1,0:T(8,128)(2,1)}), s16[16,1712,128]{2,1,0:T(8,128)(2,1)}, u32[]{:S(2)}, u32[]{:S(2)}) %all-to-all-start) | async-done | bytes 7012384 | tf_op jit(solution)/shard_map/all_to_all | solution.py:515
  143.5 31.0 %all-to-all-start.1 = ((s16[16,384,128]{2,1,0:T(8,128)(2,1)}), s16[16,384,128]{2,1,0:T(8,128)(2,1)S(1)}, u32[]{:S(2)}, u32[]{:S(2)}) async-start(s16[16,384,128]{2,1,0:T(8,128)(2,1)} %get-tuple-element.17), calls=%async_computation.1 | async-start | bytes 3145728 | tf_op jit(solution)/shard_map/all_to_all | solution.py:515
  174.4 1.0 slice_convert_fusion
  175.6 1.0 convert_reduce_fusion
  176.6 0.3 select_reduce_fusion.3
  177.0 0.1 sub.13
  177.0 0.0 copy-done.2
  177.1 0.3 convert_reduce_fusion.1
  177.4 0.6 convert_reduce_fusion.3.fold_bound
  178.0 0.7 select_reduce_fusion.2.fold_list
  178.7 0.7 select_reduce_fusion.1.score_list
  179.4 0.1 select_reduce_fusion
  179.5 0.6 fusion.6.mods_in
  180.1 0.6 negate_select_fusion.signed_in
  180.7 20.1 %stage.2 = (f32[32,128]{1,0:T(8,128)}, f32[256,4096]{1,0:T(8,128)}, f32[256,256]{1,0:T(8,128)}, f32[33,128,128]{2,1,0:T(8,128)}, bf16[33,128,256]{2,1,0:T(8,128)(2,1)}, /*index=5*/bf16[208,128,128]{2,1,0:T(8,128)(2,1)}) custom-call(s32[256]{0:T(256)} %select_reduce_fusion.2.fold_list, s32[35]{0:T(128)} %convert_reduce_fusion.3.fold_bound, ...), custom_call_target="tpu_custom_call" | custom-call | flops 1744830464 | bytes 1048576 | tf_op jit(solution)/shard_map/stage/pallas_call | solution.py:405
  200.8 5.6 %all-to-all-done.1.x_hbm = s16[16,384,128]{2,1,0:T(8,128)(2,1)S(1)} async-done(((s16[16,384,128]{2,1,0:T(8,128)(2,1)}), s16[16,384,128]{2,1,0:T(8,128)(2,1)S(1)}, u32[]{:S(2)}, u32[]{:S(2)}) %all-to-all-start.1) | async-done | bytes 1572896 | tf_op jit(solution)/shard_map/all_to_all | solution.py:515
  206.4 1.1 copy-done
  207.5 6.0 %stage.3 = (f32[16,1,768]{2,1,0:T(1,128)}, f32[256,4096]{1,0:T(8,128)}) custom-call(s32[256]{0:T(256)} %select_reduce_fusion.2.fold_list, s32[35]{0:T(128)} %convert_reduce_fusion.3.fold_bound, s32[256]{0:T(256)} %select_reduce_fusion.1.score_list, f32[32,128]{1,0:T(8,128)} %fusion.6.mods_in, ...), custom_call_target="tpu_custom_call", output_to_operand_aliasing={{1}: (8, {})} | custom-call | flops 402653184 | bytes 1048576 | tf_op jit(solution)/shard_map/stage/pallas_call | solution.py:405
  213.5 21.7 %all_to_all.15.got_hbm = f32[16,1,768]{2,1,0:T(1,128)} all-to-all(f32[16,1,768]{2,1,0:T(1,128)} %get-tuple-element.24), channel_id=1, replica_groups=mesh['groups'=2,'dp'=16] {'dp'}, dimensions={0} | all-to-all | bytes 98304 | tf_op jit(solution)/shard_map/all_to_all | solution.py:515
  235.2 3.5 %close.1 = (bf16[512,2048]{1,0:T(8,128)(2,1)}, f32[2,128]{1,0:T(2,128)}) custom-call(s32[2,128]{1,0:T(2,128)} %bitcast.15, f32[16,1,768]{2,1,0:T(1,128)} %all_to_all.15.got_hbm, f32[256,4096]{1,0:T(8,128)} %get-tuple-element.25.sums_hbm), custom_call_target="tpu_custom_call" | custom-call | flops 2097152 | bytes 6291456 | tf_op jit(solution)/shard_map/close/pallas_call | solution.py:491
  (13 shorter events, 0.1 us)
Async XLA Ops:
  9.3 134.2 %all-to-all-start = ((s16[16,1712,128]{2,1,0:T(8,128)(2,1)}), s16[16,1712,128]{2,1,0:T(8,128)(2,1)}, u32[]{:S(2)}, u32[]{:S(2)}) async-start(s16[16,1712,128]{2,1,0:T(8,128)(2,1)} %get-tuple-element.15), calls=%async_computation | async-start | bytes 14024704 | tf_op jit(solution)/shard_map/all_to_all | solution.py:515
  16.7 160.3 %copy-start.2 = (s32[256]{0:T(256)S(1)}, s32[256]{0:T(256)}, u32[]{:S(2)}) copy-start(s32[256]{0:T(256)} %constant.83.clone) | copy-start | bytes 3076
  16.7 160.6 %copy-start.1 = (s32[256]{0:T(256)S(1)}, s32[256]{0:T(256)}, u32[]{:S(2)}) copy-start(s32[256]{0:T(256)} %constant.84.clone) | copy-start | bytes 3076
  143.5 62.9 %all-to-all-start.1 = ((s16[16,384,128]{2,1,0:T(8,128)(2,1)}), s16[16,384,128]{2,1,0:T(8,128)(2,1)S(1)}, u32[]{:S(2)}, u32[]{:S(2)}) async-start(s16[16,384,128]{2,1,0:T(8,128)(2,1)} %get-tuple-element.17), calls=%async_computation.1 | async-start | bytes 3145728 | tf_op jit(solution)/shard_map/all_to_all | solution.py:515
  206.4 1.1 copy-start

commit v23 on v21

--- a/solution.py
+++ b/solution.py
@@ -76,12 +76,12 @@
         some = pl.ds(c * step, step)
         return pltpu.make_async_copy(x_hbm.at[some], x.at[some], x_sems.at[c])
 
-    for c in range(tiles // step):
-        read(c).start()
     pairs = zip((owner_hbm, row_hbm, *told_hbms), (owner_ref, row_ref, *told_refs))
     small = [pltpu.make_async_copy(*pair, small_sems.at[i]) for i, pair in enumerate(pairs)]
     for copy in small:
         copy.start()
+    for c in range(tiles // step):
+        read(c).start()
     for copy in small:
         copy.wait()
     labels, owner, row, sub = [ref[...] for ref in told_refs]
@@ -190,15 +190,13 @@
     needed = [pltpu.make_async_copy(x_hbm.at[:, pl.ds(0, width * LANES)], x, sems.at[0])]
     if q:
         needed.append(pltpu.make_async_copy(made_in[0], spread, sems.at[1]))
-    for copy in needed:
-        copy.start()
     for held, empty in ((mods, -1.0), (signed, 0.0)):
         held[none : none + 1, :] = jnp.full((1, LANES), empty, jnp.float32)
     pairs = [(fold_list_in, fold_list), (fold_bound_in, fold_bound), (score_list_in, score_list)]
     pairs += [(mods_in, mods.at[pl.ds(0, none)]), (signed_in, signed.at[pl.ds(0, none)])]
     pairs += [(before, scores), (squares_in, squares)] if q else []
     small = [pltpu.make_async_copy(*pair, small_sems.at[i]) for i, pair in enumerate(pairs)]
-    for copy in small:
+    for copy in small + needed:
         copy.start()
     for copy in small:
         copy.wait()

time: 242 us -> 241 us (level)
  transfers between devices with their start and end apart: 2 -> 2, of which waited for: 2 -> 2; matrix products, arithmetic and copies ran while one was open for 3% -> 3% of each run, Pallas kernels for 9% -> 8%
where the time goes in v23:
time: 241 us; the launch traced here: 240 us
  waiting for transfers between devices  133 us (55%)
  Pallas kernels  38.7 us (16%)
  starting transfers between devices  38.4 us (16%)
  blocking collectives  22.1 us (9%)
  other arithmetic  6.01 us (2%)
    all_to_all x2, waiting for transfers between devices, exchange(): return lax.all_to_all(x, 'dp', split_axis=0, concat_axis=0, tiled=True)  133 us
    all_to_all x2, starting transfers between devices, exchange(): return lax.all_to_all(x, 'dp', split_axis=0, concat_axis=0, tiled=True)  38.4 us
    pallas_call x2, Pallas kernels, stage(): pl.pallas_call(functools.partial(stage_kernel, q, [devices * cut for cut...  24.9 us
    all_to_all x1, blocking collectives, exchange(): return lax.all_to_all(x, 'dp', split_axis=0, concat_axis=0, tiled=True)  22.1 us
    pallas_call x1, Pallas kernels, pack(): pl.pallas_call(functools.partial(pack_kernel, cuts), in_specs=[ANY] * 7,...  10.3 us
  transfers between devices with their start and end apart: 2, of which 2 were waited for; matrix products, arithmetic and copies ran while one was open for 3% of the time, Pallas kernels for 8%

profile of v23, /device:TPU:0, one launch (start us, length us, event | category | flops | bytes accessed | tf_op | source)
XLA Modules:
  0.0 240.2 jit_solution(16270827309430849365)
XLA Ops:
  0.6 10.3 %pack.1 = (s16[16,1712,128]{2,1,0:T(8,128)(2,1)}, s16[16,384,128]{2,1,0:T(8,128)(2,1)}) custom-call(s32[128]{0:T(128)} %bitcast.16, s32[128]{0:T(128)} %row_hbm.1, s32[2,128]{1,0:T(2,128)} %bitcast.14, s32[1,128]{1,0:T(1,128)} %bitcast.17, s32[1,128]{1,0:T(1,128)} %bitcast.18, s32[1,128]{1,0:T(1,128)} %bitcast.19, f32[128,128,128]{2,1,0:T(8,128)} %refs_4_.1), custom_call_target="tpu_custom_call" | custom-call | flops 16777216 | bytes 12582912 | tf_op jit(solution)/shard_map/pack/pallas_call | solution.py:147
  11.0 7.4 %all-to-all-start = ((s16[16,1712,128]{2,1,0:T(8,128)(2,1)}), s16[16,1712,128]{2,1,0:T(8,128)(2,1)}, u32[]{:S(2)}, u32[]{:S(2)}) async-start(s16[16,1712,128]{2,1,0:T(8,128)(2,1)} %get-tuple-element.15), calls=%async_computation | async-start | bytes 14024704 | tf_op jit(solution)/shard_map/all_to_all | solution.py:532
  18.4 0.0 copy-start.2
  18.4 0.0 copy-start.1
  18.4 126.7 %all-to-all-done.x_hbm = s16[16,1712,128]{2,1,0:T(8,128)(2,1)} async-done(((s16[16,1712,128]{2,1,0:T(8,128)(2,1)}), s16[16,1712,128]{2,1,0:T(8,128)(2,1)}, u32[]{:S(2)}, u32[]{:S(2)}) %all-to-all-start) | async-done | bytes 7012384 | tf_op jit(solution)/shard_map/all_to_all | solution.py:532
  145.1 31.0 %all-to-all-start.1 = ((s16[16,384,128]{2,1,0:T(8,128)(2,1)}), s16[16,384,128]{2,1,0:T(8,128)(2,1)S(1)}, u32[]{:S(2)}, u32[]{:S(2)}) async-start(s16[16,384,128]{2,1,0:T(8,128)(2,1)} %get-tuple-element.17), calls=%async_computation.1 | async-start | bytes 3145728 | tf_op jit(solution)/shard_map/all_to_all | solution.py:532
  176.1 1.0 slice_convert_fusion
  177.2 1.0 convert_reduce_fusion
  178.3 0.3 select_reduce_fusion.3
  178.6 0.1 sub.13
  178.7 0.3 convert_reduce_fusion.1
  179.0 0.0 copy-done.1
  179.1 0.6 convert_reduce_fusion.3.fold_bound_in
  179.7 0.7 select_reduce_fusion.2.fold_list_in
  180.4 0.7 select_reduce_fusion.1.score_list_in
  181.1 0.1 select_reduce_fusion
  181.2 0.6 fusion.6.mods_in
  181.8 0.6 negate_select_fusion.signed_in
  182.4 19.5 %stage.2 = (f32[32,128]{1,0:T(8,128)}, f32[256,4096]{1,0:T(8,128)}, f32[256,256]{1,0:T(8,128)}, f32[33,128,128]{2,1,0:T(8,128)}, bf16[33,128,256]{2,1,0:T(8,128)(2,1)}, /*index=5*/bf16[208,128,128]{2,1,0:T(8,128)(2,1)}) custom-call(s32[256]{0:T(256)} %select_reduce_fusion.2.fold_list_in, s32[128]{0:T(128)} %convert_reduce_fusion.3.fold_bound_in, ...), custom_call_target="tpu_custom_call" | custom-call | flops 1744830464 | bytes 1048576 | tf_op jit(solution)/shard_map/stage/pallas_call | solution.py:420
  201.9 6.2 %all-to-all-done.1.x_hbm = s16[16,384,128]{2,1,0:T(8,128)(2,1)S(1)} async-done(((s16[16,384,128]{2,1,0:T(8,128)(2,1)}), s16[16,384,128]{2,1,0:T(8,128)(2,1)S(1)}, u32[]{:S(2)}, u32[]{:S(2)}) %all-to-all-start.1) | async-done | bytes 1572896 | tf_op jit(solution)/shard_map/all_to_all | solution.py:532
  208.1 1.1 copy-done
  209.2 5.4 %stage.3 = (f32[16,1,768]{2,1,0:T(1,128)}, f32[256,4096]{1,0:T(8,128)}) custom-call(s32[256]{0:T(256)} %select_reduce_fusion.2.fold_list_in, s32[128]{0:T(128)} %convert_reduce_fusion.3.fold_bound_in, s32[256]{0:T(256)} %select_reduce_fusion.1.score_list_in, f32[32,128]{1,0:T(8,128)} %fusion.6.mods_in, ...), custom_call_target="tpu_custom_call", output_to_operand_aliasing={{1}: (8, {})} | custom-call | flops 402653184 | bytes 1048576 | tf_op jit(solution)/shard_map/stage/pallas_call | solution.py:420
  214.6 22.1 %all_to_all.15.got_hbm = f32[16,1,768]{2,1,0:T(1,128)} all-to-all(f32[16,1,768]{2,1,0:T(1,128)} %get-tuple-element.24), channel_id=1, replica_groups=mesh['groups'=2,'dp'=16] {'dp'}, dimensions={0} | all-to-all | bytes 98304 | tf_op jit(solution)/shard_map/all_to_all | solution.py:532
  236.7 3.5 %close.1 = (bf16[512,2048]{1,0:T(8,128)(2,1)}, f32[2,128]{1,0:T(2,128)}) custom-call(s32[2,128]{1,0:T(2,128)} %bitcast.15, f32[16,1,768]{2,1,0:T(1,128)} %all_to_all.15.got_hbm, f32[256,4096]{1,0:T(8,128)} %get-tuple-element.25.sums_hbm), custom_call_target="tpu_custom_call" | custom-call | flops 2097152 | bytes 6291456 | tf_op jit(solution)/shard_map/close/pallas_call | solution.py:508
  (13 shorter events, 0.1 us)
Async XLA Ops:
  11.0 134.2 %all-to-all-start = ((s16[16,1712,128]{2,1,0:T(8,128)(2,1)}), s16[16,1712,128]{2,1,0:T(8,128)(2,1)}, u32[]{:S(2)}, u32[]{:S(2)}) async-start(s16[16,1712,128]{2,1,0:T(8,128)(2,1)} %get-tuple-element.15), calls=%async_computation | async-start | bytes 14024704 | tf_op jit(solution)/shard_map/all_to_all | solution.py:532
  18.4 160.3 %copy-start.2 = (s32[256]{0:T(256)S(1)}, s32[256]{0:T(256)}, u32[]{:S(2)}) copy-start(s32[256]{0:T(256)} %constant.83.clone) | copy-start | bytes 3076
  18.4 160.6 %copy-start.1 = (s32[256]{0:T(256)S(1)}, s32[256]{0:T(256)}, u32[]{:S(2)}) copy-start(s32[256]{0:T(256)} %constant.84.clone) | copy-start | bytes 3076
  145.1 62.9 %all-to-all-start.1 = ((s16[16,384,128]{2,1,0:T(8,128)(2,1)}), s16[16,384,128]{2,1,0:T(8,128)(2,1)S(1)}, u32[]{:S(2)}, u32[]{:S(2)}) async-start(s16[16,384,128]{2,1,0:T(8,128)(2,1)} %get-tuple-element.17), calls=%async_computation.1 | async-start | bytes 3145728 | tf_op jit(solution)/shard_map/all_to_all | solution.py:532
  208.1 1.1 copy-start

commit v24 on v23

--- a/solution.py
+++ b/solution.py
@@ -61,12 +61,11 @@
     return pltpu.CompilerParams(vmem_limit_bytes=VMEM_BYTES)
 
 
-def pack_kernel(cuts, owner_hbm, row_hbm, *refs):
+def pack_kernel(cuts, owner_ref, row_ref, *refs):
     parts = len(cuts) - 1
-    (*told_hbms, x_hbm), refs = refs[:5], refs[5:]
+    (*told_refs, x_hbm), refs = refs[:5], refs[5:]
     outs = refs[:parts]
-    x, coded, square, sums, words, notes, rank_row, rank_ref, *refs = refs[parts:]
-    owner_ref, row_ref, *told_refs, sems, x_sems, small_sems = refs
+    x, coded, square, sums, words, notes, rank_row, rank_ref, sems, x_sems = refs[parts:]
     tiles = x.shape[0]
     devices = coded.shape[0]
     blocks = square.shape[0]
@@ -76,14 +75,8 @@
         some = pl.ds(c * step, step)
         return pltpu.make_async_copy(x_hbm.at[some], x.at[some], x_sems.at[c])
 
-    pairs = zip((owner_hbm, row_hbm, *told_hbms), (owner_ref, row_ref, *told_refs))
-    small = [pltpu.make_async_copy(*pair, small_sems.at[i]) for i, pair in enumerate(pairs)]
-    for copy in small:
-        copy.start()
     for c in range(tiles // step):
         read(c).start()
-    for copy in small:
-        copy.wait()
     labels, owner, row, sub = [ref[...] for ref in told_refs]
     own, sub_own = [jnp.broadcast_to(v.astype(jnp.float32), (tiles, tiles)) for v in (owner, sub)]
     other, sub_other = jnp.transpose(own), jnp.transpose(sub_own)
@@ -146,7 +139,7 @@
     rows[0] += noted
     return pl.pallas_call(
         functools.partial(pack_kernel, cuts),
-        in_specs=[ANY] * 7,
+        in_specs=[SMEM] * 2 + [VMEM] * 4 + [ANY],
         out_specs=[ANY] * len(rows),
         out_shape=[jax.ShapeDtypeStruct((devices, some, LANES), jnp.int16) for some in rows],
         scratch_shapes=[
@@ -158,12 +151,8 @@
             pltpu.VMEM((devices, noted, LANES), jnp.int16),
             pltpu.VMEM((1, tiles), jnp.int32),
             pltpu.SMEM((1, tiles), jnp.int32),
-            pltpu.SMEM((tiles,), jnp.int32),
-            pltpu.SMEM((tiles,), jnp.int32),
-            *[pltpu.VMEM(some.shape, jnp.int32) for some in told],
             pltpu.SemaphoreType.DMA((len(rows) + 4,)),
             pltpu.SemaphoreType.DMA((tiles // math.gcd(STEP_TILES, tiles),)),
-            pltpu.SemaphoreType.DMA((6,)),
         ],
         compiler_params=params(),
         cost_estimate=pl.CostEstimate(

time: 241 us -> 240 us (level)
  Pallas kernels: 38.7 us -> 44.4 us
  waiting for transfers between devices: 133 us -> 128 us
    pallas_call x2, Pallas kernels: 24.9 us -> 32.2 us  [stage(): pl.pallas_call(functools.partial(stage_kernel, q, [devices * cut for cut...]
    all_to_all x2, waiting for transfers between devices: 133 us -> 128 us  [exchange(): return lax.all_to_all(x, 'dp', split_axis=0, concat_axis=0, tiled=True)]
  transfers between devices with their start and end apart: 2 -> 2, of which waited for: 2 -> 2; matrix products, arithmetic and copies ran while one was open for 3% -> 3% of each run, Pallas kernels for 8% -> 10%
where the time goes in v24:
time: 240 us; the launch traced here: 239 us
  waiting for transfers between devices  128 us (53%)
  Pallas kernels  44.4 us (18%)
  starting transfers between devices  38.4 us (16%)
  blocking collectives  19.7 us (8%)
  other arithmetic  6.01 us (3%)
    all_to_all x2, waiting for transfers between devices, exchange(): return lax.all_to_all(x, 'dp', split_axis=0, concat_axis=0, tiled=True)  128 us
    all_to_all x2, starting transfers between devices, exchange(): return lax.all_to_all(x, 'dp', split_axis=0, concat_axis=0, tiled=True)  38.4 us
    pallas_call x2, Pallas kernels, stage(): pl.pallas_call(functools.partial(stage_kernel, q, [devices * cut for cut...  32.2 us
    all_to_all x1, blocking collectives, exchange(): return lax.all_to_all(x, 'dp', split_axis=0, concat_axis=0, tiled=True)  19.7 us
    pallas_call x1, Pallas kernels, pack(): pl.pallas_call(functools.partial(pack_kernel, cuts), in_specs=[SMEM] * 2...  8.65 us
  transfers between devices with their start and end apart: 2, of which 2 were waited for; matrix products, arithmetic and copies ran while one was open for 3% of the time, Pallas kernels for 10%

profile of v24, /device:TPU:0, one launch (start us, length us, event | category | flops | bytes accessed | tf_op | source)
XLA Modules:
  0.0 238.7 jit_solution(9013535169715624918)
XLA Ops:
  0.6 8.6 %pack.1 = (s16[16,1712,128]{2,1,0:T(8,128)(2,1)}, s16[16,384,128]{2,1,0:T(8,128)(2,1)}) custom-call(s32[128]{0:T(128)} %bitcast.16, s32[128]{0:T(128)} %row_ref.1, s32[2,128]{1,0:T(2,128)} %bitcast.14, s32[1,128]{1,0:T(1,128)} %bitcast.17, s32[1,128]{1,0:T(1,128)} %bitcast.18, s32[1,128]{1,0:T(1,128)} %bitcast.19, f32[128,128,128]{2,1,0:T(8,128)} %refs_4_.1), custom_call_target="tpu_custom_call" | custom-call | flops 16777216 | bytes 12582912 | tf_op jit(solution)/shard_map/pack/pallas_call | solution.py:140
  9.3 7.4 %all-to-all-start = ((s16[16,1712,128]{2,1,0:T(8,128)(2,1)}), s16[16,1712,128]{2,1,0:T(8,128)(2,1)}, u32[]{:S(2)}, u32[]{:S(2)}) async-start(s16[16,1712,128]{2,1,0:T(8,128)(2,1)} %get-tuple-element.15), calls=%async_computation | async-start | bytes 14024704 | tf_op jit(solution)/shard_map/all_to_all | solution.py:521
  16.7 0.0 copy-start.2
  16.7 0.0 copy-start.1
  16.7 126.7 %all-to-all-done.x_hbm = s16[16,1712,128]{2,1,0:T(8,128)(2,1)} async-done(((s16[16,1712,128]{2,1,0:T(8,128)(2,1)}), s16[16,1712,128]{2,1,0:T(8,128)(2,1)}, u32[]{:S(2)}, u32[]{:S(2)}) %all-to-all-start) | async-done | bytes 7012384 | tf_op jit(solution)/shard_map/all_to_all | solution.py:521
  143.5 31.0 %all-to-all-start.1 = ((s16[16,384,128]{2,1,0:T(8,128)(2,1)}), s16[16,384,128]{2,1,0:T(8,128)(2,1)S(1)}, u32[]{:S(2)}, u32[]{:S(2)}) async-start(s16[16,384,128]{2,1,0:T(8,128)(2,1)} %get-tuple-element.17), calls=%async_computation.1 | async-start | bytes 3145728 | tf_op jit(solution)/shard_map/all_to_all | solution.py:521
  174.4 1.0 slice_convert_fusion
  175.6 1.0 convert_reduce_fusion
  176.6 0.3 select_reduce_fusion.3
  177.0 0.1 sub.13
  177.0 0.0 copy-done.2
  177.1 0.3 convert_reduce_fusion.1
  177.4 0.6 convert_reduce_fusion.3.fold_bound_in
  178.0 0.7 select_reduce_fusion.2.fold_list_in
  178.7 0.7 select_reduce_fusion.1.score_list_in
  179.4 0.1 select_reduce_fusion
  179.5 0.6 fusion.6.mods_in
  180.1 0.6 negate_select_fusion.signed_in
  180.7 24.3 %stage.2 = (f32[32,128]{1,0:T(8,128)}, f32[256,4096]{1,0:T(8,128)}, f32[256,256]{1,0:T(8,128)}, f32[33,128,128]{2,1,0:T(8,128)}, bf16[33,128,256]{2,1,0:T(8,128)(2,1)}, /*index=5*/bf16[208,128,128]{2,1,0:T(8,128)(2,1)}) custom-call(s32[256]{0:T(256)} %select_reduce_fusion.2.fold_list_in, s32[128]{0:T(128)} %convert_reduce_fusion.3.fold_bound_in, ...), custom_call_target="tpu_custom_call" | custom-call | flops 1744830464 | bytes 1048576 | tf_op jit(solution)/shard_map/stage/pallas_call | solution.py:409
  205.0 1.4 all-to-all-done.1.x_hbm
  206.4 1.1 copy-done
  207.5 7.9 %stage.3 = (f32[16,1,768]{2,1,0:T(1,128)}, f32[256,4096]{1,0:T(8,128)}) custom-call(s32[256]{0:T(256)} %select_reduce_fusion.2.fold_list_in, s32[128]{0:T(128)} %convert_reduce_fusion.3.fold_bound_in, s32[256]{0:T(256)} %select_reduce_fusion.1.score_list_in, f32[32,128]{1,0:T(8,128)} %fusion.6.mods_in, ...), custom_call_target="tpu_custom_call", output_to_operand_aliasing={{1}: (8, {})} | custom-call | flops 402653184 | bytes 1048576 | tf_op jit(solution)/shard_map/stage/pallas_call | solution.py:409
  215.4 19.7 %all_to_all.15.got_hbm = f32[16,1,768]{2,1,0:T(1,128)} all-to-all(f32[16,1,768]{2,1,0:T(1,128)} %get-tuple-element.24), channel_id=1, replica_groups=mesh['groups'=2,'dp'=16] {'dp'}, dimensions={0} | all-to-all | bytes 98304 | tf_op jit(solution)/shard_map/all_to_all | solution.py:521
  235.1 3.5 %close.1 = (bf16[512,2048]{1,0:T(8,128)(2,1)}, f32[2,128]{1,0:T(2,128)}) custom-call(s32[2,128]{1,0:T(2,128)} %bitcast.15, f32[16,1,768]{2,1,0:T(1,128)} %all_to_all.15.got_hbm, f32[256,4096]{1,0:T(8,128)} %get-tuple-element.25.sums_hbm), custom_call_target="tpu_custom_call" | custom-call | flops 2097152 | bytes 6291456 | tf_op jit(solution)/shard_map/close/pallas_call | solution.py:497
  (13 shorter events, 0.1 us)
Async XLA Ops:
  9.3 134.2 %all-to-all-start = ((s16[16,1712,128]{2,1,0:T(8,128)(2,1)}), s16[16,1712,128]{2,1,0:T(8,128)(2,1)}, u32[]{:S(2)}, u32[]{:S(2)}) async-start(s16[16,1712,128]{2,1,0:T(8,128)(2,1)} %get-tuple-element.15), calls=%async_computation | async-start | bytes 14024704 | tf_op jit(solution)/shard_map/all_to_all | solution.py:521
  16.7 160.3 %copy-start.2 = (s32[256]{0:T(256)S(1)}, s32[256]{0:T(256)}, u32[]{:S(2)}) copy-start(s32[256]{0:T(256)} %constant.83.clone) | copy-start | bytes 3076
  16.7 160.6 %copy-start.1 = (s32[256]{0:T(256)S(1)}, s32[256]{0:T(256)}, u32[]{:S(2)}) copy-start(s32[256]{0:T(256)} %constant.84.clone) | copy-start | bytes 3076
  143.5 62.9 %all-to-all-start.1 = ((s16[16,384,128]{2,1,0:T(8,128)(2,1)}), s16[16,384,128]{2,1,0:T(8,128)(2,1)S(1)}, u32[]{:S(2)}, u32[]{:S(2)}) async-start(s16[16,384,128]{2,1,0:T(8,128)(2,1)} %get-tuple-element.17), calls=%async_computation.1 | async-start | bytes 3145728 | tf_op jit(solution)/shard_map/all_to_all | solution.py:521
  206.4 1.1 copy-start

commit v25 on v24

--- a/solution.py
+++ b/solution.py
@@ -29,7 +29,7 @@
 BLOCKS = 4
 ROW_SHIFT, SOURCE_SHIFT = 16, 8
 PLACE_MASK, SOURCE_MASK, SLOT_MASK = 0xFFFF, 0xFF, 0xFF
-BATCH = 8
+BATCH = 32
 NT = (((1,), (1,)), ((), ()))
 SMEM = pl.BlockSpec(memory_space=pltpu.SMEM)
 VMEM = pl.BlockSpec(memory_space=pltpu.VMEM)

time: 240 us -> 240 us (level); the launches traced: 239 us -> 242 us
  Pallas kernels: 44.4 us -> 38 us
  blocking collectives: 19.7 us -> 25.4 us
  waiting for transfers between devices: 128 us -> 132 us
    pallas_call x2, Pallas kernels: 32.2 us -> 25.8 us  [stage(): pl.pallas_call(functools.partial(stage_kernel, q, [devices * cut for cut...]
    all_to_all x1, blocking collectives: 19.7 us -> 25.4 us  [exchange(): return lax.all_to_all(x, 'dp', split_axis=0, concat_axis=0, tiled=True)]
    all_to_all x2, waiting for transfers between devices: 128 us -> 132 us  [exchange(): return lax.all_to_all(x, 'dp', split_axis=0, concat_axis=0, tiled=True)]
  transfers between devices with their start and end apart: 2 -> 2, of which waited for: 2 -> 2; matrix products, arithmetic and copies ran while one was open for 3% -> 3% of each run, Pallas kernels for 10% -> 9%
where the time goes in v25:
time: 240 us; the launch traced here: 242 us
  waiting for transfers between devices  132 us (55%)
  starting transfers between devices  38.4 us (16%)
  Pallas kernels  38 us (16%)
  blocking collectives  25.4 us (11%)
  other arithmetic  6.01 us (3%)
    all_to_all x2, waiting for transfers between devices, exchange(): return lax.all_to_all(x, 'dp', split_axis=0, concat_axis=0, tiled=True)  132 us
    all_to_all x2, starting transfers between devices, exchange(): return lax.all_to_all(x, 'dp', split_axis=0, concat_axis=0, tiled=True)  38.4 us
    pallas_call x2, Pallas kernels, stage(): pl.pallas_call(functools.partial(stage_kernel, q, [devices * cut for cut...  25.8 us
    all_to_all x1, blocking collectives, exchange(): return lax.all_to_all(x, 'dp', split_axis=0, concat_axis=0, tiled=True)  25.4 us
    pallas_call x1, Pallas kernels, pack(): pl.pallas_call(functools.partial(pack_kernel, cuts), in_specs=[SMEM] * 2...  8.66 us
  transfers between devices with their start and end apart: 2, of which 2 were waited for; matrix products, arithmetic and copies ran while one was open for 3% of the time, Pallas kernels for 9%

profile of v25, /device:TPU:0, one launch (start us, length us, event | category | flops | bytes accessed | tf_op | source)
XLA Modules:
  0.0 241.5 jit_solution(7703430750140405476)
XLA Ops:
  0.6 8.7 %pack.1 = (s16[16,1712,128]{2,1,0:T(8,128)(2,1)}, s16[16,384,128]{2,1,0:T(8,128)(2,1)}) custom-call(s32[128]{0:T(128)} %bitcast.16, s32[128]{0:T(128)} %row_ref.1, s32[2,128]{1,0:T(2,128)} %bitcast.14, s32[1,128]{1,0:T(1,128)} %bitcast.17, s32[1,128]{1,0:T(1,128)} %bitcast.18, s32[1,128]{1,0:T(1,128)} %bitcast.19, f32[128,128,128]{2,1,0:T(8,128)} %refs_4_.1), custom_call_target="tpu_custom_call" | custom-call | flops 16777216 | bytes 12582912 | tf_op jit(solution)/shard_map/pack/pallas_call | solution.py:140
  9.3 7.4 %all-to-all-start = ((s16[16,1712,128]{2,1,0:T(8,128)(2,1)}), s16[16,1712,128]{2,1,0:T(8,128)(2,1)}, u32[]{:S(2)}, u32[]{:S(2)}) async-start(s16[16,1712,128]{2,1,0:T(8,128)(2,1)} %get-tuple-element.15), calls=%async_computation | async-start | bytes 14024704 | tf_op jit(solution)/shard_map/all_to_all | solution.py:521
  16.7 0.0 copy-start.2
  16.7 0.0 copy-start.1
  16.8 126.7 %all-to-all-done.x_hbm = s16[16,1712,128]{2,1,0:T(8,128)(2,1)} async-done(((s16[16,1712,128]{2,1,0:T(8,128)(2,1)}), s16[16,1712,128]{2,1,0:T(8,128)(2,1)}, u32[]{:S(2)}, u32[]{:S(2)}) %all-to-all-start) | async-done | bytes 7012384 | tf_op jit(solution)/shard_map/all_to_all | solution.py:521
  143.5 31.0 %all-to-all-start.1 = ((s16[16,384,128]{2,1,0:T(8,128)(2,1)}), s16[16,384,128]{2,1,0:T(8,128)(2,1)S(1)}, u32[]{:S(2)}, u32[]{:S(2)}) async-start(s16[16,384,128]{2,1,0:T(8,128)(2,1)} %get-tuple-element.17), calls=%async_computation.1 | async-start | bytes 3145728 | tf_op jit(solution)/shard_map/all_to_all | solution.py:521
  174.5 1.0 slice_convert_fusion
  175.6 1.0 convert_reduce_fusion
  176.6 0.3 select_reduce_fusion.3
  177.0 0.1 sub.13
  177.1 0.0 copy-done.2
  177.1 0.3 convert_reduce_fusion.1
  177.4 0.6 convert_reduce_fusion.3.fold_bound_in
  178.0 0.7 select_reduce_fusion.2.fold_list_in
  178.7 0.7 select_reduce_fusion.1.score_list_in
  179.4 0.1 select_reduce_fusion
  179.5 0.6 fusion.6.mods_in
  180.1 0.6 negate_select_fusion.signed_in
  180.7 20.8 %stage.2 = (f32[32,128]{1,0:T(8,128)}, f32[256,4096]{1,0:T(8,128)}, f32[256,256]{1,0:T(8,128)}, f32[33,128,128]{2,1,0:T(8,128)}, bf16[33,128,256]{2,1,0:T(8,128)(2,1)}, /*index=5*/bf16[208,128,128]{2,1,0:T(8,128)(2,1)}) custom-call(s32[256]{0:T(256)} %select_reduce_fusion.2.fold_list_in, s32[128]{0:T(128)} %convert_reduce_fusion.3.fold_bound_in, ...), custom_call_target="tpu_custom_call" | custom-call | flops 1744830464 | bytes 1048576 | tf_op jit(solution)/shard_map/stage/pallas_call | solution.py:409
  201.5 4.9 %all-to-all-done.1.x_hbm = s16[16,384,128]{2,1,0:T(8,128)(2,1)S(1)} async-done(((s16[16,384,128]{2,1,0:T(8,128)(2,1)}), s16[16,384,128]{2,1,0:T(8,128)(2,1)S(1)}, u32[]{:S(2)}, u32[]{:S(2)}) %all-to-all-start.1) | async-done | bytes 1572896 | tf_op jit(solution)/shard_map/all_to_all | solution.py:521
  206.4 1.1 copy-done
  207.6 5.0 %stage.3 = (f32[16,1,768]{2,1,0:T(1,128)}, f32[256,4096]{1,0:T(8,128)}) custom-call(s32[256]{0:T(256)} %select_reduce_fusion.2.fold_list_in, s32[128]{0:T(128)} %convert_reduce_fusion.3.fold_bound_in, s32[256]{0:T(256)} %select_reduce_fusion.1.score_list_in, f32[32,128]{1,0:T(8,128)} %fusion.6.mods_in, ...), custom_call_target="tpu_custom_call", output_to_operand_aliasing={{1}: (8, {})} | custom-call | flops 402653184 | bytes 1048576 | tf_op jit(solution)/shard_map/stage/pallas_call | solution.py:409
  212.6 25.4 %all_to_all.15.got_hbm = f32[16,1,768]{2,1,0:T(1,128)} all-to-all(f32[16,1,768]{2,1,0:T(1,128)} %get-tuple-element.24), channel_id=1, replica_groups=mesh['groups'=2,'dp'=16] {'dp'}, dimensions={0} | all-to-all | bytes 98304 | tf_op jit(solution)/shard_map/all_to_all | solution.py:521
  238.0 3.5 %close.1 = (bf16[512,2048]{1,0:T(8,128)(2,1)}, f32[2,128]{1,0:T(2,128)}) custom-call(s32[2,128]{1,0:T(2,128)} %bitcast.15, f32[16,1,768]{2,1,0:T(1,128)} %all_to_all.15.got_hbm, f32[256,4096]{1,0:T(8,128)} %get-tuple-element.25.sums_hbm), custom_call_target="tpu_custom_call" | custom-call | flops 2097152 | bytes 6291456 | tf_op jit(solution)/shard_map/close/pallas_call | solution.py:497
  (13 shorter events, 0.1 us)
Async XLA Ops:
  9.3 134.2 %all-to-all-start = ((s16[16,1712,128]{2,1,0:T(8,128)(2,1)}), s16[16,1712,128]{2,1,0:T(8,128)(2,1)}, u32[]{:S(2)}, u32[]{:S(2)}) async-start(s16[16,1712,128]{2,1,0:T(8,128)(2,1)} %get-tuple-element.15), calls=%async_computation | async-start | bytes 14024704 | tf_op jit(solution)/shard_map/all_to_all | solution.py:521
  16.7 160.3 %copy-start.2 = (s32[256]{0:T(256)S(1)}, s32[256]{0:T(256)}, u32[]{:S(2)}) copy-start(s32[256]{0:T(256)} %constant.83.clone) | copy-start | bytes 3076
  16.7 160.6 %copy-start.1 = (s32[256]{0:T(256)S(1)}, s32[256]{0:T(256)}, u32[]{:S(2)}) copy-start(s32[256]{0:T(256)} %constant.84.clone) | copy-start | bytes 3076
  143.5 62.9 %all-to-all-start.1 = ((s16[16,384,128]{2,1,0:T(8,128)(2,1)}), s16[16,384,128]{2,1,0:T(8,128)(2,1)S(1)}, u32[]{:S(2)}, u32[]{:S(2)}) async-start(s16[16,384,128]{2,1,0:T(8,128)(2,1)} %get-tuple-element.17), calls=%async_computation.1 | async-start | bytes 3145728 | tf_op jit(solution)/shard_map/all_to_all | solution.py:521
  206.4 1.1 copy-start
